TPU v7x, 32 devices: a whole 2x2x4 slice. The times are simulated.
32 devices in a mesh: wide: 8 (over z, x), narrow: 4 (over y, core).
Axes of the slice: x: 2, y: 2, z: 4, core: 2. Of those that a mesh axis runs over, the one named last changes fastest.
Arguments:
- charges: bfloat16 [16, 32, 256, 256], P('narrow', 'wide'), may hold values from -6 to 6
- positions: float32 [16, 32, 2, 256], P('narrow', 'wide'), may hold values from -1 to 2
- noise: float32 [16, 32, 256], P('narrow', 'wide'), may hold values from 0.1 to 1
- leaf_basis: bfloat16 [16, 32, 64, 256], P('narrow', 'wide'), may hold values from -0.375 to 0.375
- transfer: bfloat16 [4, 8, 21, 64, 64], P('narrow', 'wide'), may hold values from -0.75 to 0.75
- near_list: int32 [16, 32, 10], P('narrow', 'wide'), may hold values from -1 to 24, as said below
Outputs:
- potential: bfloat16 [16, 32, 256, 256], P('narrow', 'wide')
Inputs may be any that keep to these rules, and one draw needn't show every extreme that they name: `near_list`: A code names the offset (dy, dx) as (dy + 2) * 5 + dx + 2. Each leaf's list holds the nine codes with max(|dy|, |dx|) <= 1 and at most one code with max(|dy|, |dx|) = 2, each code once, in any order, with -1 in a slot left empty; some leaf holds ten codes.
All inputs are finite; a program needn't handle non-finite values.
Results may differ from a plain program's by a relative error of at most 0.006.
Values may be sent and summed in bfloat16 or wider, within the bound.
No kernel may reach another device: no remote copies, remote signals or barrier semaphores. Data moves between devices by JAX's collectives and lax.ppermute only.
A program may use at most 128 MiB of HBM per device.

v0:
```python
import math

import jax
import jax.numpy as jnp
import numpy as np
from jax import lax
from jax.sharding import PartitionSpec as P

LEAF = 256
CHEB = 8
RANK = 64
LEVELS = 2
SIDE = 4


short_len = 0.125
long_weight = 0.03125
wave_number = 20.0 * math.pi


def passed_along(value, axis, steps):
    count = lax.axis_size(axis)
    first, last = (max(0, -steps), min(count, count - steps))
    return lax.ppermute(value, axis, [(source, source + steps) for source in range(first, last)])


def with_halo(block, sides, width):
    for axis, dim in sides:
        count = lax.axis_size(axis)
        forward = [(i, i + 1) for i in range(count - 1)]
        backward = [(target, source) for source, target in forward]
        low = lax.ppermute(
            lax.slice_in_dim(block, block.shape[dim] - width, None, axis=dim), axis, forward
        )
        high = lax.ppermute(lax.slice_in_dim(block, 0, width, axis=dim), axis, backward)
        block = jnp.concatenate([low, block, high], axis=dim)
    return block


def partner(array, axis, apart):
    return lax.ppermute(array, axis, [(i, i ^ 1 << apart) for i in range(lax.axis_size(axis))])


def kernel(squared):
    envelope = jnp.exp(squared * (-0.5 / (3.0 * SIDE * 3.0 * SIDE)))
    return jnp.exp(squared * (-0.5 / (short_len * short_len))) + long_weight * envelope * jnp.cos(
        wave_number * jnp.sqrt(squared)
    )


def coupling(box_width, shift_y, shift_x):
    angles = (2.0 * jnp.arange(CHEB, dtype=jnp.float32) + 1.0) * (math.pi / (2.0 * CHEB))
    points = 0.5 * box_width * (1.0 + jnp.cos(angles))
    node_x = jnp.tile(points, CHEB)
    node_y = jnp.repeat(points, CHEB)
    offset_x = jnp.asarray(shift_x, jnp.float32)[..., None, None] * box_width
    offset_y = jnp.asarray(shift_y, jnp.float32)[..., None, None] * box_width
    gap_x = node_x[:, None] - node_x[None, :] - offset_x
    gap_y = node_y[:, None] - node_y[None, :] - offset_y
    return kernel(gap_x * gap_x + gap_y * gap_y)


def offset_tables(outer_y, outer_x):
    pair_range = np.arange(2)
    corner_grid = np.meshgrid(pair_range, pair_range, pair_range, pair_range, indexing="ij")
    shift_y = 2 * outer_y + corner_grid[0] - corner_grid[2]
    shift_x = 2 * outer_x + corner_grid[1] - corner_grid[3]
    reach_max = np.maximum(np.abs(shift_y), np.abs(shift_x))
    cycle_mask = (reach_max >= 2).astype(np.float32)
    return (shift_y, shift_x, cycle_mask)


def level_offset(height):
    return sum(((SIDE >> lower_level) ** 2 for lower_level in range(height)))


def local_far(padded, height):
    extent = padded.shape[0] - 4
    half_extent = extent // 2
    sample_count = padded.shape[-1]
    blocks = padded.reshape(half_extent + 2, 2, half_extent + 2, 2, RANK, sample_count)
    box_width = float(2**height)
    accumulated = jnp.zeros((half_extent, 2, half_extent, 2, RANK, sample_count), jnp.float32)
    for outer_y in (-1, 0, 1):
        for outer_x in (-1, 0, 1):
            source = blocks[
                1 + outer_y : 1 + outer_y + half_extent, :, 1 + outer_x : 1 + outer_x + half_extent
            ]
            shift_y, shift_x, cycle_mask = offset_tables(outer_y, outer_x)
            couple = (
                coupling(box_width, shift_y, shift_x) * jnp.asarray(cycle_mask)[..., None, None]
            ).astype(jnp.bfloat16)
            accumulated = accumulated + jnp.einsum(
                "abcdkm,yaxbmr->ycxdkr", couple, source, preferred_element_type=jnp.float32
            )
    return accumulated.reshape(extent, extent, RANK, sample_count)


def listed_correction(padded, near_list):
    padded_side = padded.shape[0]
    extent = padded_side - 4
    code_y = near_list // 5 - 2
    code_x = near_list % 5 - 2
    cycle_flag = (near_list >= 0) & (jnp.maximum(jnp.abs(code_y), jnp.abs(code_x)) == 2)
    chosen = jnp.max(jnp.where(cycle_flag, near_list, -1), axis=-1)
    present = chosen >= 0
    safe_code = jnp.where(present, chosen, 12)
    shift_y = safe_code // 5 - 2
    shift_x = safe_code % 5 - 2
    local_ids = jnp.arange(extent, dtype=jnp.int32)
    source_index = (
        (local_ids[:, None] + 2 + shift_y) * padded_side + local_ids[None, :] + 2 + shift_x
    )
    sources = jnp.take(
        padded.reshape(padded_side * padded_side, RANK, padded.shape[-1]), source_index, axis=0
    )
    all_codes = np.arange(25)
    code_couplings = coupling(1.0, all_codes // 5 - 2, all_codes % 5 - 2).astype(jnp.bfloat16)
    picked = jnp.take(code_couplings, safe_code, axis=0)
    picked = jnp.where(present[..., None, None], picked, jnp.zeros_like(picked))
    return jnp.einsum("yxkm,yxmr->yxkr", picked, sources, preferred_element_type=jnp.float32)


def window_far(window, box_width, parity_y, parity_x):
    shift_values = np.arange(7) - 3
    shift_y, shift_x = np.meshgrid(shift_values, shift_values, indexing="ij")
    cycle_mask = jnp.asarray(np.maximum(np.abs(shift_y), np.abs(shift_x)) >= 2)
    shift_ids = jnp.asarray(shift_values, jnp.int32)
    inside_y = (parity_y + shift_ids >= -2) & (parity_y + shift_ids <= 3)
    inside_x = (parity_x + shift_ids >= -2) & (parity_x + shift_ids <= 3)
    keep_mask = (cycle_mask & inside_y[:, None] & inside_x[None, :]).astype(jnp.float32)
    couple = (coupling(box_width, shift_y, shift_x) * keep_mask[..., None, None]).astype(
        jnp.bfloat16
    )
    return jnp.einsum("yxkm,yxmr->kr", couple, window, preferred_element_type=jnp.float32)


def device_window(device_coef):
    strip = jnp.stack(
        [
            device_coef if offset == 0 else passed_along(device_coef, "wide", -offset)
            for offset in range(-3, 4)
        ]
    )
    window = jnp.stack(
        [
            strip if offset == 0 else passed_along(strip, "narrow", -offset)
            for offset in range(-3, 4)
        ]
    )
    return window


def parent_window(parent_coef):
    strip = jnp.stack(
        [
            parent_coef if offset == 0 else passed_along(parent_coef, "wide", -2 * offset)
            for offset in range(-3, 4)
        ]
    )
    window = jnp.stack(
        [
            strip if offset == 0 else passed_along(strip, "narrow", -2 * offset)
            for offset in range(-3, 4)
        ]
    )
    return window


def near_part(charges, positions, near_list):
    padded = with_halo(charges, (("wide", 1), ("narrow", 0)), 2)
    placed = with_halo(positions, (("wide", 1), ("narrow", 0)), 2)
    padded_side = SIDE + 4
    flat_charges = padded.reshape(padded_side * padded_side, LEAF, charges.shape[-1])
    flat_points = placed.reshape(padded_side * padded_side, 2, LEAF)
    column_ids = jnp.arange(SIDE, dtype=jnp.int32)

    def leaf_row(row_index):
        code_row = near_list[row_index]
        present = code_row >= 0
        shift_y = jnp.where(present, code_row // 5 - 2, 0)
        shift_x = jnp.where(present, code_row % 5 - 2, 0)
        source_index = (row_index + 2 + shift_y) * padded_side + column_ids[:, None] + 2 + shift_x
        sources = jnp.take(flat_charges, source_index, axis=0)
        source_points = jnp.take(flat_points, source_index, axis=0)
        target = positions[row_index]
        gap_x = (
            target[:, None, 0, :, None]
            - source_points[:, :, 0, None, :]
            - shift_x.astype(jnp.float32)[:, :, None, None]
        )
        gap_y = (
            target[:, None, 1, :, None]
            - source_points[:, :, 1, None, :]
            - shift_y.astype(jnp.float32)[:, :, None, None]
        )
        blocks = jnp.where(
            present[:, :, None, None], kernel(gap_x * gap_x + gap_y * gap_y), 0.0
        ).astype(jnp.bfloat16)
        return jnp.einsum("lsij,lsjr->lir", blocks, sources, preferred_element_type=jnp.float32)

    return lax.map(leaf_row, jnp.arange(SIDE, dtype=jnp.int32))


def far_part(charges, leaf_basis, transfer, near_list):
    packed_tree = transfer[0, 0]
    sample_count = charges.shape[-1]
    coeffs = [
        jnp.einsum(
            "yxkp,yxpr->yxkr", leaf_basis, charges, preferred_element_type=jnp.float32
        ).astype(jnp.bfloat16)
    ]
    for height in range(LEVELS):
        extent = SIDE >> height
        start = level_offset(height)
        matrices = packed_tree[start : start + extent * extent].reshape(extent, extent, RANK, RANK)
        lifted = jnp.einsum(
            "yxkm,yxmr->yxkr", matrices, coeffs[-1], preferred_element_type=jnp.float32
        )
        lifted = lifted.reshape(extent // 2, 2, extent // 2, 2, RANK, sample_count).sum(axis=(1, 3))
        coeffs.append(lifted.astype(jnp.bfloat16))
    device_coef = coeffs[LEVELS][0, 0]
    top_matrix = packed_tree[level_offset(LEVELS)]
    raised = jnp.dot(top_matrix, device_coef, preferred_element_type=jnp.float32)
    raised = raised + partner(raised.astype(jnp.bfloat16), "wide", 0).astype(raised.dtype)
    raised = raised + partner(raised.astype(jnp.bfloat16), "narrow", 0).astype(raised.dtype)
    parent_coef = raised.astype(jnp.bfloat16)
    row_index = lax.axis_index("narrow")
    col_index = lax.axis_index("wide")
    coupled_parent = window_far(
        parent_window(parent_coef), float(2 * SIDE), row_index // 2 % 2, col_index // 2 % 2
    )
    coupled_device = window_far(
        device_window(device_coef), float(SIDE), row_index % 2, col_index % 2
    )
    coupled = []
    for height in range(LEVELS):
        padded = with_halo(coeffs[height], (("wide", 1), ("narrow", 0)), 2)
        level_sum = local_far(padded, height)
        if height == 0:
            level_sum = level_sum - listed_correction(padded, near_list)
        coupled.append(level_sum)
    field = coupled_parent.astype(jnp.bfloat16)
    summed = coupled_device + jnp.einsum(
        "km,kr->mr", top_matrix, field, preferred_element_type=jnp.float32
    )
    field = summed.astype(jnp.bfloat16)[None, None]
    for height in range(LEVELS - 1, -1, -1):
        extent = SIDE >> height
        start = level_offset(height)
        matrices = packed_tree[start : start + extent * extent].reshape(extent, extent, RANK, RANK)
        spread = jnp.broadcast_to(
            field[:, None, :, None], (extent // 2, 2, extent // 2, 2, RANK, sample_count)
        )
        spread = spread.reshape(extent, extent, RANK, sample_count)
        summed = coupled[height] + jnp.einsum(
            "yxkm,yxkr->yxmr", matrices, spread, preferred_element_type=jnp.float32
        )
        field = summed.astype(jnp.bfloat16)
    return jnp.einsum("yxkp,yxkr->yxpr", leaf_basis, field, preferred_element_type=jnp.float32)


def per_device(charges, positions, noise, leaf_basis, transfer, near_list):
    near_field = near_part(charges, positions, near_list)
    far_field = far_part(charges, leaf_basis, transfer, near_list)
    combined = near_field + noise[..., None] * charges.astype(jnp.float32) + far_field
    return combined.astype(jnp.bfloat16)


def solution(mesh):
    in_specs = (
        P("narrow", "wide", None, None),
        P("narrow", "wide", None, None),
        P("narrow", "wide", None),
        P("narrow", "wide", None, None),
        P("narrow", "wide", None, None, None),
        P("narrow", "wide", None),
    )
    out_specs = P("narrow", "wide", None, None)
    return jax.shard_map(
        per_device, mesh=mesh, in_specs=in_specs, out_specs=out_specs, check_vma=False
    )
```

profile of v0, /device:TPU:1, one launch (start us, length us, event | category | flops | bytes accessed | tf_op | source)
XLA Modules:
  0.0 552.3 jit_solution(10795821547638426188)
XLA Ops:
  8.5 5.5 %collective-permute-start.16 = (bf16[64,256]{1,0:T(8,128)(2,1)S(1)}, bf16[64,256]{1,0:T(8,128)(2,1)}, u32[]{:S(2)}, u32[]{:S(2)}) collective-permute-start(bf16[64,256]{1,0:T(8,128)(2,1)S(1)} %bitcast.557), channel_id=1, source_target_pairs={{0,12},{4,16},{8,20},{12,24},{16,28},{1,13},{5,17},{9,21},{13,25},... | collective-permute-start | bytes 98312 | tf_op jit(solution)/shard_map/ppermute | solution.py:24
  14.0 3.8 collective-permute-start.17
  22.9 4.6 collective-permute-start
  53.7 4.7 fusion.123
  82.9 4.0 collective-permute-start.8
  87.7 7.9 %collective-permute-start.2 = (f32[2,8,2,256]{3,2,1,0:T(2,128)S(1)}, f32[2,8,2,256]{3,2,1,0:T(2,128)S(1)}, u32[]{:S(2)}, u32[]{:S(2)}) collective-permute-start(f32[2,8,2,256]{3,2,1,0:T(2,128)S(1)} %get-tuple-element.225), channel_id=1, source_target_pairs={{0,1},{1,2},{2,3},{4,5},{5,6},{6,7},{8,9},{9,10},{10,11},{12,13},{... | collective-permute-start | bytes 98312 | tf_op jit(solution)/shard_map/ppermute | solution.py:32
  102.2 8.5 %collective-permute-start.30 = (bf16[64,256]{1,0:T(8,128)(2,1)S(1)}, bf16[64,256]{1,0:T(8,128)(2,1)S(1)}, u32[]{:S(2)}, u32[]{:S(2)}) collective-permute-start(bf16[64,256]{1,0:T(8,128)(2,1)S(1)} %add_convert_fusion), channel_id=1, source_target_pairs={{0,24},{4,28},{1,25},{5,29},{2,26},{6,30},{3,27},{7,31}} | collective-permute-start | bytes 98312 | tf_op jit(solution)/shard_map/ppermute | solution.py:24
  114.0 6.8 %collective-permute-start.32 = (bf16[64,256]{1,0:T(8,128)(2,1)S(1)}, bf16[64,256]{1,0:T(8,128)(2,1)S(1)}, u32[]{:S(2)}, u32[]{:S(2)}) collective-permute-start(bf16[64,256]{1,0:T(8,128)(2,1)S(1)} %add_convert_fusion), channel_id=1, source_target_pairs={{0,8},{4,12},{8,16},{12,20},{16,24},{20,28},{1,9},{5,13},{9,17},{1... | collective-permute-start | bytes 98312 | tf_op jit(solution)/shard_map/ppermute | solution.py:24
  128.0 4.2 collective-permute-done.34
  133.6 5.1 collective-permute-done.35
  146.8 9.6 %collective-permute-start.24 = (bf16[7,64,256]{2,1,0:T(8,128)(2,1)S(1)}, bf16[7,64,256]{2,1,0:T(8,128)(2,1)S(1)}, u32[]{:S(2)}, u32[]{:S(2)}) collective-permute-start(bf16[7,64,256]{2,1,0:T(8,128)(2,1)S(1)} %constant_dynamic-update-slice_fusion.6), channel_id=1, source_target_pairs={{0,1},{1,2},{2,3},{4,5},{5,6},{6,7},{8,9},{9,10},{10,11},{12,13},{... | collective-permute-start | bytes 688136 | tf_op jit(solution)/shard_map/ppermute | solution.py:24
  162.1 3.9 collective-permute-done.25
  172.3 6.3 %collective-permute-start.14 = (bf16[2,6,64,256]{3,2,1,0:T(8,128)(2,1)}, bf16[2,6,64,256]{3,2,1,0:T(8,128)(2,1)}, u32[]{:S(2)}, u32[]{:S(2)}) collective-permute-start(bf16[2,6,64,256]{3,2,1,0:T(8,128)(2,1)} %pad_maximum_fusion.4), channel_id=1, source_target_pairs={{0,1},{1,2},{2,3},{4,5},{5,6},{6,7},{8,9},{9,10},{10,11},{12,13},{... | collective-permute-start | bytes 1179656 | tf_op jit(solution)/shard_map/ppermute | solution.py:32
  180.6 3.9 collective-permute-start.10
  185.7 8.8 %convolution_bitcast_fusion.22 = f32[64,256]{1,0:T(8,128)} fusion(bf16[7,7,64,256]{3,2,1,0:T(8,128)(2,1)} %copy-done.25, bf16[1,1,21,64,64]{4,3,2,1,0:T(8,128)(2,1)} %param.76, f32[7,7]{1,0:T(8,128)} %constant.421, f32[7,7]{1,0:T(8,128)} %constant.420, f32[7,7]{1,0:T(8,128)} %get-tuple-element.235, f32[64,64]{1,0:T(8,128)} %get-tuple-element.246, ...), kind=kOutput, calls=%fused_computation.157 | convolution fusion | flops 107483136 | bytes 1765376 | tf_op jit(solution)/shard_map/km,kr->mr/dot_general | solution.py:244
  194.6 8.9 %fusion.109 = bf16[64,256]{1,0:T(8,128)(2,1)S(1)} fusion(f32[64,256]{1,0:T(8,128)} %convolution_bitcast_fusion.22, bf16[7,7,64,256]{3,2,1,0:T(8,128)(2,1)} %copy-done.24, f32[7,7]{1,0:T(8,128)} %constant.419, f32[7,7]{1,0:T(8,128)} %constant.418, f32[7,7]{1,0:T(8,128)S(1)} %copy-done.32, f32[64,64]{1,0:T(8,128)} %get-tuple-element.248, ...), kind=kOutput, calls=%fused_computation.162 | convolution fusion | flops 105402368 | bytes 1737292 | tf_op jit(solution)/shard_map/yxkm,yxmr->kr/dot_general | solution.py:135
  276.7 7.2 %pad_maximum_fusion = bf16[8,8,256,256]{3,2,1,0:T(8,128)(2,1)} fusion(bf16[2,8,256,256]{3,2,1,0:T(8,128)(2,1)} %collective-permute-done.7, bf16[4,8,256,256]{3,2,1,0:T(8,128)(2,1)} %copy-done.4, bf16[2,8,256,256]{3,2,1,0:T(8,128)(2,1)} %collective-permute-done.6), kind=kLoop, calls=%fused_computation.71 | loop fusion | flops 8388608 | bytes 16777216 | tf_op jit(solution)/shard_map/concatenate | solution.py:36
  283.9 258.3 %while.15 = (s32[]{:T(128)}, f32[4,4,256,256]{2,3,1,0:T(8,128)}, s32[4]{0:T(128)S(1)}, s32[4,4,10]{2,1,0:T(4,128)S(1)}, f32[4,4,2,256]{3,2,1,0:T(2,128)}, /*inde...) while((s32[]{:T(128)}, f32[4,4,256,256]{2,3,1,0:T(8,128)}, ...), condition=%wide.region_1.2_spmd.clone, body=%wide.region_0.1_spmd.clone.sunk | while | flops 1384144384 | bytes 28065356 | solution.py:202
  287.6 8.0 %gather_fusion.1 = bf16[40,256,256]{2,1,0:T(8,128)(2,1)} fusion(bf16[64,256,256]{2,1,0:T(8,128)(2,1)} %get-tuple-element.337, s32[1024]{0:T(1024)S(1)} %pad_clamp_fusion.4), kind=kCustom, calls=%fused_computation.1.clone.1 | custom fusion | bytes 10485920 | tf_op jit(solution)/shard_map/while/body/eval_jaxpr/jit(_take)/gather | solution.py:184
  295.5 5.4 fusion.698
  302.6 46.0 %fusion.699 = f32[4,4,256,256]{2,3,1,0:T(8,128)} fusion(f32[4,4,256,256]{2,3,1,0:T(8,128)} %get-tuple-element.321, s32[]{:T(128)} %get-tuple-element.320, f32[4,10]{1,0:T(4,128)S(1)} %get-tuple-element.302, f32[4,10,256]{2,1,0:T(8,128)S(1)} %copy.238, f32[4,256]{1,0:T(4,128)S(1)} %get-tuple-element.305, f32[4,10]{1,0:T(4,128)S(1)} %get-tuple-element.306, ...), kind=kOutput, calls=%fused_computation.22.clone.3 | convolution fusion | flops 1381498880 | bytes 6382440 | tf_op jit(solution)/shard_map/while/body/eval_jaxpr/lsij,lsjr->lir/dot_general | solution.py:200
  352.1 8.0 %gather_fusion.1 = bf16[40,256,256]{2,1,0:T(8,128)(2,1)} fusion(bf16[64,256,256]{2,1,0:T(8,128)(2,1)} %get-tuple-element.337, s32[1024]{0:T(1024)S(1)} %pad_clamp_fusion.4), kind=kCustom, calls=%fused_computation.1.clone.1 | custom fusion | bytes 10485920 | tf_op jit(solution)/shard_map/while/body/eval_jaxpr/jit(_take)/gather | solution.py:184
  360.1 5.4 fusion.698
  367.1 46.0 %fusion.699 = f32[4,4,256,256]{2,3,1,0:T(8,128)} fusion(f32[4,4,256,256]{2,3,1,0:T(8,128)} %get-tuple-element.321, s32[]{:T(128)} %get-tuple-element.320, f32[4,10]{1,0:T(4,128)S(1)} %get-tuple-element.302, f32[4,10,256]{2,1,0:T(8,128)S(1)} %copy.238, f32[4,256]{1,0:T(4,128)S(1)} %get-tuple-element.305, f32[4,10]{1,0:T(4,128)S(1)} %get-tuple-element.306, ...), kind=kOutput, calls=%fused_computation.22.clone.3 | convolution fusion | flops 1381498880 | bytes 6382440 | tf_op jit(solution)/shard_map/while/body/eval_jaxpr/lsij,lsjr->lir/dot_general | solution.py:200
  416.6 8.0 %gather_fusion.1 = bf16[40,256,256]{2,1,0:T(8,128)(2,1)} fusion(bf16[64,256,256]{2,1,0:T(8,128)(2,1)} %get-tuple-element.337, s32[1024]{0:T(1024)S(1)} %pad_clamp_fusion.4), kind=kCustom, calls=%fused_computation.1.clone.1 | custom fusion | bytes 10485920 | tf_op jit(solution)/shard_map/while/body/eval_jaxpr/jit(_take)/gather | solution.py:184
  424.6 5.4 fusion.698
  431.7 46.0 %fusion.699 = f32[4,4,256,256]{2,3,1,0:T(8,128)} fusion(f32[4,4,256,256]{2,3,1,0:T(8,128)} %get-tuple-element.321, s32[]{:T(128)} %get-tuple-element.320, f32[4,10]{1,0:T(4,128)S(1)} %get-tuple-element.302, f32[4,10,256]{2,1,0:T(8,128)S(1)} %copy.238, f32[4,256]{1,0:T(4,128)S(1)} %get-tuple-element.305, f32[4,10]{1,0:T(4,128)S(1)} %get-tuple-element.306, ...), kind=kOutput, calls=%fused_computation.22.clone.3 | convolution fusion | flops 1381498880 | bytes 6382440 | tf_op jit(solution)/shard_map/while/body/eval_jaxpr/lsij,lsjr->lir/dot_general | solution.py:200
  481.2 8.0 %gather_fusion.1 = bf16[40,256,256]{2,1,0:T(8,128)(2,1)} fusion(bf16[64,256,256]{2,1,0:T(8,128)(2,1)} %get-tuple-element.337, s32[1024]{0:T(1024)S(1)} %pad_clamp_fusion.4), kind=kCustom, calls=%fused_computation.1.clone.1 | custom fusion | bytes 10485920 | tf_op jit(solution)/shard_map/while/body/eval_jaxpr/jit(_take)/gather | solution.py:184
  489.1 5.4 fusion.698
  496.2 46.0 %fusion.699 = f32[4,4,256,256]{2,3,1,0:T(8,128)} fusion(f32[4,4,256,256]{2,3,1,0:T(8,128)} %get-tuple-element.321, s32[]{:T(128)} %get-tuple-element.320, f32[4,10]{1,0:T(4,128)S(1)} %get-tuple-element.302, f32[4,10,256]{2,1,0:T(8,128)S(1)} %copy.238, f32[4,256]{1,0:T(4,128)S(1)} %get-tuple-element.305, f32[4,10]{1,0:T(4,128)S(1)} %get-tuple-element.306, ...), kind=kOutput, calls=%fused_computation.22.clone.3 | convolution fusion | flops 1381498880 | bytes 6382440 | tf_op jit(solution)/shard_map/while/body/eval_jaxpr/lsij,lsjr->lir/dot_general | solution.py:200
  542.2 5.8 %fusion.45 = bf16[4,4,256,256]{2,3,1,0:T(8,128)(2,1)} fusion(f32[4,4,256,256]{3,2,1,0:T(8,128)} %fusion.87, f32[4,4,256,256]{2,3,1,0:T(8,128)} %get-tuple-element.152, bf16[4,4,256,256]{2,3,1,0:T(8,128)(2,1)S(1)} %copy-done.5, f32[4,4,256]{2,1,0:T(4,128)S(1)} %copy-done.28), kind=kLoop, calls=%fused_computation.73 | loop fusion | flops 5242880 | bytes 12599296 | tf_op jit(solution)/shard_map/convert_element_type | solution.py:267
  548.0 4.1 copy.112
  (348 shorter events, 188.7 us)
Async XLA Ops:
  8.5 63.3 %collective-permute-start.16 = (bf16[64,256]{1,0:T(8,128)(2,1)S(1)}, bf16[64,256]{1,0:T(8,128)(2,1)}, u32[]{:S(2)}, u32[]{:S(2)}) collective-permute-start(bf16[64,256]{1,0:T(8,128)(2,1)S(1)} %bitcast.557), channel_id=1, source_target_pairs={{0,12},{4,16},{8,20},{12,24},{16,28},{1,13},{5,17},{9,21},{13,25},... | collective-permute-start | bytes 98312 | tf_op jit(solution)/shard_map/ppermute | solution.py:24
  14.0 59.8 %collective-permute-start.17 = (bf16[64,256]{1,0:T(8,128)(2,1)S(1)}, bf16[64,256]{1,0:T(8,128)(2,1)}, u32[]{:S(2)}, u32[]{:S(2)}) collective-permute-start(bf16[64,256]{1,0:T(8,128)(2,1)S(1)} %bitcast.558), channel_id=1, source_target_pairs={{0,8},{4,12},{8,16},{12,20},{16,24},{20,28},{1,9},{5,13},{9,17},{1... | collective-permute-start | bytes 98312 | tf_op jit(solution)/shard_map/ppermute | solution.py:24
  17.8 60.0 %collective-permute-start.18 = (bf16[64,256]{1,0:T(8,128)(2,1)S(1)}, bf16[64,256]{1,0:T(8,128)(2,1)}, u32[]{:S(2)}, u32[]{:S(2)}) collective-permute-start(bf16[64,256]{1,0:T(8,128)(2,1)S(1)} %bitcast.559), channel_id=1, source_target_pairs={{0,4},{4,8},{8,12},{12,16},{16,20},{20,24},{24,28},{1,5},{5,9},{9,... | collective-permute-start | bytes 98312 | tf_op jit(solution)/shard_map/ppermute | solution.py:24
  21.0 61.9 %collective-permute-start.19 = (bf16[64,256]{1,0:T(8,128)(2,1)S(1)}, bf16[64,256]{1,0:T(8,128)(2,1)}, u32[]{:S(2)}, u32[]{:S(2)}) collective-permute-start(bf16[64,256]{1,0:T(8,128)(2,1)S(1)} %bitcast.560), channel_id=1, source_target_pairs={{4,0},{8,4},{12,8},{16,12},{20,16},{24,20},{28,24},{5,1},{9,5},{13... | collective-permute-start | bytes 98312 | tf_op jit(solution)/shard_map/ppermute | solution.py:24
  22.9 42.8 %collective-permute-start = (f32[4,2,2,256]{3,2,1,0:T(2,128)}, f32[4,2,2,256]{3,2,1,0:T(2,128)}, u32[]{:S(2)}, u32[]{:S(2)}) collective-permute-start(f32[4,2,2,256]{3,2,1,0:T(2,128)} %get-tuple-element.228), channel_id=1, source_target_pairs={{0,4},{4,8},{8,12},{12,16},{16,20},{20,24},{24,28},{1,5},{5,9},{9,... | collective-permute-start | bytes 49160 | tf_op jit(solution)/shard_map/ppermute | solution.py:32
  70.5 17.2 %collective-permute-start.20 = (bf16[64,256]{1,0:T(8,128)(2,1)S(1)}, bf16[64,256]{1,0:T(8,128)(2,1)S(1)}, u32[]{:S(2)}, u32[]{:S(2)}) collective-permute-start(bf16[64,256]{1,0:T(8,128)(2,1)S(1)} %bitcast.561), channel_id=1, source_target_pairs={{8,0},{12,4},{16,8},{20,12},{24,16},{28,20},{9,1},{13,5},{17,9},{2... | collective-permute-start | bytes 98312 | tf_op jit(solution)/shard_map/ppermute | solution.py:24
  71.8 23.9 %collective-permute-start.21 = (bf16[64,256]{1,0:T(8,128)(2,1)S(1)}, bf16[64,256]{1,0:T(8,128)(2,1)S(1)}, u32[]{:S(2)}, u32[]{:S(2)}) collective-permute-start(bf16[64,256]{1,0:T(8,128)(2,1)S(1)} %bitcast.562), channel_id=1, source_target_pairs={{12,0},{16,4},{20,8},{24,12},{28,16},{13,1},{17,5},{21,9},{25,13},... | collective-permute-start | bytes 98312 | tf_op jit(solution)/shard_map/ppermute | solution.py:24
  73.8 67.2 %collective-permute-start.12 = (bf16[2,2,64,256]{3,2,1,0:T(8,128)(2,1)}, bf16[2,2,64,256]{3,2,1,0:T(8,128)(2,1)S(1)}, u32[]{:S(2)}, u32[]{:S(2)}) collective-permute-start(bf16[2,2,64,256]{3,2,1,0:T(8,128)(2,1)} %reduce_sum.8), channel_id=1, source_target_pairs={{0,4},{4,8},{8,12},{12,16},{16,20},{20,24},{24,28},{1,5},{5,9},{9,... | collective-permute-start | bytes 393224 | tf_op jit(solution)/shard_map/ppermute | solution.py:32
  81.6 60.7 %collective-permute-start.13 = (bf16[2,2,64,256]{3,2,1,0:T(8,128)(2,1)}, bf16[2,2,64,256]{3,2,1,0:T(8,128)(2,1)S(1)}, u32[]{:S(2)}, u32[]{:S(2)}) collective-permute-start(bf16[2,2,64,256]{3,2,1,0:T(8,128)(2,1)} %reduce_sum.8), channel_id=1, source_target_pairs={{4,0},{8,4},{12,8},{16,12},{20,16},{24,20},{28,24},{5,1},{9,5},{13... | collective-permute-start | bytes 393224 | tf_op jit(solution)/shard_map/ppermute | solution.py:35
  82.9 61.8 %collective-permute-start.8 = (bf16[4,2,64,256]{3,2,1,0:T(8,128)(2,1)}, bf16[4,2,64,256]{3,2,1,0:T(8,128)(2,1)S(1)}, u32[]{:S(2)}, u32[]{:S(2)}) collective-permute-start(bf16[4,2,64,256]{3,2,1,0:T(8,128)(2,1)} %get-tuple-element.223), channel_id=1, source_target_pairs={{0,4},{4,8},{8,12},{12,16},{16,20},{20,24},{24,28},{1,5},{5,9},{9,... | collective-permute-start | bytes 786440 | tf_op jit(solution)/shard_map/ppermute | solution.py:32
  87.7 11.3 %collective-permute-start.2 = (f32[2,8,2,256]{3,2,1,0:T(2,128)S(1)}, f32[2,8,2,256]{3,2,1,0:T(2,128)S(1)}, u32[]{:S(2)}, u32[]{:S(2)}) collective-permute-start(f32[2,8,2,256]{3,2,1,0:T(2,128)S(1)} %get-tuple-element.225), channel_id=1, source_target_pairs={{0,1},{1,2},{2,3},{4,5},{5,6},{6,7},{8,9},{9,10},{10,11},{12,13},{... | collective-permute-start | bytes 98312 | tf_op jit(solution)/shard_map/ppermute | solution.py:32
  99.0 47.7 %collective-permute-start.9 = (bf16[4,2,64,256]{3,2,1,0:T(8,128)(2,1)}, bf16[4,2,64,256]{3,2,1,0:T(8,128)(2,1)S(1)}, u32[]{:S(2)}, u32[]{:S(2)}) collective-permute-start(bf16[4,2,64,256]{3,2,1,0:T(8,128)(2,1)} %get-tuple-element.224), channel_id=1, source_target_pairs={{4,0},{8,4},{12,8},{16,12},{20,16},{24,20},{28,24},{5,1},{9,5},{13... | collective-permute-start | bytes 786440 | tf_op jit(solution)/shard_map/ppermute | solution.py:35
  102.2 9.5 %collective-permute-start.30 = (bf16[64,256]{1,0:T(8,128)(2,1)S(1)}, bf16[64,256]{1,0:T(8,128)(2,1)S(1)}, u32[]{:S(2)}, u32[]{:S(2)}) collective-permute-start(bf16[64,256]{1,0:T(8,128)(2,1)S(1)} %add_convert_fusion), channel_id=1, source_target_pairs={{0,24},{4,28},{1,25},{5,29},{2,26},{6,30},{3,27},{7,31}} | collective-permute-start | bytes 98312 | tf_op jit(solution)/shard_map/ppermute | solution.py:24
  114.0 7.8 %collective-permute-start.32 = (bf16[64,256]{1,0:T(8,128)(2,1)S(1)}, bf16[64,256]{1,0:T(8,128)(2,1)S(1)}, u32[]{:S(2)}, u32[]{:S(2)}) collective-permute-start(bf16[64,256]{1,0:T(8,128)(2,1)S(1)} %add_convert_fusion), channel_id=1, source_target_pairs={{0,8},{4,12},{8,16},{12,20},{16,24},{20,28},{1,9},{5,13},{9,17},{1... | collective-permute-start | bytes 98312 | tf_op jit(solution)/shard_map/ppermute | solution.py:24
  132.3 6.4 %collective-permute-start.35 = (bf16[64,256]{1,0:T(8,128)(2,1)S(1)}, bf16[64,256]{1,0:T(8,128)(2,1)S(1)}, u32[]{:S(2)}, u32[]{:S(2)}) collective-permute-start(bf16[64,256]{1,0:T(8,128)(2,1)S(1)} %add_convert_fusion), channel_id=1, source_target_pairs={{24,0},{28,4},{25,1},{29,5},{26,2},{30,6},{27,3},{31,7}} | collective-permute-start | bytes 98312 | tf_op jit(solution)/shard_map/ppermute | solution.py:24
  138.7 100.7 %collective-permute-start.4 = (bf16[4,2,256,256]{3,2,1,0:T(8,128)(2,1)}, bf16[4,2,256,256]{3,2,1,0:T(8,128)(2,1)}, u32[]{:S(2)}, u32[]{:S(2)}) collective-permute-start(bf16[4,2,256,256]{3,2,1,0:T(8,128)(2,1)} %get-tuple-element.211), channel_id=1, source_target_pairs={{0,4},{4,8},{8,12},{12,16},{16,20},{20,24},{24,28},{1,5},{5,9},{9,... | collective-permute-start | bytes 3145736 | tf_op jit(solution)/shard_map/ppermute | solution.py:32
  141.0 99.9 %collective-permute-start.5 = (bf16[4,2,256,256]{3,2,1,0:T(8,128)(2,1)}, bf16[4,2,256,256]{3,2,1,0:T(8,128)(2,1)}, u32[]{:S(2)}, u32[]{:S(2)}) collective-permute-start(bf16[4,2,256,256]{3,2,1,0:T(8,128)(2,1)} %get-tuple-element.210), channel_id=1, source_target_pairs={{4,0},{8,4},{12,8},{16,12},{20,16},{24,20},{28,24},{5,1},{9,5},{13... | collective-permute-start | bytes 3145736 | tf_op jit(solution)/shard_map/ppermute | solution.py:35
  142.3 15.3 %collective-permute-start.22 = (bf16[7,64,256]{2,1,0:T(8,128)(2,1)S(1)}, bf16[7,64,256]{2,1,0:T(8,128)(2,1)S(1)}, u32[]{:S(2)}, u32[]{:S(2)}) collective-permute-start(bf16[7,64,256]{2,1,0:T(8,128)(2,1)S(1)} %constant_dynamic-update-slice_fusion.6), channel_id=1, source_target_pairs={{0,3},{4,7},{8,11},{12,15},{16,19},{20,23},{24,27},{28,31}} | collective-permute-start | bytes 688136 | tf_op jit(solution)/shard_map/ppermute | solution.py:24
  144.7 15.3 %collective-permute-start.23 = (bf16[7,64,256]{2,1,0:T(8,128)(2,1)S(1)}, bf16[7,64,256]{2,1,0:T(8,128)(2,1)S(1)}, u32[]{:S(2)}, u32[]{:S(2)}) collective-permute-start(bf16[7,64,256]{2,1,0:T(8,128)(2,1)S(1)} %constant_dynamic-update-slice_fusion.6), channel_id=1, source_target_pairs={{0,2},{1,3},{4,6},{5,7},{8,10},{9,11},{12,14},{13,15},{16,18},{17,... | collective-permute-start | bytes 688136 | tf_op jit(solution)/shard_map/ppermute | solution.py:24
  146.8 14.5 %collective-permute-start.24 = (bf16[7,64,256]{2,1,0:T(8,128)(2,1)S(1)}, bf16[7,64,256]{2,1,0:T(8,128)(2,1)S(1)}, u32[]{:S(2)}, u32[]{:S(2)}) collective-permute-start(bf16[7,64,256]{2,1,0:T(8,128)(2,1)S(1)} %constant_dynamic-update-slice_fusion.6), channel_id=1, source_target_pairs={{0,1},{1,2},{2,3},{4,5},{5,6},{6,7},{8,9},{9,10},{10,11},{12,13},{... | collective-permute-start | bytes 688136 | tf_op jit(solution)/shard_map/ppermute | solution.py:24
  157.6 8.3 %collective-permute-start.25 = (bf16[7,64,256]{2,1,0:T(8,128)(2,1)S(1)}, bf16[7,64,256]{2,1,0:T(8,128)(2,1)S(1)}, u32[]{:S(2)}, u32[]{:S(2)}) collective-permute-start(bf16[7,64,256]{2,1,0:T(8,128)(2,1)S(1)} %constant_dynamic-update-slice_fusion.6), channel_id=1, source_target_pairs={{1,0},{2,1},{3,2},{5,4},{6,5},{7,6},{9,8},{10,9},{11,10},{13,12},{... | collective-permute-start | bytes 688136 | tf_op jit(solution)/shard_map/ppermute | solution.py:24
  160.0 9.6 %collective-permute-start.26 = (bf16[7,64,256]{2,1,0:T(8,128)(2,1)S(1)}, bf16[7,64,256]{2,1,0:T(8,128)(2,1)S(1)}, u32[]{:S(2)}, u32[]{:S(2)}) collective-permute-start(bf16[7,64,256]{2,1,0:T(8,128)(2,1)S(1)} %constant_dynamic-update-slice_fusion.6), channel_id=1, source_target_pairs={{2,0},{3,1},{6,4},{7,5},{10,8},{11,9},{14,12},{15,13},{18,16},{19,... | collective-permute-start | bytes 688136 | tf_op jit(solution)/shard_map/ppermute | solution.py:24
  161.3 9.6 %collective-permute-start.27 = (bf16[7,64,256]{2,1,0:T(8,128)(2,1)S(1)}, bf16[7,64,256]{2,1,0:T(8,128)(2,1)S(1)}, u32[]{:S(2)}, u32[]{:S(2)}) collective-permute-start(bf16[7,64,256]{2,1,0:T(8,128)(2,1)S(1)} %constant_dynamic-update-slice_fusion.6), channel_id=1, source_target_pairs={{3,0},{7,4},{11,8},{15,12},{19,16},{23,20},{27,24},{31,28}} | collective-permute-start | bytes 688136 | tf_op jit(solution)/shard_map/ppermute | solution.py:24
  166.0 6.3 %collective-permute-start.36 = (bf16[7,64,256]{2,1,0:T(8,128)(2,1)S(1)}, bf16[7,64,256]{2,1,0:T(8,128)(2,1)S(1)}, u32[]{:S(2)}, u32[]{:S(2)}) collective-permute-start(bf16[7,64,256]{2,1,0:T(8,128)(2,1)S(1)} %constant_dynamic-update-slice_fusion.13), channel_id=1, source_target_pairs={} | collective-permute-start | bytes 688136 | tf_op jit(solution)/shard_map/ppermute | solution.py:24
  169.6 9.0 %collective-permute-start.37 = (bf16[7,64,256]{2,1,0:T(8,128)(2,1)S(1)}, bf16[7,64,256]{2,1,0:T(8,128)(2,1)S(1)}, u32[]{:S(2)}, u32[]{:S(2)}) collective-permute-start(bf16[7,64,256]{2,1,0:T(8,128)(2,1)S(1)} %constant_dynamic-update-slice_fusion.13), channel_id=1, source_target_pairs={{0,2},{1,3},{4,6},{5,7},{8,10},{9,11},{12,14},{13,15},{16,18},{17,... | collective-permute-start | bytes 688136 | tf_op jit(solution)/shard_map/ppermute | solution.py:24
  170.9 9.7 %collective-permute-start.38 = (bf16[7,64,256]{2,1,0:T(8,128)(2,1)S(1)}, bf16[7,64,256]{2,1,0:T(8,128)(2,1)S(1)}, u32[]{:S(2)}, u32[]{:S(2)}) collective-permute-start(bf16[7,64,256]{2,1,0:T(8,128)(2,1)S(1)} %constant_dynamic-update-slice_fusion.13), channel_id=1, source_target_pairs={{2,0},{3,1},{6,4},{7,5},{10,8},{11,9},{14,12},{15,13},{18,16},{19,... | collective-permute-start | bytes 688136 | tf_op jit(solution)/shard_map/ppermute | solution.py:24
  172.3 31.3 %collective-permute-start.14 = (bf16[2,6,64,256]{3,2,1,0:T(8,128)(2,1)}, bf16[2,6,64,256]{3,2,1,0:T(8,128)(2,1)}, u32[]{:S(2)}, u32[]{:S(2)}) collective-permute-start(bf16[2,6,64,256]{3,2,1,0:T(8,128)(2,1)} %pad_maximum_fusion.4), channel_id=1, source_target_pairs={{0,1},{1,2},{2,3},{4,5},{5,6},{6,7},{8,9},{9,10},{10,11},{12,13},{... | collective-permute-start | bytes 1179656 | tf_op jit(solution)/shard_map/ppermute | solution.py:32
  178.6 27.3 %collective-permute-start.15 = (bf16[2,6,64,256]{3,2,1,0:T(8,128)(2,1)}, bf16[2,6,64,256]{3,2,1,0:T(8,128)(2,1)}, u32[]{:S(2)}, u32[]{:S(2)}) collective-permute-start(bf16[2,6,64,256]{3,2,1,0:T(8,128)(2,1)} %pad_maximum_fusion.4), channel_id=1, source_target_pairs={{1,0},{2,1},{3,2},{5,4},{6,5},{7,6},{9,8},{10,9},{11,10},{13,12},{... | collective-permute-start | bytes 1179656 | tf_op jit(solution)/shard_map/ppermute | solution.py:35
  180.6 48.7 %collective-permute-start.10 = (bf16[2,8,64,256]{3,2,1,0:T(8,128)(2,1)}, bf16[2,8,64,256]{3,2,1,0:T(8,128)(2,1)}, u32[]{:S(2)}, u32[]{:S(2)}) collective-permute-start(bf16[2,8,64,256]{3,2,1,0:T(8,128)(2,1)} %get-tuple-element.221), channel_id=1, source_target_pairs={{0,1},{1,2},{2,3},{4,5},{5,6},{6,7},{8,9},{9,10},{10,11},{12,13},{... | collective-permute-start | bytes 1572872 | tf_op jit(solution)/shard_map/ppermute | solution.py:32
  203.6 25.7 %collective-permute-start.11 = (bf16[2,8,64,256]{3,2,1,0:T(8,128)(2,1)S(1)}, bf16[2,8,64,256]{3,2,1,0:T(8,128)(2,1)S(1)}, u32[]{:S(2)}, u32[]{:S(2)}) collective-permute-start(bf16[2,8,64,256]{3,2,1,0:T(8,128)(2,1)S(1)} %copy-done.17), channel_id=1, source_target_pairs={{1,0},{2,1},{3,2},{5,4},{6,5},{7,6},{9,8},{10,9},{11,10},{13,12},{... | collective-permute-start | bytes 1572872 | tf_op jit(solution)/shard_map/ppermute | solution.py:35
  245.4 27.8 %collective-permute-start.6 = (bf16[2,8,256,256]{3,2,1,0:T(8,128)(2,1)}, bf16[2,8,256,256]{3,2,1,0:T(8,128)(2,1)}, u32[]{:S(2)}, u32[]{:S(2)}) collective-permute-start(bf16[2,8,256,256]{3,2,1,0:T(8,128)(2,1)} %get-tuple-element.208), channel_id=1, source_target_pairs={{0,1},{1,2},{2,3},{4,5},{5,6},{6,7},{8,9},{9,10},{10,11},{12,13},{... | collective-permute-start | bytes 6291464 | tf_op jit(solution)/shard_map/ppermute | solution.py:32
  249.1 27.7 %collective-permute-start.7 = (bf16[2,8,256,256]{3,2,1,0:T(8,128)(2,1)}, bf16[2,8,256,256]{3,2,1,0:T(8,128)(2,1)}, u32[]{:S(2)}, u32[]{:S(2)}) collective-permute-start(bf16[2,8,256,256]{3,2,1,0:T(8,128)(2,1)} %get-tuple-element.209), channel_id=1, source_target_pairs={{1,0},{2,1},{3,2},{5,4},{6,5},{7,6},{9,8},{10,9},{11,10},{13,12},{... | collective-permute-start | bytes 6291464 | tf_op jit(solution)/shard_map/ppermute | solution.py:35
  (58 other events, 804.7 us)
where the time goes:
time: 562 us; the launch traced here: 552 us
  matrix products  256 us (46%)
  starting transfers between devices  108 us (19%)
  local copies, waits for them, and re-layouts  83 us (15%)
  other arithmetic  59.7 us (11%)
  waiting for transfers between devices  33.1 us (6%)
  loops' own time  10.7 us (2%)
    dot_general x4, matrix products, leaf_row(): jnp.einsum('lsij,lsjr->lir', blocks, sources, preferred_element_type=jnp....  184 us
    ppermute x21, starting transfers between devices, passed_along(): lax.ppermute(value, axis, [(source, source + steps) for source in range(f...  56.6 us
    dot_general x18, matrix products, local_far(): jnp.einsum('abcdkm,yaxbmr->ycxdkr', couple, source, preferred_element_typ...  43 us
    ppermute x8, starting transfers between devices, with_halo(): lax.ppermute(lax.slice_in_dim(block, block.shape[dim] - width, None, axis...  35.7 us
    gather x4, local copies, waits for them, and re-layouts, leaf_row(): sources = jnp.take(flat_charges, source_index, axis=0)  31.9 us
    ppermute x21, waiting for transfers between devices, passed_along(): lax.ppermute(value, axis, [(source, source + steps) for source in range(f...  22.8 us
    dot_general x4, other arithmetic, leaf_row(): jnp.einsum('lsij,lsjr->lir', blocks, sources, preferred_element_type=jnp....  21.8 us
    ppermute x8, starting transfers between devices, with_halo(): lax.ppermute(lax.slice_in_dim(block, 0, width, axis=dim), axis, backward)  13.9 us
  transfers between devices with their start and end apart: 39, of which 13 were waited for; matrix products, arithmetic and copies ran while one was open for 21% of the time, Pallas kernels for 0%

commit v1 on v0

v1 whole, which is shorter than its diff:
```python
import math

import jax
import jax.numpy as jnp
import ml_dtypes
import numpy as np
from jax import lax
from jax.experimental import pallas as pl
from jax.experimental.pallas import tpu as pltpu
from jax.sharding import PartitionSpec as P

LEAF = 256
CHEB = 8
RANK = 64
NEAR = 10
SIDE = 4
LEAVES = SIDE * SIDE
TOP = 20
WINDOW = 36
PACK = RANK + 16
SIDEWAYS = 8 * RANK + 4 * RANK + 48
CORNER = 4 * RANK + 4 * RANK + 48
BF = jnp.bfloat16
F32 = jnp.float32

short_len = 0.125
long_weight = 0.03125
reach = 3.0 * SIDE
waves = 10.0
LOG2E = math.log2(math.e)
long_rate = -0.5 / (reach * reach) * LOG2E / (waves * waves)
short_rate = -0.5 / (short_len * short_len) * LOG2E / (waves * waves)
rounder = 1.5 * 2.0**23


def sine_terms(count):
    w = np.cos(np.pi * (np.arange(2000) + 0.5) / 2000) * 0.25
    powers = np.stack([w ** (2 * i + 1) for i in range(count)], 1)
    return [float(c) for c in np.linalg.lstsq(powers, np.sin(2 * np.pi * w) * long_weight, rcond=None)[0]]


SINE = sine_terms(4)


def coupling(height, shift_y, shift_x):
    points = 0.5 * (1.0 + np.cos((2.0 * np.arange(CHEB) + 1.0) * (math.pi / (2.0 * CHEB))))
    node_x = np.tile(points, CHEB)
    node_y = np.repeat(points, CHEB)
    gap_x = (node_x[:, None] - node_x[None, :] - shift_x) * 2.0**height
    gap_y = (node_y[:, None] - node_y[None, :] - shift_y) * 2.0**height
    squared = gap_x * gap_x + gap_y * gap_y
    return np.exp(squared * (-0.5 / (short_len * short_len))) + long_weight * np.exp(
        squared * (-0.5 / (reach * reach))
    ) * np.cos(2.0 * math.pi * waves * np.sqrt(squared))


def window_coupling(height):
    table = np.zeros((2, 2, RANK, 6, 6, RANK))
    for py in range(2):
        for px in range(2):
            for wy in range(6):
                for wx in range(6):
                    shift_y, shift_x = wy - 2 - py, wx - 2 - px
                    if max(abs(shift_y), abs(shift_x)) >= 2:
                        table[py, px, :, wy, wx] = coupling(height, shift_y, shift_x)
    return table.reshape(4 * RANK, WINDOW * RANK).astype(ml_dtypes.bfloat16)


def code_coupling():
    return np.stack([coupling(0, code // 5 - 2, code % 5 - 2) for code in range(25)]).astype(ml_dtypes.bfloat16)


def halo_slot(row, col):
    if 0 <= row < 4 and 0 <= col < 4:
        return row * 4 + col
    if 0 <= row < 4:
        return 16 + row * 2 + col + 2 if col < 0 else 24 + row * 2 + col - 4
    base, r = (32, row + 2) if row < 0 else (48, row - 4)
    if 0 <= col < 4:
        return base + r * 4 + col
    return base + 8 + r * 2 + col + 2 if col < 0 else base + 12 + r * 2 + col - 4


SLOT_OF = np.array([halo_slot(r - 2, c - 2) for r in range(8) for c in range(8)], np.int32)


def near_table(own):
    width = 9 if own else 5
    table = np.zeros((LEAVES, width, 3), np.int32)
    table[:, :, 0] = -1
    for r in range(SIDE):
        for c in range(SIDE):
            at = 0
            for dy in (-1, 0, 1):
                for dx in (-1, 0, 1):
                    slot = halo_slot(r + dy, c + dx)
                    if (slot < LEAVES) == own:
                        table[r * SIDE + c, at] = (slot, dy, dx)
                        at += 1
    return table


def bits(count):
    return [1 << i for i in range(count.bit_length() - 1)]


def gather_steps(wide, narrow):
    return (
        [("wide", 1), ("narrow", 1)]
        + [("wide", b) for b in reversed(bits(wide)[1:])]
        + [("narrow", b) for b in reversed(bits(narrow)[1:])]
    )


def shift(value, axis, steps):
    count = lax.axis_size(axis)
    return lax.ppermute(value, axis, [(i, i + steps) for i in range(count) if 0 <= i + steps < count])


def dot(a, b):
    return jnp.dot(a, b, preferred_element_type=F32)


def dot_first(a, b):
    return lax.dot_general(a, b, (((0,), (0,)), ((), ())), preferred_element_type=F32)


def up_body(q_ref, basis_ref, tree_ref, pos_ref, east_ref, west_ref, north_ref, south_ref, coef_ref, give_ref):
    level0 = []
    for leaf in range(LEAVES):
        coef = dot(basis_ref[leaf], q_ref[leaf]).astype(BF)
        level0.append(coef)
        r, c = leaf // SIDE, leaf % SIDE
        coef_ref[leaf * RANK : (leaf + 1) * RANK] = coef
        ref, at = (west_ref, r * 2 + c) if c < 2 else (east_ref, r * 2 + c - 2)
        ref[at * RANK : (at + 1) * RANK] = coef
        ref, at = (north_ref, r * 4 + c) if r < 2 else (south_ref, r * 4 + c - 8)
        ref[at * RANK : (at + 1) * RANK] = coef
    level1 = []
    for r in range(2):
        for c in range(2):
            total = None
            for dr in range(2):
                for dc in range(2):
                    leaf = (2 * r + dr) * SIDE + 2 * c + dc
                    part = dot(tree_ref[leaf], level0[leaf])
                    total = part if total is None else total + part
            coef = total.astype(BF)
            at = r * 2 + c
            level1.append(coef)
            coef_ref[(LEAVES + at) * RANK : (LEAVES + at + 1) * RANK] = coef
            for ref in (east_ref, west_ref, north_ref, south_ref):
                ref[(8 + at) * RANK : (9 + at) * RANK] = coef
    total = None
    for at in range(4):
        part = dot(tree_ref[LEAVES + at], level1[at])
        total = part if total is None else total + part
    give_ref[0:RANK] = total.astype(BF)
    top = tree_ref[TOP]
    give_ref[RANK:PACK] = jnp.concatenate([top[16 * k : 16 * k + 16] for k in range(4)], axis=1)
    for ref, leaves in (
        (west_ref, [r * 4 + c for r in range(4) for c in (0, 1)]),
        (east_ref, [r * 4 + c for r in range(4) for c in (2, 3)]),
        (north_ref, range(8)),
        (south_ref, range(8, 16)),
    ):
        rest = jnp.concatenate([pos_ref[leaf] for leaf in leaves], axis=0)
        for part in range(3):
            held = rest.astype(BF)
            at = 12 * RANK + 16 * part
            ref[at : at + 16] = held
            rest = rest - held.astype(F32)


def go_up(q, basis, tree, points):
    vmem = pl.BlockSpec(memory_space=pltpu.VMEM)
    side = jax.ShapeDtypeStruct((SIDEWAYS, LEAF), BF)
    return pl.pallas_call(
        up_body,
        out_shape=(
            side,
            side,
            side,
            side,
            jax.ShapeDtypeStruct(((LEAVES + 4) * RANK, LEAF), BF),
            jax.ShapeDtypeStruct((PACK, LEAF), BF),
        ),
        in_specs=[vmem] * 4,
        out_specs=[vmem] * 6,
        compiler_params=pltpu.CompilerParams(vmem_limit_bytes=32 << 20),
        cost_estimate=pl.CostEstimate(flops=300_000_000, bytes_accessed=5_000_000, transcendentals=0),
        name="upward",
    )(q, basis, tree, points)


def far_body(
    list_ref,
    meta_ref,
    coef_ref,
    west_ref,
    east_ref,
    north_ref,
    south_ref,
    all_ref,
    c0_ref,
    c1_ref,
    c2_ref,
    c3_ref,
    code_ref,
    tree_ref,
    field_ref,
    pad0,
    pad1,
    win,
    parents,
    sum0,
):
    def put(pad, extent, row, col, ref, at, count):
        to = ((row + 2) * (extent + 4) + col + 2) * RANK
        pad[to : to + count * RANK] = ref[at * RANK : (at + count) * RANK]

    for r in range(4):
        put(pad0, 4, r, 0, coef_ref, r * 4, 4)
        put(pad0, 4, r, -2, west_ref, r * 2, 2)
        put(pad0, 4, r, 4, east_ref, r * 2, 2)
    for ref, row in ((north_ref, -2), (south_ref, 4)):
        for r in range(2):
            put(pad0, 4, row + r, 0, ref, r * 4, 4)
    for r in range(2):
        put(pad1, 2, r, 0, coef_ref, LEAVES + r * 2, 2)
        put(pad1, 2, r, -2, west_ref, 8 + r * 2, 2)
        put(pad1, 2, r, 2, east_ref, 8 + r * 2, 2)
    for ref, row in ((north_ref, -2), (south_ref, 2)):
        for r in range(2):
            put(pad1, 2, row + r, 0, ref, 8 + r * 2, 2)
    for ref, row0, row1 in ((north_ref, -2, -2), (south_ref, 4, 2)):
        for col0, col1, base in ((-2, -2, SIDEWAYS), (4, 2, SIDEWAYS + CORNER)):
            for r in range(2):
                to = ((row0 + r + 2) * 8 + col0 + 2) * RANK
                pad0[to : to + 2 * RANK] = ref[base + r * 2 * RANK : base + (r + 1) * 2 * RANK]
                to = ((row1 + r + 2) * 6 + col1 + 2) * RANK
                pad1[to : to + 2 * RANK] = ref[base + (4 + r * 2) * RANK : base + (6 + r * 2) * RANK]

    for a in range(2):
        for b in range(2):
            total = None
            for wy in range(6):
                at = ((2 * a + wy) * 8 + 2 * b) * RANK
                part = dot(c0_ref[:, wy * 6 * RANK : (wy + 1) * 6 * RANK], pad0[at : at + 6 * RANK])
                total = part if total is None else total + part
            for child in range(4):
                leaf = (2 * a + child // 2) * SIDE + 2 * b + child % 2
                sum0[leaf] = total[child * RANK : (child + 1) * RANK]

    def listed(leaf, carry):
        code = second_cycle(list_ref, leaf)

        @pl.when(code >= 0)
        def _():
            row = leaf // SIDE + code // 5
            col = leaf % SIDE + code % 5
            at = pl.multiple_of((row * 8 + col) * RANK, RANK)
            sum0[leaf] = sum0[leaf] - dot(code_ref[code], pad0[pl.ds(at, RANK)])

        return carry

    lax.fori_loop(0, LEAVES, listed, 0)
    sum1 = dot(c1_ref[...], pad1[...])

    def lift(group, carry):
        total = jnp.zeros((RANK, LEAF), F32)
        for child in range(4):
            at = pl.multiple_of((group * 4 + child) * PACK, 16)
            packed = all_ref[pl.ds(at + RANK, 16)]
            matrix = jnp.concatenate([packed[:, k * RANK : (k + 1) * RANK] for k in range(4)], axis=0)
            total = total + dot(matrix, all_ref[pl.ds(at, RANK)])
        parents[pl.ds(pl.multiple_of(group * RANK, RANK), RANK)] = total.astype(BF)
        return carry

    lax.fori_loop(0, parents.shape[0] // RANK, lift, 0)

    def fill(start, source, stride):
        def one(i, carry):
            slot = meta_ref[start + i]
            to = pl.ds(pl.multiple_of(i * RANK, RANK), RANK)

            @pl.when(slot >= 0)
            def _():
                win[to] = source[pl.ds(pl.multiple_of(slot * stride, 16), RANK)]

            @pl.when(slot < 0)
            def _():
                win[to] = jnp.zeros((RANK, LEAF), BF)

            return carry

        lax.fori_loop(0, WINDOW, one, 0)

    fill(WINDOW, parents, RANK)
    part = pl.ds(pl.multiple_of(meta_ref[2 * WINDOW + 1] * RANK, RANK), RANK)
    field3 = dot(c3_ref[part], win[...]).astype(BF)
    fill(0, all_ref, PACK)
    part = pl.ds(pl.multiple_of(meta_ref[2 * WINDOW] * RANK, RANK), RANK)
    field2 = (dot(c2_ref[part], win[...]) + dot_first(tree_ref[TOP], field3)).astype(BF)
    field1 = []
    for at in range(4):
        field1.append(
            (sum1[at * RANK : (at + 1) * RANK] + dot_first(tree_ref[LEAVES + at], field2)).astype(BF)
        )
    for leaf in range(LEAVES):
        above = field1[leaf // SIDE // 2 * 2 + leaf % SIDE // 2]
        field_ref[leaf] = (sum0[leaf] + dot_first(tree_ref[leaf], above)).astype(BF)


def second_cycle(list_ref, leaf):
    found = jnp.int32(-1)
    for j in range(NEAR):
        code = list_ref[leaf * NEAR + j]
        y, x = code // 5, code % 5
        outer = (code >= 0) & ((y == 0) | (y == 4) | (x == 0) | (x == 4))
        found = jnp.where(outer, code, found)
    return found


def far_field(near_list, meta, coefs, west, east, north, south, gathered, tree):
    vmem = pl.BlockSpec(memory_space=pltpu.VMEM)
    smem = pl.BlockSpec(memory_space=pltpu.SMEM)
    devices = gathered.shape[0] // PACK
    return pl.pallas_call(
        far_body,
        out_shape=jax.ShapeDtypeStruct((LEAVES, RANK, LEAF), BF),
        in_specs=[smem, smem] + [vmem] * 12,
        out_specs=vmem,
        scratch_shapes=[
            pltpu.VMEM((64 * RANK, LEAF), BF),
            pltpu.VMEM((WINDOW * RANK, LEAF), BF),
            pltpu.VMEM((WINDOW * RANK, LEAF), BF),
            pltpu.VMEM((devices // 4 * RANK, LEAF), BF),
            pltpu.VMEM((LEAVES, RANK, LEAF), F32),
        ],
        compiler_params=pltpu.CompilerParams(vmem_limit_bytes=40 << 20),
        cost_estimate=pl.CostEstimate(flops=2_500_000_000, bytes_accessed=12_000_000, transcendentals=0),
        name="far",
    )(
        near_list,
        meta,
        coefs,
        west,
        east,
        north,
        south,
        gathered,
        *[jnp.asarray(window_coupling(height)) for height in range(4)],
        jnp.asarray(code_coupling()),
        tree,
    )


def kernel_of(target_x, target_y, source_x, source_y):
    gap_x = target_x - source_x
    gap_y = target_y - source_y
    squared = jnp.maximum(gap_x * gap_x + gap_y * gap_y, 1e-12)
    length = squared * lax.rsqrt(squared)
    phase = length - ((length + rounder) - rounder)
    w = 0.25 - jnp.abs(phase)
    s = w * w
    wave = w * (SINE[0] + s * (SINE[1] + s * (SINE[2] + s * SINE[3])))
    return (jnp.exp2(squared * short_rate) + jnp.exp2(squared * long_rate) * wave).astype(BF)


def spread_columns(rows, columns):
    turned = rows.T
    for k in range(columns.shape[1] // 128):
        columns[:, 128 * k : 128 * (k + 1)] = jnp.broadcast_to(turned[:, k : k + 1], (LEAF, 128))


def block_into(to, columns, points, shift_y, shift_x):
    source_x = (points[0:1] + shift_x.astype(F32)) * waves
    source_y = (points[1:2] + shift_y.astype(F32)) * waves
    rows = 32
    for i in range(0, LEAF, rows):
        for j in (0, 128):
            to[i : i + rows, j : j + 128] = kernel_of(
                columns[i : i + rows, 0:128],
                columns[i : i + rows, 128:256],
                jnp.broadcast_to(source_x[:, j : j + 128], (rows, 128)),
                jnp.broadcast_to(source_y[:, j : j + 128], (rows, 128)),
            )


def near_own_body(list_ref, table_ref, slot_ref, q_ref, pos_ref, noise_ref, out_ref, columns, blocks):
    leaf = pl.program_id(0)
    rows = jnp.concatenate([pos_ref[leaf] * waves, noise_ref[leaf], jnp.zeros((5, LEAF), F32)], axis=0)
    spread_columns(rows, columns)
    width = table_ref.shape[0] // (3 * LEAVES)
    own = q_ref[leaf].astype(F32)
    for j in (0, 128):
        out_ref[0, :, j : j + 128] = columns[:, 256:384] * own[:, j : j + 128]

    def one(j, carry):
        at = (leaf * width + j) * 3
        slot = table_ref[at]

        @pl.when(slot >= 0)
        def _():
            block_into(blocks.at[j], columns, pos_ref[slot], table_ref[at + 1], table_ref[at + 2])

        @pl.when(slot < 0)
        def _():
            blocks[j] = jnp.zeros((LEAF, LEAF), BF)

        return carry

    lax.fori_loop(0, width, one, 0)
    total = out_ref[0]
    for j in range(width):
        slot = jnp.maximum(table_ref[(leaf * width + j) * 3], 0)
        total = total + dot(blocks[j], q_ref[slot])
    out_ref[0] = total
    code = second_cycle(list_ref, leaf)
    place = (leaf // SIDE + code // 5) * 8 + leaf % SIDE + code % 5
    slot = slot_ref[jnp.where(code >= 0, place, 0)]

    @pl.when((code >= 0) & (slot < LEAVES))
    def _():
        block_into(blocks.at[0], columns, pos_ref[slot], code // 5 - 2, code % 5 - 2)
        out_ref[0] += dot(blocks[0], q_ref[slot])


def near_own(near_list, q, points, noise):
    vmem = pl.BlockSpec(memory_space=pltpu.VMEM)
    smem = pl.BlockSpec(memory_space=pltpu.SMEM)
    return pl.pallas_call(
        near_own_body,
        grid=(LEAVES,),
        out_shape=jax.ShapeDtypeStruct((LEAVES, LEAF, LEAF), F32),
        in_specs=[smem, smem, smem, vmem, vmem, vmem],
        out_specs=pl.BlockSpec((1, LEAF, LEAF), lambda i: (i, 0, 0)),
        scratch_shapes=[pltpu.VMEM((LEAF, 384), F32), pltpu.VMEM((9, LEAF, LEAF), BF)],
        compiler_params=pltpu.CompilerParams(vmem_limit_bytes=32 << 20),
        cost_estimate=pl.CostEstimate(flops=20_000_000_000, bytes_accessed=7_000_000, transcendentals=20_000_000),
        name="near_own",
    )(near_list, jnp.asarray(near_table(True).reshape(-1)), jnp.asarray(SLOT_OF), q, points, noise)


def near_halo_body(
    list_ref,
    table_ref,
    slot_ref,
    west_ref,
    east_ref,
    north_ref,
    north_corner_ref,
    south_ref,
    south_corner_ref,
    own_pos_ref,
    pos_ref,
    sum_ref,
    basis_ref,
    field_ref,
    out_ref,
    columns,
    blocks,
    held,
    total_ref,
    sems,
):
    leaf = pl.program_id(0)
    copies = [
        pltpu.make_async_copy(ref, held.at[pl.ds(8 * k, 8)], sems.at[k])
        for k, ref in enumerate(
            (west_ref, east_ref, north_ref, north_corner_ref, south_ref, south_corner_ref)
        )
    ]

    @pl.when(leaf == 0)
    def _():
        for copy in copies:
            copy.start()

    rows = jnp.concatenate([own_pos_ref[leaf] * waves, jnp.zeros((6, LEAF), F32)], axis=0)
    spread_columns(rows, columns)
    width = table_ref.shape[0] // (3 * LEAVES)

    def one(j, carry):
        at = (leaf * width + j) * 3
        slot = table_ref[at]

        @pl.when(slot >= 0)
        def _():
            block_into(blocks.at[j], columns, pos_ref[slot - LEAVES], table_ref[at + 1], table_ref[at + 2])

        return carry

    lax.fori_loop(0, width, one, 0)

    @pl.when(leaf == 0)
    def _():
        for copy in copies:
            copy.wait()


    def add(j, total):
        slot = table_ref[(leaf * width + j) * 3]
        return total + dot(blocks[j], held[slot - LEAVES])

    row, col = leaf // SIDE, leaf % SIDE
    edge_y = (row == 0) | (row == SIDE - 1)
    edge_x = (col == 0) | (col == SIDE - 1)
    corner = edge_y & edge_x
    total_ref[...] = sum_ref[0] + dot_first(basis_ref[leaf], field_ref[leaf])

    @pl.when(edge_y | edge_x)
    def _():
        total = total_ref[...]
        for j in range(3):
            total = add(j, total)
        total_ref[...] = total

    @pl.when(corner)
    def _():
        total = total_ref[...]
        for j in range(3, 5):
            total = add(j, total)
        total_ref[...] = total

    code = second_cycle(list_ref, leaf)
    place = (leaf // SIDE + code // 5) * 8 + leaf % SIDE + code % 5
    slot = slot_ref[jnp.where(code >= 0, place, 0)]

    @pl.when((code >= 0) & (slot >= LEAVES))
    def _():
        block_into(blocks.at[0], columns, pos_ref[slot - LEAVES], code // 5 - 2, code % 5 - 2)
        total_ref[...] += dot(blocks[0], held[slot - LEAVES])

    out_ref[0] = total_ref[...].astype(BF)


def near_halo(near_list, halos, own_points, halo_points, near_sum, basis, field):
    vmem = pl.BlockSpec(memory_space=pltpu.VMEM)
    smem = pl.BlockSpec(memory_space=pltpu.SMEM)
    block = pl.BlockSpec((1, LEAF, LEAF), lambda i: (i, 0, 0))
    return pl.pallas_call(
        near_halo_body,
        grid=(LEAVES,),
        out_shape=jax.ShapeDtypeStruct((LEAVES, LEAF, LEAF), BF),
        in_specs=[smem, smem, smem] + [pl.BlockSpec(memory_space=pl.ANY)] * 6 + [vmem, vmem, block, vmem, vmem],
        out_specs=block,
        scratch_shapes=[
            pltpu.VMEM((LEAF, 256), F32),
            pltpu.VMEM((5, LEAF, LEAF), BF),
            pltpu.VMEM((48, LEAF, LEAF), BF),
            pltpu.VMEM((LEAF, LEAF), F32),
            pltpu.SemaphoreType.DMA((6,)),
        ],
        compiler_params=pltpu.CompilerParams(vmem_limit_bytes=32 << 20),
        cost_estimate=pl.CostEstimate(flops=8_000_000_000, bytes_accessed=14_000_000, transcendentals=8_000_000),
        name="near_halo",
    )(
        near_list,
        jnp.asarray(near_table(False).reshape(-1)),
        jnp.asarray(SLOT_OF),
        *halos,
        own_points,
        halo_points,
        near_sum,
        basis,
        field,
    )


def points_of(message, leaves_at):
    parts = message[leaves_at : leaves_at + 48].astype(F32)
    whole = (parts[0:16] + parts[16:32]) + parts[32:48]
    return whole.reshape(8, 2, LEAF)


def window_slots(wide, narrow, steps):
    row, col = lax.axis_index("narrow"), lax.axis_index("wide")
    wy, wx = np.arange(WINDOW) // 6, np.arange(WINDOW) % 6

    def slots(target_y, target_x, scale):
        y = target_y // 2 * 2 - 2 + wy
        x = target_x // 2 * 2 - 2 + wx
        inside = (y >= 0) & (y < narrow // scale) & (x >= 0) & (x < wide // scale)
        apart = {"narrow": (y * scale) ^ row, "wide": (x * scale) ^ col}
        slot = 0
        for at, (axis, bit) in enumerate(steps):
            slot = slot + (apart[axis] // bit & 1) * (1 << at)
        return jnp.where(inside, slot if scale == 1 else slot // 4, -1)

    parity2 = row % 2 * 2 + col % 2
    parity3 = row // 2 % 2 * 2 + col // 2 % 2
    return jnp.concatenate(
        [slots(row, col, 1), slots(row // 2, col // 2, 2), jnp.stack([parity2, parity3])]
    ).astype(jnp.int32)


def per_device(wide, narrow, charges, positions, noise, leaf_basis, transfer, near_list):
    q = charges.reshape(LEAVES, LEAF, LEAF)
    points = positions.reshape(LEAVES, 2, LEAF)
    basis = leaf_basis.reshape(LEAVES, RANK, LEAF)
    tree = transfer[0, 0]
    listing = near_list.reshape(-1)
    steps = gather_steps(wide, narrow)
    meta = window_slots(wide, narrow, steps)

    east, west, north, south, coefs, give = go_up(q, basis, tree, points)
    from_west = shift(east, "wide", 1)
    from_east = shift(west, "wide", -1)
    gathered = give
    for axis, bit in steps:
        other = lax.ppermute(gathered, axis, [(i, i ^ bit) for i in range(lax.axis_size(axis))])
        gathered = jnp.concatenate([gathered, other], axis=0)

    def corner(message, lower):
        at = 4 * RANK if lower else 0
        return [message[at : at + 4 * RANK], message[8 * RANK :]]

    north = jnp.concatenate([north] + corner(from_west, False) + corner(from_east, False), axis=0)
    south = jnp.concatenate([south] + corner(from_west, True) + corner(from_east, True), axis=0)
    from_south = shift(north, "narrow", -1)
    from_north = shift(south, "narrow", 1)

    q_west = shift(charges[:, 2:4], "wide", 1)
    q_east = shift(charges[:, 0:2], "wide", -1)
    q_north = shift(charges[2:4], "narrow", 1)
    q_south = shift(charges[0:2], "narrow", -1)
    q_north_corner = shift(jnp.stack([q_west[2:4], q_east[2:4]]), "narrow", 1)
    q_south_corner = shift(jnp.stack([q_west[0:2], q_east[0:2]]), "narrow", -1)
    halos = [
        value.reshape(8, LEAF, LEAF)
        for value in (q_west, q_east, q_north, q_north_corner, q_south, q_south_corner)
    ]

    def corner_points(message, lower):
        first = points_of(message, SIDEWAYS + 8 * RANK)
        second = points_of(message, SIDEWAYS + CORNER + 8 * RANK)
        at = 4 if lower else 0
        return [first[at : at + 4], second[at : at + 4]]

    halo_points = jnp.concatenate(
        [points_of(from_west, 12 * RANK), points_of(from_east, 12 * RANK), points_of(from_north, 12 * RANK)]
        + corner_points(from_north, True)
        + [points_of(from_south, 12 * RANK)]
        + corner_points(from_south, False),
        axis=0,
    )

    near_sum = near_own(listing, q, points, noise.reshape(LEAVES, 1, LEAF))
    field = far_field(listing, meta, coefs, from_west, from_east, from_north, from_south, gathered, tree)
    out = near_halo(listing, halos, points, halo_points, near_sum, basis, field)
    return out.reshape(SIDE, SIDE, LEAF, LEAF)


def solution(mesh):
    wide, narrow = mesh.shape["wide"], mesh.shape["narrow"]
    in_specs = (
        P("narrow", "wide", None, None),
        P("narrow", "wide", None, None),
        P("narrow", "wide", None),
        P("narrow", "wide", None, None),
        P("narrow", "wide", None, None, None),
        P("narrow", "wide", None),
    )
    out_specs = P("narrow", "wide", None, None)

    def step(*arrays):
        return per_device(wide, narrow, *arrays)

    return jax.shard_map(step, mesh=mesh, in_specs=in_specs, out_specs=out_specs, check_vma=False)
```

time: 562 us -> 188 us (0.33); the launches traced: 552 us -> 187 us
  matrix products: 256 us -> 0 us
  Pallas kernels: 0 us -> 86.6 us
  starting transfers between devices: 108 us -> 45.4 us
  local copies, waits for them, and re-layouts: 83 us -> 27.8 us
  other arithmetic: 59.7 us -> 4.91 us
  waiting for transfers between devices: 33.1 us -> 21.7 us
  loops' own time: 10.7 us -> 0 us
    dot_general x31 -> x0, matrix products: 256 us -> none  [the longest x4 184 us: leaf_row(): jnp.einsum('lsij,lsjr->lir', blocks, sources, preferred_element_type=jnp....]
    pallas_call x0 -> x4, Pallas kernels: none -> 86.6 us  [the longest x1 44.1 us: near_own(): pl.pallas_call(near_own_body, grid=(LEAVES,), out_shape=jax.ShapeDtypeStr...]
    ppermute x39 -> x15, starting transfers between devices: 108 us -> 45.4 us  [the longest x10 35.6 us: shift(): lax.ppermute(value, axis, [(i, i + steps) for i in range(count) if 0 <= i...]
    gather x10 -> x0, local copies, waits for them, and re-layouts: 38.9 us -> none  [the longest x4 31.9 us: leaf_row(): sources = jnp.take(flat_charges, source_index, axis=0)]
    dot_general x4 -> x0, other arithmetic: 21.8 us -> none  [leaf_row(): jnp.einsum('lsij,lsjr->lir', blocks, sources, preferred_element_type=jnp....]
    ppermute x39 -> x15, waiting for transfers between devices: 33.1 us -> 21.7 us  [the longest x5 21.7 us: per_device(): lax.ppermute(gathered, axis, [(i, i ^ bit) for i in range(lax.axis_size(a...]
    convert_element_type x13 -> x4, other arithmetic: 12.1 us -> 0.81 us  [points_of(): parts = message[leaves_at:leaves_at + 48].astype(F32)]
    another operation x1 -> x0, loops' own time: 10.7 us -> none  [near_part(): return lax.map(leaf_row, jnp.arange(SIDE, dtype=jnp.int32))]
  transfers between devices with their start and end apart: 39 -> 15, of which waited for: 13 -> 4; matrix products, arithmetic and copies ran while one was open for 21% -> 10% of each run, Pallas kernels for 0% -> 29%
where the time goes in v1:
time: 188 us; the launch traced here: 187 us
  Pallas kernels  86.6 us (46%)
  starting transfers between devices  45.4 us (24%)
  local copies, waits for them, and re-layouts  27.8 us (15%)
  waiting for transfers between devices  21.7 us (12%)
  other arithmetic  4.91 us (3%)
    pallas_call x1, Pallas kernels, near_own(): pl.pallas_call(near_own_body, grid=(LEAVES,), out_shape=jax.ShapeDtypeStr...  44.1 us
    ppermute x10, starting transfers between devices, shift(): lax.ppermute(value, axis, [(i, i + steps) for i in range(count) if 0 <= i...  35.6 us
    pallas_call x1, Pallas kernels, near_halo(): pl.pallas_call(near_halo_body, grid=(LEAVES,), out_shape=jax.ShapeDtypeSt...  30.7 us
    ppermute x5, waiting for transfers between devices, per_device(): lax.ppermute(gathered, axis, [(i, i ^ bit) for i in range(lax.axis_size(a...  21.7 us
    unnamed x75, local copies, waits for them, and re-layouts  20.2 us
    pallas_call x1, Pallas kernels, far_field(): pl.pallas_call(far_body, out_shape=jax.ShapeDtypeStruct((LEAVES, RANK, LE...  10.1 us
    ppermute x5, starting transfers between devices, per_device(): lax.ppermute(gathered, axis, [(i, i ^ bit) for i in range(lax.axis_size(a...  9.77 us
  transfers between devices with their start and end apart: 15, of which 4 were waited for; matrix products, arithmetic and copies ran while one was open for 10% of the time, Pallas kernels for 29%

profile of v1, /device:TPU:1, one launch (start us, length us, event | category | flops | bytes accessed | tf_op | source)
XLA Modules:
  0.0 187.0 jit_solution(4008084731018166261)
XLA Ops:
  0.0 1.6 copy-done
  4.4 1.6 upward.1
  6.0 2.0 %collective-permute-start.10 = (bf16[80,256]{1,0:T(8,128)(2,1)S(1)}, bf16[80,256]{1,0:T(8,128)(2,1)S(1)}, u32[]{:S(2)}, u32[]{:S(2)}) collective-permute-start(bf16[80,256]{1,0:T(8,128)(2,1)S(1)} %get-tuple-element.16), channel_id=1, source_target_pairs={{0,4},{4,0},{8,12},{12,8},{16,20},{20,16},{24,28},{28,24},{1,5},{5... | collective-permute-start | bytes 122888 | tf_op jit(solution)/shard_map/ppermute | solution.py:613
  8.0 1.9 %collective-permute-start.6 = (bf16[816,256]{1,0:T(8,128)(2,1)}, bf16[816,256]{1,0:T(8,128)(2,1)S(1)}, u32[]{:S(2)}, u32[]{:S(2)}) collective-permute-start(bf16[816,256]{1,0:T(8,128)(2,1)} %get-tuple-element.11), channel_id=1, source_target_pairs={{0,4},{4,8},{8,12},{12,16},{16,20},{20,24},{24,28},{1,5},{5,9},{9,... | collective-permute-start | bytes 1253384 | tf_op jit(solution)/shard_map/ppermute | solution.py:117
  10.0 1.4 collective-permute-start.7
  11.4 1.5 fusion.3
  12.9 6.0 %collective-permute-start = (bf16[4,2,256,256]{3,2,1,0:T(8,128)(2,1)}, bf16[4,2,256,256]{3,2,1,0:T(8,128)(2,1)}, u32[]{:S(2)}, u32[]{:S(2)}) collective-permute-start(bf16[4,2,256,256]{3,2,1,0:T(8,128)(2,1)} %get-tuple-element.20), channel_id=1, source_target_pairs={{0,4},{4,8},{8,12},{12,16},{16,20},{20,24},{24,28},{1,5},{5,9},{9,... | collective-permute-start | bytes 3145736 | tf_op jit(solution)/shard_map/ppermute | solution.py:117
  18.9 1.3 collective-permute-start.1
  20.3 1.5 fusion.2
  22.8 44.1 %near_own.1.sum_ref = f32[16,256,256]{2,1,0:T(8,128)S(1)} custom-call(s32[160]{0:T(256)S(1)} %reshape.56.list_ref, s32[432]{0:T(512)S(1)} %copy-done.19, s32[64]{0:T(128)S(1)} %copy-done.21, bf16[16,256,256]{2,1,0:T(8,128)(2,1)S(1)} %bitcast.22, f32[16,2,256]{2,1,0:T(2,128)S(1)} %bitcast.28, f32[16,1,256]{2,1,0:T(1,128)S(1)} %reshape.70.noise_ref), custom_call_target="tpu_custom_call" | custom-call | flops 20000000000 | bytes 7000000 | tf_op jit(solution)/shard_map/near_own/pallas_call | solution.py:433
  66.9 2.0 %copy-done.22 = f32[16,256,256]{2,1,0:T(8,128)} copy-done((f32[16,256,256]{2,1,0:T(8,128)}, f32[16,256,256]{2,1,0:T(8,128)S(1)}, u32[]{:S(2)}) %copy-start.22) | copy-done | bytes 4194328
  69.6 1.6 collective-permute-start.11
  72.1 5.5 %collective-permute-start.12 = (bf16[320,256]{1,0:T(8,128)(2,1)S(1)}, bf16[320,256]{1,0:T(8,128)(2,1)S(1)}, u32[]{:S(2)}, u32[]{:S(2)}) collective-permute-start(bf16[320,256]{1,0:T(8,128)(2,1)S(1)} %pad_maximum_fusion.4), channel_id=1, source_target_pairs={{0,16},{4,20},{8,24},{12,28},{16,0},{20,4},{24,8},{28,12},{1,17},{... | collective-permute-start | bytes 491528 | tf_op jit(solution)/shard_map/ppermute | solution.py:613
  78.9 6.5 %collective-permute-done.12 = bf16[320,256]{1,0:T(8,128)(2,1)S(1)} collective-permute-done((bf16[320,256]{1,0:T(8,128)(2,1)S(1)}, bf16[320,256]{1,0:T(8,128)(2,1)S(1)}, u32[]{:S(2)}, u32[]{:S(2)}) %collective-permute-start.12) | collective-permute-done | bytes 163872 | tf_op jit(solution)/shard_map/ppermute | solution.py:613
  85.4 2.4 %collective-permute-start.2 = (bf16[2,4,256,256]{3,2,1,0:T(8,128)(2,1)}, bf16[2,4,256,256]{3,2,1,0:T(8,128)(2,1)}, u32[]{:S(2)}, u32[]{:S(2)}) collective-permute-start(bf16[2,4,256,256]{3,2,1,0:T(8,128)(2,1)} %get-tuple-element.18), channel_id=1, source_target_pairs={{0,1},{1,2},{2,3},{4,5},{5,6},{6,7},{8,9},{9,10},{10,11},{12,13},{... | collective-permute-start | bytes 3145736 | tf_op jit(solution)/shard_map/ppermute | solution.py:117
  89.3 2.9 %collective-permute-start.4 = (bf16[2,4,256,256]{3,2,1,0:T(8,128)(2,1)}, bf16[2,4,256,256]{3,2,1,0:T(8,128)(2,1)}, u32[]{:S(2)}, u32[]{:S(2)}) collective-permute-start(bf16[2,4,256,256]{3,2,1,0:T(8,128)(2,1)} %get-tuple-element.17), channel_id=1, source_target_pairs={{1,0},{2,1},{3,2},{5,4},{6,5},{7,6},{9,8},{10,9},{11,10},{13,12},{... | collective-permute-start | bytes 3145736 | tf_op jit(solution)/shard_map/ppermute | solution.py:117
  96.2 5.9 %collective-permute-done.13 = bf16[640,256]{1,0:T(8,128)(2,1)} collective-permute-done((bf16[640,256]{1,0:T(8,128)(2,1)}, bf16[640,256]{1,0:T(8,128)(2,1)}, u32[]{:S(2)}, u32[]{:S(2)}) %collective-permute-start.13) | collective-permute-done | bytes 327712 | tf_op jit(solution)/shard_map/ppermute | solution.py:613
  102.0 2.3 %collective-permute-start.9 = (bf16[1936,256]{1,0:T(8,128)(2,1)S(1)}, bf16[1936,256]{1,0:T(8,128)(2,1)S(1)}, u32[]{:S(2)}, u32[]{:S(2)}) collective-permute-start(bf16[1936,256]{1,0:T(8,128)(2,1)S(1)} %copy-done.24), channel_id=1, source_target_pairs={{1,0},{2,1},{3,2},{5,4},{6,5},{7,6},{9,8},{10,9},{11,10},{13,12},{... | collective-permute-start | bytes 2973704 | tf_op jit(solution)/shard_map/ppermute | solution.py:117
  105.9 1.3 slice_bitcast_fusion.1
  107.2 2.8 %collective-permute-start.8 = (bf16[1936,256]{1,0:T(8,128)(2,1)}, bf16[1936,256]{1,0:T(8,128)(2,1)}, u32[]{:S(2)}, u32[]{:S(2)}) collective-permute-start(bf16[1936,256]{1,0:T(8,128)(2,1)} %pad_maximum_fusion.2), channel_id=1, source_target_pairs={{0,1},{1,2},{2,3},{4,5},{5,6},{6,7},{8,9},{9,10},{10,11},{12,13},{... | collective-permute-start | bytes 2973704 | tf_op jit(solution)/shard_map/ppermute | solution.py:117
  110.0 1.3 slice_bitcast_fusion
  113.4 8.5 %collective-permute-done.14 = bf16[1280,256]{1,0:T(8,128)(2,1)S(1)} collective-permute-done((bf16[1280,256]{1,0:T(8,128)(2,1)S(1)}, bf16[1280,256]{1,0:T(8,128)(2,1)S(1)}, u32[]{:S(2)}, u32[]{:S(2)}) %collective-permute-start.14) | collective-permute-done | bytes 655392 | tf_op jit(solution)/shard_map/ppermute | solution.py:613
  121.9 11.4 %collective-permute-start.3 = (bf16[2,2,2,256,256]{4,3,2,1,0:T(8,128)(2,1)}, bf16[2,2,2,256,256]{4,3,2,1,0:T(8,128)(2,1)}, u32[]{:S(2)}, u32[]{:S(2)}) collective-permute-start(bf16[2,2,2,256,256]{4,3,2,1,0:T(8,128)(2,1)} %pad_maximum_fusion), channel_id=1, source_target_pairs={{0,1},{1,2},{2,3},{4,5},{5,6},{6,7},{8,9},{9,10},{10,11},{12,13},{... | collective-permute-start | bytes 3145736 | tf_op jit(solution)/shard_map/ppermute | solution.py:117
  133.4 3.2 %collective-permute-start.5 = (bf16[2,2,2,256,256]{4,3,2,1,0:T(8,128)(2,1)}, bf16[2,2,2,256,256]{4,3,2,1,0:T(8,128)(2,1)}, u32[]{:S(2)}, u32[]{:S(2)}) collective-permute-start(bf16[2,2,2,256,256]{4,3,2,1,0:T(8,128)(2,1)} %pad_maximum_fusion.1), channel_id=1, source_target_pairs={{1,0},{2,1},{3,2},{5,4},{6,5},{7,6},{9,8},{10,9},{11,10},{13,12},{... | collective-permute-start | bytes 3145736 | tf_op jit(solution)/shard_map/ppermute | solution.py:117
  138.7 1.3 copy-done.4
  140.0 1.3 copy-done.5
  141.3 1.3 copy-done.6
  142.5 1.3 copy-done.7
  143.8 1.2 copy-done.9
  145.0 1.1 copy-done.11
  146.1 10.1 %far.1.field_ref = bf16[16,64,256]{2,1,0:T(8,128)(2,1)S(1)} custom-call(s32[160]{0:T(256)S(1)} %reshape.56.list_ref, s32[74]{0:T(128)S(1)} %pad_add_fusion.meta_ref, bf16[1280,256]{1,0:T(8,128)(2,1)S(1)} %copy-done.11, bf16[816,256]{1,0:T(8,128)(2,1)S(1)} %collective-permute-done.6.west_ref, bf16[816,256]{1,0:T(8,128)(2,1)S(1)} %collective-permute-done.7.east_ref, ...), custom_call_target="tpu_custom_call" | custom-call | flops 2500000000 | bytes 12000000 | tf_op jit(solution)/shard_map/far/pallas_call | solution.py:329
  156.3 30.7 %near_halo.1 = bf16[16,256,256]{2,1,0:T(8,128)(2,1)} custom-call(s32[160]{0:T(256)S(1)} %reshape.56.list_ref, s32[240]{0:T(256)S(1)} %copy-done.20, s32[64]{0:T(128)S(1)} %copy-done.21, bf16[8,256,256]{2,1,0:T(8,128)(2,1)} %bitcast.west_ref, bf16[8,256,256]{2,1,0:T(8,128)(2,1)} %bitcast.1.east_ref, bf16[8,256,256]{2,1,0:T(8,128)(2,1)} %bitcast.2.north_ref, ...), custom_call_target="tpu_custom_call" | custom-call | flops 8000000000 | bytes 14000000 | tf_op jit(solution)/shard_map/near_halo/pallas_call | solution.py:543
  (119 shorter events, 17.7 us)
Async XLA Ops:
  6.0 6.9 %copy-start.10 = (bf16[1280,256]{1,0:T(8,128)(2,1)}, bf16[1280,256]{1,0:T(8,128)(2,1)S(1)}, u32[]{:S(2)}) copy-start(bf16[1280,256]{1,0:T(8,128)(2,1)S(1)} %get-tuple-element.15.coef_ref) | copy-start | bytes 1966084
  6.0 6.9 %copy-start.14 = (bf16[816,256]{1,0:T(8,128)(2,1)}, bf16[816,256]{1,0:T(8,128)(2,1)S(1)}, u32[]{:S(2)}) copy-start(bf16[816,256]{1,0:T(8,128)(2,1)S(1)} %get-tuple-element.13) | copy-start | bytes 1253380
  6.0 63.6 %collective-permute-start.10 = (bf16[80,256]{1,0:T(8,128)(2,1)S(1)}, bf16[80,256]{1,0:T(8,128)(2,1)S(1)}, u32[]{:S(2)}, u32[]{:S(2)}) collective-permute-start(bf16[80,256]{1,0:T(8,128)(2,1)S(1)} %get-tuple-element.16), channel_id=1, source_target_pairs={{0,4},{4,0},{8,12},{12,8},{16,20},{20,16},{24,28},{28,24},{1,5},{5... | collective-permute-start | bytes 122888 | tf_op jit(solution)/shard_map/ppermute | solution.py:613
  8.0 81.2 %collective-permute-start.6 = (bf16[816,256]{1,0:T(8,128)(2,1)}, bf16[816,256]{1,0:T(8,128)(2,1)S(1)}, u32[]{:S(2)}, u32[]{:S(2)}) collective-permute-start(bf16[816,256]{1,0:T(8,128)(2,1)} %get-tuple-element.11), channel_id=1, source_target_pairs={{0,4},{4,8},{8,12},{12,16},{16,20},{20,24},{24,28},{1,5},{5,9},{9,... | collective-permute-start | bytes 1253384 | tf_op jit(solution)/shard_map/ppermute | solution.py:117
  10.0 10.3 %copy-start.1 = (bf16[4,4,256,256]{3,2,1,0:T(8,128)(2,1)S(1)}, bf16[4,4,256,256]{3,2,1,0:T(8,128)(2,1)}, u32[]{:S(2)}) copy-start(bf16[4,4,256,256]{3,2,1,0:T(8,128)(2,1)} %param.16) | copy-start | bytes 6291460
  10.0 82.2 %collective-permute-start.7 = (bf16[816,256]{1,0:T(8,128)(2,1)}, bf16[816,256]{1,0:T(8,128)(2,1)S(1)}, u32[]{:S(2)}, u32[]{:S(2)}) collective-permute-start(bf16[816,256]{1,0:T(8,128)(2,1)} %get-tuple-element.12), channel_id=1, source_target_pairs={{4,0},{8,4},{12,8},{16,12},{20,16},{24,20},{28,24},{5,1},{9,5},{13... | collective-permute-start | bytes 1253384 | tf_op jit(solution)/shard_map/ppermute | solution.py:117
  12.9 92.4 %collective-permute-start = (bf16[4,2,256,256]{3,2,1,0:T(8,128)(2,1)}, bf16[4,2,256,256]{3,2,1,0:T(8,128)(2,1)}, u32[]{:S(2)}, u32[]{:S(2)}) collective-permute-start(bf16[4,2,256,256]{3,2,1,0:T(8,128)(2,1)} %get-tuple-element.20), channel_id=1, source_target_pairs={{0,4},{4,8},{8,12},{12,16},{16,20},{20,24},{24,28},{1,5},{5,9},{9,... | collective-permute-start | bytes 3145736 | tf_op jit(solution)/shard_map/ppermute | solution.py:117
  18.9 88.3 %collective-permute-start.1 = (bf16[4,2,256,256]{3,2,1,0:T(8,128)(2,1)}, bf16[4,2,256,256]{3,2,1,0:T(8,128)(2,1)}, u32[]{:S(2)}, u32[]{:S(2)}) collective-permute-start(bf16[4,2,256,256]{3,2,1,0:T(8,128)(2,1)} %get-tuple-element.19), channel_id=1, source_target_pairs={{4,0},{8,4},{12,8},{16,12},{20,16},{24,20},{28,24},{5,1},{9,5},{13... | collective-permute-start | bytes 3145736 | tf_op jit(solution)/shard_map/ppermute | solution.py:117
  20.3 2.5 %copy-start.25 = (f32[4,4,256]{2,1,0:T(4,128)S(1)}, f32[4,4,256]{2,1,0:T(4,128)}, u32[]{:S(2)}) copy-start(f32[4,4,256]{2,1,0:T(4,128)} %param.18) | copy-start | bytes 49156
  20.3 2.5 %copy-start.18 = (f32[4,4,2,256]{3,2,1,0:T(2,128)S(1)}, f32[4,4,2,256]{3,2,1,0:T(2,128)}, u32[]{:S(2)}) copy-start(f32[4,4,2,256]{3,2,1,0:T(2,128)} %param.17) | copy-start | bytes 98308
  20.3 2.5 %copy-start.19 = (s32[432]{0:T(512)S(1)}, s32[432]{0:T(512)}, u32[]{:S(2)}) copy-start(s32[432]{0:T(512)} %constant.195.clone.table_ref) | copy-start | bytes 5188
  20.3 2.5 %copy-start.21 = (s32[64]{0:T(128)S(1)}, s32[64]{0:T(128)}, u32[]{:S(2)}) copy-start(s32[64]{0:T(128)} %constant.196.clone.slot_ref) | copy-start | bytes 772
  22.8 46.1 %copy-start.28 = (s32[36]{0:T(128)S(1)}, s32[36]{0:T(128)}, u32[]{:S(2)}) copy-start(s32[36]{0:T(128)} %constant.193.clone) | copy-start | bytes 436
  22.8 46.1 %copy-start.29 = (s32[36]{0:T(128)S(1)}, s32[36]{0:T(128)}, u32[]{:S(2)}) copy-start(s32[36]{0:T(128)} %constant.194.clone) | copy-start | bytes 436
  69.6 2.5 %collective-permute-start.11 = (bf16[160,256]{1,0:T(8,128)(2,1)S(1)}, bf16[160,256]{1,0:T(8,128)(2,1)S(1)}, u32[]{:S(2)}, u32[]{:S(2)}) collective-permute-start(bf16[160,256]{1,0:T(8,128)(2,1)S(1)} %pad_maximum_fusion.5), channel_id=1, source_target_pairs={{0,1},{1,0},{2,3},{3,2},{4,5},{5,4},{6,7},{7,6},{8,9},{9,8},{10,11... | collective-permute-start | bytes 245768 | tf_op jit(solution)/shard_map/ppermute | solution.py:613
  72.1 13.3 %collective-permute-start.12 = (bf16[320,256]{1,0:T(8,128)(2,1)S(1)}, bf16[320,256]{1,0:T(8,128)(2,1)S(1)}, u32[]{:S(2)}, u32[]{:S(2)}) collective-permute-start(bf16[320,256]{1,0:T(8,128)(2,1)S(1)} %pad_maximum_fusion.4), channel_id=1, source_target_pairs={{0,16},{4,20},{8,24},{12,28},{16,0},{20,4},{24,8},{28,12},{1,17},{... | collective-permute-start | bytes 491528 | tf_op jit(solution)/shard_map/ppermute | solution.py:613
  85.4 70.8 %collective-permute-start.2 = (bf16[2,4,256,256]{3,2,1,0:T(8,128)(2,1)}, bf16[2,4,256,256]{3,2,1,0:T(8,128)(2,1)}, u32[]{:S(2)}, u32[]{:S(2)}) collective-permute-start(bf16[2,4,256,256]{3,2,1,0:T(8,128)(2,1)} %get-tuple-element.18), channel_id=1, source_target_pairs={{0,1},{1,2},{2,3},{4,5},{5,6},{6,7},{8,9},{9,10},{10,11},{12,13},{... | collective-permute-start | bytes 3145736 | tf_op jit(solution)/shard_map/ppermute | solution.py:117
  89.3 66.9 %collective-permute-start.4 = (bf16[2,4,256,256]{3,2,1,0:T(8,128)(2,1)}, bf16[2,4,256,256]{3,2,1,0:T(8,128)(2,1)}, u32[]{:S(2)}, u32[]{:S(2)}) collective-permute-start(bf16[2,4,256,256]{3,2,1,0:T(8,128)(2,1)} %get-tuple-element.17), channel_id=1, source_target_pairs={{1,0},{2,1},{3,2},{5,4},{6,5},{7,6},{9,8},{10,9},{11,10},{13,12},{... | collective-permute-start | bytes 3145736 | tf_op jit(solution)/shard_map/ppermute | solution.py:117
  92.2 3.0 %copy-start.15 = (bf16[816,256]{1,0:T(8,128)(2,1)S(1)}, bf16[816,256]{1,0:T(8,128)(2,1)}, u32[]{:S(2)}) copy-start(bf16[816,256]{1,0:T(8,128)(2,1)} %copy-done.14) | copy-start | bytes 1253380
  92.2 9.8 %collective-permute-start.13 = (bf16[640,256]{1,0:T(8,128)(2,1)}, bf16[640,256]{1,0:T(8,128)(2,1)}, u32[]{:S(2)}, u32[]{:S(2)}) collective-permute-start(bf16[640,256]{1,0:T(8,128)(2,1)} %pad_maximum_fusion.3), channel_id=1, source_target_pairs={{0,8},{4,12},{8,0},{12,4},{16,24},{20,28},{24,16},{28,20},{1,9},{5... | collective-permute-start | bytes 983048 | tf_op jit(solution)/shard_map/ppermute | solution.py:613
  93.8 10.6 %copy-start.27 = (bf16[1280,256]{1,0:T(8,128)(2,1)S(1)}, bf16[1280,256]{1,0:T(8,128)(2,1)}, u32[]{:S(2)}) copy-start(bf16[1280,256]{1,0:T(8,128)(2,1)} %get-tuple-element.33) | copy-start | bytes 1966084
  95.1 6.9 %copy-start.24 = (bf16[1936,256]{1,0:T(8,128)(2,1)S(1)}, bf16[1936,256]{1,0:T(8,128)(2,1)}, u32[]{:S(2)}) copy-start(bf16[1936,256]{1,0:T(8,128)(2,1)} %slice_dynamic-update-slice_fusion) | copy-start | bytes 2973700
  102.0 31.4 %collective-permute-start.9 = (bf16[1936,256]{1,0:T(8,128)(2,1)S(1)}, bf16[1936,256]{1,0:T(8,128)(2,1)S(1)}, u32[]{:S(2)}, u32[]{:S(2)}) collective-permute-start(bf16[1936,256]{1,0:T(8,128)(2,1)S(1)} %copy-done.24), channel_id=1, source_target_pairs={{1,0},{2,1},{3,2},{5,4},{6,5},{7,6},{9,8},{10,9},{11,10},{13,12},{... | collective-permute-start | bytes 2973704 | tf_op jit(solution)/shard_map/ppermute | solution.py:117
  105.4 16.5 %collective-permute-start.14 = (bf16[1280,256]{1,0:T(8,128)(2,1)S(1)}, bf16[1280,256]{1,0:T(8,128)(2,1)S(1)}, u32[]{:S(2)}, u32[]{:S(2)}) collective-permute-start(bf16[1280,256]{1,0:T(8,128)(2,1)S(1)} %get-tuple-element.31), channel_id=1, source_target_pairs={{0,2},{1,3},{2,0},{3,1},{4,6},{5,7},{6,4},{7,5},{8,10},{9,11},{10,... | collective-permute-start | bytes 1966088 | tf_op jit(solution)/shard_map/ppermute | solution.py:613
  107.2 30.4 %collective-permute-start.8 = (bf16[1936,256]{1,0:T(8,128)(2,1)}, bf16[1936,256]{1,0:T(8,128)(2,1)}, u32[]{:S(2)}, u32[]{:S(2)}) collective-permute-start(bf16[1936,256]{1,0:T(8,128)(2,1)} %pad_maximum_fusion.2), channel_id=1, source_target_pairs={{0,1},{1,2},{2,3},{4,5},{5,6},{6,7},{8,9},{9,10},{10,11},{12,13},{... | collective-permute-start | bytes 2973704 | tf_op jit(solution)/shard_map/ppermute | solution.py:117
  121.9 34.4 %collective-permute-start.3 = (bf16[2,2,2,256,256]{4,3,2,1,0:T(8,128)(2,1)}, bf16[2,2,2,256,256]{4,3,2,1,0:T(8,128)(2,1)}, u32[]{:S(2)}, u32[]{:S(2)}) collective-permute-start(bf16[2,2,2,256,256]{4,3,2,1,0:T(8,128)(2,1)} %pad_maximum_fusion), channel_id=1, source_target_pairs={{0,1},{1,2},{2,3},{4,5},{5,6},{6,7},{8,9},{9,10},{10,11},{12,13},{... | collective-permute-start | bytes 3145736 | tf_op jit(solution)/shard_map/ppermute | solution.py:117
  133.3 5.4 %copy-start.3 = (bf16[1,1,21,64,64]{4,3,2,1,0:T(8,128)(2,1)S(1)}, bf16[1,1,21,64,64]{4,3,2,1,0:T(8,128)(2,1)}, u32[]{:S(2)}) copy-start(bf16[1,1,21,64,64]{4,3,2,1,0:T(8,128)(2,1)} %param.20) | copy-start | bytes 516100
  133.3 5.4 %copy-start.16 = (bf16[25,64,64]{2,1,0:T(8,128)(2,1)S(1)}, bf16[25,64,64]{2,1,0:T(8,128)(2,1)}, u32[]{:S(2)}) copy-start(bf16[25,64,64]{2,1,0:T(8,128)(2,1)} %constant.201.clone.code_ref) | copy-start | bytes 614404
  133.4 22.8 %collective-permute-start.5 = (bf16[2,2,2,256,256]{4,3,2,1,0:T(8,128)(2,1)}, bf16[2,2,2,256,256]{4,3,2,1,0:T(8,128)(2,1)}, u32[]{:S(2)}, u32[]{:S(2)}) collective-permute-start(bf16[2,2,2,256,256]{4,3,2,1,0:T(8,128)(2,1)} %pad_maximum_fusion.1), channel_id=1, source_target_pairs={{1,0},{2,1},{3,2},{5,4},{6,5},{7,6},{9,8},{10,9},{11,10},{13,12},{... | collective-permute-start | bytes 3145736 | tf_op jit(solution)/shard_map/ppermute | solution.py:117
  146.1 10.2 %copy-start.13 = (bf16[4,4,64,256]{3,2,1,0:T(8,128)(2,1)S(1)}, bf16[4,4,64,256]{3,2,1,0:T(8,128)(2,1)}, u32[]{:S(2)}) copy-start(bf16[4,4,64,256]{3,2,1,0:T(8,128)(2,1)} %param.19) | copy-start | bytes 1572868
  146.1 10.2 %copy-start.20 = (s32[240]{0:T(256)S(1)}, s32[240]{0:T(256)}, u32[]{:S(2)}) copy-start(s32[240]{0:T(256)} %constant.202.clone.table_ref) | copy-start | bytes 2884
  146.1 10.2 %copy-start.23 = (f32[16,256,256]{2,1,0:T(8,128)S(1)}, f32[16,256,256]{2,1,0:T(8,128)}, u32[]{:S(2)}) copy-start(f32[16,256,256]{2,1,0:T(8,128)} %copy-done.22) | copy-start | bytes 12582916
  (13 other events, 17.1 us)

commit v2 on v1

--- a/solution.py
+++ b/solution.py
@@ -20,6 +20,7 @@
 PACK = RANK + 16
 SIDEWAYS = 8 * RANK + 4 * RANK + 48
 CORNER = 4 * RANK + 4 * RANK + 48
+COPIES = 42
 BF = jnp.bfloat16
 F32 = jnp.float32
 
@@ -125,9 +126,22 @@
     return lax.dot_general(a, b, (((0,), (0,)), ((), ())), preferred_element_type=F32)
 
 
-def up_body(q_ref, basis_ref, tree_ref, pos_ref, east_ref, west_ref, north_ref, south_ref, coef_ref, give_ref):
+def up_body(
+    q_any, basis_any, tree_any, pos_ref, east_ref, west_ref, north_ref, south_ref, coef_ref, give_ref, q_ref, basis_ref, tree_ref, sems
+):
+    loads = []
+    for k in range(4):
+        part = pl.ds(4 * k, 4)
+        loads.append(pltpu.make_async_copy(basis_any.at[part], basis_ref.at[part], sems.at[2 * k]))
+        loads.append(pltpu.make_async_copy(q_any.at[part], q_ref.at[part], sems.at[2 * k + 1]))
+    loads.append(pltpu.make_async_copy(tree_any, tree_ref, sems.at[8]))
+    for load in loads:
+        load.start()
     level0 = []
     for leaf in range(LEAVES):
+        if leaf % 4 == 0:
+            loads[leaf // 2].wait()
+            loads[leaf // 2 + 1].wait()
         coef = dot(basis_ref[leaf], q_ref[leaf]).astype(BF)
         level0.append(coef)
         r, c = leaf // SIDE, leaf % SIDE
@@ -136,6 +150,7 @@
         ref[at * RANK : (at + 1) * RANK] = coef
         ref, at = (north_ref, r * 4 + c) if r < 2 else (south_ref, r * 4 + c - 8)
         ref[at * RANK : (at + 1) * RANK] = coef
+    loads[8].wait()
     level1 = []
     for r in range(2):
         for c in range(2):
@@ -185,8 +200,14 @@
             jax.ShapeDtypeStruct(((LEAVES + 4) * RANK, LEAF), BF),
             jax.ShapeDtypeStruct((PACK, LEAF), BF),
         ),
-        in_specs=[vmem] * 4,
+        in_specs=[pl.BlockSpec(memory_space=pl.ANY)] * 3 + [vmem],
         out_specs=[vmem] * 6,
+        scratch_shapes=[
+            pltpu.VMEM((LEAVES, LEAF, LEAF), BF),
+            pltpu.VMEM((LEAVES, RANK, LEAF), BF),
+            pltpu.VMEM((TOP + 1, RANK, RANK), BF),
+            pltpu.SemaphoreType.DMA((9,)),
+        ],
         compiler_params=pltpu.CompilerParams(vmem_limit_bytes=32 << 20),
         cost_estimate=pl.CostEstimate(flops=300_000_000, bytes_accessed=5_000_000, transcendentals=0),
         name="upward",
@@ -196,11 +217,24 @@
 def far_body(
     list_ref,
     meta_ref,
-    coef_ref,
-    west_ref,
-    east_ref,
-    north_ref,
-    south_ref,
+    coef_any,
+    west_any,
+    east_any,
+    north_any,
+    south_any,
+    all_any,
+    c0_any,
+    c1_any,
+    c2_any,
+    c3_any,
+    code_any,
+    tree_any,
+    field_ref,
+    pad0,
+    pad1,
+    win,
+    parents,
+    sum0,
     all_ref,
     c0_ref,
     c1_ref,
@@ -208,38 +242,47 @@
     c3_ref,
     code_ref,
     tree_ref,
-    field_ref,
-    pad0,
-    pad1,
-    win,
-    parents,
-    sum0,
+    sems,
 ):
+    loads = []
+
+    def load(source, at, to, row, count):
+        rows = pl.ds(at * RANK if at < 100 else at, count * RANK)
+        copy = pltpu.make_async_copy(source.at[rows], to.at[pl.ds(row, count * RANK)], sems.at[len(loads)])
+        copy.start()
+        loads.append(copy)
+
     def put(pad, extent, row, col, ref, at, count):
-        to = ((row + 2) * (extent + 4) + col + 2) * RANK
-        pad[to : to + count * RANK] = ref[at * RANK : (at + count) * RANK]
-
+        load(ref, at, pad, ((row + 2) * (extent + 4) + col + 2) * RANK, count)
+
+    whole = []
+    for k, (source, to) in enumerate(((c0_any, c0_ref), (c1_any, c1_ref), (code_any, code_ref), (tree_any, tree_ref), (all_any, all_ref), (c3_any, c3_ref), (c2_any, c2_ref))):
+        whole.append(pltpu.make_async_copy(source, to, sems.at[COPIES + k]))
+    whole[0].start()
     for r in range(4):
-        put(pad0, 4, r, 0, coef_ref, r * 4, 4)
-        put(pad0, 4, r, -2, west_ref, r * 2, 2)
-        put(pad0, 4, r, 4, east_ref, r * 2, 2)
-    for ref, row in ((north_ref, -2), (south_ref, 4)):
+        put(pad0, 4, r, 0, coef_any, r * 4, 4)
+        put(pad0, 4, r, -2, west_any, r * 2, 2)
+        put(pad0, 4, r, 4, east_any, r * 2, 2)
+    for ref, row in ((north_any, -2), (south_any, 4)):
         for r in range(2):
             put(pad0, 4, row + r, 0, ref, r * 4, 4)
+            for col, base in ((-2, SIDEWAYS), (4, SIDEWAYS + CORNER)):
+                load(ref, base + r * 2 * RANK, pad0, ((row + r + 2) * 8 + col + 2) * RANK, 2)
+    split = len(loads)
+    for copy in whole[1:]:
+        copy.start()
     for r in range(2):
-        put(pad1, 2, r, 0, coef_ref, LEAVES + r * 2, 2)
-        put(pad1, 2, r, -2, west_ref, 8 + r * 2, 2)
-        put(pad1, 2, r, 2, east_ref, 8 + r * 2, 2)
-    for ref, row in ((north_ref, -2), (south_ref, 2)):
+        put(pad1, 2, r, 0, coef_any, LEAVES + r * 2, 2)
+        put(pad1, 2, r, -2, west_any, 8 + r * 2, 2)
+        put(pad1, 2, r, 2, east_any, 8 + r * 2, 2)
+    for ref, row in ((north_any, -2), (south_any, 2)):
         for r in range(2):
             put(pad1, 2, row + r, 0, ref, 8 + r * 2, 2)
-    for ref, row0, row1 in ((north_ref, -2, -2), (south_ref, 4, 2)):
-        for col0, col1, base in ((-2, -2, SIDEWAYS), (4, 2, SIDEWAYS + CORNER)):
-            for r in range(2):
-                to = ((row0 + r + 2) * 8 + col0 + 2) * RANK
-                pad0[to : to + 2 * RANK] = ref[base + r * 2 * RANK : base + (r + 1) * 2 * RANK]
-                to = ((row1 + r + 2) * 6 + col1 + 2) * RANK
-                pad1[to : to + 2 * RANK] = ref[base + (4 + r * 2) * RANK : base + (6 + r * 2) * RANK]
+            for col, base in ((-2, SIDEWAYS), (2, SIDEWAYS + CORNER)):
+                load(ref, base + (4 + r * 2) * RANK, pad1, ((row + r + 2) * 6 + col + 2) * RANK, 2)
+    whole[0].wait()
+    for copy in loads[:split]:
+        copy.wait()
 
     for a in range(2):
         for b in range(2):
@@ -251,6 +294,9 @@
             for child in range(4):
                 leaf = (2 * a + child // 2) * SIDE + 2 * b + child % 2
                 sum0[leaf] = total[child * RANK : (child + 1) * RANK]
+
+    for copy in loads[split:] + whole[1:]:
+        copy.wait()
 
     def listed(leaf, carry):
         code = second_cycle(list_ref, leaf)
@@ -329,7 +375,7 @@
     return pl.pallas_call(
         far_body,
         out_shape=jax.ShapeDtypeStruct((LEAVES, RANK, LEAF), BF),
-        in_specs=[smem, smem] + [vmem] * 12,
+        in_specs=[smem, smem] + [pl.BlockSpec(memory_space=pl.ANY)] * 12,
         out_specs=vmem,
         scratch_shapes=[
             pltpu.VMEM((64 * RANK, LEAF), BF),
@@ -337,6 +383,13 @@
             pltpu.VMEM((WINDOW * RANK, LEAF), BF),
             pltpu.VMEM((devices // 4 * RANK, LEAF), BF),
             pltpu.VMEM((LEAVES, RANK, LEAF), F32),
+            pltpu.VMEM(gathered.shape, BF),
+        ]
+        + [pltpu.VMEM((4 * RANK, WINDOW * RANK), BF)] * 4
+        + [
+            pltpu.VMEM((25, RANK, RANK), BF),
+            pltpu.VMEM((TOP + 1, RANK, RANK), BF),
+            pltpu.SemaphoreType.DMA((COPIES + 7,)),
         ],
         compiler_params=pltpu.CompilerParams(vmem_limit_bytes=40 << 20),
         cost_estimate=pl.CostEstimate(flops=2_500_000_000, bytes_accessed=12_000_000, transcendentals=0),
@@ -388,14 +441,13 @@
             )
 
 
-def near_own_body(list_ref, table_ref, slot_ref, q_ref, pos_ref, noise_ref, out_ref, columns, blocks):
-    leaf = pl.program_id(0)
+def near_own_body(first, table_ref, q_ref, pos_ref, noise_ref, *refs):
+    out_ref, columns, blocks = refs[-3:]
+    leaf = pl.program_id(0) + first
     rows = jnp.concatenate([pos_ref[leaf] * waves, noise_ref[leaf], jnp.zeros((5, LEAF), F32)], axis=0)
     spread_columns(rows, columns)
     width = table_ref.shape[0] // (3 * LEAVES)
-    own = q_ref[leaf].astype(F32)
-    for j in (0, 128):
-        out_ref[0, :, j : j + 128] = columns[:, 256:384] * own[:, j : j + 128]
+    wide = 6 if first in (0, LEAVES - SIDE) else width
 
     def one(j, carry):
         at = (leaf * width + j) * 3
@@ -411,162 +463,225 @@
 
         return carry
 
-    lax.fori_loop(0, width, one, 0)
-    total = out_ref[0]
-    for j in range(width):
+    lax.fori_loop(0, wide, one, 0)
+    total = None
+    for j in range(wide):
         slot = jnp.maximum(table_ref[(leaf * width + j) * 3], 0)
-        total = total + dot(blocks[j], q_ref[slot])
-    out_ref[0] = total
+        part = dot(blocks[j], q_ref[slot])
+        total = part if total is None else total + part
+    own = q_ref[leaf].astype(F32)
+    noise = jnp.concatenate([columns[:, 256:384]] * 2, axis=1)
+    out_ref[0] = total + noise * own
+
+
+def near_own(row, q, points, noise, before, held):
+    vmem = pl.BlockSpec(memory_space=pltpu.VMEM)
+    smem = pl.BlockSpec(memory_space=pltpu.SMEM)
+    kept = [before] + ([] if held is None else [held])
+
+    def body(*refs):
+        near_own_body(SIDE * row, *refs)
+
+    return pl.pallas_call(
+        body,
+        grid=(SIDE,),
+        out_shape=jax.ShapeDtypeStruct((LEAVES, LEAF, LEAF), F32),
+        in_specs=[smem, vmem, vmem, vmem] + [pl.BlockSpec(memory_space=pl.ANY)] * len(kept),
+        out_specs=pl.BlockSpec((1, LEAF, LEAF), lambda i: (i + SIDE * row, 0, 0)),
+        scratch_shapes=[pltpu.VMEM((LEAF, 384), F32), pltpu.VMEM((9, LEAF, LEAF), BF)],
+        input_output_aliases={} if held is None else {5: 0},
+        compiler_params=pltpu.CompilerParams(vmem_limit_bytes=32 << 20),
+        cost_estimate=pl.CostEstimate(flops=6_000_000_000, bytes_accessed=4_000_000, transcendentals=5_000_000),
+        name="near_own",
+    )(jnp.asarray(near_table(True).reshape(-1)), q, points, noise, *kept)
+
+
+def edge_items():
+    table = near_table(False)
+    items = [[leaf, *table[leaf, j]] for leaf in range(LEAVES) for j in range(5) if table[leaf, j, 0] >= 0]
+    plain = [item for item in items if not is_corner(item[1])]
+    return plain + [item for item in items if is_corner(item[1])]
+
+
+def is_corner(slot):
+    return (slot >= 32) & (slot // 8 % 2 == 1)
+
+
+ITEMS = edge_items()
+PLAIN = sum(not is_corner(item[1]) for item in ITEMS)
+EDGES = len(ITEMS)
+
+
+def extra_of(list_ref, slot_ref, leaf):
     code = second_cycle(list_ref, leaf)
     place = (leaf // SIDE + code // 5) * 8 + leaf % SIDE + code % 5
     slot = slot_ref[jnp.where(code >= 0, place, 0)]
-
-    @pl.when((code >= 0) & (slot < LEAVES))
+    return code, slot
+
+
+def edge_body(list_ref, table_ref, slot_ref, own_pos_ref, pos_ref, out_ref, columns):
+    item = pl.program_id(0)
+
+    def turn(leaf):
+        spread_columns(jnp.concatenate([own_pos_ref[leaf] * waves, jnp.zeros((6, LEAF), F32)], axis=0), columns)
+
+    @pl.when(item < EDGES)
     def _():
-        block_into(blocks.at[0], columns, pos_ref[slot], code // 5 - 2, code % 5 - 2)
-        out_ref[0] += dot(blocks[0], q_ref[slot])
-
-
-def near_own(near_list, q, points, noise):
+        at = item * 4
+        leaf = table_ref[at]
+
+        @pl.when((item == 0) | (table_ref[jnp.maximum(at - 4, 0)] != leaf))
+        def _():
+            turn(leaf)
+
+        block_into(out_ref.at[0], columns, pos_ref[table_ref[at + 1] - LEAVES], table_ref[at + 2], table_ref[at + 3])
+
+    @pl.when(item >= EDGES)
+    def _():
+        leaf = item - EDGES
+        code, slot = extra_of(list_ref, slot_ref, leaf)
+
+        @pl.when(code >= 0)
+        def _():
+            turn(leaf)
+
+        @pl.when((code >= 0) & (slot >= LEAVES))
+        def _():
+            block_into(out_ref.at[0], columns, pos_ref[jnp.maximum(slot - LEAVES, 0)], code // 5 - 2, code % 5 - 2)
+
+        @pl.when((code >= 0) & (slot < LEAVES))
+        def _():
+            block_into(out_ref.at[0], columns, own_pos_ref[jnp.minimum(slot, LEAVES - 1)], code // 5 - 2, code % 5 - 2)
+
+
+def edge_blocks(near_list, own_points, halo_points, before):
     vmem = pl.BlockSpec(memory_space=pltpu.VMEM)
     smem = pl.BlockSpec(memory_space=pltpu.SMEM)
+
+    def body(list_ref, table_ref, slot_ref, own_pos_ref, pos_ref, before_ref, out_ref, columns):
+        edge_body(list_ref, table_ref, slot_ref, own_pos_ref, pos_ref, out_ref, columns)
+
     return pl.pallas_call(
-        near_own_body,
-        grid=(LEAVES,),
+        body,
+        grid=(EDGES + LEAVES,),
+        out_shape=jax.ShapeDtypeStruct((EDGES + LEAVES, LEAF, LEAF), BF),
+        in_specs=[smem, smem, smem, vmem, vmem, pl.BlockSpec(memory_space=pl.ANY)],
+        out_specs=pl.BlockSpec((1, LEAF, LEAF), lambda i: (i, 0, 0)),
+        scratch_shapes=[pltpu.VMEM((LEAF, 256), F32)],
+        compiler_params=pltpu.CompilerParams(vmem_limit_bytes=32 << 20),
+        cost_estimate=pl.CostEstimate(flops=12_000_000_000, bytes_accessed=8_000_000, transcendentals=12_000_000),
+        name="edge_blocks",
+    )(near_list, jnp.asarray(np.array(ITEMS, np.int32).reshape(-1)), jnp.asarray(SLOT_OF), own_points, halo_points, before)
+
+
+def side_body(
+    list_ref, slot_ref, q_any, west_any, east_any, north_any, south_any, block_any, sum_any, basis_ref, field_ref,
+    out_ref, total_ref, held, blocks, sems,
+):
+    copies = []
+    pieces = ((q_any, 0, 16), (west_any, 16, 8), (east_any, 24, 8), (north_any, 32, 8), (south_any, 48, 8))
+    for source, at, count in pieces:
+        copies.append(pltpu.make_async_copy(source, held.at[pl.ds(at, count)], sems.at[len(copies)]))
+    copies.append(pltpu.make_async_copy(block_any, blocks, sems.at[5]))
+    copies.append(pltpu.make_async_copy(sum_any, total_ref, sems.at[6]))
+    for copy in copies:
+        copy.start()
+    for copy in copies:
+        copy.wait()
+    of_leaf = {}
+    for at in range(PLAIN):
+        of_leaf.setdefault(ITEMS[at][0], []).append((at, ITEMS[at][1]))
+    for leaf in range(LEAVES):
+        total = dot_first(basis_ref[leaf], field_ref[leaf])
+        for at, slot in of_leaf.get(leaf, []):
+            total = total + dot(blocks[at], held[slot])
+        total_ref[leaf] += total
+
+    def extra(leaf, carry):
+        code, slot = extra_of(list_ref, slot_ref, leaf)
+
+        @pl.when((code >= 0) & jnp.logical_not(is_corner(slot)))
+        def _():
+            total_ref[leaf] += dot(blocks[EDGES + leaf], held[slot])
+
+        return carry
+
+    lax.fori_loop(0, LEAVES, extra, 0)
+    back = pltpu.make_async_copy(total_ref, out_ref, sems.at[7])
+    back.start()
+    back.wait()
+
+
+def add_sides(near_list, q, halos, blocks, near_sum, basis, field, before):
+    vmem = pl.BlockSpec(memory_space=pltpu.VMEM)
+    smem = pl.BlockSpec(memory_space=pltpu.SMEM)
+    anywhere = pl.BlockSpec(memory_space=pl.ANY)
+
+    def body(list_ref, slot_ref, before_ref, *refs):
+        side_body(list_ref, slot_ref, *refs)
+
+    return pl.pallas_call(
+        body,
         out_shape=jax.ShapeDtypeStruct((LEAVES, LEAF, LEAF), F32),
-        in_specs=[smem, smem, smem, vmem, vmem, vmem],
-        out_specs=pl.BlockSpec((1, LEAF, LEAF), lambda i: (i, 0, 0)),
-        scratch_shapes=[pltpu.VMEM((LEAF, 384), F32), pltpu.VMEM((9, LEAF, LEAF), BF)],
-        compiler_params=pltpu.CompilerParams(vmem_limit_bytes=32 << 20),
-        cost_estimate=pl.CostEstimate(flops=20_000_000_000, bytes_accessed=7_000_000, transcendentals=20_000_000),
-        name="near_own",
-    )(near_list, jnp.asarray(near_table(True).reshape(-1)), jnp.asarray(SLOT_OF), q, points, noise)
-
-
-def near_halo_body(
-    list_ref,
-    table_ref,
-    slot_ref,
-    west_ref,
-    east_ref,
-    north_ref,
-    north_corner_ref,
-    south_ref,
-    south_corner_ref,
-    own_pos_ref,
-    pos_ref,
-    sum_ref,
-    basis_ref,
-    field_ref,
-    out_ref,
-    columns,
-    blocks,
-    held,
-    total_ref,
-    sems,
-):
+        in_specs=[smem, smem, anywhere] + [anywhere] * 7 + [vmem, vmem],
+        out_specs=anywhere,
+        scratch_shapes=[
+            pltpu.VMEM((LEAVES, LEAF, LEAF), F32),
+            pltpu.VMEM((64, LEAF, LEAF), BF),
+            pltpu.VMEM((EDGES + LEAVES, LEAF, LEAF), BF),
+            pltpu.SemaphoreType.DMA((8,)),
+        ],
+        compiler_params=pltpu.CompilerParams(vmem_limit_bytes=48 << 20),
+        cost_estimate=pl.CostEstimate(flops=4_000_000_000, bytes_accessed=24_000_000, transcendentals=0),
+        name="add_sides",
+    )(near_list, jnp.asarray(SLOT_OF), before, q, *halos, blocks, near_sum, basis, field)
+
+
+def corner_body(list_ref, slot_ref, north_ref, south_ref, block_ref, extra_ref, sum_ref, out_ref, total):
     leaf = pl.program_id(0)
-    copies = [
-        pltpu.make_async_copy(ref, held.at[pl.ds(8 * k, 8)], sems.at[k])
-        for k, ref in enumerate(
-            (west_ref, east_ref, north_ref, north_corner_ref, south_ref, south_corner_ref)
-        )
-    ]
-
-    @pl.when(leaf == 0)
+    total[...] = sum_ref[0]
+    for at in range(PLAIN, EDGES):
+
+        @pl.when(leaf == ITEMS[at][0])
+        def _(at=at):
+            slot = ITEMS[at][1]
+            ref, start = (north_ref, 40) if slot < 48 else (south_ref, 56)
+            total[...] += dot(block_ref[at - PLAIN], ref[slot - start])
+
+    code, slot = extra_of(list_ref, slot_ref, leaf)
+
+    @pl.when((code >= 0) & is_corner(slot))
     def _():
-        for copy in copies:
-            copy.start()
-
-    rows = jnp.concatenate([own_pos_ref[leaf] * waves, jnp.zeros((6, LEAF), F32)], axis=0)
-    spread_columns(rows, columns)
-    width = table_ref.shape[0] // (3 * LEAVES)
-
-    def one(j, carry):
-        at = (leaf * width + j) * 3
-        slot = table_ref[at]
-
-        @pl.when(slot >= 0)
-        def _():
-            block_into(blocks.at[j], columns, pos_ref[slot - LEAVES], table_ref[at + 1], table_ref[at + 2])
-
-        return carry
-
-    lax.fori_loop(0, width, one, 0)
-
-    @pl.when(leaf == 0)
-    def _():
-        for copy in copies:
-            copy.wait()
-
-
-    def add(j, total):
-        slot = table_ref[(leaf * width + j) * 3]
-        return total + dot(blocks[j], held[slot - LEAVES])
-
-    row, col = leaf // SIDE, leaf % SIDE
-    edge_y = (row == 0) | (row == SIDE - 1)
-    edge_x = (col == 0) | (col == SIDE - 1)
-    corner = edge_y & edge_x
-    total_ref[...] = sum_ref[0] + dot_first(basis_ref[leaf], field_ref[leaf])
-
-    @pl.when(edge_y | edge_x)
-    def _():
-        total = total_ref[...]
-        for j in range(3):
-            total = add(j, total)
-        total_ref[...] = total
-
-    @pl.when(corner)
-    def _():
-        total = total_ref[...]
-        for j in range(3, 5):
-            total = add(j, total)
-        total_ref[...] = total
-
-    code = second_cycle(list_ref, leaf)
-    place = (leaf // SIDE + code // 5) * 8 + leaf % SIDE + code % 5
-    slot = slot_ref[jnp.where(code >= 0, place, 0)]
-
-    @pl.when((code >= 0) & (slot >= LEAVES))
-    def _():
-        block_into(blocks.at[0], columns, pos_ref[slot - LEAVES], code // 5 - 2, code % 5 - 2)
-        total_ref[...] += dot(blocks[0], held[slot - LEAVES])
-
-    out_ref[0] = total_ref[...].astype(BF)
-
-
-def near_halo(near_list, halos, own_points, halo_points, near_sum, basis, field):
+        source = jnp.where(slot < 48, north_ref[slot % 8], south_ref[slot % 8])
+        total[...] += dot(extra_ref[0], source)
+
+    out_ref[0] = total[...].astype(BF)
+
+
+def add_corners(near_list, north, south, blocks, total):
     vmem = pl.BlockSpec(memory_space=pltpu.VMEM)
     smem = pl.BlockSpec(memory_space=pltpu.SMEM)
     block = pl.BlockSpec((1, LEAF, LEAF), lambda i: (i, 0, 0))
+    corners = EDGES - PLAIN
     return pl.pallas_call(
-        near_halo_body,
+        corner_body,
         grid=(LEAVES,),
         out_shape=jax.ShapeDtypeStruct((LEAVES, LEAF, LEAF), BF),
-        in_specs=[smem, smem, smem] + [pl.BlockSpec(memory_space=pl.ANY)] * 6 + [vmem, vmem, block, vmem, vmem],
+        in_specs=[
+            smem,
+            smem,
+            vmem,
+            vmem,
+            pl.BlockSpec((corners, LEAF, LEAF), lambda i: (PLAIN // corners, 0, 0)),
+            pl.BlockSpec((1, LEAF, LEAF), lambda i: (EDGES + i, 0, 0)),
+            block,
+        ],
         out_specs=block,
-        scratch_shapes=[
-            pltpu.VMEM((LEAF, 256), F32),
-            pltpu.VMEM((5, LEAF, LEAF), BF),
-            pltpu.VMEM((48, LEAF, LEAF), BF),
-            pltpu.VMEM((LEAF, LEAF), F32),
-            pltpu.SemaphoreType.DMA((6,)),
-        ],
+        scratch_shapes=[pltpu.VMEM((LEAF, LEAF), F32)],
         compiler_params=pltpu.CompilerParams(vmem_limit_bytes=32 << 20),
-        cost_estimate=pl.CostEstimate(flops=8_000_000_000, bytes_accessed=14_000_000, transcendentals=8_000_000),
-        name="near_halo",
-    )(
-        near_list,
-        jnp.asarray(near_table(False).reshape(-1)),
-        jnp.asarray(SLOT_OF),
-        *halos,
-        own_points,
-        halo_points,
-        near_sum,
-        basis,
-        field,
-    )
+        cost_estimate=pl.CostEstimate(flops=500_000_000, bytes_accessed=10_000_000, transcendentals=0),
+        name="add_corners",
+    )(near_list, jnp.asarray(SLOT_OF), north, south, blocks, blocks, total)
 
 
 def points_of(message, leaves_at):
@@ -608,30 +723,25 @@
     east, west, north, south, coefs, give = go_up(q, basis, tree, points)
     from_west = shift(east, "wide", 1)
     from_east = shift(west, "wide", -1)
-    gathered = give
-    for axis, bit in steps:
-        other = lax.ppermute(gathered, axis, [(i, i ^ bit) for i in range(lax.axis_size(axis))])
-        gathered = jnp.concatenate([gathered, other], axis=0)
-
-    def corner(message, lower):
-        at = 4 * RANK if lower else 0
-        return [message[at : at + 4 * RANK], message[8 * RANK :]]
-
-    north = jnp.concatenate([north] + corner(from_west, False) + corner(from_east, False), axis=0)
-    south = jnp.concatenate([south] + corner(from_west, True) + corner(from_east, True), axis=0)
-    from_south = shift(north, "narrow", -1)
-    from_north = shift(south, "narrow", 1)
-
     q_west = shift(charges[:, 2:4], "wide", 1)
     q_east = shift(charges[:, 0:2], "wide", -1)
     q_north = shift(charges[2:4], "narrow", 1)
     q_south = shift(charges[0:2], "narrow", -1)
-    q_north_corner = shift(jnp.stack([q_west[2:4], q_east[2:4]]), "narrow", 1)
-    q_south_corner = shift(jnp.stack([q_west[0:2], q_east[0:2]]), "narrow", -1)
-    halos = [
-        value.reshape(8, LEAF, LEAF)
-        for value in (q_west, q_east, q_north, q_north_corner, q_south, q_south_corner)
-    ]
+
+    noise_rows = noise.reshape(LEAVES, 1, LEAF)
+    near_sum = None
+    gathered, before = give, give
+    for at, (axis, bit) in enumerate(steps):
+        other = lax.ppermute(gathered, axis, [(i, i ^ bit) for i in range(lax.axis_size(axis))])
+        if at < SIDE:
+            near_sum = near_own(at, q, points, noise_rows, before, near_sum)
+            other, near_sum = lax.optimization_barrier((other, near_sum))
+        if at == 1:
+            from_west, from_east, near_sum = lax.optimization_barrier((from_west, from_east, near_sum))
+        if at == 2:
+            north, south, from_south, from_north = narrow_messages(north, south, from_west, from_east)
+        before = other
+        gathered = jnp.concatenate([gathered, other], axis=0)
 
     def corner_points(message, lower):
         first = points_of(message, SIDEWAYS + 8 * RANK)
@@ -646,11 +756,29 @@
         + corner_points(from_south, False),
         axis=0,
     )
-
-    near_sum = near_own(listing, q, points, noise.reshape(LEAVES, 1, LEAF))
+    blocks = edge_blocks(listing, points, halo_points, near_sum)
+    gathered, blocks = lax.optimization_barrier((gathered, blocks))
     field = far_field(listing, meta, coefs, from_west, from_east, from_north, from_south, gathered, tree)
-    out = near_halo(listing, halos, points, halo_points, near_sum, basis, field)
+    q_west, q_east, field = lax.optimization_barrier((q_west, q_east, field))
+    q_north_corner = shift(jnp.stack([q_west[2:4], q_east[2:4]]), "narrow", 1)
+    q_south_corner = shift(jnp.stack([q_west[0:2], q_east[0:2]]), "narrow", -1)
+    halos = [value.reshape(8, LEAF, LEAF) for value in (q_west, q_east, q_north, q_south)]
+    total = add_sides(listing, q, halos, blocks, near_sum, basis, field, q_west)
+    q_north_corner, q_south_corner, total = lax.optimization_barrier((q_north_corner, q_south_corner, total))
+    out = add_corners(
+        listing, q_north_corner.reshape(8, LEAF, LEAF), q_south_corner.reshape(8, LEAF, LEAF), blocks, total
+    )
     return out.reshape(SIDE, SIDE, LEAF, LEAF)
+
+
+def narrow_messages(north, south, from_west, from_east):
+    def corner(message, lower):
+        at = 4 * RANK if lower else 0
+        return [message[at : at + 4 * RANK], message[8 * RANK :]]
+
+    north = jnp.concatenate([north] + corner(from_west, False) + corner(from_east, False), axis=0)
+    south = jnp.concatenate([south] + corner(from_west, True) + corner(from_east, True), axis=0)
+    return north, south, shift(north, "narrow", -1), shift(south, "narrow", 1)
 
 
 def solution(mesh):

time: 188 us -> 225 us (1.20)
  Pallas kernels: 86.6 us -> 104 us
  local copies, waits for them, and re-layouts: 27.8 us -> 39.7 us
  waiting for transfers between devices: 21.7 us -> 31.8 us
  starting transfers between devices: 45.4 us -> 41.2 us
    pallas_call x2 -> x7, Pallas kernels: 74.8 us -> 88.9 us  [the longest x4 42.2 us: near_own(): pl.pallas_call(body, grid=(SIDE,), out_shape=jax.ShapeDtypeStruct((LEAVES...]
    ppermute x10, waiting for transfers between devices: 0.03 us -> 10.5 us  [shift(): lax.ppermute(value, axis, [(i, i + steps) for i in range(count) if 0 <= i...]
    unnamed x75 -> x89, local copies, waits for them, and re-layouts: 20.2 us -> 28.2 us
    ppermute x10, starting transfers between devices: 35.6 us -> 30.1 us  [shift(): lax.ppermute(value, axis, [(i, i + steps) for i in range(count) if 0 <= i...]
    slice x2, local copies, waits for them, and re-layouts: 0.04 us -> 3.38 us  [corner(): return [message[at:at + 4 * RANK], message[8 * RANK:]]]
  transfers between devices with their start and end apart: 15 -> 15, of which waited for: 4 -> 4; matrix products, arithmetic and copies ran while one was open for 10% -> 12% of each run, Pallas kernels for 29% -> 41%
where the time goes in v2:
time: 225 us; the launch traced here: 224 us
  Pallas kernels  104 us (46%)
  starting transfers between devices  41.2 us (18%)
  local copies, waits for them, and re-layouts  39.7 us (18%)
  waiting for transfers between devices  31.8 us (14%)
  other arithmetic  6.44 us (3%)
    pallas_call x4, Pallas kernels, near_own(): pl.pallas_call(body, grid=(SIDE,), out_shape=jax.ShapeDtypeStruct((LEAVES...  42.2 us
    ppermute x10, starting transfers between devices, shift(): lax.ppermute(value, axis, [(i, i + steps) for i in range(count) if 0 <= i...  30.1 us
    unnamed x89, local copies, waits for them, and re-layouts  28.2 us
    pallas_call x1, Pallas kernels, edge_blocks(): pl.pallas_call(body, grid=(EDGES + LEAVES,), out_shape=jax.ShapeDtypeStru...  24.4 us
    ppermute x5, waiting for transfers between devices, per_device(): lax.ppermute(gathered, axis, [(i, i ^ bit) for i in range(lax.axis_size(a...  21.3 us
    pallas_call x1, Pallas kernels, add_sides(): pl.pallas_call(body, out_shape=jax.ShapeDtypeStruct((LEAVES, LEAF, LEAF),...  14.1 us
    pallas_call x1, Pallas kernels, far_field(): pl.pallas_call(far_body, out_shape=jax.ShapeDtypeStruct((LEAVES, RANK, LE...  12 us
    ppermute x5, starting transfers between devices, per_device(): lax.ppermute(gathered, axis, [(i, i ^ bit) for i in range(lax.axis_size(a...  11.1 us
  transfers between devices with their start and end apart: 15, of which 4 were waited for; matrix products, arithmetic and copies ran while one was open for 12% of the time, Pallas kernels for 41%

profile of v2, /device:TPU:1, one launch (start us, length us, event | category | flops | bytes accessed | tf_op | source)
XLA Modules:
  0.0 223.9 jit_solution(9174067988328994359)
XLA Ops:
  4.4 3.1 %upward.1 = (bf16[816,256]{1,0:T(8,128)(2,1)}, bf16[816,256]{1,0:T(8,128)(2,1)}, bf16[816,256]{1,0:T(8,128)(2,1)S(1)}, bf16[816,256]{1,0:T(8,128)(2,1)S(1)}, bf1...) custom-call(bf16[16,256,256]{2,1,0:T(8,128)(2,1)S(1)} %bitcast.24, bf16[16,64,256]{2,1,0:T(8,128)(2,1)S(1)} %bitcast.30, ...), custom_call_target="tpu_custom_call" | custom-call | flops 300000000 | bytes 5000000 | tf_op jit(solution)/shard_map/upward/pallas_call | solution.py:193
  8.3 2.0 collective-permute-start.4
  10.3 2.7 %collective-permute-start.2 = (bf16[816,256]{1,0:T(8,128)(2,1)}, bf16[816,256]{1,0:T(8,128)(2,1)}, u32[]{:S(2)}, u32[]{:S(2)}) collective-permute-start(bf16[816,256]{1,0:T(8,128)(2,1)} %get-tuple-element.31), channel_id=1, source_target_pairs={{0,4},{4,8},{8,12},{12,16},{16,20},{20,24},{24,28},{1,5},{5,9},{9,... | collective-permute-start | bytes 1253384 | tf_op jit(solution)/shard_map/ppermute | solution.py:118
  15.9 4.3 %collective-permute-start = (bf16[4,2,256,256]{3,2,1,0:T(8,128)(2,1)}, bf16[4,2,256,256]{3,2,1,0:T(8,128)(2,1)S(1)}, u32[]{:S(2)}, u32[]{:S(2)}) collective-permute-start(bf16[4,2,256,256]{3,2,1,0:T(8,128)(2,1)} %get-tuple-element.58), channel_id=1, source_target_pairs={{0,4},{4,8},{8,12},{12,16},{16,20},{20,24},{24,28},{1,5},{5,9},{9,... | collective-permute-start | bytes 3145736 | tf_op jit(solution)/shard_map/ppermute | solution.py:118
  23.7 1.8 constant_dynamic-update-slice_fusion
  25.5 9.0 %near_own.4.refs_5_ = f32[16,256,256]{2,1,0:T(8,128)S(1)} custom-call(s32[432]{0:T(512)S(1)} %copy-done.28, bf16[16,256,256]{2,1,0:T(8,128)(2,1)S(1)} %bitcast.25, f32[16,2,256]{2,1,0:T(2,128)S(1)} %bitcast.37, f32[16,1,256]{2,1,0:T(1,128)S(1)} %reshape.60.refs_3_, bf16[80,256]{1,0:T(8,128)(2,1)S(1)} %get-tuple-element.33.refs_4_), custom_call_target="tpu_custom_call" | custom-call | flops 6000000000 | bytes 4000000 | tf_op jit(solution)/shard_map/near_own/pallas_call | solution.py:485
  34.5 2.0 copy-done.4
  36.7 2.2 copy-done.5
  38.9 12.1 %near_own.5.refs_5_ = f32[16,256,256]{2,1,0:T(8,128)S(1)} custom-call(s32[432]{0:T(512)S(1)} %copy-done.28, bf16[16,256,256]{2,1,0:T(8,128)(2,1)S(1)} %bitcast.26, f32[16,2,256]{2,1,0:T(2,128)S(1)} %bitcast.38, f32[16,1,256]{2,1,0:T(1,128)S(1)} %reshape.60.refs_3_, ...), custom_call_target="tpu_custom_call", output_to_operand_aliasing={{}: (5, {})} | custom-call | flops 6000000000 | bytes 4000000 | tf_op jit(solution)/shard_map/near_own/pallas_call | solution.py:485
  53.6 3.6 %collective-permute-start.13 = (bf16[2,4,256,256]{3,2,1,0:T(8,128)(2,1)}, bf16[2,4,256,256]{3,2,1,0:T(8,128)(2,1)}, u32[]{:S(2)}, u32[]{:S(2)}) collective-permute-start(bf16[2,4,256,256]{3,2,1,0:T(8,128)(2,1)} %get-tuple-element.56), channel_id=1, source_target_pairs={{0,1},{1,2},{2,3},{4,5},{5,6},{6,7},{8,9},{9,10},{10,11},{12,13},{... | collective-permute-start | bytes 3145736 | tf_op jit(solution)/shard_map/ppermute | solution.py:118
  57.9 5.4 %collective-permute-start.8 = (bf16[320,256]{1,0:T(8,128)(2,1)S(1)}, bf16[320,256]{1,0:T(8,128)(2,1)S(1)}, u32[]{:S(2)}, u32[]{:S(2)}) collective-permute-start(bf16[320,256]{1,0:T(8,128)(2,1)S(1)} %pad_maximum_fusion.4), channel_id=1, source_target_pairs={{0,16},{4,20},{8,24},{12,28},{16,0},{20,4},{24,8},{28,12},{1,17},{... | collective-permute-start | bytes 491528 | tf_op jit(solution)/shard_map/ppermute | solution.py:735
  63.3 1.7 slice.168
  68.2 1.7 slice.169
  73.0 2.2 collective-permute-start.7
  75.2 12.2 %near_own.6.refs_5_ = f32[16,256,256]{2,1,0:T(8,128)S(1)} custom-call(s32[432]{0:T(512)S(1)} %copy-done.28, bf16[16,256,256]{2,1,0:T(8,128)(2,1)S(1)} %bitcast.27, f32[16,2,256]{2,1,0:T(2,128)S(1)} %bitcast.39, f32[16,1,256]{2,1,0:T(1,128)S(1)} %reshape.60.refs_3_, ...), custom_call_target="tpu_custom_call", output_to_operand_aliasing={{}: (5, {})} | custom-call | flops 6000000000 | bytes 4000000 | tf_op jit(solution)/shard_map/near_own/pallas_call | solution.py:485
  88.9 9.0 %near_own.7.before_ref.refs_6_ = f32[16,256,256]{2,1,0:T(8,128)S(1)} custom-call(s32[432]{0:T(512)S(1)} %copy-done.28, bf16[16,256,256]{2,1,0:T(8,128)(2,1)S(1)} %bitcast.28, f32[16,2,256]{2,1,0:T(2,128)S(1)} %bitcast.40, f32[16,1,256]{2,1,0:T(1,128)S(1)} %reshape.60.refs_3_, ...), custom_call_target="tpu_custom_call", output_to_operand_aliasing={{}: (5, {})} | custom-call | flops 6000000000 | bytes 4000000 | tf_op jit(solution)/shard_map/near_own/pallas_call | solution.py:485
  97.9 2.0 copy-done.6
  101.9 7.6 %collective-permute-done.9 = bf16[640,256]{1,0:T(8,128)(2,1)S(1)} collective-permute-done((bf16[640,256]{1,0:T(8,128)(2,1)}, bf16[640,256]{1,0:T(8,128)(2,1)S(1)}, u32[]{:S(2)}, u32[]{:S(2)}) %collective-permute-start.9) | collective-permute-done | bytes 327712 | tf_op jit(solution)/shard_map/ppermute | solution.py:735
  111.2 2.0 pad_maximum_fusion.2
  113.2 13.4 %collective-permute-done.10 = bf16[1280,256]{1,0:T(8,128)(2,1)} collective-permute-done((bf16[1280,256]{1,0:T(8,128)(2,1)}, bf16[1280,256]{1,0:T(8,128)(2,1)}, u32[]{:S(2)}, u32[]{:S(2)}) %collective-permute-start.10) | collective-permute-done | bytes 655392 | tf_op jit(solution)/shard_map/ppermute | solution.py:735
  126.6 3.1 %collective-permute-start.14 = (bf16[2,4,256,256]{3,2,1,0:T(8,128)(2,1)}, bf16[2,4,256,256]{3,2,1,0:T(8,128)(2,1)}, u32[]{:S(2)}, u32[]{:S(2)}) collective-permute-start(bf16[2,4,256,256]{3,2,1,0:T(8,128)(2,1)} %get-tuple-element.55), channel_id=1, source_target_pairs={{1,0},{2,1},{3,2},{5,4},{6,5},{7,6},{9,8},{10,9},{11,10},{13,12},{... | collective-permute-start | bytes 3145736 | tf_op jit(solution)/shard_map/ppermute | solution.py:118
  130.9 2.5 %collective-permute-start.6 = (bf16[1936,256]{1,0:T(8,128)(2,1)}, bf16[1936,256]{1,0:T(8,128)(2,1)}, u32[]{:S(2)}, u32[]{:S(2)}) collective-permute-start(bf16[1936,256]{1,0:T(8,128)(2,1)} %pad_maximum_fusion.2), channel_id=1, source_target_pairs={{0,1},{1,2},{2,3},{4,5},{5,6},{6,7},{8,9},{9,10},{10,11},{12,13},{... | collective-permute-start | bytes 2973704 | tf_op jit(solution)/shard_map/ppermute | solution.py:118
  134.4 10.5 %collective-permute-done.6.north_any = bf16[1936,256]{1,0:T(8,128)(2,1)} collective-permute-done((bf16[1936,256]{1,0:T(8,128)(2,1)}, bf16[1936,256]{1,0:T(8,128)(2,1)}, u32[]{:S(2)}, u32[]{:S(2)}) %collective-permute-start.6) | collective-permute-done | bytes 991264 | tf_op jit(solution)/shard_map/ppermute | solution.py:118
  145.9 2.2 copy-done.7
  148.1 24.4 %edge_blocks.1.refs_5_.block_ref.extra_ref = bf16[60,256,256]{2,1,0:T(8,128)(2,1)S(1)} custom-call(s32[160]{0:T(256)S(1)} %reshape.56.list_ref, s32[176]{0:T(256)S(1)} %copy-done.29, s32[64]{0:T(128)S(1)} %copy-done.27, f32[16,2,256]{2,1,0:T(2,128)S(1)} %bitcast.41, f32[48,2,256]{2,1,0:T(2,128)S(1)} %constant_dynamic-update-slice_fusion.12.pos_ref, ...), custom_call_target="tpu_custom_call" | custom-call | flops 12000000000 | bytes 8000000 | tf_op jit(solution)/shard_map/edge_blocks/pallas_call | solution.py:564
  172.6 3.1 %copy-done = bf16[60,256,256]{2,1,0:T(8,128)(2,1)} copy-done((bf16[60,256,256]{2,1,0:T(8,128)(2,1)}, bf16[60,256,256]{2,1,0:T(8,128)(2,1)S(1)}, u32[]{:S(2)}) %copy-start) | copy-done | bytes 7864344
  175.8 12.0 %far.1.refs_8_ = bf16[16,64,256]{2,1,0:T(8,128)(2,1)S(1)} custom-call(s32[160]{0:T(256)S(1)} %reshape.56.list_ref, s32[74]{0:T(128)S(1)} %pad_add_fusion.meta_ref, bf16[1280,256]{1,0:T(8,128)(2,1)S(1)} %copy-done.20, bf16[816,256]{1,0:T(8,128)(2,1)} %collective-permute-done.2.west_any, bf16[816,256]{1,0:T(8,128)(2,1)} %collective-permute-done.3.east_any, ...), custom_call_target="tpu_custom_call" | custom-call | flops 2500000000 | bytes 12000000 | tf_op jit(solution)/shard_map/far/pallas_call | solution.py:375
  189.2 2.1 collective-permute-start.12
  192.4 6.9 %collective-permute-start.11 = (bf16[2,2,2,256,256]{4,3,2,1,0:T(8,128)(2,1)}, bf16[2,2,2,256,256]{4,3,2,1,0:T(8,128)(2,1)S(1)}, u32[]{:S(2)}, u32[]{:S(2)}) collective-permute-start(bf16[2,2,2,256,256]{4,3,2,1,0:T(8,128)(2,1)} %pad_maximum_fusion), channel_id=1, source_target_pairs={{0,1},{1,2},{2,3},{4,5},{5,6},{6,7},{8,9},{9,10},{10,11},{12,13},{... | collective-permute-start | bytes 3145736 | tf_op jit(solution)/shard_map/ppermute | solution.py:118
  199.3 14.1 %add_sides.1.sum_ref = f32[16,256,256]{2,1,0:T(8,128)} custom-call(s32[160]{0:T(256)S(1)} %reshape.56.list_ref, s32[64]{0:T(128)S(1)} %copy-done.27, bf16[4,2,256,256]{3,2,1,0:T(8,128)(2,1)S(1)} %collective-permute-done.before_ref, bf16[16,256,256]{2,1,0:T(8,128)(2,1)} %bitcast.23, bf16[8,256,256]{2,1,0:T(8,128)(2,1)S(1)} %bitcast.29, ...), custom_call_target="tpu_custom_call" | custom-call | flops 4000000000 | bytes 24000000 | tf_op jit(solution)/shard_map/add_sides/pallas_call | solution.py:623
  213.5 2.2 copy-done.3
  215.7 8.2 %add_corners.1 = bf16[16,256,256]{2,1,0:T(8,128)(2,1)} custom-call(s32[160]{0:T(256)S(1)} %reshape.56.list_ref, s32[64]{0:T(128)S(1)} %copy-done.27, bf16[8,256,256]{2,1,0:T(8,128)(2,1)S(1)} %bitcast.35, bf16[8,256,256]{2,1,0:T(8,128)(2,1)S(1)} %bitcast.34, bf16[60,256,256]{2,1,0:T(8,128)(2,1)S(1)} %bitcast.22, bf16[60,256,256]{2,1,0:T(8,128)(2,1)S(1)} %bitcast.22, ...), custom_call_target="tpu_custom_call" | custom-call | flops 500000000 | bytes 10000000 | tf_op jit(solution)/shard_map/add_corners/pallas_call | solution.py:666
  (138 shorter events, 31.9 us)
Async XLA Ops:
  8.3 28.4 %collective-permute-start.4 = (bf16[80,256]{1,0:T(8,128)(2,1)S(1)}, bf16[80,256]{1,0:T(8,128)(2,1)S(1)}, u32[]{:S(2)}, u32[]{:S(2)}) collective-permute-start(bf16[80,256]{1,0:T(8,128)(2,1)S(1)} %get-tuple-element.33.refs_4_), channel_id=1, source_target_pairs={{0,4},{4,0},{8,12},{12,8},{16,20},{20,16},{24,28},{28,24},{1,5},{5... | collective-permute-start | bytes 122888 | tf_op jit(solution)/shard_map/ppermute | solution.py:735
  10.3 47.6 %collective-permute-start.2 = (bf16[816,256]{1,0:T(8,128)(2,1)}, bf16[816,256]{1,0:T(8,128)(2,1)}, u32[]{:S(2)}, u32[]{:S(2)}) collective-permute-start(bf16[816,256]{1,0:T(8,128)(2,1)} %get-tuple-element.31), channel_id=1, source_target_pairs={{0,4},{4,8},{8,12},{12,16},{16,20},{20,24},{24,28},{1,5},{5,9},{9,... | collective-permute-start | bytes 1253384 | tf_op jit(solution)/shard_map/ppermute | solution.py:118
  13.0 50.3 %collective-permute-start.3 = (bf16[816,256]{1,0:T(8,128)(2,1)}, bf16[816,256]{1,0:T(8,128)(2,1)}, u32[]{:S(2)}, u32[]{:S(2)}) collective-permute-start(bf16[816,256]{1,0:T(8,128)(2,1)} %get-tuple-element.32), channel_id=1, source_target_pairs={{4,0},{8,4},{12,8},{16,12},{20,16},{24,20},{28,24},{5,1},{9,5},{13... | collective-permute-start | bytes 1253384 | tf_op jit(solution)/shard_map/ppermute | solution.py:118
  15.9 171.9 %collective-permute-start = (bf16[4,2,256,256]{3,2,1,0:T(8,128)(2,1)}, bf16[4,2,256,256]{3,2,1,0:T(8,128)(2,1)S(1)}, u32[]{:S(2)}, u32[]{:S(2)}) collective-permute-start(bf16[4,2,256,256]{3,2,1,0:T(8,128)(2,1)} %get-tuple-element.58), channel_id=1, source_target_pairs={{0,4},{4,8},{8,12},{12,16},{16,20},{20,24},{24,28},{1,5},{5,9},{9,... | collective-permute-start | bytes 3145736 | tf_op jit(solution)/shard_map/ppermute | solution.py:118
  20.2 167.6 %collective-permute-start.1 = (bf16[4,2,256,256]{3,2,1,0:T(8,128)(2,1)}, bf16[4,2,256,256]{3,2,1,0:T(8,128)(2,1)}, u32[]{:S(2)}, u32[]{:S(2)}) collective-permute-start(bf16[4,2,256,256]{3,2,1,0:T(8,128)(2,1)} %get-tuple-element.57), channel_id=1, source_target_pairs={{4,0},{8,4},{12,8},{16,12},{20,16},{24,20},{28,24},{5,1},{9,5},{13... | collective-permute-start | bytes 3145736 | tf_op jit(solution)/shard_map/ppermute | solution.py:118
  25.5 11.1 %copy-start.32 = (s32[4,4,10]{2,1,0:T(4,128)S(1)}, s32[4,4,10]{2,1,0:T(4,128)}, u32[]{:S(2)}) copy-start(s32[4,4,10]{2,1,0:T(4,128)} %param.24) | copy-start | bytes 1924
  51.0 2.5 %collective-permute-start.5 = (bf16[160,256]{1,0:T(8,128)(2,1)S(1)}, bf16[160,256]{1,0:T(8,128)(2,1)S(1)}, u32[]{:S(2)}, u32[]{:S(2)}) collective-permute-start(bf16[160,256]{1,0:T(8,128)(2,1)S(1)} %pad_maximum_fusion.5), channel_id=1, source_target_pairs={{0,1},{1,0},{2,3},{3,2},{4,5},{5,4},{6,7},{7,6},{8,9},{9,8},{10,11... | collective-permute-start | bytes 245768 | tf_op jit(solution)/shard_map/ppermute | solution.py:735
  53.6 145.7 %collective-permute-start.13 = (bf16[2,4,256,256]{3,2,1,0:T(8,128)(2,1)}, bf16[2,4,256,256]{3,2,1,0:T(8,128)(2,1)}, u32[]{:S(2)}, u32[]{:S(2)}) collective-permute-start(bf16[2,4,256,256]{3,2,1,0:T(8,128)(2,1)} %get-tuple-element.56), channel_id=1, source_target_pairs={{0,1},{1,2},{2,3},{4,5},{5,6},{6,7},{8,9},{9,10},{10,11},{12,13},{... | collective-permute-start | bytes 3145736 | tf_op jit(solution)/shard_map/ppermute | solution.py:118
  57.9 30.2 %collective-permute-start.8 = (bf16[320,256]{1,0:T(8,128)(2,1)S(1)}, bf16[320,256]{1,0:T(8,128)(2,1)S(1)}, u32[]{:S(2)}, u32[]{:S(2)}) collective-permute-start(bf16[320,256]{1,0:T(8,128)(2,1)S(1)} %pad_maximum_fusion.4), channel_id=1, source_target_pairs={{0,16},{4,20},{8,24},{12,28},{16,0},{20,4},{24,8},{28,12},{1,17},{... | collective-permute-start | bytes 491528 | tf_op jit(solution)/shard_map/ppermute | solution.py:735
  73.0 57.9 %collective-permute-start.7 = (bf16[1936,256]{1,0:T(8,128)(2,1)}, bf16[1936,256]{1,0:T(8,128)(2,1)}, u32[]{:S(2)}, u32[]{:S(2)}) collective-permute-start(bf16[1936,256]{1,0:T(8,128)(2,1)} %slice_dynamic-update-slice_fusion), channel_id=1, source_target_pairs={{1,0},{2,1},{3,2},{5,4},{6,5},{7,6},{9,8},{10,9},{11,10},{13,12},{... | collective-permute-start | bytes 2973704 | tf_op jit(solution)/shard_map/ppermute | solution.py:118
  99.9 11.3 %copy-start.23 = (bf16[816,256]{1,0:T(8,128)(2,1)S(1)}, bf16[816,256]{1,0:T(8,128)(2,1)}, u32[]{:S(2)}) copy-start(bf16[816,256]{1,0:T(8,128)(2,1)} %copy-done.22) | copy-start | bytes 1253380
  99.9 11.3 %copy-start.30 = (bf16[560,256]{1,0:T(8,128)(2,1)S(1)}, bf16[560,256]{1,0:T(8,128)(2,1)}, u32[]{:S(2)}) copy-start(bf16[560,256]{1,0:T(8,128)(2,1)} %slice.168) | copy-start | bytes 860164
  99.9 9.6 %collective-permute-start.9 = (bf16[640,256]{1,0:T(8,128)(2,1)}, bf16[640,256]{1,0:T(8,128)(2,1)S(1)}, u32[]{:S(2)}, u32[]{:S(2)}) collective-permute-start(bf16[640,256]{1,0:T(8,128)(2,1)} %pad_maximum_fusion.3), channel_id=1, source_target_pairs={{0,8},{4,12},{8,0},{12,4},{16,24},{20,28},{24,16},{28,20},{1,9},{5... | collective-permute-start | bytes 983048 | tf_op jit(solution)/shard_map/ppermute | solution.py:735
  110.4 19.4 %copy-start.10 = (bf16[2560,256]{1,0:T(8,128)(2,1)S(1)}, bf16[2560,256]{1,0:T(8,128)(2,1)}, u32[]{:S(2)}) copy-start(bf16[2560,256]{1,0:T(8,128)(2,1)} %get-tuple-element.70) | copy-start | bytes 3932164
  110.4 16.2 %collective-permute-start.10 = (bf16[1280,256]{1,0:T(8,128)(2,1)}, bf16[1280,256]{1,0:T(8,128)(2,1)}, u32[]{:S(2)}, u32[]{:S(2)}) collective-permute-start(bf16[1280,256]{1,0:T(8,128)(2,1)} %get-tuple-element.69), channel_id=1, source_target_pairs={{0,2},{1,3},{2,0},{3,1},{4,6},{5,7},{6,4},{7,5},{8,10},{9,11},{10,... | collective-permute-start | bytes 1966088 | tf_op jit(solution)/shard_map/ppermute | solution.py:735
  126.6 72.7 %collective-permute-start.14 = (bf16[2,4,256,256]{3,2,1,0:T(8,128)(2,1)}, bf16[2,4,256,256]{3,2,1,0:T(8,128)(2,1)}, u32[]{:S(2)}, u32[]{:S(2)}) collective-permute-start(bf16[2,4,256,256]{3,2,1,0:T(8,128)(2,1)} %get-tuple-element.55), channel_id=1, source_target_pairs={{1,0},{2,1},{3,2},{5,4},{6,5},{7,6},{9,8},{10,9},{11,10},{13,12},{... | collective-permute-start | bytes 3145736 | tf_op jit(solution)/shard_map/ppermute | solution.py:118
  129.7 16.1 %copy-start.27 = (s32[64]{0:T(128)S(1)}, s32[64]{0:T(128)}, u32[]{:S(2)}) copy-start(s32[64]{0:T(128)} %constant.197.clone.slot_ref) | copy-start | bytes 772
  129.8 16.1 %copy-start.29 = (s32[176]{0:T(256)S(1)}, s32[176]{0:T(256)}, u32[]{:S(2)}) copy-start(s32[176]{0:T(256)} %constant.196.clone.table_ref) | copy-start | bytes 2116
  130.9 14.9 %copy-start.11 = (bf16[2560,256]{1,0:T(8,128)(2,1)}, bf16[2560,256]{1,0:T(8,128)(2,1)S(1)}, u32[]{:S(2)}) copy-start(bf16[2560,256]{1,0:T(8,128)(2,1)S(1)} %constant_dynamic-update-slice_fusion.6.all_any) | copy-start | bytes 3932164
  130.9 14.0 %collective-permute-start.6 = (bf16[1936,256]{1,0:T(8,128)(2,1)}, bf16[1936,256]{1,0:T(8,128)(2,1)}, u32[]{:S(2)}, u32[]{:S(2)}) collective-permute-start(bf16[1936,256]{1,0:T(8,128)(2,1)} %pad_maximum_fusion.2), channel_id=1, source_target_pairs={{0,1},{1,2},{2,3},{4,5},{5,6},{6,7},{8,9},{9,10},{10,11},{12,13},{... | collective-permute-start | bytes 2973704 | tf_op jit(solution)/shard_map/ppermute | solution.py:118
  148.1 27.6 %copy-start.12 = (bf16[2560,256]{1,0:T(8,128)(2,1)S(1)}, bf16[2560,256]{1,0:T(8,128)(2,1)}, u32[]{:S(2)}) copy-start(bf16[2560,256]{1,0:T(8,128)(2,1)} %copy-done.11) | copy-start | bytes 3932164
  148.1 27.6 %copy-start.14 = (bf16[1,1,21,64,64]{4,3,2,1,0:T(8,128)(2,1)S(1)}, bf16[1,1,21,64,64]{4,3,2,1,0:T(8,128)(2,1)}, u32[]{:S(2)}) copy-start(bf16[1,1,21,64,64]{4,3,2,1,0:T(8,128)(2,1)} %param.23) | copy-start | bytes 516100
  148.1 27.6 %copy-start.15 = (bf16[256,2304]{1,0:T(8,128)(2,1)S(1)}, bf16[256,2304]{1,0:T(8,128)(2,1)}, u32[]{:S(2)}) copy-start(bf16[256,2304]{1,0:T(8,128)(2,1)} %constant.198.clone.c0_any) | copy-start | bytes 3538948
  148.1 27.6 %copy-start.16 = (bf16[256,2304]{1,0:T(8,128)(2,1)S(1)}, bf16[256,2304]{1,0:T(8,128)(2,1)}, u32[]{:S(2)}) copy-start(bf16[256,2304]{1,0:T(8,128)(2,1)} %constant.199.clone.c1_any) | copy-start | bytes 3538948
  148.1 27.6 %copy-start.17 = (bf16[256,2304]{1,0:T(8,128)(2,1)S(1)}, bf16[256,2304]{1,0:T(8,128)(2,1)}, u32[]{:S(2)}) copy-start(bf16[256,2304]{1,0:T(8,128)(2,1)} %constant.200.clone.c2_any) | copy-start | bytes 3538948
  148.1 27.6 %copy-start.18 = (bf16[256,2304]{1,0:T(8,128)(2,1)S(1)}, bf16[256,2304]{1,0:T(8,128)(2,1)}, u32[]{:S(2)}) copy-start(bf16[256,2304]{1,0:T(8,128)(2,1)} %constant.201.clone.c3_any) | copy-start | bytes 3538948
  148.1 27.6 %copy-start.20 = (bf16[1280,256]{1,0:T(8,128)(2,1)S(1)}, bf16[1280,256]{1,0:T(8,128)(2,1)}, u32[]{:S(2)}) copy-start(bf16[1280,256]{1,0:T(8,128)(2,1)} %copy-done.19) | copy-start | bytes 1966084
  148.1 27.6 %copy-start.24 = (bf16[25,64,64]{2,1,0:T(8,128)(2,1)S(1)}, bf16[25,64,64]{2,1,0:T(8,128)(2,1)}, u32[]{:S(2)}) copy-start(bf16[25,64,64]{2,1,0:T(8,128)(2,1)} %constant.202.clone.code_any) | copy-start | bytes 614404
  189.2 24.2 %collective-permute-start.12 = (bf16[2,2,2,256,256]{4,3,2,1,0:T(8,128)(2,1)S(1)}, bf16[2,2,2,256,256]{4,3,2,1,0:T(8,128)(2,1)S(1)}, u32[]{:S(2)}, u32[]{:S(2)}) collective-permute-start(bf16[2,2,2,256,256]{4,3,2,1,0:T(8,128)(2,1)S(1)} %pad_maximum_fusion.1), channel_id=1, source_target_pairs={{1,0},{2,1},{3,2},{5,4},{6,5},{7,6},{9,8},{10,9},{11,10},{13,12},{... | collective-permute-start | bytes 3145736 | tf_op jit(solution)/shard_map/ppermute | solution.py:118
  192.4 21.1 %collective-permute-start.11 = (bf16[2,2,2,256,256]{4,3,2,1,0:T(8,128)(2,1)}, bf16[2,2,2,256,256]{4,3,2,1,0:T(8,128)(2,1)S(1)}, u32[]{:S(2)}, u32[]{:S(2)}) collective-permute-start(bf16[2,2,2,256,256]{4,3,2,1,0:T(8,128)(2,1)} %pad_maximum_fusion), channel_id=1, source_target_pairs={{0,1},{1,2},{2,3},{4,5},{5,6},{6,7},{8,9},{9,10},{10,11},{12,13},{... | collective-permute-start | bytes 3145736 | tf_op jit(solution)/shard_map/ppermute | solution.py:118
  199.3 14.1 %slice-start = ((s8[7864320]{0:T(1024)(128)(4,1)}), s8[4194304]{0:T(1024)(128)(4,1)S(1)}, s32[]{:S(2)}) async-start(s8[7864320]{0:T(1024)(128)(4,1)} %bitcast.21), calls=%async_computation | async-start | bytes 8388608
  199.3 14.1 %slice-start.1 = ((s8[7864320]{0:T(1024)(128)(4,1)}), s8[3670016]{0:T(1024)(128)(4,1)S(1)}, s32[]{:S(2)}) async-start(s8[7864320]{0:T(1024)(128)(4,1)} %bitcast.21), calls=%async_computation.1 | async-start | bytes 7340032
  (20 other events, 83.4 us)

commit v3 on v2

v3 whole, which is shorter than its diff:
```python
import math

import jax
import jax.numpy as jnp
import ml_dtypes
import numpy as np
from jax import lax
from jax.experimental import pallas as pl
from jax.experimental.pallas import tpu as pltpu
from jax.sharding import PartitionSpec as P

LEAF = 256
CHEB = 8
RANK = 64
NEAR = 10
SIDE = 4
LEAVES = SIDE * SIDE
TOP = 20
WINDOW = 36
PACK = RANK + 16
SIDEWAYS = 8 * RANK + 4 * RANK + 48
CORNER = 4 * RANK + 4 * RANK + 48
COPIES = 42
BF = jnp.bfloat16
F32 = jnp.float32

short_len = 0.125
long_weight = 0.03125
reach = 3.0 * SIDE
waves = 10.0
LOG2E = math.log2(math.e)
long_rate = -0.5 / (reach * reach) * LOG2E / (waves * waves)
short_rate = -0.5 / (short_len * short_len) * LOG2E / (waves * waves)
rounder = 1.5 * 2.0**23


def sine_terms(count):
    w = np.cos(np.pi * (np.arange(2000) + 0.5) / 2000) * 0.25
    powers = np.stack([w ** (2 * i + 1) for i in range(count)], 1)
    return [float(c) for c in np.linalg.lstsq(powers, np.sin(2 * np.pi * w) * long_weight, rcond=None)[0]]


SINE = sine_terms(4)


def coupling(height, shift_y, shift_x):
    points = 0.5 * (1.0 + np.cos((2.0 * np.arange(CHEB) + 1.0) * (math.pi / (2.0 * CHEB))))
    node_x = np.tile(points, CHEB)
    node_y = np.repeat(points, CHEB)
    gap_x = (node_x[:, None] - node_x[None, :] - shift_x) * 2.0**height
    gap_y = (node_y[:, None] - node_y[None, :] - shift_y) * 2.0**height
    squared = gap_x * gap_x + gap_y * gap_y
    return np.exp(squared * (-0.5 / (short_len * short_len))) + long_weight * np.exp(
        squared * (-0.5 / (reach * reach))
    ) * np.cos(2.0 * math.pi * waves * np.sqrt(squared))


def window_coupling(height):
    table = np.zeros((2, 2, RANK, 6, 6, RANK))
    for py in range(2):
        for px in range(2):
            for wy in range(6):
                for wx in range(6):
                    shift_y, shift_x = wy - 2 - py, wx - 2 - px
                    if max(abs(shift_y), abs(shift_x)) >= 2:
                        table[py, px, :, wy, wx] = coupling(height, shift_y, shift_x)
    return table.reshape(4 * RANK, WINDOW * RANK).astype(ml_dtypes.bfloat16)


def code_coupling():
    return np.stack([coupling(0, code // 5 - 2, code % 5 - 2) for code in range(25)]).astype(ml_dtypes.bfloat16)


def halo_slot(row, col):
    if 0 <= row < 4 and 0 <= col < 4:
        return row * 4 + col
    if 0 <= row < 4:
        return 16 + row * 2 + col + 2 if col < 0 else 24 + row * 2 + col - 4
    base, r = (32, row + 2) if row < 0 else (48, row - 4)
    if 0 <= col < 4:
        return base + r * 4 + col
    return base + 8 + r * 2 + col + 2 if col < 0 else base + 12 + r * 2 + col - 4


SLOT_OF = np.array([halo_slot(r - 2, c - 2) for r in range(8) for c in range(8)], np.int32)


def near_table(own):
    width = 9 if own else 5
    table = np.zeros((LEAVES, width, 3), np.int32)
    table[:, :, 0] = -1
    for r in range(SIDE):
        for c in range(SIDE):
            at = 0
            for dy in (-1, 0, 1):
                for dx in (-1, 0, 1):
                    slot = halo_slot(r + dy, c + dx)
                    if (slot < LEAVES) == own:
                        table[r * SIDE + c, at] = (slot, dy, dx)
                        at += 1
    return table


def bits(count):
    return [1 << i for i in range(count.bit_length() - 1)]


def gather_steps(wide, narrow):
    return (
        [("wide", 1), ("narrow", 1)]
        + [("wide", b) for b in reversed(bits(wide)[1:])]
        + [("narrow", b) for b in reversed(bits(narrow)[1:])]
    )


def shift(value, axis, steps):
    count = lax.axis_size(axis)
    return lax.ppermute(value, axis, [(i, i + steps) for i in range(count) if 0 <= i + steps < count])


def dot(a, b):
    return jnp.dot(a, b, preferred_element_type=F32)


def dot_first(a, b):
    return lax.dot_general(a, b, (((0,), (0,)), ((), ())), preferred_element_type=F32)


def up_body(q_ref, basis_ref, tree_ref, pos_ref, east_ref, west_ref, north_ref, south_ref, coef_ref, give_ref):
    level0 = []
    for leaf in range(LEAVES):
        coef = dot(basis_ref[leaf], q_ref[leaf]).astype(BF)
        level0.append(coef)
        r, c = leaf // SIDE, leaf % SIDE
        coef_ref[leaf * RANK : (leaf + 1) * RANK] = coef
        ref, at = (west_ref, r * 2 + c) if c < 2 else (east_ref, r * 2 + c - 2)
        ref[at * RANK : (at + 1) * RANK] = coef
        ref, at = (north_ref, r * 4 + c) if r < 2 else (south_ref, r * 4 + c - 8)
        ref[at * RANK : (at + 1) * RANK] = coef
    level1 = []
    for r in range(2):
        for c in range(2):
            total = None
            for dr in range(2):
                for dc in range(2):
                    leaf = (2 * r + dr) * SIDE + 2 * c + dc
                    part = dot(tree_ref[leaf], level0[leaf])
                    total = part if total is None else total + part
            coef = total.astype(BF)
            at = r * 2 + c
            level1.append(coef)
            coef_ref[(LEAVES + at) * RANK : (LEAVES + at + 1) * RANK] = coef
            for ref in (east_ref, west_ref, north_ref, south_ref):
                ref[(8 + at) * RANK : (9 + at) * RANK] = coef
    total = None
    for at in range(4):
        part = dot(tree_ref[LEAVES + at], level1[at])
        total = part if total is None else total + part
    give_ref[0:RANK] = total.astype(BF)
    top = tree_ref[TOP]
    give_ref[RANK:PACK] = jnp.concatenate([top[16 * k : 16 * k + 16] for k in range(4)], axis=1)
    for ref, leaves in (
        (west_ref, [r * 4 + c for r in range(4) for c in (0, 1)]),
        (east_ref, [r * 4 + c for r in range(4) for c in (2, 3)]),
        (north_ref, range(8)),
        (south_ref, range(8, 16)),
    ):
        rest = jnp.concatenate([pos_ref[leaf] for leaf in leaves], axis=0)
        for part in range(3):
            held = rest.astype(BF)
            at = 12 * RANK + 16 * part
            ref[at : at + 16] = held
            rest = rest - held.astype(F32)


def go_up(q, basis, tree, points):
    vmem = pl.BlockSpec(memory_space=pltpu.VMEM)
    side = jax.ShapeDtypeStruct((SIDEWAYS, LEAF), BF)
    return pl.pallas_call(
        up_body,
        out_shape=(
            side,
            side,
            side,
            side,
            jax.ShapeDtypeStruct(((LEAVES + 4) * RANK, LEAF), BF),
            jax.ShapeDtypeStruct((PACK, LEAF), BF),
        ),
        in_specs=[vmem] * 4,
        out_specs=[vmem] * 6,
        compiler_params=pltpu.CompilerParams(vmem_limit_bytes=32 << 20),
        cost_estimate=pl.CostEstimate(flops=300_000_000, bytes_accessed=5_000_000, transcendentals=0),
        name="upward",
    )(q, basis, tree, points)


def local_body(
    list_ref, coef_any, west_any, east_any, north_any, south_any, c0_any, c1_any, code_any, sum0, sum1, pad0, pad1, c0_ref, c1_ref, code_ref, sems
):
    loads = []

    def load(source, at, to, row, count):
        rows = pl.ds(at * RANK if at < 100 else at, count * RANK)
        copy = pltpu.make_async_copy(source.at[rows], to.at[pl.ds(row, count * RANK)], sems.at[len(loads)])
        copy.start()
        loads.append(copy)

    def put(pad, extent, row, col, ref, at, count):
        load(ref, at, pad, ((row + 2) * (extent + 4) + col + 2) * RANK, count)

    whole = []
    for k, (source, to) in enumerate(((c0_any, c0_ref), (c1_any, c1_ref), (code_any, code_ref))):
        whole.append(pltpu.make_async_copy(source, to, sems.at[COPIES + k]))
    whole[0].start()
    for r in range(4):
        put(pad0, 4, r, 0, coef_any, r * 4, 4)
        put(pad0, 4, r, -2, west_any, r * 2, 2)
        put(pad0, 4, r, 4, east_any, r * 2, 2)
    for ref, row in ((north_any, -2), (south_any, 4)):
        for r in range(2):
            put(pad0, 4, row + r, 0, ref, r * 4, 4)
            for col, base in ((-2, SIDEWAYS), (4, SIDEWAYS + CORNER)):
                load(ref, base + r * 2 * RANK, pad0, ((row + r + 2) * 8 + col + 2) * RANK, 2)
    split = len(loads)
    for copy in whole[1:]:
        copy.start()
    for r in range(2):
        put(pad1, 2, r, 0, coef_any, LEAVES + r * 2, 2)
        put(pad1, 2, r, -2, west_any, 8 + r * 2, 2)
        put(pad1, 2, r, 2, east_any, 8 + r * 2, 2)
    for ref, row in ((north_any, -2), (south_any, 2)):
        for r in range(2):
            put(pad1, 2, row + r, 0, ref, 8 + r * 2, 2)
            for col, base in ((-2, SIDEWAYS), (2, SIDEWAYS + CORNER)):
                load(ref, base + (4 + r * 2) * RANK, pad1, ((row + r + 2) * 6 + col + 2) * RANK, 2)
    whole[0].wait()
    for copy in loads[:split]:
        copy.wait()
    for a in range(2):
        for b in range(2):
            total = None
            for wy in range(6):
                at = ((2 * a + wy) * 8 + 2 * b) * RANK
                part = dot(c0_ref[:, wy * 6 * RANK : (wy + 1) * 6 * RANK], pad0[at : at + 6 * RANK])
                total = part if total is None else total + part
            for child in range(4):
                leaf = (2 * a + child // 2) * SIDE + 2 * b + child % 2
                sum0[leaf] = total[child * RANK : (child + 1) * RANK]
    for copy in loads[split:] + whole[1:]:
        copy.wait()

    def listed(leaf, carry):
        code = second_cycle(list_ref, leaf)

        @pl.when(code >= 0)
        def _():
            row = leaf // SIDE + code // 5
            col = leaf % SIDE + code % 5
            at = pl.multiple_of((row * 8 + col) * RANK, RANK)
            sum0[leaf] = sum0[leaf] - dot(code_ref[code], pad0[pl.ds(at, RANK)])

        return carry

    lax.fori_loop(0, LEAVES, listed, 0)
    sum1[...] = dot(c1_ref[...], pad1[...])


def local_far(near_list, coefs, west, east, north, south):
    vmem = pl.BlockSpec(memory_space=pltpu.VMEM)
    smem = pl.BlockSpec(memory_space=pltpu.SMEM)
    return pl.pallas_call(
        local_body,
        out_shape=(
            jax.ShapeDtypeStruct((LEAVES, RANK, LEAF), F32),
            jax.ShapeDtypeStruct((4 * RANK, LEAF), F32),
        ),
        in_specs=[smem] + [pl.BlockSpec(memory_space=pl.ANY)] * 8,
        out_specs=[vmem] * 2,
        scratch_shapes=[
            pltpu.VMEM((64 * RANK, LEAF), BF),
            pltpu.VMEM((WINDOW * RANK, LEAF), BF),
            pltpu.VMEM((4 * RANK, WINDOW * RANK), BF),
            pltpu.VMEM((4 * RANK, WINDOW * RANK), BF),
            pltpu.VMEM((25, RANK, RANK), BF),
            pltpu.SemaphoreType.DMA((COPIES + 3,)),
        ],
        compiler_params=pltpu.CompilerParams(vmem_limit_bytes=32 << 20),
        cost_estimate=pl.CostEstimate(flops=5_000_000_000, bytes_accessed=8_000_000, transcendentals=0),
        name="local_far",
    )(
        near_list,
        coefs,
        west,
        east,
        north,
        south,
        jnp.asarray(window_coupling(0)),
        jnp.asarray(window_coupling(1)),
        jnp.asarray(code_coupling()),
    )


def top_body(meta_ref, all_ref, c2_any, c3_any, tree_ref, sum0, sum1, field_ref, win, parents, c2_ref, c3_ref, sems):
    def slab(source, to, at):
        part = pl.ds(pl.multiple_of(meta_ref[2 * WINDOW + at] * RANK, RANK), RANK)
        copy = pltpu.make_async_copy(source.at[part], to, sems.at[at])
        copy.start()
        return copy

    slabs = [slab(c2_any, c2_ref, 0), slab(c3_any, c3_ref, 1)]

    def lift(group, carry):
        total = jnp.zeros((RANK, LEAF), F32)
        for child in range(4):
            at = pl.multiple_of((group * 4 + child) * PACK, 16)
            packed = all_ref[pl.ds(at + RANK, 16)]
            matrix = jnp.concatenate([packed[:, k * RANK : (k + 1) * RANK] for k in range(4)], axis=0)
            total = total + dot(matrix, all_ref[pl.ds(at, RANK)])
        parents[pl.ds(pl.multiple_of(group * RANK, RANK), RANK)] = total.astype(BF)
        return carry

    lax.fori_loop(0, parents.shape[0] // RANK, lift, 0)

    def fill(start, source, stride):
        def one(i, carry):
            slot = meta_ref[start + i]
            to = pl.ds(pl.multiple_of(i * RANK, RANK), RANK)

            @pl.when(slot >= 0)
            def _():
                win[to] = source[pl.ds(pl.multiple_of(slot * stride, 16), RANK)]

            @pl.when(slot < 0)
            def _():
                win[to] = jnp.zeros((RANK, LEAF), BF)

            return carry

        lax.fori_loop(0, WINDOW, one, 0)

    fill(WINDOW, parents, RANK)
    slabs[1].wait()
    field3 = dot(c3_ref[...], win[...]).astype(BF)
    fill(0, all_ref, PACK)
    slabs[0].wait()
    field2 = (dot(c2_ref[...], win[...]) + dot_first(tree_ref[TOP], field3)).astype(BF)
    field1 = []
    for at in range(4):
        field1.append(
            (sum1[at * RANK : (at + 1) * RANK] + dot_first(tree_ref[LEAVES + at], field2)).astype(BF)
        )
    for leaf in range(LEAVES):
        above = field1[leaf // SIDE // 2 * 2 + leaf % SIDE // 2]
        field_ref[leaf] = (sum0[leaf] + dot_first(tree_ref[leaf], above)).astype(BF)


def second_cycle(list_ref, leaf):
    found = jnp.int32(-1)
    for j in range(NEAR):
        code = list_ref[leaf * NEAR + j]
        y, x = code // 5, code % 5
        outer = (code >= 0) & ((y == 0) | (y == 4) | (x == 0) | (x == 4))
        found = jnp.where(outer, code, found)
    return found


def top_far(meta, gathered, tree, sum0, sum1):
    vmem = pl.BlockSpec(memory_space=pltpu.VMEM)
    smem = pl.BlockSpec(memory_space=pltpu.SMEM)
    anywhere = pl.BlockSpec(memory_space=pl.ANY)
    devices = gathered.shape[0] // PACK
    return pl.pallas_call(
        top_body,
        out_shape=jax.ShapeDtypeStruct((LEAVES, RANK, LEAF), BF),
        in_specs=[smem, vmem, anywhere, anywhere, vmem, vmem, vmem],
        out_specs=vmem,
        scratch_shapes=[
            pltpu.VMEM((WINDOW * RANK, LEAF), BF),
            pltpu.VMEM((devices // 4 * RANK, LEAF), BF),
            pltpu.VMEM((RANK, WINDOW * RANK), BF),
            pltpu.VMEM((RANK, WINDOW * RANK), BF),
            pltpu.SemaphoreType.DMA((2,)),
        ],
        compiler_params=pltpu.CompilerParams(vmem_limit_bytes=32 << 20),
        cost_estimate=pl.CostEstimate(flops=3_000_000_000, bytes_accessed=5_000_000, transcendentals=0),
        name="top_far",
    )(meta, gathered, jnp.asarray(window_coupling(2)), jnp.asarray(window_coupling(3)), tree, sum0, sum1)


def join_body(north_ref, south_ref, west_ref, east_ref, to_north, to_south, sems):
    copies = []

    def move(source, at, to, row, count):
        copy = pltpu.make_async_copy(source.at[pl.ds(at, count)], to.at[pl.ds(row, count)], sems.at[len(copies)])
        copy.start()
        copies.append(copy)

    for own, to, lower in ((north_ref, to_north, 0), (south_ref, to_south, 1)):
        move(own, 0, to, 0, SIDEWAYS)
        for side, base in ((west_ref, SIDEWAYS), (east_ref, SIDEWAYS + CORNER)):
            move(side, 4 * RANK * lower, to, base, 4 * RANK)
            move(side, 8 * RANK, to, base + 4 * RANK, CORNER - 4 * RANK)
    for copy in copies:
        copy.wait()


def join(north, south, west, east):
    anywhere = pl.BlockSpec(memory_space=pl.ANY)
    message = jax.ShapeDtypeStruct((SIDEWAYS + 2 * CORNER, LEAF), BF)
    return pl.pallas_call(
        join_body,
        out_shape=(message, message),
        in_specs=[anywhere] * 4,
        out_specs=[anywhere] * 2,
        scratch_shapes=[pltpu.SemaphoreType.DMA((10,))],
        cost_estimate=pl.CostEstimate(flops=0, bytes_accessed=4_000_000, transcendentals=0),
        name="join",
    )(north, south, west, east)


def kernel_of(target_x, target_y, source_x, source_y):
    gap_x = target_x - source_x
    gap_y = target_y - source_y
    squared = jnp.maximum(gap_x * gap_x + gap_y * gap_y, 1e-12)
    length = squared * lax.rsqrt(squared)
    phase = length - ((length + rounder) - rounder)
    w = 0.25 - jnp.abs(phase)
    s = w * w
    wave = w * (SINE[0] + s * (SINE[1] + s * (SINE[2] + s * SINE[3])))
    return (jnp.exp2(squared * short_rate) + jnp.exp2(squared * long_rate) * wave).astype(BF)


def spread_columns(rows, columns):
    turned = rows.T
    for k in range(columns.shape[1] // 128):
        columns[:, 128 * k : 128 * (k + 1)] = jnp.broadcast_to(turned[:, k : k + 1], (LEAF, 128))


def block_into(to, columns, points, shift_y, shift_x):
    source_x = (points[0:1] + shift_x.astype(F32)) * waves
    source_y = (points[1:2] + shift_y.astype(F32)) * waves
    rows = 32
    for i in range(0, LEAF, rows):
        for j in (0, 128):
            to[i : i + rows, j : j + 128] = kernel_of(
                columns[i : i + rows, 0:128],
                columns[i : i + rows, 128:256],
                jnp.broadcast_to(source_x[:, j : j + 128], (rows, 128)),
                jnp.broadcast_to(source_y[:, j : j + 128], (rows, 128)),
            )


def turn_points(columns, leaf, position, noise):
    rows = jnp.concatenate([position * waves, noise, jnp.zeros((5, LEAF), F32)], axis=0)
    spread_columns(rows, columns.at[leaf])


def own_pairs(first):
    pairs = []
    for r in (first, first + 1):
        for c in range(SIDE):
            for dy, dx in ((0, 1), (1, -1), (1, 0), (1, 1)):
                if r + dy < SIDE and 0 <= c + dx < SIDE:
                    pairs.append((r * SIDE + c, (r + dy) * SIDE + c + dx, dy, dx))
    return pairs


def near_own_body(first, table_ref, q_ref, pos_ref, noise_ref, *refs):
    before_ref, out_ref, columns, blocks = (None,) * (4 - len(refs)) + refs
    pairs = own_pairs(first)
    start = first * SIDE

    def turn(leaf, carry):
        turn_points(columns, leaf, pos_ref[leaf], noise_ref[leaf])
        return carry

    lax.fori_loop(start, start + 8, turn, 0)
    zero = jnp.int32(0)

    def selves(i, carry):
        for half in range(2):
            leaf = start + 2 * i + half
            block_into(blocks.at[2 * i + half], columns.at[leaf], pos_ref[leaf], zero, zero)
        return carry

    lax.fori_loop(0, 4, selves, 0)

    def both(i, carry):
        for half in range(2):
            at = 8 * i + 4 * half
            place = 8 + 4 * i + 2 * half
            target, source = table_ref[at], table_ref[at + 1]
            block_into(
                blocks.at[place], columns.at[target], pos_ref[source], table_ref[at + 2], table_ref[at + 3]
            )
            blocks[place + 1] = blocks[place].T
        return carry

    lax.fori_loop(0, len(pairs) // 2, both, 0)
    parts = {leaf: [(leaf - start, leaf)] for leaf in range(start, start + 8)}
    for i, (target, source, _, _) in enumerate(pairs):
        parts[target].append((8 + 2 * i, source))
        parts.setdefault(source, []).append((9 + 2 * i, target))
    for leaf, terms in sorted(parts.items()):
        total = None
        for place, source in terms:
            part = dot(blocks[place], q_ref[source])
            total = part if total is None else total + part
        if leaf < start + 8:
            noise = jnp.concatenate([columns[leaf, :, 256:384]] * 2, axis=1)
            total = total + noise * q_ref[leaf].astype(F32)
        if before_ref is not None and leaf < start + SIDE:
            total = total + before_ref[leaf]
        out_ref[leaf - start] = total


def near_own(first, q, points, noise, after, before):
    vmem = pl.BlockSpec(memory_space=pltpu.VMEM)
    smem = pl.BlockSpec(memory_space=pltpu.SMEM)
    anywhere = pl.BlockSpec(memory_space=pl.ANY)
    pairs = own_pairs(first)

    def body(after_ref, *refs):
        near_own_body(first, *refs)

    return pl.pallas_call(
        body,
        out_shape=jax.ShapeDtypeStruct((12 if first == 0 else 8, LEAF, LEAF), F32),
        in_specs=[anywhere, smem, vmem, vmem, vmem] + [vmem] * len(before),
        out_specs=vmem,
        scratch_shapes=[
            pltpu.VMEM((LEAVES, LEAF, 384), F32),
            pltpu.VMEM((8 + 2 * len(pairs), LEAF, LEAF), BF),
        ],
        compiler_params=pltpu.CompilerParams(vmem_limit_bytes=40 << 20),
        cost_estimate=pl.CostEstimate(flops=10_000_000_000, bytes_accessed=4_000_000, transcendentals=8_000_000),
        name="near_own",
    )(after, jnp.asarray(np.array(pairs, np.int32).reshape(-1)), q, points, noise, *before)


def edge_items():
    table = near_table(False)
    return [[leaf, *table[leaf, j]] for leaf in range(LEAVES) for j in range(5) if table[leaf, j, 0] >= 0]


ITEMS = edge_items()
EDGES = len(ITEMS)


def extra_of(list_ref, slot_ref, leaf):
    code = second_cycle(list_ref, leaf)
    place = (leaf // SIDE + code // 5) * 8 + leaf % SIDE + code % 5
    slot = slot_ref[jnp.where(code >= 0, place, 0)]
    return code, slot


def edge_body(
    list_ref, table_ref, slot_ref, after_ref, own_pos_ref, west_any, east_any, north_any, south_any, out_ref,
    columns, parts, points, sems,
):
    copies = []
    sources = (
        (west_any, 12 * RANK),
        (east_any, 12 * RANK),
        (north_any, 12 * RANK),
        (north_any, SIDEWAYS + 8 * RANK),
        (north_any, SIDEWAYS + CORNER + 8 * RANK),
        (south_any, 12 * RANK),
        (south_any, SIDEWAYS + 8 * RANK),
        (south_any, SIDEWAYS + CORNER + 8 * RANK),
    )
    for k, (source, at) in enumerate(sources):
        copies.append(pltpu.make_async_copy(source.at[pl.ds(at, 48)], parts.at[k], sems.at[k]))
    for copy in copies:
        copy.start()

    def turn(leaf, carry):
        turn_points(columns, leaf, own_pos_ref[leaf], jnp.zeros((1, LEAF), F32))
        points[leaf] = own_pos_ref[leaf]
        return carry

    lax.fori_loop(0, LEAVES, turn, 0)
    for copy in copies:
        copy.wait()
    slots = (16, 24, 32, 40, 44, 48, 56, 60)
    for k in range(8):
        whole = parts[k].astype(F32)
        whole = (whole[0:16] + whole[16:32]) + whole[32:48]
        first, count = {3: (4, 4), 4: (4, 4), 6: (0, 4), 7: (0, 4)}.get(k, (0, 8))
        for i in range(count):
            points[slots[k] + i] = whole[2 * (first + i) : 2 * (first + i) + 2]

    def fixed(i, carry):
        for half in range(2):
            at = 8 * i + 4 * half
            block_into(
                out_ref.at[2 * i + half],
                columns.at[table_ref[at]],
                points[table_ref[at + 1]],
                table_ref[at + 2],
                table_ref[at + 3],
            )
        return carry

    lax.fori_loop(0, EDGES // 2, fixed, 0)

    def extra(i, carry):
        for half in range(2):
            leaf = 2 * i + half
            code, slot = extra_of(list_ref, slot_ref, leaf)
            code = jnp.maximum(code, 0)
            block_into(out_ref.at[EDGES + leaf], columns.at[leaf], points[slot], code // 5 - 2, code % 5 - 2)
        return carry

    lax.fori_loop(0, LEAVES // 2, extra, 0)


def edge_blocks(near_list, after, own_points, west, east, north, south):
    vmem = pl.BlockSpec(memory_space=pltpu.VMEM)
    smem = pl.BlockSpec(memory_space=pltpu.SMEM)
    anywhere = pl.BlockSpec(memory_space=pl.ANY)
    return pl.pallas_call(
        edge_body,
        out_shape=jax.ShapeDtypeStruct((EDGES + LEAVES, LEAF, LEAF), BF),
        in_specs=[smem, smem, smem, anywhere, vmem] + [anywhere] * 4,
        out_specs=vmem,
        scratch_shapes=[
            pltpu.VMEM((LEAVES, LEAF, 384), F32),
            pltpu.VMEM((8, 48, LEAF), BF),
            pltpu.VMEM((64, 2, LEAF), F32),
            pltpu.SemaphoreType.DMA((8,)),
        ],
        compiler_params=pltpu.CompilerParams(vmem_limit_bytes=40 << 20),
        cost_estimate=pl.CostEstimate(flops=12_000_000_000, bytes_accessed=8_000_000, transcendentals=12_000_000),
        name="edge_blocks",
    )(
        near_list, jnp.asarray(np.array(ITEMS, np.int32).reshape(-1)), jnp.asarray(SLOT_OF), after, own_points,
        west, east, north, south,
    )


def final_body(
    list_ref, slot_ref, q_any, west_any, east_any, north_any, north_corner_any, south_any, south_corner_any,
    block_any, upper_any, lower_any, basis_ref, field_ref, out_any, held, blocks, sums, extra_sum, outs, sems,
):
    firsts = [min(at for at in range(EDGES) if ITEMS[at][0] // SIDE == r) for r in range(SIDE)] + [EDGES]
    stages = [[], [], [], []]
    count = 0

    def copy(stage, source, to):
        nonlocal count
        made = pltpu.make_async_copy(source, to, sems.at[count])
        count += 1
        stages[stage].append(made)
        made.start()

    for r in range(SIDE):
        if r == 0:
            for source, at in ((north_any, 32), (north_corner_any, 40), (west_any, 16), (east_any, 24)):
                copy(r, source, held.at[pl.ds(at, 8)])
        if r == SIDE - 1:
            for source, at in ((south_any, 48), (south_corner_any, 56)):
                copy(r, source, held.at[pl.ds(at, 8)])
        part = pl.ds(firsts[r], firsts[r + 1] - firsts[r])
        copy(r, block_any.at[part], blocks.at[part])
        source = upper_any.at[pl.ds(SIDE * r, SIDE)] if r < 2 else lower_any.at[pl.ds(SIDE * (r - 2), SIDE)]
        copy(r, source, sums.at[pl.ds(SIDE * r, SIDE)])
    copy(SIDE - 1, q_any, held.at[pl.ds(0, 16)])
    part = pl.ds(EDGES, LEAVES)
    copy(SIDE - 1, block_any.at[part], blocks.at[part])
    for leaf in range(LEAVES):
        if leaf % SIDE == 0:
            for made in stages[leaf // SIDE]:
                made.wait()
        total = dot_first(basis_ref[leaf], field_ref[leaf])
        for at in range(EDGES):
            if ITEMS[at][0] == leaf:
                total = total + dot(blocks[at], held[ITEMS[at][1]])
        sums[leaf] += total

    backs = []
    for r in range(SIDE):
        part = pl.ds(SIDE * r, SIDE)
        backs.append(pltpu.make_async_copy(outs.at[part], out_any.at[part], sems.at[count + r]))

    for r in range(SIDE):

        def finish(leaf, carry):
            code, slot = extra_of(list_ref, slot_ref, leaf)

            @pl.when(code >= 0)
            def _():
                outs[leaf] = (sums[leaf] + dot(blocks[EDGES + leaf], held[slot])).astype(BF)

            @pl.when(code < 0)
            def _():
                outs[leaf] = sums[leaf].astype(BF)

            return carry

        lax.fori_loop(SIDE * r, SIDE * (r + 1), finish, 0)
        backs[r].start()
    for back in backs:
        back.wait()


def finish(near_list, q, halos, blocks, upper, lower, basis, field):
    vmem = pl.BlockSpec(memory_space=pltpu.VMEM)
    smem = pl.BlockSpec(memory_space=pltpu.SMEM)
    anywhere = pl.BlockSpec(memory_space=pl.ANY)

    return pl.pallas_call(
        final_body,
        out_shape=jax.ShapeDtypeStruct((LEAVES, LEAF, LEAF), BF),
        in_specs=[smem, smem] + [anywhere] * 10 + [vmem, vmem],
        out_specs=anywhere,
        scratch_shapes=[
            pltpu.VMEM((64, LEAF, LEAF), BF),
            pltpu.VMEM((EDGES + LEAVES, LEAF, LEAF), BF),
            pltpu.VMEM((LEAVES, LEAF, LEAF), F32),
            pltpu.VMEM((LEAF, LEAF), F32),
            pltpu.VMEM((LEAVES, LEAF, LEAF), BF),
            pltpu.SemaphoreType.DMA((20,)),
        ],
        compiler_params=pltpu.CompilerParams(vmem_limit_bytes=48 << 20),
        cost_estimate=pl.CostEstimate(flops=4_000_000_000, bytes_accessed=24_000_000, transcendentals=0),
        name="finish",
    )(near_list, jnp.asarray(SLOT_OF), q, *halos, blocks, upper, lower, basis, field)


def window_slots(wide, narrow, steps):
    row, col = lax.axis_index("narrow"), lax.axis_index("wide")
    wy, wx = np.arange(WINDOW) // 6, np.arange(WINDOW) % 6

    def slots(target_y, target_x, scale):
        y = target_y // 2 * 2 - 2 + wy
        x = target_x // 2 * 2 - 2 + wx
        inside = (y >= 0) & (y < narrow // scale) & (x >= 0) & (x < wide // scale)
        apart = {"narrow": (y * scale) ^ row, "wide": (x * scale) ^ col}
        slot = 0
        for at, (axis, bit) in enumerate(steps):
            slot = slot + (apart[axis] // bit & 1) * (1 << at)
        return jnp.where(inside, slot if scale == 1 else slot // 4, -1)

    parity2 = row % 2 * 2 + col % 2
    parity3 = row // 2 % 2 * 2 + col // 2 % 2
    return jnp.concatenate(
        [slots(row, col, 1), slots(row // 2, col // 2, 2), jnp.stack([parity2, parity3])]
    ).astype(jnp.int32)


def per_device(wide, narrow, charges, positions, noise, leaf_basis, transfer, near_list):
    q = charges.reshape(LEAVES, LEAF, LEAF)
    points = positions.reshape(LEAVES, 2, LEAF)
    basis = leaf_basis.reshape(LEAVES, RANK, LEAF)
    tree = transfer[0, 0]
    listing = near_list.reshape(-1)
    steps = gather_steps(wide, narrow)
    meta = window_slots(wide, narrow, steps)

    east, west, north, south, coefs, give = go_up(q, basis, tree, points)
    from_west = shift(east, "wide", 1)
    from_east = shift(west, "wide", -1)
    q_west = shift(charges[:, 2:4], "wide", 1)
    q_east = shift(charges[:, 0:2], "wide", -1)
    q_north = shift(charges[2:4], "narrow", 1)
    q_south = shift(charges[0:2], "narrow", -1)

    noise_rows = noise.reshape(LEAVES, 1, LEAF)

    def step(value, at):
        axis, bit = steps[at]
        return lax.ppermute(value, axis, [(i, i ^ bit) for i in range(lax.axis_size(axis))])

    def tie(*values):
        return lax.optimization_barrier(values)

    gathered = give
    other = step(gathered, 0)
    upper = near_own(0, q, points, noise_rows, give, [])
    other, from_west, from_east, upper = tie(other, from_west, from_east, upper)
    gathered = jnp.concatenate([gathered, other], axis=0)
    other = step(gathered, 1)
    to_north, to_south = join(north, south, from_west, from_east)
    from_south = shift(to_north, "narrow", -1)
    from_north = shift(to_south, "narrow", 1)
    lower = near_own(2, q, points, noise_rows, from_west, [upper])
    other, from_south, from_north, lower = tie(other, from_south, from_north, lower)
    for at in range(2, len(steps)):
        gathered = jnp.concatenate([gathered, other], axis=0)
        other = step(gathered, at)
        if at == 2:
            sums = local_far(listing, coefs, from_west, from_east, from_north, from_south)
            other, *sums = tie(other, *sums)
        if at == 3:
            blocks = edge_blocks(listing, sums[1], points, from_west, from_east, from_north, from_south)
            other, blocks = tie(other, blocks)
    gathered = jnp.concatenate([gathered, other], axis=0)
    q_west, q_east, blocks = tie(q_west, q_east, blocks)
    q_north_corner = shift(jnp.stack([q_west[2:4], q_east[2:4]]), "narrow", 1)
    q_south_corner = shift(jnp.stack([q_west[0:2], q_east[0:2]]), "narrow", -1)
    field = top_far(meta, gathered, tree, *sums)
    q_north_corner, q_south_corner, field = tie(q_north_corner, q_south_corner, field)
    halos = [
        value.reshape(8, LEAF, LEAF)
        for value in (q_west, q_east, q_north, q_north_corner, q_south, q_south_corner)
    ]
    out = finish(listing, q, halos, blocks, upper, lower, basis, field)
    return out.reshape(SIDE, SIDE, LEAF, LEAF)


def solution(mesh):
    wide, narrow = mesh.shape["wide"], mesh.shape["narrow"]
    in_specs = (
        P("narrow", "wide", None, None),
        P("narrow", "wide", None, None),
        P("narrow", "wide", None),
        P("narrow", "wide", None, None),
        P("narrow", "wide", None, None, None),
        P("narrow", "wide", None),
    )
    out_specs = P("narrow", "wide", None, None)

    def step(*arrays):
        return per_device(wide, narrow, *arrays)

    return jax.shard_map(step, mesh=mesh, in_specs=in_specs, out_specs=out_specs, check_vma=False)
```

time: 225 us -> 229 us (1.018)
  Pallas kernels: 104 us -> 138 us
  local copies, waits for them, and re-layouts: 39.7 us -> 26.2 us
  waiting for transfers between devices: 31.8 us -> 23.2 us
  other arithmetic: 6.44 us -> 2.34 us
  starting transfers between devices: 41.2 us -> 37.6 us
    pallas_call x8 -> x7, Pallas kernels: 101 us -> 137 us  [the longest x1 61.2 us: join(): pl.pallas_call(join_body, out_shape=(message, message), in_specs=[anywher...]
    ppermute x5, waiting for transfers between devices: 21.3 us -> 0.01 us  [step(): lax.ppermute(value, axis, [(i, i ^ bit) for i in range(lax.axis_size(axis...]
    ppermute x10, waiting for transfers between devices: 10.5 us -> 23.2 us  [shift(): lax.ppermute(value, axis, [(i, i + steps) for i in range(count) if 0 <= i...]
    unnamed x89 -> x72, local copies, waits for them, and re-layouts: 28.2 us -> 18.5 us
    slice x8 -> x0, local copies, waits for them, and re-layouts: 3.44 us -> none  [the longest x2 3.38 us: corner(): return [message[at:at + 4 * RANK], message[8 * RANK:]]]
    ppermute x5, starting transfers between devices: 11.1 us -> 7.92 us  [step(): lax.ppermute(value, axis, [(i, i ^ bit) for i in range(lax.axis_size(axis...]
    convert_element_type x3 -> x0, other arithmetic: 2.34 us -> none  [points_of(): parts = message[leaves_at:leaves_at + 48].astype(F32)]
  transfers between devices with their start and end apart: 15 -> 15, of which waited for: 4 -> 2; matrix products, arithmetic and copies ran while one was open for 12% -> 6% of each run, Pallas kernels for 41% -> 55%
where the time goes in v3:
time: 229 us; the launch traced here: 228 us
  Pallas kernels  138 us (60%)
  starting transfers between devices  37.6 us (16%)
  local copies, waits for them, and re-layouts  26.2 us (11%)
  waiting for transfers between devices  23.2 us (10%)
  other arithmetic  2.34 us (1%)
    pallas_call x1, Pallas kernels, join(): pl.pallas_call(join_body, out_shape=(message, message), in_specs=[anywher...  61.2 us
    ppermute x10, starting transfers between devices, shift(): lax.ppermute(value, axis, [(i, i + steps) for i in range(count) if 0 <= i...  29.6 us
    pallas_call x2, Pallas kernels, near_own(): pl.pallas_call(body, out_shape=jax.ShapeDtypeStruct((12 if first == 0 els...  27.1 us
    ppermute x10, waiting for transfers between devices, shift(): lax.ppermute(value, axis, [(i, i + steps) for i in range(count) if 0 <= i...  23.2 us
    pallas_call x1, Pallas kernels, edge_blocks(): pl.pallas_call(edge_body, out_shape=jax.ShapeDtypeStruct((EDGES + LEAVES,...  22 us
    unnamed x72, local copies, waits for them, and re-layouts  18.5 us
    pallas_call x1, Pallas kernels, finish(): pl.pallas_call(final_body, out_shape=jax.ShapeDtypeStruct((LEAVES, LEAF,...  12.2 us
    pallas_call x1, Pallas kernels, local_far(): pl.pallas_call(local_body, out_shape=(jax.ShapeDtypeStruct((LEAVES, RANK,...  9.08 us
  transfers between devices with their start and end apart: 15, of which 2 were waited for; matrix products, arithmetic and copies ran while one was open for 6% of the time, Pallas kernels for 55%

profile of v3, /device:TPU:1, one launch (start us, length us, event | category | flops | bytes accessed | tf_op | source)
XLA Modules:
  0.0 228.4 jit_solution(8186009471566608641)
XLA Ops:
  0.0 1.6 copy-done
  4.4 1.6 upward.1
  6.8 2.0 collective-permute-start.2
  8.9 2.7 %collective-permute-start.3 = (bf16[816,256]{1,0:T(8,128)(2,1)}, bf16[816,256]{1,0:T(8,128)(2,1)}, u32[]{:S(2)}, u32[]{:S(2)}) collective-permute-start(bf16[816,256]{1,0:T(8,128)(2,1)} %get-tuple-element.35), channel_id=1, source_target_pairs={{0,4},{4,8},{8,12},{12,16},{16,20},{20,24},{24,28},{1,5},{5,9},{9,... | collective-permute-start | bytes 1253384 | tf_op jit(solution)/shard_map/ppermute | solution.py:118
  11.6 1.4 collective-permute-start.4
  13.0 1.5 fusion.3
  14.5 4.3 %collective-permute-start = (bf16[4,2,256,256]{3,2,1,0:T(8,128)(2,1)}, bf16[4,2,256,256]{3,2,1,0:T(8,128)(2,1)S(1)}, u32[]{:S(2)}, u32[]{:S(2)}) collective-permute-start(bf16[4,2,256,256]{3,2,1,0:T(8,128)(2,1)} %get-tuple-element.66), channel_id=1, source_target_pairs={{0,4},{4,8},{8,12},{12,16},{16,20},{20,24},{24,28},{1,5},{5,9},{9,... | collective-permute-start | bytes 3145736 | tf_op jit(solution)/shard_map/ppermute | solution.py:118
  18.9 1.3 collective-permute-start.1
  20.2 15.4 %near_own.2.refs_4_.upper_any = f32[12,256,256]{2,1,0:T(8,128)S(1)} custom-call(bf16[80,256]{1,0:T(8,128)(2,1)S(1)} %get-tuple-element.34.after_ref, s32[104]{0:T(128)S(1)} %copy-done.25, bf16[16,256,256]{2,1,0:T(8,128)(2,1)S(1)} %bitcast.23, f32[16,2,256]{2,1,0:T(2,128)S(1)} %bitcast.33, f32[16,1,256]{2,1,0:T(1,128)S(1)} %reshape.40.refs_3_), custom_call_target="tpu_custom_call" | custom-call | flops 10000000000 | bytes 4000000 | tf_op jit(solution)/shard_map/near_own/pallas_call | solution.py:526
  35.7 1.7 fusion.2
  38.7 12.1 %collective-permute-done.3.west_ref.after_ref.west_any = bf16[816,256]{1,0:T(8,128)(2,1)} collective-permute-done((bf16[816,256]{1,0:T(8,128)(2,1)}, bf16[816,256]{1,0:T(8,128)(2,1)}, u32[]{:S(2)}, u32[]{:S(2)}) %collective-permute-start.3) | collective-permute-done | bytes 417824 | tf_op jit(solution)/shard_map/ppermute | solution.py:118
  50.8 61.2 %join.1 = (bf16[1936,256]{1,0:T(8,128)(2,1)}, bf16[1936,256]{1,0:T(8,128)(2,1)}) custom-call(bf16[816,256]{1,0:T(8,128)(2,1)} %copy-done.8, bf16[816,256]{1,0:T(8,128)(2,1)} %copy-done.9, bf16[816,256]{1,0:T(8,128)(2,1)} %collective-permute-done.3.west_ref.after_ref.west_any, bf16[816,256]{1,0:T(8,128)(2,1)} %collective-permute-done.4.east_ref.east_any), custom_call_target="tpu_custom_call" | custom-call | bytes 4000000 | tf_op jit(solution)/shard_map/join/pallas_call | solution.py:410
  112.1 4.6 %collective-permute-start.6 = (bf16[1936,256]{1,0:T(8,128)(2,1)}, bf16[1936,256]{1,0:T(8,128)(2,1)S(1)}, u32[]{:S(2)}, u32[]{:S(2)}) collective-permute-start(bf16[1936,256]{1,0:T(8,128)(2,1)} %get-tuple-element.42), channel_id=1, source_target_pairs={{1,0},{2,1},{3,2},{5,4},{6,5},{7,6},{9,8},{10,9},{11,10},{13,12},{... | collective-permute-start | bytes 2973704 | tf_op jit(solution)/shard_map/ppermute | solution.py:118
  116.7 3.6 %collective-permute-start.7 = (bf16[1936,256]{1,0:T(8,128)(2,1)}, bf16[1936,256]{1,0:T(8,128)(2,1)S(1)}, u32[]{:S(2)}, u32[]{:S(2)}) collective-permute-start(bf16[1936,256]{1,0:T(8,128)(2,1)} %get-tuple-element.43), channel_id=1, source_target_pairs={{0,1},{1,2},{2,3},{4,5},{5,6},{6,7},{8,9},{9,10},{10,11},{12,13},{... | collective-permute-start | bytes 2973704 | tf_op jit(solution)/shard_map/ppermute | solution.py:118
  120.4 1.9 copy-done.4
  122.3 11.7 %near_own.3.lower_any = f32[8,256,256]{2,1,0:T(8,128)S(1)} custom-call(bf16[816,256]{1,0:T(8,128)(2,1)} %collective-permute-done.3.west_ref.after_ref.west_any, s32[64]{0:T(128)S(1)} %copy-done.24, bf16[16,256,256]{2,1,0:T(8,128)(2,1)S(1)} %bitcast.24, f32[16,2,256]{2,1,0:T(2,128)S(1)} %bitcast.34, f32[16,1,256]{2,1,0:T(1,128)S(1)} %reshape.40.refs_3_, ...), custom_call_target="tpu_custom_call" | custom-call | flops 10000000000 | bytes 4000000 | tf_op jit(solution)/shard_map/near_own/pallas_call | solution.py:526
  134.8 3.9 %collective-permute-start.8 = (bf16[320,256]{1,0:T(8,128)(2,1)S(1)}, bf16[320,256]{1,0:T(8,128)(2,1)S(1)}, u32[]{:S(2)}, u32[]{:S(2)}) collective-permute-start(bf16[320,256]{1,0:T(8,128)(2,1)S(1)} %pad_maximum_fusion.3), channel_id=1, source_target_pairs={{0,16},{4,20},{8,24},{12,28},{16,0},{20,4},{24,8},{28,12},{1,17},{... | collective-permute-start | bytes 491528 | tf_op jit(solution)/shard_map/ppermute | solution.py:773
  138.7 9.1 %local_far.1 = (f32[16,64,256]{2,1,0:T(8,128)S(1)}, f32[256,256]{1,0:T(8,128)S(1)}) custom-call(s32[160]{0:T(256)S(1)} %reshape.36.list_ref, bf16[1280,256]{1,0:T(8,128)(2,1)S(1)} %copy-done.17, bf16[816,256]{1,0:T(8,128)(2,1)} %collective-permute-done.3.west_ref.after_ref.west_any, bf16[816,256]{1,0:T(8,128)(2,1)} %collective-permute-done.4.east_ref.east_any, ...), custom_call_target="tpu_custom_call" | custom-call | flops 5000000000 | bytes 8000000 | tf_op jit(solution)/shard_map/local_far/pallas_call | solution.py:271
  148.6 1.5 collective-permute-start.9
  150.1 22.0 %edge_blocks.1.block_any = bf16[60,256,256]{2,1,0:T(8,128)(2,1)S(1)} custom-call(s32[160]{0:T(256)S(1)} %reshape.36.list_ref, s32[176]{0:T(256)S(1)} %copy-done.23, s32[64]{0:T(128)S(1)} %copy-done.15, f32[256,256]{1,0:T(8,128)S(1)} %get-tuple-element.52.after_ref.sum1, f32[16,2,256]{2,1,0:T(2,128)S(1)} %bitcast.35, ...), custom_call_target="tpu_custom_call" | custom-call | flops 12000000000 | bytes 8000000 | tf_op jit(solution)/shard_map/edge_blocks/pallas_call | solution.py:622
  172.1 3.1 %copy-done.2 = bf16[60,256,256]{2,1,0:T(8,128)(2,1)} copy-done((bf16[60,256,256]{2,1,0:T(8,128)(2,1)}, bf16[60,256,256]{2,1,0:T(8,128)(2,1)S(1)}, u32[]{:S(2)}) %copy-start.2) | copy-done | bytes 7864344
  177.3 1.5 slice_bitcast_fusion
  179.9 2.9 %collective-permute-start.12 = (bf16[2,2,2,256,256]{4,3,2,1,0:T(8,128)(2,1)}, bf16[2,2,2,256,256]{4,3,2,1,0:T(8,128)(2,1)}, u32[]{:S(2)}, u32[]{:S(2)}) collective-permute-start(bf16[2,2,2,256,256]{4,3,2,1,0:T(8,128)(2,1)} %pad_maximum_fusion.1), channel_id=1, source_target_pairs={{1,0},{2,1},{3,2},{5,4},{6,5},{7,6},{9,8},{10,9},{11,10},{13,12},{... | collective-permute-start | bytes 3145736 | tf_op jit(solution)/shard_map/ppermute | solution.py:118
  183.9 3.3 %collective-permute-start.11 = (bf16[2,2,2,256,256]{4,3,2,1,0:T(8,128)(2,1)}, bf16[2,2,2,256,256]{4,3,2,1,0:T(8,128)(2,1)S(1)}, u32[]{:S(2)}, u32[]{:S(2)}) collective-permute-start(bf16[2,2,2,256,256]{4,3,2,1,0:T(8,128)(2,1)} %pad_maximum_fusion), channel_id=1, source_target_pairs={{0,1},{1,2},{2,3},{4,5},{5,6},{6,7},{8,9},{9,10},{10,11},{12,13},{... | collective-permute-start | bytes 3145736 | tf_op jit(solution)/shard_map/ppermute | solution.py:118
  187.1 1.9 collective-permute-start.14
  189.1 3.6 %collective-permute-start.10 = (bf16[2,4,256,256]{3,2,1,0:T(8,128)(2,1)}, bf16[2,4,256,256]{3,2,1,0:T(8,128)(2,1)S(1)}, u32[]{:S(2)}, u32[]{:S(2)}) collective-permute-start(bf16[2,4,256,256]{3,2,1,0:T(8,128)(2,1)} %get-tuple-element.64), channel_id=1, source_target_pairs={{0,1},{1,2},{2,3},{4,5},{5,6},{6,7},{8,9},{9,10},{10,11},{12,13},{... | collective-permute-start | bytes 3145736 | tf_op jit(solution)/shard_map/ppermute | solution.py:118
  193.0 2.0 constant_dynamic-update-slice_fusion.5.all_ref
  195.0 1.3 copy-done.14
  196.3 1.3 copy-done.19
  199.8 5.2 %top_far.1.field_ref = bf16[16,64,256]{2,1,0:T(8,128)(2,1)S(1)} custom-call(s32[74]{0:T(128)S(1)} %pad_add_fusion.meta_ref, bf16[2560,256]{1,0:T(8,128)(2,1)S(1)} %copy-done.14, bf16[256,2304]{1,0:T(8,128)(2,1)S(1)} %copy-done.18, bf16[256,2304]{1,0:T(8,128)(2,1)S(1)} %copy-done.19, bf16[21,64,64]{2,1,0:T(8,128)(2,1)S(1)} %bitcast.31, ...), custom_call_target="tpu_custom_call" | custom-call | flops 3000000000 | bytes 5000000 | tf_op jit(solution)/shard_map/top_far/pallas_call | solution.py:372
  205.0 11.1 %collective-permute-done.14 = bf16[2,4,256,256]{3,2,1,0:T(8,128)(2,1)} collective-permute-done((bf16[2,4,256,256]{3,2,1,0:T(8,128)(2,1)}, bf16[2,4,256,256]{3,2,1,0:T(8,128)(2,1)}, u32[]{:S(2)}, u32[]{:S(2)}) %collective-permute-start.14) | collective-permute-done | bytes 1048608 | tf_op jit(solution)/shard_map/ppermute | solution.py:118
  216.1 12.2 %finish.1 = bf16[16,256,256]{2,1,0:T(8,128)(2,1)} custom-call(s32[160]{0:T(256)S(1)} %reshape.36.list_ref, s32[64]{0:T(128)S(1)} %copy-done.15, bf16[16,256,256]{2,1,0:T(8,128)(2,1)} %bitcast.21, bf16[8,256,256]{2,1,0:T(8,128)(2,1)S(1)} %bitcast.25, bf16[8,256,256]{2,1,0:T(8,128)(2,1)} %bitcast.5.east_any, bf16[8,256,256]{2,1,0:T(8,128)(2,1)S(1)} %bitcast.29, ...), custom_call_target="tpu_custom_call" | custom-call | flops 4000000000 | bytes 24000000 | tf_op jit(solution)/shard_map/finish/pallas_call | solution.py:712
  (92 shorter events, 13.2 us)
Async XLA Ops:
  6.8 31.9 %collective-permute-start.2 = (bf16[80,256]{1,0:T(8,128)(2,1)S(1)}, bf16[80,256]{1,0:T(8,128)(2,1)S(1)}, u32[]{:S(2)}, u32[]{:S(2)}) collective-permute-start(bf16[80,256]{1,0:T(8,128)(2,1)S(1)} %get-tuple-element.34.after_ref), channel_id=1, source_target_pairs={{0,4},{4,0},{8,12},{12,8},{16,20},{20,16},{24,28},{28,24},{1,5},{5... | collective-permute-start | bytes 122888 | tf_op jit(solution)/shard_map/ppermute | solution.py:773
  8.9 41.9 %collective-permute-start.3 = (bf16[816,256]{1,0:T(8,128)(2,1)}, bf16[816,256]{1,0:T(8,128)(2,1)}, u32[]{:S(2)}, u32[]{:S(2)}) collective-permute-start(bf16[816,256]{1,0:T(8,128)(2,1)} %get-tuple-element.35), channel_id=1, source_target_pairs={{0,4},{4,8},{8,12},{12,16},{16,20},{20,24},{24,28},{1,5},{5,9},{9,... | collective-permute-start | bytes 1253384 | tf_op jit(solution)/shard_map/ppermute | solution.py:118
  11.5 8.7 %copy-start.1 = (bf16[4,4,256,256]{3,2,1,0:T(8,128)(2,1)S(1)}, bf16[4,4,256,256]{3,2,1,0:T(8,128)(2,1)}, u32[]{:S(2)}) copy-start(bf16[4,4,256,256]{3,2,1,0:T(8,128)(2,1)} %param.17) | copy-start | bytes 6291460
  11.5 8.7 %copy-start.13 = (f32[4,4,2,256]{3,2,1,0:T(2,128)S(1)}, f32[4,4,2,256]{3,2,1,0:T(2,128)}, u32[]{:S(2)}) copy-start(f32[4,4,2,256]{3,2,1,0:T(2,128)} %param.18) | copy-start | bytes 98308
  11.6 8.7 %copy-start.25 = (s32[104]{0:T(128)S(1)}, s32[104]{0:T(128)}, u32[]{:S(2)}) copy-start(s32[104]{0:T(128)} %constant.197.clone.refs_0_) | copy-start | bytes 1252
  11.6 39.3 %collective-permute-start.4 = (bf16[816,256]{1,0:T(8,128)(2,1)}, bf16[816,256]{1,0:T(8,128)(2,1)}, u32[]{:S(2)}, u32[]{:S(2)}) collective-permute-start(bf16[816,256]{1,0:T(8,128)(2,1)} %get-tuple-element.36), channel_id=1, source_target_pairs={{4,0},{8,4},{12,8},{16,12},{20,16},{24,20},{28,24},{5,1},{9,5},{13... | collective-permute-start | bytes 1253384 | tf_op jit(solution)/shard_map/ppermute | solution.py:118
  14.5 162.8 %collective-permute-start = (bf16[4,2,256,256]{3,2,1,0:T(8,128)(2,1)}, bf16[4,2,256,256]{3,2,1,0:T(8,128)(2,1)S(1)}, u32[]{:S(2)}, u32[]{:S(2)}) collective-permute-start(bf16[4,2,256,256]{3,2,1,0:T(8,128)(2,1)} %get-tuple-element.66), channel_id=1, source_target_pairs={{0,4},{4,8},{8,12},{12,16},{16,20},{20,24},{24,28},{1,5},{5,9},{9,... | collective-permute-start | bytes 3145736 | tf_op jit(solution)/shard_map/ppermute | solution.py:118
  18.9 158.4 %collective-permute-start.1 = (bf16[4,2,256,256]{3,2,1,0:T(8,128)(2,1)}, bf16[4,2,256,256]{3,2,1,0:T(8,128)(2,1)}, u32[]{:S(2)}, u32[]{:S(2)}) collective-permute-start(bf16[4,2,256,256]{3,2,1,0:T(8,128)(2,1)} %get-tuple-element.65), channel_id=1, source_target_pairs={{4,0},{8,4},{12,8},{16,12},{20,16},{24,20},{28,24},{5,1},{9,5},{13... | collective-permute-start | bytes 3145736 | tf_op jit(solution)/shard_map/ppermute | solution.py:118
  38.0 82.4 %copy-start.24 = (s32[64]{0:T(128)S(1)}, s32[64]{0:T(128)}, u32[]{:S(2)}) copy-start(s32[64]{0:T(128)} %constant.198.clone.refs_0_) | copy-start | bytes 772
  112.1 22.7 %collective-permute-start.6 = (bf16[1936,256]{1,0:T(8,128)(2,1)}, bf16[1936,256]{1,0:T(8,128)(2,1)S(1)}, u32[]{:S(2)}, u32[]{:S(2)}) collective-permute-start(bf16[1936,256]{1,0:T(8,128)(2,1)} %get-tuple-element.42), channel_id=1, source_target_pairs={{1,0},{2,1},{3,2},{5,4},{6,5},{7,6},{9,8},{10,9},{11,10},{13,12},{... | collective-permute-start | bytes 2973704 | tf_op jit(solution)/shard_map/ppermute | solution.py:118
  116.7 18.1 %collective-permute-start.7 = (bf16[1936,256]{1,0:T(8,128)(2,1)}, bf16[1936,256]{1,0:T(8,128)(2,1)S(1)}, u32[]{:S(2)}, u32[]{:S(2)}) collective-permute-start(bf16[1936,256]{1,0:T(8,128)(2,1)} %get-tuple-element.43), channel_id=1, source_target_pairs={{0,1},{1,2},{2,3},{4,5},{5,6},{6,7},{8,9},{9,10},{10,11},{12,13},{... | collective-permute-start | bytes 2973704 | tf_op jit(solution)/shard_map/ppermute | solution.py:118
  120.3 14.4 %collective-permute-start.5 = (bf16[160,256]{1,0:T(8,128)(2,1)S(1)}, bf16[160,256]{1,0:T(8,128)(2,1)S(1)}, u32[]{:S(2)}, u32[]{:S(2)}) collective-permute-start(bf16[160,256]{1,0:T(8,128)(2,1)S(1)} %pad_maximum_fusion.4), channel_id=1, source_target_pairs={{0,1},{1,0},{2,3},{3,2},{4,5},{5,4},{6,7},{7,6},{8,9},{9,8},{10,11... | collective-permute-start | bytes 245768 | tf_op jit(solution)/shard_map/ppermute | solution.py:773
  122.3 16.4 %copy-start.17 = (bf16[1280,256]{1,0:T(8,128)(2,1)S(1)}, bf16[1280,256]{1,0:T(8,128)(2,1)}, u32[]{:S(2)}) copy-start(bf16[1280,256]{1,0:T(8,128)(2,1)} %copy-done.16) | copy-start | bytes 1966084
  122.3 16.4 %copy-start.20 = (bf16[256,2304]{1,0:T(8,128)(2,1)S(1)}, bf16[256,2304]{1,0:T(8,128)(2,1)}, u32[]{:S(2)}) copy-start(bf16[256,2304]{1,0:T(8,128)(2,1)} %constant.199.clone.c0_any) | copy-start | bytes 3538948
  122.3 16.4 %copy-start.21 = (bf16[256,2304]{1,0:T(8,128)(2,1)S(1)}, bf16[256,2304]{1,0:T(8,128)(2,1)}, u32[]{:S(2)}) copy-start(bf16[256,2304]{1,0:T(8,128)(2,1)} %constant.200.clone.c1_any) | copy-start | bytes 3538948
  122.3 16.4 %copy-start.22 = (bf16[25,64,64]{2,1,0:T(8,128)(2,1)S(1)}, bf16[25,64,64]{2,1,0:T(8,128)(2,1)}, u32[]{:S(2)}) copy-start(bf16[25,64,64]{2,1,0:T(8,128)(2,1)} %constant.201.clone.code_any) | copy-start | bytes 614404
  134.0 13.7 %copy-start.7 = (f32[8,256,256]{2,1,0:T(8,128)}, f32[8,256,256]{2,1,0:T(8,128)S(1)}, u32[]{:S(2)}) copy-start(f32[8,256,256]{2,1,0:T(8,128)S(1)} %near_own.3.lower_any) | copy-start | bytes 6291460
  134.8 13.8 %collective-permute-start.8 = (bf16[320,256]{1,0:T(8,128)(2,1)S(1)}, bf16[320,256]{1,0:T(8,128)(2,1)S(1)}, u32[]{:S(2)}, u32[]{:S(2)}) collective-permute-start(bf16[320,256]{1,0:T(8,128)(2,1)S(1)} %pad_maximum_fusion.3), channel_id=1, source_target_pairs={{0,16},{4,20},{8,24},{12,28},{16,0},{20,4},{24,8},{28,12},{1,17},{... | collective-permute-start | bytes 491528 | tf_op jit(solution)/shard_map/ppermute | solution.py:773
  138.7 11.4 %copy-start.15 = (s32[64]{0:T(128)S(1)}, s32[64]{0:T(128)}, u32[]{:S(2)}) copy-start(s32[64]{0:T(128)} %constant.203.clone.slot_ref) | copy-start | bytes 772
  138.7 11.4 %copy-start.23 = (s32[176]{0:T(256)S(1)}, s32[176]{0:T(256)}, u32[]{:S(2)}) copy-start(s32[176]{0:T(256)} %constant.202.clone.table_ref) | copy-start | bytes 2116
  147.8 24.3 %copy-start.26 = (f32[16,64,256]{2,1,0:T(8,128)}, f32[16,64,256]{2,1,0:T(8,128)S(1)}, u32[]{:S(2)}) copy-start(f32[16,64,256]{2,1,0:T(8,128)S(1)} %get-tuple-element.57.sum0) | copy-start | bytes 3145732
  147.8 24.3 %copy-start.28 = (f32[256,256]{1,0:T(8,128)}, f32[256,256]{1,0:T(8,128)S(1)}, u32[]{:S(2)}) copy-start(f32[256,256]{1,0:T(8,128)S(1)} %get-tuple-element.52.after_ref.sum1) | copy-start | bytes 786436
  148.6 27.4 %collective-permute-start.9 = (bf16[640,256]{1,0:T(8,128)(2,1)S(1)}, bf16[640,256]{1,0:T(8,128)(2,1)S(1)}, u32[]{:S(2)}, u32[]{:S(2)}) collective-permute-start(bf16[640,256]{1,0:T(8,128)(2,1)S(1)} %pad_maximum_fusion.2), channel_id=1, source_target_pairs={{0,8},{4,12},{8,0},{12,4},{16,24},{20,28},{24,16},{28,20},{1,9},{5... | collective-permute-start | bytes 983048 | tf_op jit(solution)/shard_map/ppermute | solution.py:773
  176.9 16.1 %collective-permute-start.13 = (bf16[1280,256]{1,0:T(8,128)(2,1)}, bf16[1280,256]{1,0:T(8,128)(2,1)}, u32[]{:S(2)}, u32[]{:S(2)}) collective-permute-start(bf16[1280,256]{1,0:T(8,128)(2,1)} %get-tuple-element.71), channel_id=1, source_target_pairs={{0,2},{1,3},{2,0},{3,1},{4,6},{5,7},{6,4},{7,5},{8,10},{9,11},{10,... | collective-permute-start | bytes 1966088 | tf_op jit(solution)/shard_map/ppermute | solution.py:773
  179.9 13.0 %copy-start.32 = (s32[36]{0:T(128)S(1)}, s32[36]{0:T(128)}, u32[]{:S(2)}) copy-start(s32[36]{0:T(128)} %constant.195.clone) | copy-start | bytes 436
  179.9 13.0 %copy-start.33 = (s32[36]{0:T(128)S(1)}, s32[36]{0:T(128)}, u32[]{:S(2)}) copy-start(s32[36]{0:T(128)} %constant.196.clone) | copy-start | bytes 436
  179.9 25.2 %collective-permute-start.12 = (bf16[2,2,2,256,256]{4,3,2,1,0:T(8,128)(2,1)}, bf16[2,2,2,256,256]{4,3,2,1,0:T(8,128)(2,1)}, u32[]{:S(2)}, u32[]{:S(2)}) collective-permute-start(bf16[2,2,2,256,256]{4,3,2,1,0:T(8,128)(2,1)} %pad_maximum_fusion.1), channel_id=1, source_target_pairs={{1,0},{2,1},{3,2},{5,4},{6,5},{7,6},{9,8},{10,9},{11,10},{13,12},{... | collective-permute-start | bytes 3145736 | tf_op jit(solution)/shard_map/ppermute | solution.py:118
  182.7 12.3 %copy-start.11 = (bf16[1,1,21,64,64]{4,3,2,1,0:T(8,128)(2,1)S(1)}, bf16[1,1,21,64,64]{4,3,2,1,0:T(8,128)(2,1)}, u32[]{:S(2)}) copy-start(bf16[1,1,21,64,64]{4,3,2,1,0:T(8,128)(2,1)} %param.21) | copy-start | bytes 516100
  183.9 21.2 %collective-permute-start.11 = (bf16[2,2,2,256,256]{4,3,2,1,0:T(8,128)(2,1)}, bf16[2,2,2,256,256]{4,3,2,1,0:T(8,128)(2,1)S(1)}, u32[]{:S(2)}, u32[]{:S(2)}) collective-permute-start(bf16[2,2,2,256,256]{4,3,2,1,0:T(8,128)(2,1)} %pad_maximum_fusion), channel_id=1, source_target_pairs={{0,1},{1,2},{2,3},{4,5},{5,6},{6,7},{8,9},{9,10},{10,11},{12,13},{... | collective-permute-start | bytes 3145736 | tf_op jit(solution)/shard_map/ppermute | solution.py:118
  187.1 29.0 %collective-permute-start.14 = (bf16[2,4,256,256]{3,2,1,0:T(8,128)(2,1)}, bf16[2,4,256,256]{3,2,1,0:T(8,128)(2,1)}, u32[]{:S(2)}, u32[]{:S(2)}) collective-permute-start(bf16[2,4,256,256]{3,2,1,0:T(8,128)(2,1)} %get-tuple-element.63), channel_id=1, source_target_pairs={{1,0},{2,1},{3,2},{5,4},{6,5},{7,6},{9,8},{10,9},{11,10},{13,12},{... | collective-permute-start | bytes 3145736 | tf_op jit(solution)/shard_map/ppermute | solution.py:118
  189.1 27.0 %collective-permute-start.10 = (bf16[2,4,256,256]{3,2,1,0:T(8,128)(2,1)}, bf16[2,4,256,256]{3,2,1,0:T(8,128)(2,1)S(1)}, u32[]{:S(2)}, u32[]{:S(2)}) collective-permute-start(bf16[2,4,256,256]{3,2,1,0:T(8,128)(2,1)} %get-tuple-element.64), channel_id=1, source_target_pairs={{0,1},{1,2},{2,3},{4,5},{5,6},{6,7},{8,9},{9,10},{10,11},{12,13},{... | collective-permute-start | bytes 3145736 | tf_op jit(solution)/shard_map/ppermute | solution.py:118
  199.8 16.3 %copy-start.6 = (bf16[4,4,64,256]{3,2,1,0:T(8,128)(2,1)S(1)}, bf16[4,4,64,256]{3,2,1,0:T(8,128)(2,1)}, u32[]{:S(2)}) copy-start(bf16[4,4,64,256]{3,2,1,0:T(8,128)(2,1)} %param.20) | copy-start | bytes 1572868
  (17 other events, 46.4 us)

commit v4 on v3

--- a/solution.py
+++ b/solution.py
@@ -20,6 +20,7 @@
 PACK = RANK + 16
 SIDEWAYS = 8 * RANK + 4 * RANK + 48
 CORNER = 4 * RANK + 4 * RANK + 48
+BIG = 58 << 20
 COPIES = 42
 BF = jnp.bfloat16
 F32 = jnp.float32
@@ -40,7 +41,7 @@
     return [float(c) for c in np.linalg.lstsq(powers, np.sin(2 * np.pi * w) * long_weight, rcond=None)[0]]
 
 
-SINE = sine_terms(4)
+SINE = sine_terms(3)
 
 
 def coupling(height, shift_y, shift_x):
@@ -126,9 +127,22 @@
     return lax.dot_general(a, b, (((0,), (0,)), ((), ())), preferred_element_type=F32)
 
 
-def up_body(q_ref, basis_ref, tree_ref, pos_ref, east_ref, west_ref, north_ref, south_ref, coef_ref, give_ref):
+def up_body(
+    q_any, basis_any, tree_any, pos_ref, east_ref, west_ref, north_ref, south_ref, coef_ref, give_ref, q_ref, basis_ref, tree_ref, sems
+):
+    loads = []
+    for k in range(4):
+        part = pl.ds(4 * k, 4)
+        loads.append(pltpu.make_async_copy(basis_any.at[part], basis_ref.at[part], sems.at[2 * k]))
+        loads.append(pltpu.make_async_copy(q_any.at[part], q_ref.at[part], sems.at[2 * k + 1]))
+    loads.append(pltpu.make_async_copy(tree_any, tree_ref, sems.at[8]))
+    for load in loads:
+        load.start()
     level0 = []
     for leaf in range(LEAVES):
+        if leaf % 4 == 0:
+            loads[leaf // 2].wait()
+            loads[leaf // 2 + 1].wait()
         coef = dot(basis_ref[leaf], q_ref[leaf]).astype(BF)
         level0.append(coef)
         r, c = leaf // SIDE, leaf % SIDE
@@ -137,6 +151,7 @@
         ref[at * RANK : (at + 1) * RANK] = coef
         ref, at = (north_ref, r * 4 + c) if r < 2 else (south_ref, r * 4 + c - 8)
         ref[at * RANK : (at + 1) * RANK] = coef
+    loads[8].wait()
     level1 = []
     for r in range(2):
         for c in range(2):
@@ -186,9 +201,15 @@
             jax.ShapeDtypeStruct(((LEAVES + 4) * RANK, LEAF), BF),
             jax.ShapeDtypeStruct((PACK, LEAF), BF),
         ),
-        in_specs=[vmem] * 4,
+        in_specs=[pl.BlockSpec(memory_space=pl.ANY)] * 3 + [vmem],
         out_specs=[vmem] * 6,
-        compiler_params=pltpu.CompilerParams(vmem_limit_bytes=32 << 20),
+        scratch_shapes=[
+            pltpu.VMEM((LEAVES, LEAF, LEAF), BF),
+            pltpu.VMEM((LEAVES, RANK, LEAF), BF),
+            pltpu.VMEM((TOP + 1, RANK, RANK), BF),
+            pltpu.SemaphoreType.DMA((9,)),
+        ],
+        compiler_params=pltpu.CompilerParams(vmem_limit_bytes=BIG),
         cost_estimate=pl.CostEstimate(flops=300_000_000, bytes_accessed=5_000_000, transcendentals=0),
         name="upward",
     )(q, basis, tree, points)
@@ -284,7 +305,7 @@
             pltpu.VMEM((25, RANK, RANK), BF),
             pltpu.SemaphoreType.DMA((COPIES + 3,)),
         ],
-        compiler_params=pltpu.CompilerParams(vmem_limit_bytes=32 << 20),
+        compiler_params=pltpu.CompilerParams(vmem_limit_bytes=BIG),
         cost_estimate=pl.CostEstimate(flops=5_000_000_000, bytes_accessed=8_000_000, transcendentals=0),
         name="local_far",
     )(
@@ -300,7 +321,14 @@
     )
 
 
-def top_body(meta_ref, all_ref, c2_any, c3_any, tree_ref, sum0, sum1, field_ref, win, parents, c2_ref, c3_ref, sems):
+def top_body(
+    meta_ref, all_any, c2_any, c3_any, tree_any, sum0_any, sum1_any, field_ref, win, parents, c2_ref, c3_ref, all_ref, tree_ref, sum0, sum1, sems
+):
+    loads = []
+    for k, (source, to) in enumerate(((all_any, all_ref), (tree_any, tree_ref), (sum1_any, sum1), (sum0_any, sum0))):
+        loads.append(pltpu.make_async_copy(source, to, sems.at[2 + k]))
+        loads[-1].start()
+
     def slab(source, to, at):
         part = pl.ds(pl.multiple_of(meta_ref[2 * WINDOW + at] * RANK, RANK), RANK)
         copy = pltpu.make_async_copy(source.at[part], to, sems.at[at])
@@ -308,6 +336,8 @@
         return copy
 
     slabs = [slab(c2_any, c2_ref, 0), slab(c3_any, c3_ref, 1)]
+
+    loads[0].wait()
 
     def lift(group, carry):
         total = jnp.zeros((RANK, LEAF), F32)
@@ -343,6 +373,8 @@
     field3 = dot(c3_ref[...], win[...]).astype(BF)
     fill(0, all_ref, PACK)
     slabs[0].wait()
+    for load in loads[1:]:
+        load.wait()
     field2 = (dot(c2_ref[...], win[...]) + dot_first(tree_ref[TOP], field3)).astype(BF)
     field1 = []
     for at in range(4):
@@ -372,16 +404,20 @@
     return pl.pallas_call(
         top_body,
         out_shape=jax.ShapeDtypeStruct((LEAVES, RANK, LEAF), BF),
-        in_specs=[smem, vmem, anywhere, anywhere, vmem, vmem, vmem],
+        in_specs=[smem] + [anywhere] * 6,
         out_specs=vmem,
         scratch_shapes=[
             pltpu.VMEM((WINDOW * RANK, LEAF), BF),
             pltpu.VMEM((devices // 4 * RANK, LEAF), BF),
             pltpu.VMEM((RANK, WINDOW * RANK), BF),
             pltpu.VMEM((RANK, WINDOW * RANK), BF),
-            pltpu.SemaphoreType.DMA((2,)),
+            pltpu.VMEM(gathered.shape, BF),
+            pltpu.VMEM((TOP + 1, RANK, RANK), BF),
+            pltpu.VMEM((LEAVES, RANK, LEAF), F32),
+            pltpu.VMEM((4 * RANK, LEAF), F32),
+            pltpu.SemaphoreType.DMA((6,)),
         ],
-        compiler_params=pltpu.CompilerParams(vmem_limit_bytes=32 << 20),
+        compiler_params=pltpu.CompilerParams(vmem_limit_bytes=BIG),
         cost_estimate=pl.CostEstimate(flops=3_000_000_000, bytes_accessed=5_000_000, transcendentals=0),
         name="top_far",
     )(meta, gathered, jnp.asarray(window_coupling(2)), jnp.asarray(window_coupling(3)), tree, sum0, sum1)
@@ -411,7 +447,7 @@
         join_body,
         out_shape=(message, message),
         in_specs=[anywhere] * 4,
-        out_specs=[anywhere] * 2,
+        out_specs=[pl.BlockSpec(memory_space=pltpu.VMEM)] * 2,
         scratch_shapes=[pltpu.SemaphoreType.DMA((10,))],
         cost_estimate=pl.CostEstimate(flops=0, bytes_accessed=4_000_000, transcendentals=0),
         name="join",
@@ -426,7 +462,7 @@
     phase = length - ((length + rounder) - rounder)
     w = 0.25 - jnp.abs(phase)
     s = w * w
-    wave = w * (SINE[0] + s * (SINE[1] + s * (SINE[2] + s * SINE[3])))
+    wave = w * (SINE[0] + s * (SINE[1] + s * SINE[2]))
     return (jnp.exp2(squared * short_rate) + jnp.exp2(squared * long_rate) * wave).astype(BF)
 
 
@@ -465,8 +501,13 @@
     return pairs
 
 
-def near_own_body(first, table_ref, q_ref, pos_ref, noise_ref, *refs):
-    before_ref, out_ref, columns, blocks = (None,) * (4 - len(refs)) + refs
+def near_own_body(first, table_ref, q_any, pos_ref, noise_ref, *refs):
+    before_any, out_ref, columns, blocks, q_ref, before_ref, sems = (None,) * (7 - len(refs)) + refs
+    loads = [pltpu.make_async_copy(q_any, q_ref, sems.at[0])]
+    if first:
+        loads.append(pltpu.make_async_copy(before_any.at[pl.ds(8, SIDE)], before_ref, sems.at[1]))
+    for load in loads:
+        load.start()
     pairs = own_pairs(first)
     start = first * SIDE
 
@@ -497,6 +538,8 @@
         return carry
 
     lax.fori_loop(0, len(pairs) // 2, both, 0)
+    for load in loads:
+        load.wait()
     parts = {leaf: [(leaf - start, leaf)] for leaf in range(start, start + 8)}
     for i, (target, source, _, _) in enumerate(pairs):
         parts[target].append((8 + 2 * i, source))
@@ -509,8 +552,8 @@
         if leaf < start + 8:
             noise = jnp.concatenate([columns[leaf, :, 256:384]] * 2, axis=1)
             total = total + noise * q_ref[leaf].astype(F32)
-        if before_ref is not None and leaf < start + SIDE:
-            total = total + before_ref[leaf]
+        if first and leaf < start + SIDE:
+            total = total + before_ref[leaf - start]
         out_ref[leaf - start] = total
 
 
@@ -526,11 +569,14 @@
     return pl.pallas_call(
         body,
         out_shape=jax.ShapeDtypeStruct((12 if first == 0 else 8, LEAF, LEAF), F32),
-        in_specs=[anywhere, smem, vmem, vmem, vmem] + [vmem] * len(before),
+        in_specs=[anywhere, smem, anywhere, vmem, vmem] + [anywhere] * len(before),
         out_specs=vmem,
         scratch_shapes=[
             pltpu.VMEM((LEAVES, LEAF, 384), F32),
             pltpu.VMEM((8 + 2 * len(pairs), LEAF, LEAF), BF),
+            pltpu.VMEM((LEAVES, LEAF, LEAF), BF),
+            pltpu.VMEM((SIDE, LEAF, LEAF), F32),
+            pltpu.SemaphoreType.DMA((2,)),
         ],
         compiler_params=pltpu.CompilerParams(vmem_limit_bytes=40 << 20),
         cost_estimate=pl.CostEstimate(flops=10_000_000_000, bytes_accessed=4_000_000, transcendentals=8_000_000),
@@ -555,9 +601,10 @@
 
 
 def edge_body(
-    list_ref, table_ref, slot_ref, after_ref, own_pos_ref, west_any, east_any, north_any, south_any, out_ref,
-    columns, parts, points, sems,
+    half_at, list_ref, table_ref, slot_ref, after_ref, own_pos_ref, west_any, east_any, north_any, south_any, out_any,
+    columns, parts, points, out_ref, sems,
 ):
+    start = 8 * half_at
     copies = []
     sources = (
         (west_any, 12 * RANK),
@@ -576,10 +623,10 @@
 
     def turn(leaf, carry):
         turn_points(columns, leaf, own_pos_ref[leaf], jnp.zeros((1, LEAF), F32))
-        points[leaf] = own_pos_ref[leaf]
         return carry
 
-    lax.fori_loop(0, LEAVES, turn, 0)
+    lax.fori_loop(start, start + 8, turn, 0)
+    points[0:LEAVES] = own_pos_ref[...]
     for copy in copies:
         copy.wait()
     slots = (16, 24, 32, 40, 44, 48, 56, 60)
@@ -602,46 +649,60 @@
             )
         return carry
 
-    lax.fori_loop(0, EDGES // 2, fixed, 0)
+    lax.fori_loop(0, EDGES // 4, fixed, 0)
+    backs = []
+    for k, part in enumerate((pl.ds(0, EDGES // 2), pl.ds(EDGES // 2, 8))):
+        backs.append(pltpu.make_async_copy(out_ref.at[part], out_any.at[part], sems.at[8 + k]))
+    backs[0].start()
 
     def extra(i, carry):
         for half in range(2):
-            leaf = 2 * i + half
+            leaf = start + 2 * i + half
             code, slot = extra_of(list_ref, slot_ref, leaf)
             code = jnp.maximum(code, 0)
-            block_into(out_ref.at[EDGES + leaf], columns.at[leaf], points[slot], code // 5 - 2, code % 5 - 2)
+            block_into(out_ref.at[EDGES // 2 + 2 * i + half], columns.at[leaf], points[slot], code // 5 - 2, code % 5 - 2)
         return carry
 
-    lax.fori_loop(0, LEAVES // 2, extra, 0)
-
-
-def edge_blocks(near_list, after, own_points, west, east, north, south):
+    lax.fori_loop(0, 4, extra, 0)
+    backs[1].start()
+    for back in backs:
+        back.wait()
+
+
+def edge_blocks(half_at, near_list, after, own_points, west, east, north, south):
     vmem = pl.BlockSpec(memory_space=pltpu.VMEM)
     smem = pl.BlockSpec(memory_space=pltpu.SMEM)
     anywhere = pl.BlockSpec(memory_space=pl.ANY)
+    items = [item for item in ITEMS if item[0] // 8 == half_at]
+    assert len(items) * 2 == EDGES
+
+    def body(*refs):
+        edge_body(half_at, *refs)
+
     return pl.pallas_call(
-        edge_body,
-        out_shape=jax.ShapeDtypeStruct((EDGES + LEAVES, LEAF, LEAF), BF),
+        body,
+        out_shape=jax.ShapeDtypeStruct((EDGES // 2 + 8, LEAF, LEAF), BF),
         in_specs=[smem, smem, smem, anywhere, vmem] + [anywhere] * 4,
-        out_specs=vmem,
+        out_specs=anywhere,
         scratch_shapes=[
             pltpu.VMEM((LEAVES, LEAF, 384), F32),
             pltpu.VMEM((8, 48, LEAF), BF),
             pltpu.VMEM((64, 2, LEAF), F32),
-            pltpu.SemaphoreType.DMA((8,)),
+            pltpu.VMEM((EDGES // 2 + 8, LEAF, LEAF), BF),
+            pltpu.SemaphoreType.DMA((10,)),
         ],
-        compiler_params=pltpu.CompilerParams(vmem_limit_bytes=40 << 20),
-        cost_estimate=pl.CostEstimate(flops=12_000_000_000, bytes_accessed=8_000_000, transcendentals=12_000_000),
+        compiler_params=pltpu.CompilerParams(vmem_limit_bytes=BIG),
+        cost_estimate=pl.CostEstimate(flops=6_000_000_000, bytes_accessed=8_000_000, transcendentals=12_000_000),
         name="edge_blocks",
     )(
-        near_list, jnp.asarray(np.array(ITEMS, np.int32).reshape(-1)), jnp.asarray(SLOT_OF), after, own_points,
+        near_list, jnp.asarray(np.array(items, np.int32).reshape(-1)), jnp.asarray(SLOT_OF), after, own_points,
         west, east, north, south,
     )
 
 
 def final_body(
     list_ref, slot_ref, q_any, west_any, east_any, north_any, north_corner_any, south_any, south_corner_any,
-    block_any, upper_any, lower_any, basis_ref, field_ref, out_any, held, blocks, sums, extra_sum, outs, sems,
+    upper_blocks_any, lower_blocks_any, upper_any, lower_any, basis_ref, field_ref, out_any, held, blocks, sums, outs, sems,
 ):
     firsts = [min(at for at in range(EDGES) if ITEMS[at][0] // SIDE == r) for r in range(SIDE)] + [EDGES]
     stages = [[], [], [], []]
@@ -662,12 +723,13 @@
             for source, at in ((south_any, 48), (south_corner_any, 56)):
                 copy(r, source, held.at[pl.ds(at, 8)])
         part = pl.ds(firsts[r], firsts[r + 1] - firsts[r])
-        copy(r, block_any.at[part], blocks.at[part])
+        source, back = (upper_blocks_any, 0) if r < 2 else (lower_blocks_any, EDGES // 2)
+        copy(r, source.at[pl.ds(firsts[r] - back, firsts[r + 1] - firsts[r])], blocks.at[part])
         source = upper_any.at[pl.ds(SIDE * r, SIDE)] if r < 2 else lower_any.at[pl.ds(SIDE * (r - 2), SIDE)]
         copy(r, source, sums.at[pl.ds(SIDE * r, SIDE)])
     copy(SIDE - 1, q_any, held.at[pl.ds(0, 16)])
-    part = pl.ds(EDGES, LEAVES)
-    copy(SIDE - 1, block_any.at[part], blocks.at[part])
+    for half_at, source in enumerate((upper_blocks_any, lower_blocks_any)):
+        copy(SIDE - 1, source.at[pl.ds(EDGES // 2, 8)], blocks.at[pl.ds(EDGES + 8 * half_at, 8)])
     for leaf in range(LEAVES):
         if leaf % SIDE == 0:
             for made in stages[leaf // SIDE]:
@@ -704,7 +766,7 @@
         back.wait()
 
 
-def finish(near_list, q, halos, blocks, upper, lower, basis, field):
+def finish(near_list, q, halos, upper_blocks, lower_blocks, upper, lower, basis, field):
     vmem = pl.BlockSpec(memory_space=pltpu.VMEM)
     smem = pl.BlockSpec(memory_space=pltpu.SMEM)
     anywhere = pl.BlockSpec(memory_space=pl.ANY)
@@ -712,20 +774,19 @@
     return pl.pallas_call(
         final_body,
         out_shape=jax.ShapeDtypeStruct((LEAVES, LEAF, LEAF), BF),
-        in_specs=[smem, smem] + [anywhere] * 10 + [vmem, vmem],
+        in_specs=[smem, smem] + [anywhere] * 11 + [vmem, vmem],
         out_specs=anywhere,
         scratch_shapes=[
             pltpu.VMEM((64, LEAF, LEAF), BF),
             pltpu.VMEM((EDGES + LEAVES, LEAF, LEAF), BF),
             pltpu.VMEM((LEAVES, LEAF, LEAF), F32),
-            pltpu.VMEM((LEAF, LEAF), F32),
             pltpu.VMEM((LEAVES, LEAF, LEAF), BF),
-            pltpu.SemaphoreType.DMA((20,)),
+            pltpu.SemaphoreType.DMA((21,)),
         ],
-        compiler_params=pltpu.CompilerParams(vmem_limit_bytes=48 << 20),
+        compiler_params=pltpu.CompilerParams(vmem_limit_bytes=BIG),
         cost_estimate=pl.CostEstimate(flops=4_000_000_000, bytes_accessed=24_000_000, transcendentals=0),
         name="finish",
-    )(near_list, jnp.asarray(SLOT_OF), q, *halos, blocks, upper, lower, basis, field)
+    )(near_list, jnp.asarray(SLOT_OF), q, *halos, upper_blocks, lower_blocks, upper, lower, basis, field)
 
 
 def window_slots(wide, narrow, steps):
@@ -761,8 +822,6 @@
     east, west, north, south, coefs, give = go_up(q, basis, tree, points)
     from_west = shift(east, "wide", 1)
     from_east = shift(west, "wide", -1)
-    q_west = shift(charges[:, 2:4], "wide", 1)
-    q_east = shift(charges[:, 0:2], "wide", -1)
     q_north = shift(charges[2:4], "narrow", 1)
     q_south = shift(charges[0:2], "narrow", -1)
 
@@ -778,13 +837,16 @@
     gathered = give
     other = step(gathered, 0)
     upper = near_own(0, q, points, noise_rows, give, [])
-    other, from_west, from_east, upper = tie(other, from_west, from_east, upper)
-    gathered = jnp.concatenate([gathered, other], axis=0)
-    other = step(gathered, 1)
+    to_east, to_west = charges[:, 2:4], charges[:, 0:2]
+    other, from_west, from_east, upper, to_east, to_west = tie(other, from_west, from_east, upper, to_east, to_west)
     to_north, to_south = join(north, south, from_west, from_east)
     from_south = shift(to_north, "narrow", -1)
     from_north = shift(to_south, "narrow", 1)
-    lower = near_own(2, q, points, noise_rows, from_west, [upper])
+    q_west = shift(to_east, "wide", 1)
+    q_east = shift(to_west, "wide", -1)
+    gathered = jnp.concatenate([gathered, other], axis=0)
+    other = step(gathered, 1)
+    lower = near_own(2, q, points, noise_rows, to_north, [upper])
     other, from_south, from_north, lower = tie(other, from_south, from_north, lower)
     for at in range(2, len(steps)):
         gathered = jnp.concatenate([gathered, other], axis=0)
@@ -793,19 +855,21 @@
             sums = local_far(listing, coefs, from_west, from_east, from_north, from_south)
             other, *sums = tie(other, *sums)
         if at == 3:
-            blocks = edge_blocks(listing, sums[1], points, from_west, from_east, from_north, from_south)
-            other, blocks = tie(other, blocks)
+            upper_blocks = edge_blocks(0, listing, sums[1], points, from_west, from_east, from_north, from_south)
+            other, upper_blocks, q_west, q_east = tie(other, upper_blocks, q_west, q_east)
+            q_north_corner = shift(jnp.stack([q_west[2:4], q_east[2:4]]), "narrow", 1)
+            q_south_corner = shift(jnp.stack([q_west[0:2], q_east[0:2]]), "narrow", -1)
+        if at == 4:
+            lower_blocks = edge_blocks(1, listing, upper_blocks, points, from_west, from_east, from_north, from_south)
+            other, lower_blocks = tie(other, lower_blocks)
     gathered = jnp.concatenate([gathered, other], axis=0)
-    q_west, q_east, blocks = tie(q_west, q_east, blocks)
-    q_north_corner = shift(jnp.stack([q_west[2:4], q_east[2:4]]), "narrow", 1)
-    q_south_corner = shift(jnp.stack([q_west[0:2], q_east[0:2]]), "narrow", -1)
     field = top_far(meta, gathered, tree, *sums)
     q_north_corner, q_south_corner, field = tie(q_north_corner, q_south_corner, field)
     halos = [
         value.reshape(8, LEAF, LEAF)
         for value in (q_west, q_east, q_north, q_north_corner, q_south, q_south_corner)
     ]
-    out = finish(listing, q, halos, blocks, upper, lower, basis, field)
+    out = finish(listing, q, halos, upper_blocks, lower_blocks, upper, lower, basis, field)
     return out.reshape(SIDE, SIDE, LEAF, LEAF)
 
 

time: 229 us -> 163 us (0.71)
  Pallas kernels: 138 us -> 86.4 us
  local copies, waits for them, and re-layouts: 26.2 us -> 16.3 us
    pallas_call x1, Pallas kernels: 61.2 us -> 2.87 us  [join(): pl.pallas_call(join_body, out_shape=(message, message), in_specs=[anywher...]
    ppermute x10, waiting for transfers between devices: 23.2 us -> 0.03 us  [shift(): lax.ppermute(value, axis, [(i, i + steps) for i in range(count) if 0 <= i...]
    ppermute x5, waiting for transfers between devices: 0.01 us -> 21.1 us  [step(): lax.ppermute(value, axis, [(i, i ^ bit) for i in range(lax.axis_size(axis...]
    unnamed x72 -> x44, local copies, waits for them, and re-layouts: 18.5 us -> 10.6 us
    pallas_call x1, Pallas kernels: 1.63 us -> 4.72 us  [go_up(): pl.pallas_call(up_body, out_shape=(side, side, side, side, jax.ShapeDtype...]
    pallas_call x1 -> x2, Pallas kernels: 22 us -> 23.9 us  [edge_blocks(): pl.pallas_call(body, out_shape=jax.ShapeDtypeStruct((EDGES // 2 + 8, LEAF...]
  transfers between devices with their start and end apart: 15 -> 15, of which waited for: 2 -> 1; matrix products, arithmetic and copies ran while one was open for 6% -> 6% of each run, Pallas kernels for 55% -> 42%
where the time goes in v4:
time: 163 us; the launch traced here: 162 us
  Pallas kernels  86.4 us (53%)
  starting transfers between devices  36.4 us (22%)
  waiting for transfers between devices  21.2 us (13%)
  local copies, waits for them, and re-layouts  16.3 us (10%)
    ppermute x10, starting transfers between devices, shift(): lax.ppermute(value, axis, [(i, i + steps) for i in range(count) if 0 <= i...  28.3 us
    pallas_call x2, Pallas kernels, near_own(): pl.pallas_call(body, out_shape=jax.ShapeDtypeStruct((12 if first == 0 els...  26.4 us
    pallas_call x2, Pallas kernels, edge_blocks(): pl.pallas_call(body, out_shape=jax.ShapeDtypeStruct((EDGES // 2 + 8, LEAF...  23.9 us
    ppermute x5, waiting for transfers between devices, step(): lax.ppermute(value, axis, [(i, i ^ bit) for i in range(lax.axis_size(axis...  21.1 us
    pallas_call x1, Pallas kernels, finish(): pl.pallas_call(final_body, out_shape=jax.ShapeDtypeStruct((LEAVES, LEAF,...  13.3 us
    unnamed x44, local copies, waits for them, and re-layouts  10.6 us
    ppermute x5, starting transfers between devices, step(): lax.ppermute(value, axis, [(i, i ^ bit) for i in range(lax.axis_size(axis...  8.09 us
    pallas_call x1, Pallas kernels, local_far(): pl.pallas_call(local_body, out_shape=(jax.ShapeDtypeStruct((LEAVES, RANK,...  7.83 us
  transfers between devices with their start and end apart: 15, of which 1 were waited for; matrix products, arithmetic and copies ran while one was open for 6% of the time, Pallas kernels for 42%

profile of v4, /device:TPU:1, one launch (start us, length us, event | category | flops | bytes accessed | tf_op | source)
XLA Modules:
  0.0 161.9 jit_solution(3402349232489492800)
XLA Ops:
  0.0 4.7 %upward.1 = (bf16[816,256]{1,0:T(8,128)(2,1)}, bf16[816,256]{1,0:T(8,128)(2,1)}, bf16[816,256]{1,0:T(8,128)(2,1)}, bf16[816,256]{1,0:T(8,128)(2,1)}, bf16[1280,256]{1,0:T(8,128)(2,1)}, /*index=5*/bf16[80,256]{1,0:T(8,128)(2,1)}) custom-call(bf16[16,256,256]{2,1,0:T(8,128)(2,1)} %bitcast.21, bf16[16,64,256]{2,1,0:T(8,128)(2,1)} %bitcast.32, ...), custom_call_target="tpu_custom_call" | custom-call | flops 300000000 | bytes 5000000 | tf_op jit(solution)/shard_map/upward/pallas_call | solution.py:194
  4.7 2.1 %collective-permute-start = (bf16[80,256]{1,0:T(8,128)(2,1)}, bf16[80,256]{1,0:T(8,128)(2,1)S(1)}, u32[]{:S(2)}, u32[]{:S(2)}) collective-permute-start(bf16[80,256]{1,0:T(8,128)(2,1)} %get-tuple-element.37.after_ref), channel_id=1, source_target_pairs={{0,4},{4,0},{8,12},{12,8},{16,20},{20,16},{24,28},{28,24},{1,5},{5... | collective-permute-start | bytes 122888 | tf_op jit(solution)/shard_map/ppermute | solution.py:832
  6.8 2.7 %collective-permute-start.1 = (bf16[816,256]{1,0:T(8,128)(2,1)}, bf16[816,256]{1,0:T(8,128)(2,1)}, u32[]{:S(2)}, u32[]{:S(2)}) collective-permute-start(bf16[816,256]{1,0:T(8,128)(2,1)} %get-tuple-element.38), channel_id=1, source_target_pairs={{0,4},{4,8},{8,12},{12,16},{16,20},{20,24},{24,28},{1,5},{5,9},{9,... | collective-permute-start | bytes 1253384 | tf_op jit(solution)/shard_map/ppermute | solution.py:119
  9.5 1.4 collective-permute-start.2
  11.0 1.5 fusion.2
  12.5 2.8 %collective-permute-start.14 = (bf16[2,4,256,256]{3,2,1,0:T(8,128)(2,1)}, bf16[2,4,256,256]{3,2,1,0:T(8,128)(2,1)S(1)}, u32[]{:S(2)}, u32[]{:S(2)}) collective-permute-start(bf16[2,4,256,256]{3,2,1,0:T(8,128)(2,1)} %get-tuple-element.69), channel_id=1, source_target_pairs={{1,0},{2,1},{3,2},{5,4},{6,5},{7,6},{9,8},{10,9},{11,10},{13,12},{... | collective-permute-start | bytes 3145736 | tf_op jit(solution)/shard_map/ppermute | solution.py:119
  15.3 3.6 %collective-permute-start.10 = (bf16[2,4,256,256]{3,2,1,0:T(8,128)(2,1)}, bf16[2,4,256,256]{3,2,1,0:T(8,128)(2,1)}, u32[]{:S(2)}, u32[]{:S(2)}) collective-permute-start(bf16[2,4,256,256]{3,2,1,0:T(8,128)(2,1)} %get-tuple-element.70), channel_id=1, source_target_pairs={{0,1},{1,2},{2,3},{4,5},{5,6},{6,7},{8,9},{9,10},{10,11},{12,13},{... | collective-permute-start | bytes 3145736 | tf_op jit(solution)/shard_map/ppermute | solution.py:119
  19.1 14.9 %near_own.2.refs_4_.upper_any = f32[12,256,256]{2,1,0:T(8,128)S(1)} custom-call(bf16[80,256]{1,0:T(8,128)(2,1)S(1)} %copy-done.4, s32[104]{0:T(128)S(1)} %copy-done.8, bf16[16,256,256]{2,1,0:T(8,128)(2,1)S(1)} %bitcast.23, f32[16,2,256]{2,1,0:T(2,128)S(1)} %bitcast.28, f32[16,1,256]{2,1,0:T(1,128)S(1)} %reshape.40.refs_3_), custom_call_target="tpu_custom_call" | custom-call | flops 10000000000 | bytes 4000000 | tf_op jit(solution)/shard_map/near_own/pallas_call | solution.py:569
  34.0 1.7 %copy-done.1 = f32[12,256,256]{2,1,0:T(8,128)} copy-done((f32[12,256,256]{2,1,0:T(8,128)}, f32[12,256,256]{2,1,0:T(8,128)S(1)}, u32[]{:S(2)}) %copy-start.1) | copy-done | bytes 3145752
  36.4 1.5 fusion.3
  39.3 2.9 %join.1 = (bf16[1936,256]{1,0:T(8,128)(2,1)}, bf16[1936,256]{1,0:T(8,128)(2,1)}) custom-call(bf16[816,256]{1,0:T(8,128)(2,1)} %get-tuple-element.41.north_ref, bf16[816,256]{1,0:T(8,128)(2,1)} %get-tuple-element.42.south_ref, bf16[816,256]{1,0:T(8,128)(2,1)} %collective-permute-done.1.west_ref.west_any.refs_5_, ...), custom_call_target="tpu_custom_call" | custom-call | bytes 4000000 | tf_op jit(solution)/shard_map/join/pallas_call | solution.py:446
  42.2 1.9 %collective-permute-start.4 = (bf16[1936,256]{1,0:T(8,128)(2,1)}, bf16[1936,256]{1,0:T(8,128)(2,1)S(1)}, u32[]{:S(2)}, u32[]{:S(2)}) collective-permute-start(bf16[1936,256]{1,0:T(8,128)(2,1)} %get-tuple-element.45.after_ref), channel_id=1, source_target_pairs={{1,0},{2,1},{3,2},{5,4},{6,5},{7,6},{9,8},{10,9},{11,10},{13,12},{... | collective-permute-start | bytes 2973704 | tf_op jit(solution)/shard_map/ppermute | solution.py:119
  44.2 3.6 %collective-permute-start.5 = (bf16[1936,256]{1,0:T(8,128)(2,1)}, bf16[1936,256]{1,0:T(8,128)(2,1)S(1)}, u32[]{:S(2)}, u32[]{:S(2)}) collective-permute-start(bf16[1936,256]{1,0:T(8,128)(2,1)} %get-tuple-element.46), channel_id=1, source_target_pairs={{0,1},{1,2},{2,3},{4,5},{5,6},{6,7},{8,9},{9,10},{10,11},{12,13},{... | collective-permute-start | bytes 2973704 | tf_op jit(solution)/shard_map/ppermute | solution.py:119
  47.9 1.9 %copy-done.2 = f32[12,256,256]{2,1,0:T(8,128)S(1)} copy-done((f32[12,256,256]{2,1,0:T(8,128)S(1)}, f32[12,256,256]{2,1,0:T(8,128)}, u32[]{:S(2)}) %copy-start.2) | copy-done | bytes 3145752
  49.8 1.2 copy-done.6
  51.0 11.5 %near_own.3.lower_any = f32[8,256,256]{2,1,0:T(8,128)S(1)} custom-call(bf16[1936,256]{1,0:T(8,128)(2,1)S(1)} %copy-done.6, s32[64]{0:T(128)S(1)} %copy-done.7, bf16[16,256,256]{2,1,0:T(8,128)(2,1)S(1)} %bitcast.24, f32[16,2,256]{2,1,0:T(2,128)S(1)} %bitcast.29, f32[16,1,256]{2,1,0:T(1,128)S(1)} %reshape.40.refs_3_, f32[12,256,256]{2,1,0:T(8,128)S(1)} %copy-done.2), custom_call_target="tpu_custom_call" | custom-call | flops 10000000000 | bytes 4000000 | tf_op jit(solution)/shard_map/near_own/pallas_call | solution.py:569
  62.5 1.4 copy-done.3
  64.6 4.3 %collective-permute-start.8 = (bf16[4,2,256,256]{3,2,1,0:T(8,128)(2,1)}, bf16[4,2,256,256]{3,2,1,0:T(8,128)(2,1)S(1)}, u32[]{:S(2)}, u32[]{:S(2)}) collective-permute-start(bf16[4,2,256,256]{3,2,1,0:T(8,128)(2,1)} %get-tuple-element.56), channel_id=1, source_target_pairs={{0,4},{4,8},{8,12},{12,16},{16,20},{20,24},{24,28},{1,5},{5,9},{9,... | collective-permute-start | bytes 3145736 | tf_op jit(solution)/shard_map/ppermute | solution.py:119
  68.9 1.3 collective-permute-start.9
  70.3 5.2 %collective-permute-start.6 = (bf16[320,256]{1,0:T(8,128)(2,1)S(1)}, bf16[320,256]{1,0:T(8,128)(2,1)S(1)}, u32[]{:S(2)}, u32[]{:S(2)}) collective-permute-start(bf16[320,256]{1,0:T(8,128)(2,1)S(1)} %pad_maximum_fusion.3), channel_id=1, source_target_pairs={{0,16},{4,20},{8,24},{12,28},{16,0},{20,4},{24,8},{28,12},{1,17},{... | collective-permute-start | bytes 491528 | tf_op jit(solution)/shard_map/ppermute | solution.py:832
  75.5 7.8 %local_far.1 = (f32[16,64,256]{2,1,0:T(8,128)}, f32[256,256]{1,0:T(8,128)}) custom-call(s32[160]{0:T(256)} %reshape.36.list_ref.refs_0_, bf16[1280,256]{1,0:T(8,128)(2,1)} %get-tuple-element.49.coef_any, bf16[816,256]{1,0:T(8,128)(2,1)} %collective-permute-done.1.west_ref.west_any.refs_5_, bf16[816,256]{1,0:T(8,128)(2,1)} %collective-permute-done.2.east_ref.east_any.refs_6_, ...), custom_call_target="tpu_custom_call" | custom-call | flops 5000000000 | bytes 8000000 | tf_op jit(solution)/shard_map/local_far/pallas_call | solution.py:292
  84.0 21.1 %collective-permute-done.6 = bf16[320,256]{1,0:T(8,128)(2,1)S(1)} collective-permute-done((bf16[320,256]{1,0:T(8,128)(2,1)S(1)}, bf16[320,256]{1,0:T(8,128)(2,1)S(1)}, u32[]{:S(2)}, u32[]{:S(2)}) %collective-permute-start.6) | collective-permute-done | bytes 163872 | tf_op jit(solution)/shard_map/ppermute | solution.py:832
  105.2 11.9 %edge_blocks.2.refs_3_.upper_blocks_any = bf16[30,256,256]{2,1,0:T(8,128)(2,1)} custom-call(s32[160]{0:T(256)} %reshape.36.list_ref.refs_0_, s32[88]{0:T(128)} %constant.204.clone.refs_1_, s32[64]{0:T(128)} %constant.205.clone.refs_2_.slot_ref, f32[256,256]{1,0:T(8,128)} %get-tuple-element.55.refs_3_.sum1_any, f32[16,2,256]{2,1,0:T(2,128)} %bitcast.26, ...), custom_call_target="tpu_custom_call" | custom-call | flops 6000000000 | bytes 8000000 | tf_op jit(solution)/shard_map/edge_blocks/pallas_call | solution.py:682
  117.2 0.7 constant_dynamic-update-slice_fusion.1
  118.0 0.9 constant_dynamic-update-slice_fusion
  119.8 3.5 %collective-permute-start.12 = (bf16[2,2,2,256,256]{4,3,2,1,0:T(8,128)(2,1)S(1)}, bf16[2,2,2,256,256]{4,3,2,1,0:T(8,128)(2,1)S(1)}, u32[]{:S(2)}, u32[]{:S(2)}) collective-permute-start(bf16[2,2,2,256,256]{4,3,2,1,0:T(8,128)(2,1)S(1)} %pad_maximum_fusion.1), channel_id=1, source_target_pairs={{1,0},{2,1},{3,2},{5,4},{6,5},{7,6},{9,8},{10,9},{11,10},{13,12},{... | collective-permute-start | bytes 3145736 | tf_op jit(solution)/shard_map/ppermute | solution.py:119
  123.4 3.1 %collective-permute-start.11 = (bf16[2,2,2,256,256]{4,3,2,1,0:T(8,128)(2,1)S(1)}, bf16[2,2,2,256,256]{4,3,2,1,0:T(8,128)(2,1)S(1)}, u32[]{:S(2)}, u32[]{:S(2)}) collective-permute-start(bf16[2,2,2,256,256]{4,3,2,1,0:T(8,128)(2,1)S(1)} %pad_maximum_fusion), channel_id=1, source_target_pairs={{0,1},{1,2},{2,3},{4,5},{5,6},{6,7},{8,9},{9,10},{10,11},{12,13},{... | collective-permute-start | bytes 3145736 | tf_op jit(solution)/shard_map/ppermute | solution.py:119
  126.6 12.0 %edge_blocks.3.lower_blocks_any = bf16[30,256,256]{2,1,0:T(8,128)(2,1)} custom-call(s32[160]{0:T(256)} %reshape.36.list_ref.refs_0_, s32[88]{0:T(128)} %constant.206.clone.refs_1_, s32[64]{0:T(128)} %constant.205.clone.refs_2_.slot_ref, bf16[30,256,256]{2,1,0:T(8,128)(2,1)} %edge_blocks.2.refs_3_.upper_blocks_any, f32[16,2,256]{2,1,0:T(2,128)} %bitcast.27, ...), custom_call_target="tpu_custom_call" | custom-call | flops 6000000000 | bytes 8000000 | tf_op jit(solution)/shard_map/edge_blocks/pallas_call | solution.py:682
  138.6 0.9 constant_dynamic-update-slice_fusion.5.all_any
  139.4 7.4 %top_far.1.field_ref = bf16[16,64,256]{2,1,0:T(8,128)(2,1)} custom-call(s32[74]{0:T(128)} %pad_add_fusion.meta_ref, bf16[2560,256]{1,0:T(8,128)(2,1)} %constant_dynamic-update-slice_fusion.5.all_any, bf16[256,2304]{1,0:T(8,128)(2,1)} %constant.207.clone.c2_any, bf16[256,2304]{1,0:T(8,128)(2,1)} %constant.208.clone.c3_any, bf16[21,64,64]{2,1,0:T(8,128)(2,1)} %bitcast.38, ...), custom_call_target="tpu_custom_call" | custom-call | flops 3000000000 | bytes 5000000 | tf_op jit(solution)/shard_map/top_far/pallas_call | solution.py:404
  146.9 0.9 copy-done.12
  148.5 13.3 %finish.1 = bf16[16,256,256]{2,1,0:T(8,128)(2,1)} custom-call(s32[160]{0:T(256)} %reshape.36.list_ref.refs_0_, s32[64]{0:T(128)} %constant.205.clone.refs_2_.slot_ref, bf16[16,256,256]{2,1,0:T(8,128)(2,1)} %bitcast.22, bf16[8,256,256]{2,1,0:T(8,128)(2,1)} %bitcast.30, bf16[8,256,256]{2,1,0:T(8,128)(2,1)} %bitcast.31, bf16[8,256,256]{2,1,0:T(8,128)(2,1)} %bitcast.6.north_any, ...), custom_call_target="tpu_custom_call" | custom-call | flops 4000000000 | bytes 24000000 | tf_op jit(solution)/shard_map/finish/pallas_call | solution.py:774
  (65 shorter events, 5.2 us)
Async XLA Ops:
  0.0 11.0 %copy-start = (bf16[4,4,256,256]{3,2,1,0:T(8,128)(2,1)S(1)}, bf16[4,4,256,256]{3,2,1,0:T(8,128)(2,1)}, u32[]{:S(2)}) copy-start(bf16[4,4,256,256]{3,2,1,0:T(8,128)(2,1)} %param.18) | copy-start | bytes 6291460
  4.7 34.6 %collective-permute-start = (bf16[80,256]{1,0:T(8,128)(2,1)}, bf16[80,256]{1,0:T(8,128)(2,1)S(1)}, u32[]{:S(2)}, u32[]{:S(2)}) collective-permute-start(bf16[80,256]{1,0:T(8,128)(2,1)} %get-tuple-element.37.after_ref), channel_id=1, source_target_pairs={{0,4},{4,0},{8,12},{12,8},{16,20},{20,16},{24,28},{28,24},{1,5},{5... | collective-permute-start | bytes 122888 | tf_op jit(solution)/shard_map/ppermute | solution.py:832
  6.8 32.5 %collective-permute-start.1 = (bf16[816,256]{1,0:T(8,128)(2,1)}, bf16[816,256]{1,0:T(8,128)(2,1)}, u32[]{:S(2)}, u32[]{:S(2)}) collective-permute-start(bf16[816,256]{1,0:T(8,128)(2,1)} %get-tuple-element.38), channel_id=1, source_target_pairs={{0,4},{4,8},{8,12},{12,16},{16,20},{20,24},{24,28},{1,5},{5,9},{9,... | collective-permute-start | bytes 1253384 | tf_op jit(solution)/shard_map/ppermute | solution.py:119
  9.5 9.4 %copy-start.14 = (f32[4,4,256]{2,1,0:T(4,128)S(1)}, f32[4,4,256]{2,1,0:T(4,128)}, u32[]{:S(2)}) copy-start(f32[4,4,256]{2,1,0:T(4,128)} %param.20) | copy-start | bytes 49156
  9.5 9.5 %copy-start.4 = (bf16[80,256]{1,0:T(8,128)(2,1)S(1)}, bf16[80,256]{1,0:T(8,128)(2,1)}, u32[]{:S(2)}) copy-start(bf16[80,256]{1,0:T(8,128)(2,1)} %get-tuple-element.37.after_ref) | copy-start | bytes 122884
  9.5 9.5 %copy-start.5 = (f32[4,4,2,256]{3,2,1,0:T(2,128)S(1)}, f32[4,4,2,256]{3,2,1,0:T(2,128)}, u32[]{:S(2)}) copy-start(f32[4,4,2,256]{3,2,1,0:T(2,128)} %param.19) | copy-start | bytes 98308
  9.5 9.5 %copy-start.8 = (s32[104]{0:T(128)S(1)}, s32[104]{0:T(128)}, u32[]{:S(2)}) copy-start(s32[104]{0:T(128)} %constant.199.clone.refs_0_) | copy-start | bytes 1252
  9.5 29.8 %collective-permute-start.2 = (bf16[816,256]{1,0:T(8,128)(2,1)}, bf16[816,256]{1,0:T(8,128)(2,1)}, u32[]{:S(2)}, u32[]{:S(2)}) collective-permute-start(bf16[816,256]{1,0:T(8,128)(2,1)} %get-tuple-element.39), channel_id=1, source_target_pairs={{4,0},{8,4},{12,8},{16,12},{20,16},{24,20},{28,24},{5,1},{9,5},{13... | collective-permute-start | bytes 1253384 | tf_op jit(solution)/shard_map/ppermute | solution.py:119
  12.5 134.4 %collective-permute-start.14 = (bf16[2,4,256,256]{3,2,1,0:T(8,128)(2,1)}, bf16[2,4,256,256]{3,2,1,0:T(8,128)(2,1)S(1)}, u32[]{:S(2)}, u32[]{:S(2)}) collective-permute-start(bf16[2,4,256,256]{3,2,1,0:T(8,128)(2,1)} %get-tuple-element.69), channel_id=1, source_target_pairs={{1,0},{2,1},{3,2},{5,4},{6,5},{7,6},{9,8},{10,9},{11,10},{13,12},{... | collective-permute-start | bytes 3145736 | tf_op jit(solution)/shard_map/ppermute | solution.py:119
  15.3 131.6 %collective-permute-start.10 = (bf16[2,4,256,256]{3,2,1,0:T(8,128)(2,1)}, bf16[2,4,256,256]{3,2,1,0:T(8,128)(2,1)}, u32[]{:S(2)}, u32[]{:S(2)}) collective-permute-start(bf16[2,4,256,256]{3,2,1,0:T(8,128)(2,1)} %get-tuple-element.70), channel_id=1, source_target_pairs={{0,1},{1,2},{2,3},{4,5},{5,6},{6,7},{8,9},{9,10},{10,11},{12,13},{... | collective-permute-start | bytes 3145736 | tf_op jit(solution)/shard_map/ppermute | solution.py:119
  19.1 16.7 %copy-start.16 = (s32[36]{0:T(128)S(1)}, s32[36]{0:T(128)}, u32[]{:S(2)}) copy-start(s32[36]{0:T(128)} %constant.197.clone) | copy-start | bytes 436
  19.1 16.7 %copy-start.17 = (s32[36]{0:T(128)S(1)}, s32[36]{0:T(128)}, u32[]{:S(2)}) copy-start(s32[36]{0:T(128)} %constant.198.clone) | copy-start | bytes 436
  34.0 1.7 %copy-start.1 = (f32[12,256,256]{2,1,0:T(8,128)}, f32[12,256,256]{2,1,0:T(8,128)S(1)}, u32[]{:S(2)}) copy-start(f32[12,256,256]{2,1,0:T(8,128)S(1)} %near_own.2.refs_4_.upper_any) | copy-start | bytes 9437188
  36.4 2.2 %copy-start.15 = (s32[4,4,10]{2,1,0:T(4,128)S(1)}, s32[4,4,10]{2,1,0:T(4,128)}, u32[]{:S(2)}) copy-start(s32[4,4,10]{2,1,0:T(4,128)} %param.23) | copy-start | bytes 1924
  38.0 9.9 %copy-start.7 = (s32[64]{0:T(128)S(1)}, s32[64]{0:T(128)}, u32[]{:S(2)}) copy-start(s32[64]{0:T(128)} %constant.200.clone.refs_0_) | copy-start | bytes 772
  42.2 26.7 %collective-permute-start.4 = (bf16[1936,256]{1,0:T(8,128)(2,1)}, bf16[1936,256]{1,0:T(8,128)(2,1)S(1)}, u32[]{:S(2)}, u32[]{:S(2)}) collective-permute-start(bf16[1936,256]{1,0:T(8,128)(2,1)} %get-tuple-element.45.after_ref), channel_id=1, source_target_pairs={{1,0},{2,1},{3,2},{5,4},{6,5},{7,6},{9,8},{10,9},{11,10},{13,12},{... | collective-permute-start | bytes 2973704 | tf_op jit(solution)/shard_map/ppermute | solution.py:119
  44.2 26.1 %collective-permute-start.5 = (bf16[1936,256]{1,0:T(8,128)(2,1)}, bf16[1936,256]{1,0:T(8,128)(2,1)S(1)}, u32[]{:S(2)}, u32[]{:S(2)}) collective-permute-start(bf16[1936,256]{1,0:T(8,128)(2,1)} %get-tuple-element.46), channel_id=1, source_target_pairs={{0,1},{1,2},{2,3},{4,5},{5,6},{6,7},{8,9},{9,10},{10,11},{12,13},{... | collective-permute-start | bytes 2973704 | tf_op jit(solution)/shard_map/ppermute | solution.py:119
  47.8 16.7 %collective-permute-start.3 = (bf16[160,256]{1,0:T(8,128)(2,1)S(1)}, bf16[160,256]{1,0:T(8,128)(2,1)S(1)}, u32[]{:S(2)}, u32[]{:S(2)}) collective-permute-start(bf16[160,256]{1,0:T(8,128)(2,1)S(1)} %pad_maximum_fusion.4), channel_id=1, source_target_pairs={{0,1},{1,0},{2,3},{3,2},{4,5},{5,4},{6,7},{7,6},{8,9},{9,8},{10,11... | collective-permute-start | bytes 245768 | tf_op jit(solution)/shard_map/ppermute | solution.py:832
  47.9 1.9 %copy-start.2 = (f32[12,256,256]{2,1,0:T(8,128)S(1)}, f32[12,256,256]{2,1,0:T(8,128)}, u32[]{:S(2)}) copy-start(f32[12,256,256]{2,1,0:T(8,128)} %copy-done.1) | copy-start | bytes 9437188
  62.5 1.5 copy-start.3
  64.6 53.4 %collective-permute-start.8 = (bf16[4,2,256,256]{3,2,1,0:T(8,128)(2,1)}, bf16[4,2,256,256]{3,2,1,0:T(8,128)(2,1)S(1)}, u32[]{:S(2)}, u32[]{:S(2)}) collective-permute-start(bf16[4,2,256,256]{3,2,1,0:T(8,128)(2,1)} %get-tuple-element.56), channel_id=1, source_target_pairs={{0,4},{4,8},{8,12},{12,16},{16,20},{20,24},{24,28},{1,5},{5,9},{9,... | collective-permute-start | bytes 3145736 | tf_op jit(solution)/shard_map/ppermute | solution.py:119
  68.9 6.6 %copy-start.18 = (bf16[1936,256]{1,0:T(8,128)(2,1)}, bf16[1936,256]{1,0:T(8,128)(2,1)S(1)}, u32[]{:S(2)}) copy-start(bf16[1936,256]{1,0:T(8,128)(2,1)S(1)} %collective-permute-done.4.south_any.refs_8_) | copy-start | bytes 2973700
  68.9 49.0 %collective-permute-start.9 = (bf16[4,2,256,256]{3,2,1,0:T(8,128)(2,1)}, bf16[4,2,256,256]{3,2,1,0:T(8,128)(2,1)S(1)}, u32[]{:S(2)}, u32[]{:S(2)}) collective-permute-start(bf16[4,2,256,256]{3,2,1,0:T(8,128)(2,1)} %get-tuple-element.57), channel_id=1, source_target_pairs={{4,0},{8,4},{12,8},{16,12},{20,16},{24,20},{28,24},{5,1},{9,5},{13... | collective-permute-start | bytes 3145736 | tf_op jit(solution)/shard_map/ppermute | solution.py:119
  70.2 5.3 %copy-start.19 = (bf16[1936,256]{1,0:T(8,128)(2,1)}, bf16[1936,256]{1,0:T(8,128)(2,1)S(1)}, u32[]{:S(2)}) copy-start(bf16[1936,256]{1,0:T(8,128)(2,1)S(1)} %collective-permute-done.5.north_any.refs_7_) | copy-start | bytes 2973700
  70.3 34.9 %collective-permute-start.6 = (bf16[320,256]{1,0:T(8,128)(2,1)S(1)}, bf16[320,256]{1,0:T(8,128)(2,1)S(1)}, u32[]{:S(2)}, u32[]{:S(2)}) collective-permute-start(bf16[320,256]{1,0:T(8,128)(2,1)S(1)} %pad_maximum_fusion.3), channel_id=1, source_target_pairs={{0,16},{4,20},{8,24},{12,28},{16,0},{20,4},{24,8},{28,12},{1,17},{... | collective-permute-start | bytes 491528 | tf_op jit(solution)/shard_map/ppermute | solution.py:832
  105.2 12.8 %collective-permute-start.7 = (bf16[640,256]{1,0:T(8,128)(2,1)S(1)}, bf16[640,256]{1,0:T(8,128)(2,1)S(1)}, u32[]{:S(2)}, u32[]{:S(2)}) collective-permute-start(bf16[640,256]{1,0:T(8,128)(2,1)S(1)} %pad_maximum_fusion.2), channel_id=1, source_target_pairs={{0,8},{4,12},{8,0},{12,4},{16,24},{20,28},{24,16},{28,20},{1,9},{5... | collective-permute-start | bytes 983048 | tf_op jit(solution)/shard_map/ppermute | solution.py:832
  117.9 1.7 %copy-start.9 = (bf16[4,2,256,256]{3,2,1,0:T(8,128)(2,1)}, bf16[4,2,256,256]{3,2,1,0:T(8,128)(2,1)S(1)}, u32[]{:S(2)}) copy-start(bf16[4,2,256,256]{3,2,1,0:T(8,128)(2,1)S(1)} %collective-permute-done.8) | copy-start | bytes 3145732
  117.9 1.7 %copy-start.10 = (bf16[4,2,256,256]{3,2,1,0:T(8,128)(2,1)}, bf16[4,2,256,256]{3,2,1,0:T(8,128)(2,1)S(1)}, u32[]{:S(2)}) copy-start(bf16[4,2,256,256]{3,2,1,0:T(8,128)(2,1)S(1)} %collective-permute-done.9) | copy-start | bytes 3145732
  118.9 19.6 %collective-permute-start.13 = (bf16[1280,256]{1,0:T(8,128)(2,1)}, bf16[1280,256]{1,0:T(8,128)(2,1)S(1)}, u32[]{:S(2)}, u32[]{:S(2)}) collective-permute-start(bf16[1280,256]{1,0:T(8,128)(2,1)} %get-tuple-element.77), channel_id=1, source_target_pairs={{0,2},{1,3},{2,0},{3,1},{4,6},{5,7},{6,4},{7,5},{8,10},{9,11},{10,... | collective-permute-start | bytes 1966088 | tf_op jit(solution)/shard_map/ppermute | solution.py:832
  119.8 27.0 %collective-permute-start.12 = (bf16[2,2,2,256,256]{4,3,2,1,0:T(8,128)(2,1)S(1)}, bf16[2,2,2,256,256]{4,3,2,1,0:T(8,128)(2,1)S(1)}, u32[]{:S(2)}, u32[]{:S(2)}) collective-permute-start(bf16[2,2,2,256,256]{4,3,2,1,0:T(8,128)(2,1)S(1)} %pad_maximum_fusion.1), channel_id=1, source_target_pairs={{1,0},{2,1},{3,2},{5,4},{6,5},{7,6},{9,8},{10,9},{11,10},{13,12},{... | collective-permute-start | bytes 3145736 | tf_op jit(solution)/shard_map/ppermute | solution.py:119
  123.4 23.4 %collective-permute-start.11 = (bf16[2,2,2,256,256]{4,3,2,1,0:T(8,128)(2,1)S(1)}, bf16[2,2,2,256,256]{4,3,2,1,0:T(8,128)(2,1)S(1)}, u32[]{:S(2)}, u32[]{:S(2)}) collective-permute-start(bf16[2,2,2,256,256]{4,3,2,1,0:T(8,128)(2,1)S(1)} %pad_maximum_fusion), channel_id=1, source_target_pairs={{0,1},{1,2},{2,3},{4,5},{5,6},{6,7},{8,9},{9,10},{10,11},{12,13},{... | collective-permute-start | bytes 3145736 | tf_op jit(solution)/shard_map/ppermute | solution.py:119
  146.9 1.6 copy-start.11
  (3 other events, 3.5 us)

commit v5 on v4

--- a/solution.py
+++ b/solution.py
@@ -423,7 +423,7 @@
     )(meta, gathered, jnp.asarray(window_coupling(2)), jnp.asarray(window_coupling(3)), tree, sum0, sum1)
 
 
-def join_body(north_ref, south_ref, west_ref, east_ref, to_north, to_south, sems):
+def join_body(north_ref, south_ref, west_ref, east_ref, north_any, south_any, to_north, to_south, sems):
     copies = []
 
     def move(source, at, to, row, count):
@@ -436,8 +436,14 @@
         for side, base in ((west_ref, SIDEWAYS), (east_ref, SIDEWAYS + CORNER)):
             move(side, 4 * RANK * lower, to, base, 4 * RANK)
             move(side, 8 * RANK, to, base + 4 * RANK, CORNER - 4 * RANK)
-    for copy in copies:
-        copy.wait()
+    backs = []
+    for k, (held, to) in enumerate(((to_north, north_any), (to_south, south_any))):
+        for copy in copies[5 * k : 5 * k + 5]:
+            copy.wait()
+        backs.append(pltpu.make_async_copy(held, to, sems.at[10 + k]))
+        backs[-1].start()
+    for back in backs:
+        back.wait()
 
 
 def join(north, south, west, east):
@@ -447,8 +453,9 @@
         join_body,
         out_shape=(message, message),
         in_specs=[anywhere] * 4,
-        out_specs=[pl.BlockSpec(memory_space=pltpu.VMEM)] * 2,
-        scratch_shapes=[pltpu.SemaphoreType.DMA((10,))],
+        out_specs=[anywhere] * 2,
+        scratch_shapes=[pltpu.VMEM(message.shape, BF)] * 2 + [pltpu.SemaphoreType.DMA((12,))],
+        compiler_params=pltpu.CompilerParams(vmem_limit_bytes=BIG),
         cost_estimate=pl.CostEstimate(flops=0, bytes_accessed=4_000_000, transcendentals=0),
         name="join",
     )(north, south, west, east)
@@ -491,9 +498,9 @@
     spread_columns(rows, columns.at[leaf])
 
 
-def own_pairs(first):
+def own_pairs(first, last):
     pairs = []
-    for r in (first, first + 1):
+    for r in range(first, last):
         for c in range(SIDE):
             for dy, dx in ((0, 1), (1, -1), (1, 0), (1, 1)):
                 if r + dy < SIDE and 0 <= c + dx < SIDE:
@@ -501,21 +508,22 @@
     return pairs
 
 
-def near_own_body(first, table_ref, q_any, pos_ref, noise_ref, *refs):
-    before_any, out_ref, columns, blocks, q_ref, before_ref, sems = (None,) * (7 - len(refs)) + refs
+def near_own_body(first, last, table_ref, q_any, pos_ref, noise_ref, *refs):
+    before_any, out_any, columns, blocks, q_ref, before_ref, out_ref, sems = (None,) * (8 - len(refs)) + refs
     loads = [pltpu.make_async_copy(q_any, q_ref, sems.at[0])]
     if first:
-        loads.append(pltpu.make_async_copy(before_any.at[pl.ds(8, SIDE)], before_ref, sems.at[1]))
+        loads.append(pltpu.make_async_copy(before_any.at[pl.ds(SIDE, SIDE)], before_ref, sems.at[1]))
     for load in loads:
         load.start()
-    pairs = own_pairs(first)
+    pairs = own_pairs(first, last)
     start = first * SIDE
+    count = (last - first) * SIDE
 
     def turn(leaf, carry):
         turn_points(columns, leaf, pos_ref[leaf], noise_ref[leaf])
         return carry
 
-    lax.fori_loop(start, start + 8, turn, 0)
+    lax.fori_loop(start, start + count, turn, 0)
     zero = jnp.int32(0)
 
     def selves(i, carry):
@@ -524,62 +532,72 @@
             block_into(blocks.at[2 * i + half], columns.at[leaf], pos_ref[leaf], zero, zero)
         return carry
 
-    lax.fori_loop(0, 4, selves, 0)
+    lax.fori_loop(0, count // 2, selves, 0)
+
+    def pair(i):
+        at = 4 * i
+        place = count + 2 * i
+        target, source = table_ref[at], table_ref[at + 1]
+        block_into(blocks.at[place], columns.at[target], pos_ref[source], table_ref[at + 2], table_ref[at + 3])
+        blocks[place + 1] = blocks[place].T
 
     def both(i, carry):
-        for half in range(2):
-            at = 8 * i + 4 * half
-            place = 8 + 4 * i + 2 * half
-            target, source = table_ref[at], table_ref[at + 1]
-            block_into(
-                blocks.at[place], columns.at[target], pos_ref[source], table_ref[at + 2], table_ref[at + 3]
-            )
-            blocks[place + 1] = blocks[place].T
+        pair(2 * i)
+        pair(2 * i + 1)
         return carry
 
     lax.fori_loop(0, len(pairs) // 2, both, 0)
+    if len(pairs) % 2:
+        pair(len(pairs) - 1)
     for load in loads:
         load.wait()
-    parts = {leaf: [(leaf - start, leaf)] for leaf in range(start, start + 8)}
+    parts = {leaf: [(leaf - start, leaf)] for leaf in range(start, start + count)}
     for i, (target, source, _, _) in enumerate(pairs):
-        parts[target].append((8 + 2 * i, source))
-        parts.setdefault(source, []).append((9 + 2 * i, target))
+        parts[target].append((count + 2 * i, source))
+        parts.setdefault(source, []).append((count + 1 + 2 * i, target))
+    backs = []
     for leaf, terms in sorted(parts.items()):
         total = None
         for place, source in terms:
             part = dot(blocks[place], q_ref[source])
             total = part if total is None else total + part
-        if leaf < start + 8:
+        if leaf < start + count:
             noise = jnp.concatenate([columns[leaf, :, 256:384]] * 2, axis=1)
             total = total + noise * q_ref[leaf].astype(F32)
         if first and leaf < start + SIDE:
             total = total + before_ref[leaf - start]
         out_ref[leaf - start] = total
-
-
-def near_own(first, q, points, noise, after, before):
+        backs.append(pltpu.make_async_copy(out_ref.at[leaf - start], out_any.at[leaf - start], sems.at[2 + leaf - start]))
+        backs[-1].start()
+    for back in backs:
+        back.wait()
+
+
+def near_own(first, last, q, points, noise, after, before):
     vmem = pl.BlockSpec(memory_space=pltpu.VMEM)
     smem = pl.BlockSpec(memory_space=pltpu.SMEM)
     anywhere = pl.BlockSpec(memory_space=pl.ANY)
-    pairs = own_pairs(first)
+    pairs = own_pairs(first, last)
+    leaves = (min(last + 1, SIDE) - first) * SIDE
 
     def body(after_ref, *refs):
-        near_own_body(first, *refs)
+        near_own_body(first, last, *refs)
 
     return pl.pallas_call(
         body,
-        out_shape=jax.ShapeDtypeStruct((12 if first == 0 else 8, LEAF, LEAF), F32),
+        out_shape=jax.ShapeDtypeStruct((leaves, LEAF, LEAF), F32),
         in_specs=[anywhere, smem, anywhere, vmem, vmem] + [anywhere] * len(before),
-        out_specs=vmem,
+        out_specs=anywhere,
         scratch_shapes=[
             pltpu.VMEM((LEAVES, LEAF, 384), F32),
-            pltpu.VMEM((8 + 2 * len(pairs), LEAF, LEAF), BF),
+            pltpu.VMEM(((last - first) * SIDE + 2 * len(pairs), LEAF, LEAF), BF),
             pltpu.VMEM((LEAVES, LEAF, LEAF), BF),
             pltpu.VMEM((SIDE, LEAF, LEAF), F32),
-            pltpu.SemaphoreType.DMA((2,)),
+            pltpu.VMEM((leaves, LEAF, LEAF), F32),
+            pltpu.SemaphoreType.DMA((2 + leaves,)),
         ],
-        compiler_params=pltpu.CompilerParams(vmem_limit_bytes=40 << 20),
-        cost_estimate=pl.CostEstimate(flops=10_000_000_000, bytes_accessed=4_000_000, transcendentals=8_000_000),
+        compiler_params=pltpu.CompilerParams(vmem_limit_bytes=BIG),
+        cost_estimate=pl.CostEstimate(flops=6_000_000_000, bytes_accessed=4_000_000, transcendentals=8_000_000),
         name="near_own",
     )(after, jnp.asarray(np.array(pairs, np.int32).reshape(-1)), q, points, noise, *before)
 
@@ -702,7 +720,7 @@
 
 def final_body(
     list_ref, slot_ref, q_any, west_any, east_any, north_any, north_corner_any, south_any, south_corner_any,
-    upper_blocks_any, lower_blocks_any, upper_any, lower_any, basis_ref, field_ref, out_any, held, blocks, sums, outs, sems,
+    upper_blocks_any, lower_blocks_any, row0_any, row1_any, row2_any, basis_ref, field_ref, out_any, held, blocks, sums, outs, sems,
 ):
     firsts = [min(at for at in range(EDGES) if ITEMS[at][0] // SIDE == r) for r in range(SIDE)] + [EDGES]
     stages = [[], [], [], []]
@@ -713,27 +731,35 @@
         made = pltpu.make_async_copy(source, to, sems.at[count])
         count += 1
         stages[stage].append(made)
-        made.start()
 
     for r in range(SIDE):
         if r == 0:
-            for source, at in ((north_any, 32), (north_corner_any, 40), (west_any, 16), (east_any, 24)):
+            for source, at in ((north_any, 32), (north_corner_any, 40)):
                 copy(r, source, held.at[pl.ds(at, 8)])
+        for source, at in ((west_any, 16), (east_any, 24)):
+            for low, high in {0: ((0, 4),), 1: ((4, 6),), 2: ((6, 8),)}.get(r, ()):
+                copy(r, source.at[pl.ds(low, high - low)], held.at[pl.ds(at + low, high - low)])
         if r == SIDE - 1:
             for source, at in ((south_any, 48), (south_corner_any, 56)):
                 copy(r, source, held.at[pl.ds(at, 8)])
         part = pl.ds(firsts[r], firsts[r + 1] - firsts[r])
         source, back = (upper_blocks_any, 0) if r < 2 else (lower_blocks_any, EDGES // 2)
         copy(r, source.at[pl.ds(firsts[r] - back, firsts[r + 1] - firsts[r])], blocks.at[part])
-        source = upper_any.at[pl.ds(SIDE * r, SIDE)] if r < 2 else lower_any.at[pl.ds(SIDE * (r - 2), SIDE)]
+        source = (row0_any, row1_any, row2_any, row2_any)[r].at[pl.ds(SIDE if r == 3 else 0, SIDE)]
         copy(r, source, sums.at[pl.ds(SIDE * r, SIDE)])
     copy(SIDE - 1, q_any, held.at[pl.ds(0, 16)])
     for half_at, source in enumerate((upper_blocks_any, lower_blocks_any)):
         copy(SIDE - 1, source.at[pl.ds(EDGES // 2, 8)], blocks.at[pl.ds(EDGES + 8 * half_at, 8)])
+    for r in range(2):
+        for made in stages[r]:
+            made.start()
     for leaf in range(LEAVES):
         if leaf % SIDE == 0:
             for made in stages[leaf // SIDE]:
                 made.wait()
+            if leaf // SIDE + 2 < SIDE:
+                for made in stages[leaf // SIDE + 2]:
+                    made.start()
         total = dot_first(basis_ref[leaf], field_ref[leaf])
         for at in range(EDGES):
             if ITEMS[at][0] == leaf:
@@ -766,7 +792,7 @@
         back.wait()
 
 
-def finish(near_list, q, halos, upper_blocks, lower_blocks, upper, lower, basis, field):
+def finish(near_list, q, halos, upper_blocks, lower_blocks, sums, basis, field):
     vmem = pl.BlockSpec(memory_space=pltpu.VMEM)
     smem = pl.BlockSpec(memory_space=pltpu.SMEM)
     anywhere = pl.BlockSpec(memory_space=pl.ANY)
@@ -774,19 +800,19 @@
     return pl.pallas_call(
         final_body,
         out_shape=jax.ShapeDtypeStruct((LEAVES, LEAF, LEAF), BF),
-        in_specs=[smem, smem] + [anywhere] * 11 + [vmem, vmem],
+        in_specs=[smem, smem] + [anywhere] * 12 + [vmem, vmem],
         out_specs=anywhere,
         scratch_shapes=[
             pltpu.VMEM((64, LEAF, LEAF), BF),
             pltpu.VMEM((EDGES + LEAVES, LEAF, LEAF), BF),
             pltpu.VMEM((LEAVES, LEAF, LEAF), F32),
             pltpu.VMEM((LEAVES, LEAF, LEAF), BF),
-            pltpu.SemaphoreType.DMA((21,)),
+            pltpu.SemaphoreType.DMA((26,)),
         ],
         compiler_params=pltpu.CompilerParams(vmem_limit_bytes=BIG),
         cost_estimate=pl.CostEstimate(flops=4_000_000_000, bytes_accessed=24_000_000, transcendentals=0),
         name="finish",
-    )(near_list, jnp.asarray(SLOT_OF), q, *halos, upper_blocks, lower_blocks, upper, lower, basis, field)
+    )(near_list, jnp.asarray(SLOT_OF), q, *halos, upper_blocks, lower_blocks, *sums, basis, field)
 
 
 def window_slots(wide, narrow, steps):
@@ -836,30 +862,33 @@
 
     gathered = give
     other = step(gathered, 0)
-    upper = near_own(0, q, points, noise_rows, give, [])
+    row0 = near_own(0, 1, q, points, noise_rows, give, [])
+    other, row0 = tie(other, row0)
+    gathered = jnp.concatenate([gathered, other], axis=0)
+    other = step(gathered, 1)
+    row1 = near_own(1, 2, q, points, noise_rows, gathered, [row0])
     to_east, to_west = charges[:, 2:4], charges[:, 0:2]
-    other, from_west, from_east, upper, to_east, to_west = tie(other, from_west, from_east, upper, to_east, to_west)
+    other, from_west, from_east, row1, to_east, to_west = tie(other, from_west, from_east, row1, to_east, to_west)
+    gathered = jnp.concatenate([gathered, other], axis=0)
+    other = step(gathered, 2)
     to_north, to_south = join(north, south, from_west, from_east)
     from_south = shift(to_north, "narrow", -1)
     from_north = shift(to_south, "narrow", 1)
     q_west = shift(to_east, "wide", 1)
     q_east = shift(to_west, "wide", -1)
+    row2 = near_own(2, 4, q, points, noise_rows, to_north, [row1])
+    other, from_south, from_north, row2 = tie(other, from_south, from_north, row2)
     gathered = jnp.concatenate([gathered, other], axis=0)
-    other = step(gathered, 1)
-    lower = near_own(2, q, points, noise_rows, to_north, [upper])
-    other, from_south, from_north, lower = tie(other, from_south, from_north, lower)
-    for at in range(2, len(steps)):
+    other = step(gathered, 3)
+    sums = local_far(listing, coefs, from_west, from_east, from_north, from_south)
+    upper_blocks = edge_blocks(0, listing, sums[1], points, from_west, from_east, from_north, from_south)
+    other, upper_blocks, q_west, q_east = tie(other, upper_blocks, q_west, q_east)
+    for at in range(4, len(steps)):
         gathered = jnp.concatenate([gathered, other], axis=0)
         other = step(gathered, at)
-        if at == 2:
-            sums = local_far(listing, coefs, from_west, from_east, from_north, from_south)
-            other, *sums = tie(other, *sums)
-        if at == 3:
-            upper_blocks = edge_blocks(0, listing, sums[1], points, from_west, from_east, from_north, from_south)
-            other, upper_blocks, q_west, q_east = tie(other, upper_blocks, q_west, q_east)
+        if at == 4:
             q_north_corner = shift(jnp.stack([q_west[2:4], q_east[2:4]]), "narrow", 1)
             q_south_corner = shift(jnp.stack([q_west[0:2], q_east[0:2]]), "narrow", -1)
-        if at == 4:
             lower_blocks = edge_blocks(1, listing, upper_blocks, points, from_west, from_east, from_north, from_south)
             other, lower_blocks = tie(other, lower_blocks)
     gathered = jnp.concatenate([gathered, other], axis=0)
@@ -869,7 +898,7 @@
         value.reshape(8, LEAF, LEAF)
         for value in (q_west, q_east, q_north, q_north_corner, q_south, q_south_corner)
     ]
-    out = finish(listing, q, halos, upper_blocks, lower_blocks, upper, lower, basis, field)
+    out = finish(listing, q, halos, upper_blocks, lower_blocks, (row0, row1, row2), basis, field)
     return out.reshape(SIDE, SIDE, LEAF, LEAF)
 
 

time: 163 us -> 163 us (level); the launches traced: 162 us -> 160 us
  Pallas kernels: 86.4 us -> 91.1 us
  local copies, waits for them, and re-layouts: 16.3 us -> 12.7 us
  waiting for transfers between devices: 21.2 us -> 18.1 us
    ppermute x5, waiting for transfers between devices: 21.1 us -> 0.01 us  [step(): lax.ppermute(value, axis, [(i, i ^ bit) for i in range(lax.axis_size(axis...]
    ppermute x10, waiting for transfers between devices: 0.03 us -> 18.1 us  [shift(): lax.ppermute(value, axis, [(i, i + steps) for i in range(count) if 0 <= i...]
    unnamed x44 -> x32, local copies, waits for them, and re-layouts: 10.6 us -> 5.35 us
    pallas_call x2 -> x3, Pallas kernels: 26.4 us -> 30.3 us  [near_own(): pl.pallas_call(body, out_shape=jax.ShapeDtypeStruct((leaves, LEAF, LEAF),...]
    ppermute x5, starting transfers between devices: 8.09 us -> 11.2 us  [step(): lax.ppermute(value, axis, [(i, i ^ bit) for i in range(lax.axis_size(axis...]
    ppermute x10, starting transfers between devices: 28.3 us -> 25.4 us  [shift(): lax.ppermute(value, axis, [(i, i + steps) for i in range(count) if 0 <= i...]
  transfers between devices with their start and end apart: 15 -> 15, of which waited for: 1 -> 1; matrix products, arithmetic and copies ran while one was open for 6% -> 7% of each run, Pallas kernels for 42% -> 45%
where the time goes in v5:
time: 163 us; the launch traced here: 160 us
  Pallas kernels  91.1 us (56%)
  starting transfers between devices  36.6 us (22%)
  waiting for transfers between devices  18.1 us (11%)
  local copies, waits for them, and re-layouts  12.7 us (8%)
    pallas_call x3, Pallas kernels, near_own(): pl.pallas_call(body, out_shape=jax.ShapeDtypeStruct((leaves, LEAF, LEAF),...  30.3 us
    ppermute x10, starting transfers between devices, shift(): lax.ppermute(value, axis, [(i, i + steps) for i in range(count) if 0 <= i...  25.4 us
    pallas_call x2, Pallas kernels, edge_blocks(): pl.pallas_call(body, out_shape=jax.ShapeDtypeStruct((EDGES // 2 + 8, LEAF...  23.9 us
    ppermute x10, waiting for transfers between devices, shift(): lax.ppermute(value, axis, [(i, i + steps) for i in range(count) if 0 <= i...  18.1 us
    pallas_call x1, Pallas kernels, finish(): pl.pallas_call(final_body, out_shape=jax.ShapeDtypeStruct((LEAVES, LEAF,...  14.2 us
    ppermute x5, starting transfers between devices, step(): lax.ppermute(value, axis, [(i, i ^ bit) for i in range(lax.axis_size(axis...  11.2 us
    pallas_call x1, Pallas kernels, local_far(): pl.pallas_call(local_body, out_shape=(jax.ShapeDtypeStruct((LEAVES, RANK,...  7.88 us
    pallas_call x1, Pallas kernels, top_far(): pl.pallas_call(top_body, out_shape=jax.ShapeDtypeStruct((LEAVES, RANK, LE...  7.39 us
  transfers between devices with their start and end apart: 15, of which 1 were waited for; matrix products, arithmetic and copies ran while one was open for 7% of the time, Pallas kernels for 45%

profile of v5, /device:TPU:1, one launch (start us, length us, event | category | flops | bytes accessed | tf_op | source)
XLA Modules:
  0.0 159.9 jit_solution(14341891865654551563)
XLA Ops:
  0.0 4.9 %upward.1 = (bf16[816,256]{1,0:T(8,128)(2,1)}, bf16[816,256]{1,0:T(8,128)(2,1)}, bf16[816,256]{1,0:T(8,128)(2,1)}, bf16[816,256]{1,0:T(8,128)(2,1)}, bf16[1280,256]{1,0:T(8,128)(2,1)}, /*index=5*/bf16[80,256]{1,0:T(8,128)(2,1)}) custom-call(bf16[16,256,256]{2,1,0:T(8,128)(2,1)} %bitcast.21, bf16[16,64,256]{2,1,0:T(8,128)(2,1)} %bitcast.28, ...), custom_call_target="tpu_custom_call" | custom-call | flops 300000000 | bytes 5000000 | tf_op jit(solution)/shard_map/upward/pallas_call | solution.py:194
  4.9 2.1 %collective-permute-start = (bf16[80,256]{1,0:T(8,128)(2,1)}, bf16[80,256]{1,0:T(8,128)(2,1)S(1)}, u32[]{:S(2)}, u32[]{:S(2)}) collective-permute-start(bf16[80,256]{1,0:T(8,128)(2,1)} %get-tuple-element.36.after_ref), channel_id=1, source_target_pairs={{0,4},{4,0},{8,12},{12,8},{16,20},{20,16},{24,28},{28,24},{1,5},{5... | collective-permute-start | bytes 122888 | tf_op jit(solution)/shard_map/ppermute | solution.py:858
  7.0 2.7 %collective-permute-start.2 = (bf16[816,256]{1,0:T(8,128)(2,1)}, bf16[816,256]{1,0:T(8,128)(2,1)}, u32[]{:S(2)}, u32[]{:S(2)}) collective-permute-start(bf16[816,256]{1,0:T(8,128)(2,1)} %get-tuple-element.38), channel_id=1, source_target_pairs={{0,4},{4,8},{8,12},{12,16},{16,20},{20,24},{24,28},{1,5},{5,9},{9,... | collective-permute-start | bytes 1253384 | tf_op jit(solution)/shard_map/ppermute | solution.py:119
  9.7 1.3 collective-permute-start.3
  11.0 1.4 fusion.2
  12.4 2.8 %collective-permute-start.14 = (bf16[2,4,256,256]{3,2,1,0:T(8,128)(2,1)}, bf16[2,4,256,256]{3,2,1,0:T(8,128)(2,1)S(1)}, u32[]{:S(2)}, u32[]{:S(2)}) collective-permute-start(bf16[2,4,256,256]{3,2,1,0:T(8,128)(2,1)} %get-tuple-element.67), channel_id=1, source_target_pairs={{1,0},{2,1},{3,2},{5,4},{6,5},{7,6},{9,8},{10,9},{11,10},{13,12},{... | collective-permute-start | bytes 3145736 | tf_op jit(solution)/shard_map/ppermute | solution.py:119
  15.3 3.6 %collective-permute-start.10 = (bf16[2,4,256,256]{3,2,1,0:T(8,128)(2,1)}, bf16[2,4,256,256]{3,2,1,0:T(8,128)(2,1)}, u32[]{:S(2)}, u32[]{:S(2)}) collective-permute-start(bf16[2,4,256,256]{3,2,1,0:T(8,128)(2,1)} %get-tuple-element.68), channel_id=1, source_target_pairs={{0,1},{1,2},{2,3},{4,5},{5,6},{6,7},{8,9},{9,10},{10,11},{12,13},{... | collective-permute-start | bytes 3145736 | tf_op jit(solution)/shard_map/ppermute | solution.py:119
  18.9 1.5 fusion.3
  21.0 9.0 %near_own.3.refs_4_.row0_any = f32[8,256,256]{2,1,0:T(8,128)} custom-call(bf16[80,256]{1,0:T(8,128)(2,1)} %get-tuple-element.36.after_ref, s32[52]{0:T(128)} %constant.201.clone.refs_0_, bf16[16,256,256]{2,1,0:T(8,128)(2,1)} %bitcast.22, f32[16,2,256]{2,1,0:T(2,128)} %bitcast.36, f32[16,1,256]{2,1,0:T(1,128)} %reshape.40.refs_3_), custom_call_target="tpu_custom_call" | custom-call | flops 6000000000 | bytes 4000000 | tf_op jit(solution)/shard_map/near_own/pallas_call | solution.py:586
  31.9 9.0 %near_own.4.refs_4_.row1_any = f32[8,256,256]{2,1,0:T(8,128)} custom-call(bf16[160,256]{1,0:T(8,128)(2,1)} %copy-done.9, s32[52]{0:T(128)} %constant.202.clone.refs_0_, bf16[16,256,256]{2,1,0:T(8,128)(2,1)} %bitcast.23, f32[16,2,256]{2,1,0:T(2,128)} %bitcast.37, f32[16,1,256]{2,1,0:T(1,128)} %reshape.40.refs_3_, f32[8,256,256]{2,1,0:T(8,128)} %near_own.3.refs_4_.row0_any), custom_call_target="tpu_custom_call" | custom-call | flops 6000000000 | bytes 4000000 | tf_op jit(solution)/shard_map/near_own/pallas_call | solution.py:586
  40.9 2.6 %join.1 = (bf16[1936,256]{1,0:T(8,128)(2,1)}, bf16[1936,256]{1,0:T(8,128)(2,1)}) custom-call(bf16[816,256]{1,0:T(8,128)(2,1)} %get-tuple-element.42.north_ref, bf16[816,256]{1,0:T(8,128)(2,1)} %get-tuple-element.43.south_ref, bf16[816,256]{1,0:T(8,128)(2,1)} %collective-permute-done.2.west_ref.west_any.refs_5_, ...), custom_call_target="tpu_custom_call" | custom-call | bytes 4000000 | tf_op jit(solution)/shard_map/join/pallas_call | solution.py:452
  43.6 1.9 %collective-permute-start.5 = (bf16[1936,256]{1,0:T(8,128)(2,1)}, bf16[1936,256]{1,0:T(8,128)(2,1)}, u32[]{:S(2)}, u32[]{:S(2)}) collective-permute-start(bf16[1936,256]{1,0:T(8,128)(2,1)} %get-tuple-element.46.after_ref), channel_id=1, source_target_pairs={{1,0},{2,1},{3,2},{5,4},{6,5},{7,6},{9,8},{10,9},{11,10},{13,12},{... | collective-permute-start | bytes 2973704 | tf_op jit(solution)/shard_map/ppermute | solution.py:119
  45.5 3.6 %collective-permute-start.6 = (bf16[1936,256]{1,0:T(8,128)(2,1)}, bf16[1936,256]{1,0:T(8,128)(2,1)}, u32[]{:S(2)}, u32[]{:S(2)}) collective-permute-start(bf16[1936,256]{1,0:T(8,128)(2,1)} %get-tuple-element.47), channel_id=1, source_target_pairs={{0,1},{1,2},{2,3},{4,5},{5,6},{6,7},{8,9},{9,10},{10,11},{12,13},{... | collective-permute-start | bytes 2973704 | tf_op jit(solution)/shard_map/ppermute | solution.py:119
  49.2 0.7 reshape.36.list_ref.refs_0_
  50.5 4.6 %collective-permute-start.4 = (bf16[320,256]{1,0:T(8,128)(2,1)S(1)}, bf16[320,256]{1,0:T(8,128)(2,1)S(1)}, u32[]{:S(2)}, u32[]{:S(2)}) collective-permute-start(bf16[320,256]{1,0:T(8,128)(2,1)S(1)} %pad_maximum_fusion.3), channel_id=1, source_target_pairs={{0,16},{4,20},{8,24},{12,28},{16,0},{20,4},{24,8},{28,12},{1,17},{... | collective-permute-start | bytes 491528 | tf_op jit(solution)/shard_map/ppermute | solution.py:858
  55.2 12.4 %near_own.5.row2_any = f32[8,256,256]{2,1,0:T(8,128)} custom-call(bf16[1936,256]{1,0:T(8,128)(2,1)} %get-tuple-element.46.after_ref, s32[64]{0:T(128)} %constant.203.clone.refs_0_, bf16[16,256,256]{2,1,0:T(8,128)(2,1)} %bitcast.24, f32[16,2,256]{2,1,0:T(2,128)} %bitcast.38, f32[16,1,256]{2,1,0:T(1,128)} %reshape.40.refs_3_, ...), custom_call_target="tpu_custom_call" | custom-call | flops 6000000000 | bytes 4000000 | tf_op jit(solution)/shard_map/near_own/pallas_call | solution.py:586
  67.5 0.7 constant_dynamic-update-slice_fusion.4
  68.2 1.8 %collective-permute-start.8 = (bf16[4,2,256,256]{3,2,1,0:T(8,128)(2,1)S(1)}, bf16[4,2,256,256]{3,2,1,0:T(8,128)(2,1)S(1)}, u32[]{:S(2)}, u32[]{:S(2)}) collective-permute-start(bf16[4,2,256,256]{3,2,1,0:T(8,128)(2,1)S(1)} %copy-done.7), channel_id=1, source_target_pairs={{0,4},{4,8},{8,12},{12,16},{16,20},{20,24},{24,28},{1,5},{5,9},{9,... | collective-permute-start | bytes 3145736 | tf_op jit(solution)/shard_map/ppermute | solution.py:119
  70.1 1.5 collective-permute-start.9
  71.6 4.4 %collective-permute-start.7 = (bf16[640,256]{1,0:T(8,128)(2,1)S(1)}, bf16[640,256]{1,0:T(8,128)(2,1)S(1)}, u32[]{:S(2)}, u32[]{:S(2)}) collective-permute-start(bf16[640,256]{1,0:T(8,128)(2,1)S(1)} %pad_maximum_fusion.2), channel_id=1, source_target_pairs={{0,8},{4,12},{8,0},{12,4},{16,24},{20,28},{24,16},{28,20},{1,9},{5... | collective-permute-start | bytes 983048 | tf_op jit(solution)/shard_map/ppermute | solution.py:858
  76.0 7.9 %local_far.1 = (f32[16,64,256]{2,1,0:T(8,128)}, f32[256,256]{1,0:T(8,128)}) custom-call(s32[160]{0:T(256)} %reshape.36.list_ref.refs_0_, bf16[1280,256]{1,0:T(8,128)(2,1)} %get-tuple-element.50.coef_any, bf16[816,256]{1,0:T(8,128)(2,1)} %collective-permute-done.2.west_ref.west_any.refs_5_, bf16[816,256]{1,0:T(8,128)(2,1)} %collective-permute-done.3.east_ref.east_any.refs_6_, ...), custom_call_target="tpu_custom_call" | custom-call | flops 5000000000 | bytes 8000000 | tf_op jit(solution)/shard_map/local_far/pallas_call | solution.py:292
  83.9 11.9 %edge_blocks.2.refs_3_.upper_blocks_any = bf16[30,256,256]{2,1,0:T(8,128)(2,1)} custom-call(s32[160]{0:T(256)} %reshape.36.list_ref.refs_0_, s32[88]{0:T(128)} %constant.207.clone.refs_1_, s32[64]{0:T(128)} %constant.208.clone.refs_2_.slot_ref, f32[256,256]{1,0:T(8,128)} %get-tuple-element.53.refs_3_.sum1_any, f32[16,2,256]{2,1,0:T(2,128)} %bitcast.39, ...), custom_call_target="tpu_custom_call" | custom-call | flops 6000000000 | bytes 8000000 | tf_op jit(solution)/shard_map/edge_blocks/pallas_call | solution.py:700
  95.8 0.7 constant_dynamic-update-slice_fusion.3
  96.6 18.1 %collective-permute-done.8 = bf16[4,2,256,256]{3,2,1,0:T(8,128)(2,1)S(1)} collective-permute-done((bf16[4,2,256,256]{3,2,1,0:T(8,128)(2,1)S(1)}, bf16[4,2,256,256]{3,2,1,0:T(8,128)(2,1)S(1)}, u32[]{:S(2)}, u32[]{:S(2)}) %collective-permute-start.8) | collective-permute-done | bytes 1048608 | tf_op jit(solution)/shard_map/ppermute | solution.py:119
  114.7 1.0 constant_dynamic-update-slice_fusion.2
  116.3 3.1 %collective-permute-start.12 = (bf16[2,2,2,256,256]{4,3,2,1,0:T(8,128)(2,1)S(1)}, bf16[2,2,2,256,256]{4,3,2,1,0:T(8,128)(2,1)S(1)}, u32[]{:S(2)}, u32[]{:S(2)}) collective-permute-start(bf16[2,2,2,256,256]{4,3,2,1,0:T(8,128)(2,1)S(1)} %pad_maximum_fusion.1), channel_id=1, source_target_pairs={{1,0},{2,1},{3,2},{5,4},{6,5},{7,6},{9,8},{10,9},{11,10},{13,12},{... | collective-permute-start | bytes 3145736 | tf_op jit(solution)/shard_map/ppermute | solution.py:119
  119.4 3.2 %collective-permute-start.11 = (bf16[2,2,2,256,256]{4,3,2,1,0:T(8,128)(2,1)S(1)}, bf16[2,2,2,256,256]{4,3,2,1,0:T(8,128)(2,1)S(1)}, u32[]{:S(2)}, u32[]{:S(2)}) collective-permute-start(bf16[2,2,2,256,256]{4,3,2,1,0:T(8,128)(2,1)S(1)} %pad_maximum_fusion), channel_id=1, source_target_pairs={{0,1},{1,2},{2,3},{4,5},{5,6},{6,7},{8,9},{9,10},{10,11},{12,13},{... | collective-permute-start | bytes 3145736 | tf_op jit(solution)/shard_map/ppermute | solution.py:119
  122.6 12.0 %edge_blocks.3.lower_blocks_any = bf16[30,256,256]{2,1,0:T(8,128)(2,1)} custom-call(s32[160]{0:T(256)} %reshape.36.list_ref.refs_0_, s32[88]{0:T(128)} %constant.209.clone.refs_1_, s32[64]{0:T(128)} %constant.208.clone.refs_2_.slot_ref, bf16[30,256,256]{2,1,0:T(8,128)(2,1)} %edge_blocks.2.refs_3_.upper_blocks_any, f32[16,2,256]{2,1,0:T(2,128)} %bitcast.40, ...), custom_call_target="tpu_custom_call" | custom-call | flops 6000000000 | bytes 8000000 | tf_op jit(solution)/shard_map/edge_blocks/pallas_call | solution.py:700
  134.6 2.0 %constant_dynamic-update-slice_fusion.7.all_any = bf16[2560,256]{1,0:T(8,128)(2,1)} fusion(bf16[2560,256]{1,0:T(8,128)(2,1)} %get-tuple-element.76, bf16[1280,256]{1,0:T(8,128)(2,1)} %collective-permute-done.13), kind=kLoop, calls=%fused_computation.15 | loop fusion | bytes 1310720 | tf_op jit(solution)/shard_map/concatenate | solution.py:894
  136.6 7.4 %top_far.1.field_ref = bf16[16,64,256]{2,1,0:T(8,128)(2,1)} custom-call(s32[74]{0:T(128)} %pad_add_fusion.meta_ref, bf16[2560,256]{1,0:T(8,128)(2,1)} %constant_dynamic-update-slice_fusion.7.all_any, bf16[256,2304]{1,0:T(8,128)(2,1)} %constant.210.clone.c2_any, bf16[256,2304]{1,0:T(8,128)(2,1)} %constant.211.clone.c3_any, bf16[21,64,64]{2,1,0:T(8,128)(2,1)} %bitcast.34, ...), custom_call_target="tpu_custom_call" | custom-call | flops 3000000000 | bytes 5000000 | tf_op jit(solution)/shard_map/top_far/pallas_call | solution.py:404
  144.0 0.9 copy-done.4
  145.6 14.2 %finish.1 = bf16[16,256,256]{2,1,0:T(8,128)(2,1)} custom-call(s32[160]{0:T(256)} %reshape.36.list_ref.refs_0_, s32[64]{0:T(128)} %constant.208.clone.refs_2_.slot_ref, bf16[16,256,256]{2,1,0:T(8,128)(2,1)} %bitcast.25, bf16[8,256,256]{2,1,0:T(8,128)(2,1)} %bitcast.26, bf16[8,256,256]{2,1,0:T(8,128)(2,1)} %bitcast.27, bf16[8,256,256]{2,1,0:T(8,128)(2,1)} %bitcast.6.north_any, ...), custom_call_target="tpu_custom_call" | custom-call | flops 4000000000 | bytes 24000000 | tf_op jit(solution)/shard_map/finish/pallas_call | solution.py:800
  (53 shorter events, 4.7 us)
Async XLA Ops:
  0.0 11.0 %copy-start = (bf16[4,4,256,256]{3,2,1,0:T(8,128)(2,1)S(1)}, bf16[4,4,256,256]{3,2,1,0:T(8,128)(2,1)}, u32[]{:S(2)}) copy-start(bf16[4,4,256,256]{3,2,1,0:T(8,128)(2,1)} %param.19) | copy-start | bytes 6291460
  4.9 25.7 %collective-permute-start = (bf16[80,256]{1,0:T(8,128)(2,1)}, bf16[80,256]{1,0:T(8,128)(2,1)S(1)}, u32[]{:S(2)}, u32[]{:S(2)}) collective-permute-start(bf16[80,256]{1,0:T(8,128)(2,1)} %get-tuple-element.36.after_ref), channel_id=1, source_target_pairs={{0,4},{4,0},{8,12},{12,8},{16,20},{20,16},{24,28},{28,24},{1,5},{5... | collective-permute-start | bytes 122888 | tf_op jit(solution)/shard_map/ppermute | solution.py:858
  7.0 33.9 %collective-permute-start.2 = (bf16[816,256]{1,0:T(8,128)(2,1)}, bf16[816,256]{1,0:T(8,128)(2,1)}, u32[]{:S(2)}, u32[]{:S(2)}) collective-permute-start(bf16[816,256]{1,0:T(8,128)(2,1)} %get-tuple-element.38), channel_id=1, source_target_pairs={{0,4},{4,8},{8,12},{12,16},{16,20},{20,24},{24,28},{1,5},{5,9},{9,... | collective-permute-start | bytes 1253384 | tf_op jit(solution)/shard_map/ppermute | solution.py:119
  9.7 31.2 %collective-permute-start.3 = (bf16[816,256]{1,0:T(8,128)(2,1)}, bf16[816,256]{1,0:T(8,128)(2,1)}, u32[]{:S(2)}, u32[]{:S(2)}) collective-permute-start(bf16[816,256]{1,0:T(8,128)(2,1)} %get-tuple-element.39), channel_id=1, source_target_pairs={{4,0},{8,4},{12,8},{16,12},{20,16},{24,20},{28,24},{5,1},{9,5},{13... | collective-permute-start | bytes 1253384 | tf_op jit(solution)/shard_map/ppermute | solution.py:119
  12.4 131.6 %collective-permute-start.14 = (bf16[2,4,256,256]{3,2,1,0:T(8,128)(2,1)}, bf16[2,4,256,256]{3,2,1,0:T(8,128)(2,1)S(1)}, u32[]{:S(2)}, u32[]{:S(2)}) collective-permute-start(bf16[2,4,256,256]{3,2,1,0:T(8,128)(2,1)} %get-tuple-element.67), channel_id=1, source_target_pairs={{1,0},{2,1},{3,2},{5,4},{6,5},{7,6},{9,8},{10,9},{11,10},{13,12},{... | collective-permute-start | bytes 3145736 | tf_op jit(solution)/shard_map/ppermute | solution.py:119
  15.3 5.1 %copy-start.10 = (f32[4,4,256]{2,1,0:T(4,128)S(1)}, f32[4,4,256]{2,1,0:T(4,128)}, u32[]{:S(2)}) copy-start(f32[4,4,256]{2,1,0:T(4,128)} %param.21) | copy-start | bytes 49156
  15.3 128.7 %collective-permute-start.10 = (bf16[2,4,256,256]{3,2,1,0:T(8,128)(2,1)}, bf16[2,4,256,256]{3,2,1,0:T(8,128)(2,1)}, u32[]{:S(2)}, u32[]{:S(2)}) collective-permute-start(bf16[2,4,256,256]{3,2,1,0:T(8,128)(2,1)} %get-tuple-element.68), channel_id=1, source_target_pairs={{0,1},{1,2},{2,3},{4,5},{5,6},{6,7},{8,9},{9,10},{10,11},{12,13},{... | collective-permute-start | bytes 3145736 | tf_op jit(solution)/shard_map/ppermute | solution.py:119
  21.0 9.0 %copy-start.8 = (bf16[80,256]{1,0:T(8,128)(2,1)S(1)}, bf16[80,256]{1,0:T(8,128)(2,1)}, u32[]{:S(2)}) copy-start(bf16[80,256]{1,0:T(8,128)(2,1)} %get-tuple-element.36.after_ref) | copy-start | bytes 122884
  31.3 0.6 copy-start.9
  31.3 9.6 %collective-permute-start.1 = (bf16[160,256]{1,0:T(8,128)(2,1)S(1)}, bf16[160,256]{1,0:T(8,128)(2,1)S(1)}, u32[]{:S(2)}, u32[]{:S(2)}) collective-permute-start(bf16[160,256]{1,0:T(8,128)(2,1)S(1)} %get-tuple-element.83.after_ref), channel_id=1, source_target_pairs={{0,1},{1,0},{2,3},{3,2},{4,5},{5,4},{6,7},{7,6},{8,9},{9,8},{10,11... | collective-permute-start | bytes 245768 | tf_op jit(solution)/shard_map/ppermute | solution.py:858
  40.9 8.3 %copy-start.12 = (s32[36]{0:T(128)S(1)}, s32[36]{0:T(128)}, u32[]{:S(2)}) copy-start(s32[36]{0:T(128)} %constant.199.clone) | copy-start | bytes 436
  40.9 8.3 %copy-start.13 = (s32[36]{0:T(128)S(1)}, s32[36]{0:T(128)}, u32[]{:S(2)}) copy-start(s32[36]{0:T(128)} %constant.200.clone) | copy-start | bytes 436
  40.9 8.3 %copy-start.11 = (s32[4,4,10]{2,1,0:T(4,128)S(1)}, s32[4,4,10]{2,1,0:T(4,128)}, u32[]{:S(2)}) copy-start(s32[4,4,10]{2,1,0:T(4,128)} %param.24) | copy-start | bytes 1924
  43.6 26.5 %collective-permute-start.5 = (bf16[1936,256]{1,0:T(8,128)(2,1)}, bf16[1936,256]{1,0:T(8,128)(2,1)}, u32[]{:S(2)}, u32[]{:S(2)}) collective-permute-start(bf16[1936,256]{1,0:T(8,128)(2,1)} %get-tuple-element.46.after_ref), channel_id=1, source_target_pairs={{1,0},{2,1},{3,2},{5,4},{6,5},{7,6},{9,8},{10,9},{11,10},{13,12},{... | collective-permute-start | bytes 2973704 | tf_op jit(solution)/shard_map/ppermute | solution.py:119
  45.5 26.1 %collective-permute-start.6 = (bf16[1936,256]{1,0:T(8,128)(2,1)}, bf16[1936,256]{1,0:T(8,128)(2,1)}, u32[]{:S(2)}, u32[]{:S(2)}) collective-permute-start(bf16[1936,256]{1,0:T(8,128)(2,1)} %get-tuple-element.47), channel_id=1, source_target_pairs={{0,1},{1,2},{2,3},{4,5},{5,6},{6,7},{8,9},{9,10},{10,11},{12,13},{... | collective-permute-start | bytes 2973704 | tf_op jit(solution)/shard_map/ppermute | solution.py:119
  50.5 17.7 %copy-start.7 = (bf16[4,2,256,256]{3,2,1,0:T(8,128)(2,1)S(1)}, bf16[4,2,256,256]{3,2,1,0:T(8,128)(2,1)}, u32[]{:S(2)}) copy-start(bf16[4,2,256,256]{3,2,1,0:T(8,128)(2,1)} %get-tuple-element.54) | copy-start | bytes 3145732
  50.5 19.5 %copy-start.6 = (bf16[4,2,256,256]{3,2,1,0:T(8,128)(2,1)S(1)}, bf16[4,2,256,256]{3,2,1,0:T(8,128)(2,1)}, u32[]{:S(2)}) copy-start(bf16[4,2,256,256]{3,2,1,0:T(8,128)(2,1)} %get-tuple-element.55) | copy-start | bytes 3145732
  50.5 17.7 %collective-permute-start.4 = (bf16[320,256]{1,0:T(8,128)(2,1)S(1)}, bf16[320,256]{1,0:T(8,128)(2,1)S(1)}, u32[]{:S(2)}, u32[]{:S(2)}) collective-permute-start(bf16[320,256]{1,0:T(8,128)(2,1)S(1)} %pad_maximum_fusion.3), channel_id=1, source_target_pairs={{0,16},{4,20},{8,24},{12,28},{16,0},{20,4},{24,8},{28,12},{1,17},{... | collective-permute-start | bytes 491528 | tf_op jit(solution)/shard_map/ppermute | solution.py:858
  68.2 46.4 %collective-permute-start.8 = (bf16[4,2,256,256]{3,2,1,0:T(8,128)(2,1)S(1)}, bf16[4,2,256,256]{3,2,1,0:T(8,128)(2,1)S(1)}, u32[]{:S(2)}, u32[]{:S(2)}) collective-permute-start(bf16[4,2,256,256]{3,2,1,0:T(8,128)(2,1)S(1)} %copy-done.7), channel_id=1, source_target_pairs={{0,4},{4,8},{8,12},{12,16},{16,20},{20,24},{24,28},{1,5},{5,9},{9,... | collective-permute-start | bytes 3145736 | tf_op jit(solution)/shard_map/ppermute | solution.py:119
  70.1 44.6 %collective-permute-start.9 = (bf16[4,2,256,256]{3,2,1,0:T(8,128)(2,1)S(1)}, bf16[4,2,256,256]{3,2,1,0:T(8,128)(2,1)S(1)}, u32[]{:S(2)}, u32[]{:S(2)}) collective-permute-start(bf16[4,2,256,256]{3,2,1,0:T(8,128)(2,1)S(1)} %copy-done.6), channel_id=1, source_target_pairs={{4,0},{8,4},{12,8},{16,12},{20,16},{24,20},{28,24},{5,1},{9,5},{13... | collective-permute-start | bytes 3145736 | tf_op jit(solution)/shard_map/ppermute | solution.py:119
  71.6 43.1 %collective-permute-start.7 = (bf16[640,256]{1,0:T(8,128)(2,1)S(1)}, bf16[640,256]{1,0:T(8,128)(2,1)S(1)}, u32[]{:S(2)}, u32[]{:S(2)}) collective-permute-start(bf16[640,256]{1,0:T(8,128)(2,1)S(1)} %pad_maximum_fusion.2), channel_id=1, source_target_pairs={{0,8},{4,12},{8,0},{12,4},{16,24},{20,28},{24,16},{28,20},{1,9},{5... | collective-permute-start | bytes 983048 | tf_op jit(solution)/shard_map/ppermute | solution.py:858
  114.6 1.2 copy-start.1
  114.7 1.5 copy-start.2
  115.6 19.0 %collective-permute-start.13 = (bf16[1280,256]{1,0:T(8,128)(2,1)}, bf16[1280,256]{1,0:T(8,128)(2,1)}, u32[]{:S(2)}, u32[]{:S(2)}) collective-permute-start(bf16[1280,256]{1,0:T(8,128)(2,1)} %get-tuple-element.75), channel_id=1, source_target_pairs={{0,2},{1,3},{2,0},{3,1},{4,6},{5,7},{6,4},{7,5},{8,10},{9,11},{10,... | collective-permute-start | bytes 1966088 | tf_op jit(solution)/shard_map/ppermute | solution.py:858
  116.3 27.7 %collective-permute-start.12 = (bf16[2,2,2,256,256]{4,3,2,1,0:T(8,128)(2,1)S(1)}, bf16[2,2,2,256,256]{4,3,2,1,0:T(8,128)(2,1)S(1)}, u32[]{:S(2)}, u32[]{:S(2)}) collective-permute-start(bf16[2,2,2,256,256]{4,3,2,1,0:T(8,128)(2,1)S(1)} %pad_maximum_fusion.1), channel_id=1, source_target_pairs={{1,0},{2,1},{3,2},{5,4},{6,5},{7,6},{9,8},{10,9},{11,10},{13,12},{... | collective-permute-start | bytes 3145736 | tf_op jit(solution)/shard_map/ppermute | solution.py:119
  119.4 24.6 %collective-permute-start.11 = (bf16[2,2,2,256,256]{4,3,2,1,0:T(8,128)(2,1)S(1)}, bf16[2,2,2,256,256]{4,3,2,1,0:T(8,128)(2,1)S(1)}, u32[]{:S(2)}, u32[]{:S(2)}) collective-permute-start(bf16[2,2,2,256,256]{4,3,2,1,0:T(8,128)(2,1)S(1)} %pad_maximum_fusion), channel_id=1, source_target_pairs={{0,1},{1,2},{2,3},{4,5},{5,6},{6,7},{8,9},{9,10},{10,11},{12,13},{... | collective-permute-start | bytes 3145736 | tf_op jit(solution)/shard_map/ppermute | solution.py:119
  144.0 1.0 copy-start.4
  144.0 1.3 copy-start.5
  144.0 1.6 copy-start.3

commit v6 on v5

--- a/solution.py
+++ b/solution.py
@@ -352,21 +352,11 @@
     lax.fori_loop(0, parents.shape[0] // RANK, lift, 0)
 
     def fill(start, source, stride):
-        def one(i, carry):
+        for i in range(WINDOW):
             slot = meta_ref[start + i]
-            to = pl.ds(pl.multiple_of(i * RANK, RANK), RANK)
-
-            @pl.when(slot >= 0)
-            def _():
-                win[to] = source[pl.ds(pl.multiple_of(slot * stride, 16), RANK)]
-
-            @pl.when(slot < 0)
-            def _():
-                win[to] = jnp.zeros((RANK, LEAF), BF)
-
-            return carry
-
-        lax.fori_loop(0, WINDOW, one, 0)
+            at = pl.multiple_of(jnp.maximum(slot, 0) * stride, 16)
+            kept = jnp.where(slot >= 0, 1.0, 0.0).astype(BF)
+            win[i * RANK : (i + 1) * RANK] = source[pl.ds(at, RANK)] * kept
 
     fill(WINDOW, parents, RANK)
     slabs[1].wait()
@@ -868,7 +858,9 @@
     other = step(gathered, 1)
     row1 = near_own(1, 2, q, points, noise_rows, gathered, [row0])
     to_east, to_west = charges[:, 2:4], charges[:, 0:2]
-    other, from_west, from_east, row1, to_east, to_west = tie(other, from_west, from_east, row1, to_east, to_west)
+    other, from_west, from_east, row1, to_east, to_west, q_north, q_south = tie(
+        other, from_west, from_east, row1, to_east, to_west, q_north, q_south
+    )
     gathered = jnp.concatenate([gathered, other], axis=0)
     other = step(gathered, 2)
     to_north, to_south = join(north, south, from_west, from_east)
@@ -882,15 +874,15 @@
     other = step(gathered, 3)
     sums = local_far(listing, coefs, from_west, from_east, from_north, from_south)
     upper_blocks = edge_blocks(0, listing, sums[1], points, from_west, from_east, from_north, from_south)
-    other, upper_blocks, q_west, q_east = tie(other, upper_blocks, q_west, q_east)
+    other, upper_blocks = tie(other, upper_blocks)
     for at in range(4, len(steps)):
         gathered = jnp.concatenate([gathered, other], axis=0)
         other = step(gathered, at)
         if at == 4:
+            lower_blocks = edge_blocks(1, listing, upper_blocks, points, from_west, from_east, from_north, from_south)
+            other, lower_blocks, q_west, q_east = tie(other, lower_blocks, q_west, q_east)
             q_north_corner = shift(jnp.stack([q_west[2:4], q_east[2:4]]), "narrow", 1)
             q_south_corner = shift(jnp.stack([q_west[0:2], q_east[0:2]]), "narrow", -1)
-            lower_blocks = edge_blocks(1, listing, upper_blocks, points, from_west, from_east, from_north, from_south)
-            other, lower_blocks = tie(other, lower_blocks)
     gathered = jnp.concatenate([gathered, other], axis=0)
     field = top_far(meta, gathered, tree, *sums)
     q_north_corner, q_south_corner, field = tie(q_north_corner, q_south_corner, field)

time: 163 us -> 150 us (0.920); the launches traced: 160 us -> 149 us
  waiting for transfers between devices: 18.1 us -> 8.21 us
  Pallas kernels: 91.1 us -> 89.3 us
    ppermute x10, waiting for transfers between devices: 18.1 us -> 5.19 us  [shift(): lax.ppermute(value, axis, [(i, i + steps) for i in range(count) if 0 <= i...]
    ppermute x5, waiting for transfers between devices: 0.01 us -> 3.02 us  [step(): lax.ppermute(value, axis, [(i, i ^ bit) for i in range(lax.axis_size(axis...]
    unnamed x32 -> x31, local copies, waits for them, and re-layouts: 5.35 us -> 5.23 us
  transfers between devices with their start and end apart: 15 -> 15, of which waited for: 1 -> 2; matrix products, arithmetic and copies ran while one was open for 7% -> 6% of each run, Pallas kernels for 45% -> 49%
where the time goes in v6:
time: 150 us; the launch traced here: 149 us
  Pallas kernels  89.3 us (60%)
  starting transfers between devices  37 us (25%)
  local copies, waits for them, and re-layouts  11.9 us (8%)
  waiting for transfers between devices  8.21 us (5%)
  other arithmetic  1.86 us (1%)
    pallas_call x3, Pallas kernels, near_own(): pl.pallas_call(body, out_shape=jax.ShapeDtypeStruct((leaves, LEAF, LEAF),...  30.4 us
    ppermute x10, starting transfers between devices, shift(): lax.ppermute(value, axis, [(i, i + steps) for i in range(count) if 0 <= i...  25.3 us
    pallas_call x2, Pallas kernels, edge_blocks(): pl.pallas_call(body, out_shape=jax.ShapeDtypeStruct((EDGES // 2 + 8, LEAF...  24 us
    pallas_call x1, Pallas kernels, finish(): pl.pallas_call(final_body, out_shape=jax.ShapeDtypeStruct((LEAVES, LEAF,...  13.5 us
    ppermute x5, starting transfers between devices, step(): lax.ppermute(value, axis, [(i, i ^ bit) for i in range(lax.axis_size(axis...  11.6 us
    pallas_call x1, Pallas kernels, local_far(): pl.pallas_call(local_body, out_shape=(jax.ShapeDtypeStruct((LEAVES, RANK,...  7.66 us
    pallas_call x1, Pallas kernels, top_far(): pl.pallas_call(top_body, out_shape=jax.ShapeDtypeStruct((LEAVES, RANK, LE...  6.25 us
    unnamed x31, local copies, waits for them, and re-layouts  5.23 us
  transfers between devices with their start and end apart: 15, of which 2 were waited for; matrix products, arithmetic and copies ran while one was open for 6% of the time, Pallas kernels for 49%

profile of v6, /device:TPU:1, one launch (start us, length us, event | category | flops | bytes accessed | tf_op | source)
XLA Modules:
  0.0 149.0 jit_solution(10972649110083182821)
XLA Ops:
  0.0 3.1 %fusion.2 = (bf16[2,4,256,256]{3,2,1,0:T(8,128)(2,1)}, bf16[2,4,256,256]{3,2,1,0:T(8,128)(2,1)}) fusion(bf16[4,4,256,256]{3,2,1,0:T(8,128)(2,1)} %param.19), kind=kLoop, calls=%fused_computation.56 | loop fusion | bytes 4194304 | tf_op jit(solution)/shard_map/slice | solution.py:842
  3.1 2.0 %collective-permute-start.5 = (bf16[2,4,256,256]{3,2,1,0:T(8,128)(2,1)}, bf16[2,4,256,256]{3,2,1,0:T(8,128)(2,1)S(1)}, u32[]{:S(2)}, u32[]{:S(2)}) collective-permute-start(bf16[2,4,256,256]{3,2,1,0:T(8,128)(2,1)} %get-tuple-element.71), channel_id=1, source_target_pairs={{1,0},{2,1},{3,2},{5,4},{6,5},{7,6},{9,8},{10,9},{11,10},{13,12},{... | collective-permute-start | bytes 3145736 | tf_op jit(solution)/shard_map/ppermute | solution.py:119
  5.0 4.5 %collective-permute-start.4 = (bf16[2,4,256,256]{3,2,1,0:T(8,128)(2,1)}, bf16[2,4,256,256]{3,2,1,0:T(8,128)(2,1)}, u32[]{:S(2)}, u32[]{:S(2)}) collective-permute-start(bf16[2,4,256,256]{3,2,1,0:T(8,128)(2,1)} %get-tuple-element.72), channel_id=1, source_target_pairs={{0,1},{1,2},{2,3},{4,5},{5,6},{6,7},{8,9},{9,10},{10,11},{12,13},{... | collective-permute-start | bytes 3145736 | tf_op jit(solution)/shard_map/ppermute | solution.py:119
  9.6 4.6 %upward.1 = (bf16[816,256]{1,0:T(8,128)(2,1)}, bf16[816,256]{1,0:T(8,128)(2,1)}, bf16[816,256]{1,0:T(8,128)(2,1)}, bf16[816,256]{1,0:T(8,128)(2,1)}, bf16[1280,256]{1,0:T(8,128)(2,1)}, /*index=5*/bf16[80,256]{1,0:T(8,128)(2,1)}) custom-call(bf16[16,256,256]{2,1,0:T(8,128)(2,1)} %bitcast.21, bf16[16,64,256]{2,1,0:T(8,128)(2,1)} %bitcast.28, ...), custom_call_target="tpu_custom_call" | custom-call | flops 300000000 | bytes 5000000 | tf_op jit(solution)/shard_map/upward/pallas_call | solution.py:194
  14.1 1.3 collective-permute-start
  15.4 2.9 %collective-permute-start.2 = (bf16[816,256]{1,0:T(8,128)(2,1)}, bf16[816,256]{1,0:T(8,128)(2,1)}, u32[]{:S(2)}, u32[]{:S(2)}) collective-permute-start(bf16[816,256]{1,0:T(8,128)(2,1)} %get-tuple-element.40), channel_id=1, source_target_pairs={{0,4},{4,8},{8,12},{12,16},{16,20},{20,24},{24,28},{1,5},{5,9},{9,... | collective-permute-start | bytes 1253384 | tf_op jit(solution)/shard_map/ppermute | solution.py:119
  18.3 1.3 collective-permute-start.3
  20.2 9.1 %near_own.3.refs_4_.row0_any = f32[8,256,256]{2,1,0:T(8,128)} custom-call(bf16[80,256]{1,0:T(8,128)(2,1)} %get-tuple-element.38.after_ref, s32[52]{0:T(128)} %constant.201.clone.refs_0_, bf16[16,256,256]{2,1,0:T(8,128)(2,1)} %bitcast.22, f32[16,2,256]{2,1,0:T(2,128)} %bitcast.36, f32[16,1,256]{2,1,0:T(1,128)} %reshape.40.refs_3_), custom_call_target="tpu_custom_call" | custom-call | flops 6000000000 | bytes 4000000 | tf_op jit(solution)/shard_map/near_own/pallas_call | solution.py:576
  32.0 9.0 %near_own.4.refs_4_.row1_any = f32[8,256,256]{2,1,0:T(8,128)} custom-call(bf16[160,256]{1,0:T(8,128)(2,1)} %copy-done.7, s32[52]{0:T(128)} %constant.202.clone.refs_0_, bf16[16,256,256]{2,1,0:T(8,128)(2,1)} %bitcast.23, f32[16,2,256]{2,1,0:T(2,128)} %bitcast.37, f32[16,1,256]{2,1,0:T(1,128)} %reshape.40.refs_3_, f32[8,256,256]{2,1,0:T(8,128)} %near_own.3.refs_4_.row0_any), custom_call_target="tpu_custom_call" | custom-call | flops 6000000000 | bytes 4000000 | tf_op jit(solution)/shard_map/near_own/pallas_call | solution.py:576
  41.1 3.0 %join.1 = (bf16[1936,256]{1,0:T(8,128)(2,1)}, bf16[1936,256]{1,0:T(8,128)(2,1)}) custom-call(bf16[816,256]{1,0:T(8,128)(2,1)} %get-tuple-element.44.north_ref, bf16[816,256]{1,0:T(8,128)(2,1)} %get-tuple-element.45.south_ref, bf16[816,256]{1,0:T(8,128)(2,1)} %collective-permute-done.2.west_ref.west_any.refs_5_, ...), custom_call_target="tpu_custom_call" | custom-call | bytes 4000000 | tf_op jit(solution)/shard_map/join/pallas_call | solution.py:442
  44.0 3.0 %collective-permute-start.8 = (bf16[1936,256]{1,0:T(8,128)(2,1)}, bf16[1936,256]{1,0:T(8,128)(2,1)}, u32[]{:S(2)}, u32[]{:S(2)}) collective-permute-start(bf16[1936,256]{1,0:T(8,128)(2,1)} %get-tuple-element.49), channel_id=1, source_target_pairs={{0,1},{1,2},{2,3},{4,5},{5,6},{6,7},{8,9},{9,10},{10,11},{12,13},{... | collective-permute-start | bytes 2973704 | tf_op jit(solution)/shard_map/ppermute | solution.py:119
  47.1 2.2 %collective-permute-start.7 = (bf16[1936,256]{1,0:T(8,128)(2,1)}, bf16[1936,256]{1,0:T(8,128)(2,1)}, u32[]{:S(2)}, u32[]{:S(2)}) collective-permute-start(bf16[1936,256]{1,0:T(8,128)(2,1)} %get-tuple-element.48.after_ref), channel_id=1, source_target_pairs={{1,0},{2,1},{3,2},{5,4},{6,5},{7,6},{9,8},{10,9},{11,10},{13,12},{... | collective-permute-start | bytes 2973704 | tf_op jit(solution)/shard_map/ppermute | solution.py:119
  50.0 4.9 %collective-permute-start.6 = (bf16[320,256]{1,0:T(8,128)(2,1)S(1)}, bf16[320,256]{1,0:T(8,128)(2,1)S(1)}, u32[]{:S(2)}, u32[]{:S(2)}) collective-permute-start(bf16[320,256]{1,0:T(8,128)(2,1)S(1)} %pad_maximum_fusion.3), channel_id=1, source_target_pairs={{0,16},{4,20},{8,24},{12,28},{16,0},{20,4},{24,8},{28,12},{1,17},{... | collective-permute-start | bytes 491528 | tf_op jit(solution)/shard_map/ppermute | solution.py:848
  55.0 1.8 %collective-permute-start.11 = (bf16[4,2,256,256]{3,2,1,0:T(8,128)(2,1)S(1)}, bf16[4,2,256,256]{3,2,1,0:T(8,128)(2,1)S(1)}, u32[]{:S(2)}, u32[]{:S(2)}) collective-permute-start(bf16[4,2,256,256]{3,2,1,0:T(8,128)(2,1)S(1)} %get-tuple-element.58), channel_id=1, source_target_pairs={{0,4},{4,8},{8,12},{12,16},{16,20},{20,24},{24,28},{1,5},{5,9},{9,... | collective-permute-start | bytes 3145736 | tf_op jit(solution)/shard_map/ppermute | solution.py:119
  56.8 1.5 collective-permute-start.12
  58.3 12.4 %near_own.5.row2_any = f32[8,256,256]{2,1,0:T(8,128)} custom-call(bf16[1936,256]{1,0:T(8,128)(2,1)} %get-tuple-element.48.after_ref, s32[64]{0:T(128)} %constant.203.clone.refs_0_, bf16[16,256,256]{2,1,0:T(8,128)(2,1)} %bitcast.24, f32[16,2,256]{2,1,0:T(2,128)} %bitcast.38, f32[16,1,256]{2,1,0:T(1,128)} %reshape.40.refs_3_, ...), custom_call_target="tpu_custom_call" | custom-call | flops 6000000000 | bytes 4000000 | tf_op jit(solution)/shard_map/near_own/pallas_call | solution.py:576
  70.7 0.7 constant_dynamic-update-slice_fusion.10
  71.4 4.4 %collective-permute-start.9 = (bf16[640,256]{1,0:T(8,128)(2,1)S(1)}, bf16[640,256]{1,0:T(8,128)(2,1)S(1)}, u32[]{:S(2)}, u32[]{:S(2)}) collective-permute-start(bf16[640,256]{1,0:T(8,128)(2,1)S(1)} %pad_maximum_fusion.2), channel_id=1, source_target_pairs={{0,8},{4,12},{8,0},{12,4},{16,24},{20,28},{24,16},{28,20},{1,9},{5... | collective-permute-start | bytes 983048 | tf_op jit(solution)/shard_map/ppermute | solution.py:848
  75.8 7.7 %local_far.1 = (f32[16,64,256]{2,1,0:T(8,128)}, f32[256,256]{1,0:T(8,128)}) custom-call(s32[160]{0:T(256)} %reshape.36.list_ref.refs_0_, bf16[1280,256]{1,0:T(8,128)(2,1)} %get-tuple-element.52.coef_any, bf16[816,256]{1,0:T(8,128)(2,1)} %collective-permute-done.2.west_ref.west_any.refs_5_, bf16[816,256]{1,0:T(8,128)(2,1)} %collective-permute-done.3.east_ref.east_any.refs_6_, ...), custom_call_target="tpu_custom_call" | custom-call | flops 5000000000 | bytes 8000000 | tf_op jit(solution)/shard_map/local_far/pallas_call | solution.py:292
  83.5 12.0 %edge_blocks.2.refs_3_.upper_blocks_any = bf16[30,256,256]{2,1,0:T(8,128)(2,1)} custom-call(s32[160]{0:T(256)} %reshape.36.list_ref.refs_0_, s32[88]{0:T(128)} %constant.207.clone.refs_1_, s32[64]{0:T(128)} %constant.208.clone.refs_2_.slot_ref, f32[256,256]{1,0:T(8,128)} %get-tuple-element.55.refs_3_.sum1_any, f32[16,2,256]{2,1,0:T(2,128)} %bitcast.39, ...), custom_call_target="tpu_custom_call" | custom-call | flops 6000000000 | bytes 8000000 | tf_op jit(solution)/shard_map/edge_blocks/pallas_call | solution.py:690
  95.5 0.7 constant_dynamic-update-slice_fusion.9
  96.2 0.8 constant_dynamic-update-slice_fusion.8
  97.5 12.0 %edge_blocks.3.lower_blocks_any = bf16[30,256,256]{2,1,0:T(8,128)(2,1)} custom-call(s32[160]{0:T(256)} %reshape.36.list_ref.refs_0_, s32[88]{0:T(128)} %constant.209.clone.refs_1_, s32[64]{0:T(128)} %constant.208.clone.refs_2_.slot_ref, bf16[30,256,256]{2,1,0:T(8,128)(2,1)} %edge_blocks.2.refs_3_.upper_blocks_any, f32[16,2,256]{2,1,0:T(2,128)} %bitcast.40, ...), custom_call_target="tpu_custom_call" | custom-call | flops 6000000000 | bytes 8000000 | tf_op jit(solution)/shard_map/edge_blocks/pallas_call | solution.py:690
  109.5 3.0 %collective-permute-done.10 = bf16[1280,256]{1,0:T(8,128)(2,1)} collective-permute-done((bf16[1280,256]{1,0:T(8,128)(2,1)S(1)}, bf16[1280,256]{1,0:T(8,128)(2,1)}, u32[]{:S(2)}, u32[]{:S(2)}) %collective-permute-start.10) | collective-permute-done | bytes 655392 | tf_op jit(solution)/shard_map/ppermute | solution.py:848
  112.9 4.0 %collective-permute-start.13 = (bf16[2,2,2,256,256]{4,3,2,1,0:T(8,128)(2,1)S(1)}, bf16[2,2,2,256,256]{4,3,2,1,0:T(8,128)(2,1)S(1)}, u32[]{:S(2)}, u32[]{:S(2)}) collective-permute-start(bf16[2,2,2,256,256]{4,3,2,1,0:T(8,128)(2,1)S(1)} %pad_maximum_fusion), channel_id=1, source_target_pairs={{0,1},{1,2},{2,3},{4,5},{5,6},{6,7},{8,9},{9,10},{10,11},{12,13},{... | collective-permute-start | bytes 3145736 | tf_op jit(solution)/shard_map/ppermute | solution.py:119
  116.9 1.1 pad_maximum_fusion.1
  118.0 2.1 %collective-permute-start.14 = (bf16[2,2,2,256,256]{4,3,2,1,0:T(8,128)(2,1)}, bf16[2,2,2,256,256]{4,3,2,1,0:T(8,128)(2,1)S(1)}, u32[]{:S(2)}, u32[]{:S(2)}) collective-permute-start(bf16[2,2,2,256,256]{4,3,2,1,0:T(8,128)(2,1)} %pad_maximum_fusion.1), channel_id=1, source_target_pairs={{1,0},{2,1},{3,2},{5,4},{6,5},{7,6},{9,8},{10,9},{11,10},{13,12},{... | collective-permute-start | bytes 3145736 | tf_op jit(solution)/shard_map/ppermute | solution.py:119
  120.9 2.0 %constant_dynamic-update-slice_fusion.7.all_any = bf16[2560,256]{1,0:T(8,128)(2,1)} fusion(bf16[2560,256]{1,0:T(8,128)(2,1)} %get-tuple-element.79, bf16[1280,256]{1,0:T(8,128)(2,1)} %collective-permute-done.10), kind=kLoop, calls=%fused_computation.15 | loop fusion | bytes 1310720 | tf_op jit(solution)/shard_map/concatenate | solution.py:886
  122.9 6.3 %top_far.1.field_ref = bf16[16,64,256]{2,1,0:T(8,128)(2,1)} custom-call(s32[74]{0:T(128)} %pad_add_fusion.meta_ref, bf16[2560,256]{1,0:T(8,128)(2,1)} %constant_dynamic-update-slice_fusion.7.all_any, bf16[256,2304]{1,0:T(8,128)(2,1)} %constant.210.clone.c2_any, bf16[256,2304]{1,0:T(8,128)(2,1)} %constant.211.clone.c3_any, bf16[21,64,64]{2,1,0:T(8,128)(2,1)} %bitcast.34, ...), custom_call_target="tpu_custom_call" | custom-call | flops 3000000000 | bytes 5000000 | tf_op jit(solution)/shard_map/top_far/pallas_call | solution.py:394
  129.2 5.2 %collective-permute-done.14 = bf16[2,2,2,256,256]{4,3,2,1,0:T(8,128)(2,1)S(1)} collective-permute-done((bf16[2,2,2,256,256]{4,3,2,1,0:T(8,128)(2,1)}, bf16[2,2,2,256,256]{4,3,2,1,0:T(8,128)(2,1)S(1)}, u32[]{:S(2)}, u32[]{:S(2)}) %collective-permute-start.14) | collective-permute-done | bytes 1048608 | tf_op jit(solution)/shard_map/ppermute | solution.py:119
  134.3 1.0 copy-done.5
  135.3 13.5 %finish.1 = bf16[16,256,256]{2,1,0:T(8,128)(2,1)} custom-call(s32[160]{0:T(256)} %reshape.36.list_ref.refs_0_, s32[64]{0:T(128)} %constant.208.clone.refs_2_.slot_ref, bf16[16,256,256]{2,1,0:T(8,128)(2,1)} %bitcast.25, bf16[8,256,256]{2,1,0:T(8,128)(2,1)} %bitcast.26, bf16[8,256,256]{2,1,0:T(8,128)(2,1)} %bitcast.27, bf16[8,256,256]{2,1,0:T(8,128)(2,1)} %bitcast.6.north_any, ...), custom_call_target="tpu_custom_call" | custom-call | flops 4000000000 | bytes 24000000 | tf_op jit(solution)/shard_map/finish/pallas_call | solution.py:790
  (51 shorter events, 5.6 us)
Async XLA Ops:
  3.1 38.0 %collective-permute-start.5 = (bf16[2,4,256,256]{3,2,1,0:T(8,128)(2,1)}, bf16[2,4,256,256]{3,2,1,0:T(8,128)(2,1)S(1)}, u32[]{:S(2)}, u32[]{:S(2)}) collective-permute-start(bf16[2,4,256,256]{3,2,1,0:T(8,128)(2,1)} %get-tuple-element.71), channel_id=1, source_target_pairs={{1,0},{2,1},{3,2},{5,4},{6,5},{7,6},{9,8},{10,9},{11,10},{13,12},{... | collective-permute-start | bytes 3145736 | tf_op jit(solution)/shard_map/ppermute | solution.py:119
  5.0 36.0 %collective-permute-start.4 = (bf16[2,4,256,256]{3,2,1,0:T(8,128)(2,1)}, bf16[2,4,256,256]{3,2,1,0:T(8,128)(2,1)}, u32[]{:S(2)}, u32[]{:S(2)}) collective-permute-start(bf16[2,4,256,256]{3,2,1,0:T(8,128)(2,1)} %get-tuple-element.72), channel_id=1, source_target_pairs={{0,1},{1,2},{2,3},{4,5},{5,6},{6,7},{8,9},{9,10},{10,11},{12,13},{... | collective-permute-start | bytes 3145736 | tf_op jit(solution)/shard_map/ppermute | solution.py:119
  9.5 10.1 %copy-start.8 = (f32[4,4,256]{2,1,0:T(4,128)S(1)}, f32[4,4,256]{2,1,0:T(4,128)}, u32[]{:S(2)}) copy-start(f32[4,4,256]{2,1,0:T(4,128)} %param.21) | copy-start | bytes 49156
  14.1 16.6 %collective-permute-start = (bf16[80,256]{1,0:T(8,128)(2,1)}, bf16[80,256]{1,0:T(8,128)(2,1)S(1)}, u32[]{:S(2)}, u32[]{:S(2)}) collective-permute-start(bf16[80,256]{1,0:T(8,128)(2,1)} %get-tuple-element.38.after_ref), channel_id=1, source_target_pairs={{0,4},{4,0},{8,12},{12,8},{16,20},{20,16},{24,28},{28,24},{1,5},{5... | collective-permute-start | bytes 122888 | tf_op jit(solution)/shard_map/ppermute | solution.py:848
  15.4 25.6 %collective-permute-start.2 = (bf16[816,256]{1,0:T(8,128)(2,1)}, bf16[816,256]{1,0:T(8,128)(2,1)}, u32[]{:S(2)}, u32[]{:S(2)}) collective-permute-start(bf16[816,256]{1,0:T(8,128)(2,1)} %get-tuple-element.40), channel_id=1, source_target_pairs={{0,4},{4,8},{8,12},{12,16},{16,20},{20,24},{24,28},{1,5},{5,9},{9,... | collective-permute-start | bytes 1253384 | tf_op jit(solution)/shard_map/ppermute | solution.py:119
  18.3 22.7 %collective-permute-start.3 = (bf16[816,256]{1,0:T(8,128)(2,1)}, bf16[816,256]{1,0:T(8,128)(2,1)}, u32[]{:S(2)}, u32[]{:S(2)}) collective-permute-start(bf16[816,256]{1,0:T(8,128)(2,1)} %get-tuple-element.41), channel_id=1, source_target_pairs={{4,0},{8,4},{12,8},{16,12},{20,16},{24,20},{28,24},{5,1},{9,5},{13... | collective-permute-start | bytes 1253384 | tf_op jit(solution)/shard_map/ppermute | solution.py:119
  20.2 9.1 %copy-start = (bf16[4,4,256,256]{3,2,1,0:T(8,128)(2,1)S(1)}, bf16[4,4,256,256]{3,2,1,0:T(8,128)(2,1)}, u32[]{:S(2)}) copy-start(bf16[4,4,256,256]{3,2,1,0:T(8,128)(2,1)} %param.19) | copy-start | bytes 6291460
  29.3 0.8 copy-start.6
  31.4 0.6 copy-start.7
  31.4 9.6 %collective-permute-start.1 = (bf16[160,256]{1,0:T(8,128)(2,1)S(1)}, bf16[160,256]{1,0:T(8,128)(2,1)S(1)}, u32[]{:S(2)}, u32[]{:S(2)}) collective-permute-start(bf16[160,256]{1,0:T(8,128)(2,1)S(1)} %get-tuple-element.87.after_ref), channel_id=1, source_target_pairs={{0,1},{1,0},{2,3},{3,2},{4,5},{5,4},{6,7},{7,6},{8,9},{9,8},{10,11... | collective-permute-start | bytes 245768 | tf_op jit(solution)/shard_map/ppermute | solution.py:848
  41.0 8.3 %copy-start.9 = (s32[4,4,10]{2,1,0:T(4,128)S(1)}, s32[4,4,10]{2,1,0:T(4,128)}, u32[]{:S(2)}) copy-start(s32[4,4,10]{2,1,0:T(4,128)} %param.24) | copy-start | bytes 1924
  41.0 29.6 %copy-start.3 = (bf16[2,4,256,256]{3,2,1,0:T(8,128)(2,1)}, bf16[2,4,256,256]{3,2,1,0:T(8,128)(2,1)S(1)}, u32[]{:S(2)}) copy-start(bf16[2,4,256,256]{3,2,1,0:T(8,128)(2,1)S(1)} %collective-permute-done.5) | copy-start | bytes 3145732
  44.0 27.3 %collective-permute-start.8 = (bf16[1936,256]{1,0:T(8,128)(2,1)}, bf16[1936,256]{1,0:T(8,128)(2,1)}, u32[]{:S(2)}, u32[]{:S(2)}) collective-permute-start(bf16[1936,256]{1,0:T(8,128)(2,1)} %get-tuple-element.49), channel_id=1, source_target_pairs={{0,1},{1,2},{2,3},{4,5},{5,6},{6,7},{8,9},{9,10},{10,11},{12,13},{... | collective-permute-start | bytes 2973704 | tf_op jit(solution)/shard_map/ppermute | solution.py:119
  47.1 24.3 %collective-permute-start.7 = (bf16[1936,256]{1,0:T(8,128)(2,1)}, bf16[1936,256]{1,0:T(8,128)(2,1)}, u32[]{:S(2)}, u32[]{:S(2)}) collective-permute-start(bf16[1936,256]{1,0:T(8,128)(2,1)} %get-tuple-element.48.after_ref), channel_id=1, source_target_pairs={{1,0},{2,1},{3,2},{5,4},{6,5},{7,6},{9,8},{10,9},{11,10},{13,12},{... | collective-permute-start | bytes 2973704 | tf_op jit(solution)/shard_map/ppermute | solution.py:119
  50.0 21.3 %collective-permute-start.6 = (bf16[320,256]{1,0:T(8,128)(2,1)S(1)}, bf16[320,256]{1,0:T(8,128)(2,1)S(1)}, u32[]{:S(2)}, u32[]{:S(2)}) collective-permute-start(bf16[320,256]{1,0:T(8,128)(2,1)S(1)} %pad_maximum_fusion.3), channel_id=1, source_target_pairs={{0,16},{4,20},{8,24},{12,28},{16,0},{20,4},{24,8},{28,12},{1,17},{... | collective-permute-start | bytes 491528 | tf_op jit(solution)/shard_map/ppermute | solution.py:848
  55.0 54.5 %collective-permute-start.11 = (bf16[4,2,256,256]{3,2,1,0:T(8,128)(2,1)S(1)}, bf16[4,2,256,256]{3,2,1,0:T(8,128)(2,1)S(1)}, u32[]{:S(2)}, u32[]{:S(2)}) collective-permute-start(bf16[4,2,256,256]{3,2,1,0:T(8,128)(2,1)S(1)} %get-tuple-element.58), channel_id=1, source_target_pairs={{0,4},{4,8},{8,12},{12,16},{16,20},{20,24},{24,28},{1,5},{5,9},{9,... | collective-permute-start | bytes 3145736 | tf_op jit(solution)/shard_map/ppermute | solution.py:119
  56.8 52.7 %collective-permute-start.12 = (bf16[4,2,256,256]{3,2,1,0:T(8,128)(2,1)S(1)}, bf16[4,2,256,256]{3,2,1,0:T(8,128)(2,1)S(1)}, u32[]{:S(2)}, u32[]{:S(2)}) collective-permute-start(bf16[4,2,256,256]{3,2,1,0:T(8,128)(2,1)S(1)} %get-tuple-element.59), channel_id=1, source_target_pairs={{4,0},{8,4},{12,8},{16,12},{20,16},{24,20},{28,24},{5,1},{9,5},{13... | collective-permute-start | bytes 3145736 | tf_op jit(solution)/shard_map/ppermute | solution.py:119
  71.4 24.8 %collective-permute-start.9 = (bf16[640,256]{1,0:T(8,128)(2,1)S(1)}, bf16[640,256]{1,0:T(8,128)(2,1)S(1)}, u32[]{:S(2)}, u32[]{:S(2)}) collective-permute-start(bf16[640,256]{1,0:T(8,128)(2,1)S(1)} %pad_maximum_fusion.2), channel_id=1, source_target_pairs={{0,8},{4,12},{8,0},{12,4},{16,24},{20,28},{24,16},{28,20},{1,9},{5... | collective-permute-start | bytes 983048 | tf_op jit(solution)/shard_map/ppermute | solution.py:848
  83.5 12.0 %copy-start.10 = (bf16[1280,256]{1,0:T(8,128)(2,1)S(1)}, bf16[1280,256]{1,0:T(8,128)(2,1)}, u32[]{:S(2)}) copy-start(bf16[1280,256]{1,0:T(8,128)(2,1)} %get-tuple-element.84) | copy-start | bytes 1966084
  97.0 15.6 %collective-permute-start.10 = (bf16[1280,256]{1,0:T(8,128)(2,1)S(1)}, bf16[1280,256]{1,0:T(8,128)(2,1)}, u32[]{:S(2)}, u32[]{:S(2)}) collective-permute-start(bf16[1280,256]{1,0:T(8,128)(2,1)S(1)} %get-tuple-element.80), channel_id=1, source_target_pairs={{0,2},{1,3},{2,0},{3,1},{4,6},{5,7},{6,4},{7,5},{8,10},{9,11},{10,... | collective-permute-start | bytes 1966088 | tf_op jit(solution)/shard_map/ppermute | solution.py:848
  109.5 3.2 %copy-start.1 = (bf16[4,2,256,256]{3,2,1,0:T(8,128)(2,1)}, bf16[4,2,256,256]{3,2,1,0:T(8,128)(2,1)S(1)}, u32[]{:S(2)}) copy-start(bf16[4,2,256,256]{3,2,1,0:T(8,128)(2,1)S(1)} %collective-permute-done.11) | copy-start | bytes 3145732
  109.5 3.2 %copy-start.2 = (bf16[4,2,256,256]{3,2,1,0:T(8,128)(2,1)}, bf16[4,2,256,256]{3,2,1,0:T(8,128)(2,1)S(1)}, u32[]{:S(2)}) copy-start(bf16[4,2,256,256]{3,2,1,0:T(8,128)(2,1)S(1)} %collective-permute-done.12) | copy-start | bytes 3145732
  112.9 7.4 %copy-start.11 = (s32[36]{0:T(128)S(1)}, s32[36]{0:T(128)}, u32[]{:S(2)}) copy-start(s32[36]{0:T(128)} %constant.200.clone) | copy-start | bytes 436
  112.9 7.4 %copy-start.12 = (s32[36]{0:T(128)S(1)}, s32[36]{0:T(128)}, u32[]{:S(2)}) copy-start(s32[36]{0:T(128)} %constant.199.clone) | copy-start | bytes 436
  112.9 16.2 %collective-permute-start.13 = (bf16[2,2,2,256,256]{4,3,2,1,0:T(8,128)(2,1)S(1)}, bf16[2,2,2,256,256]{4,3,2,1,0:T(8,128)(2,1)S(1)}, u32[]{:S(2)}, u32[]{:S(2)}) collective-permute-start(bf16[2,2,2,256,256]{4,3,2,1,0:T(8,128)(2,1)S(1)} %pad_maximum_fusion), channel_id=1, source_target_pairs={{0,1},{1,2},{2,3},{4,5},{5,6},{6,7},{8,9},{9,10},{10,11},{12,13},{... | collective-permute-start | bytes 3145736 | tf_op jit(solution)/shard_map/ppermute | solution.py:119
  118.0 16.3 %collective-permute-start.14 = (bf16[2,2,2,256,256]{4,3,2,1,0:T(8,128)(2,1)}, bf16[2,2,2,256,256]{4,3,2,1,0:T(8,128)(2,1)S(1)}, u32[]{:S(2)}, u32[]{:S(2)}) collective-permute-start(bf16[2,2,2,256,256]{4,3,2,1,0:T(8,128)(2,1)} %pad_maximum_fusion.1), channel_id=1, source_target_pairs={{1,0},{2,1},{3,2},{5,4},{6,5},{7,6},{9,8},{10,9},{11,10},{13,12},{... | collective-permute-start | bytes 3145736 | tf_op jit(solution)/shard_map/ppermute | solution.py:119
  129.1 5.2 %copy-start.4 = (bf16[2,2,2,256,256]{4,3,2,1,0:T(8,128)(2,1)}, bf16[2,2,2,256,256]{4,3,2,1,0:T(8,128)(2,1)S(1)}, u32[]{:S(2)}) copy-start(bf16[2,2,2,256,256]{4,3,2,1,0:T(8,128)(2,1)S(1)} %collective-permute-done.13) | copy-start | bytes 3145732
  134.3 1.0 copy-start.5

commit v7 on v6

--- a/solution.py
+++ b/solution.py
@@ -377,13 +377,7 @@
 
 
 def second_cycle(list_ref, leaf):
-    found = jnp.int32(-1)
-    for j in range(NEAR):
-        code = list_ref[leaf * NEAR + j]
-        y, x = code // 5, code % 5
-        outer = (code >= 0) & ((y == 0) | (y == 4) | (x == 0) | (x == 4))
-        found = jnp.where(outer, code, found)
-    return found
+    return list_ref[leaf]
 
 
 def top_far(meta, gathered, tree, sum0, sum1):
@@ -716,30 +710,30 @@
     stages = [[], [], [], []]
     count = 0
 
-    def copy(stage, source, to):
+    def copy(stage, source, at, rows, to, row):
         nonlocal count
-        made = pltpu.make_async_copy(source, to, sems.at[count])
+        made = pltpu.make_async_copy(source.at[pl.ds(at, rows)], to.at[pl.ds(row, rows)], sems.at[count])
         count += 1
         stages[stage].append(made)
 
+    copy(0, north_any, 0, 8, held, 32)
+    copy(0, north_corner_any, 0, 8, held, 40)
+    for stage, low, high in ((0, 0, 3), (1, 3, 4)):
+        copy(stage, west_any, 2 * low, 2 * (high - low), held, 16 + 2 * low)
+        copy(stage, east_any, 2 * low, 2 * (high - low), held, 24 + 2 * low)
+        copy(stage, q_any, 4 * low, 4 * (high - low), held, 4 * low)
+    copy(2, south_any, 0, 8, held, 48)
+    copy(2, south_corner_any, 0, 8, held, 56)
     for r in range(SIDE):
-        if r == 0:
-            for source, at in ((north_any, 32), (north_corner_any, 40)):
-                copy(r, source, held.at[pl.ds(at, 8)])
-        for source, at in ((west_any, 16), (east_any, 24)):
-            for low, high in {0: ((0, 4),), 1: ((4, 6),), 2: ((6, 8),)}.get(r, ()):
-                copy(r, source.at[pl.ds(low, high - low)], held.at[pl.ds(at + low, high - low)])
-        if r == SIDE - 1:
-            for source, at in ((south_any, 48), (south_corner_any, 56)):
-                copy(r, source, held.at[pl.ds(at, 8)])
-        part = pl.ds(firsts[r], firsts[r + 1] - firsts[r])
-        source, back = (upper_blocks_any, 0) if r < 2 else (lower_blocks_any, EDGES // 2)
-        copy(r, source.at[pl.ds(firsts[r] - back, firsts[r + 1] - firsts[r])], blocks.at[part])
-        source = (row0_any, row1_any, row2_any, row2_any)[r].at[pl.ds(SIDE if r == 3 else 0, SIDE)]
-        copy(r, source, sums.at[pl.ds(SIDE * r, SIDE)])
-    copy(SIDE - 1, q_any, held.at[pl.ds(0, 16)])
-    for half_at, source in enumerate((upper_blocks_any, lower_blocks_any)):
-        copy(SIDE - 1, source.at[pl.ds(EDGES // 2, 8)], blocks.at[pl.ds(EDGES + 8 * half_at, 8)])
+        source = upper_blocks_any if r < 2 else lower_blocks_any
+        back = 0 if r < 2 else EDGES // 2
+        copy(r, source, firsts[r] - back, firsts[r + 1] - firsts[r], blocks, firsts[r])
+        copy(r, source, EDGES // 2 + SIDE * (r % 2), SIDE, blocks, EDGES + SIDE * r)
+        copy(r, (row0_any, row1_any, row2_any, row2_any)[r], SIDE if r == 3 else 0, SIDE, sums, SIDE * r)
+    backs = []
+    for r in range(SIDE):
+        part = pl.ds(SIDE * r, SIDE)
+        backs.append(pltpu.make_async_copy(outs.at[part], out_any.at[part], sems.at[count + r]))
     for r in range(2):
         for made in stages[r]:
             made.start()
@@ -754,30 +748,17 @@
         for at in range(EDGES):
             if ITEMS[at][0] == leaf:
                 total = total + dot(blocks[at], held[ITEMS[at][1]])
-        sums[leaf] += total
-
-    backs = []
-    for r in range(SIDE):
-        part = pl.ds(SIDE * r, SIDE)
-        backs.append(pltpu.make_async_copy(outs.at[part], out_any.at[part], sems.at[count + r]))
-
-    for r in range(SIDE):
-
-        def finish(leaf, carry):
-            code, slot = extra_of(list_ref, slot_ref, leaf)
-
-            @pl.when(code >= 0)
-            def _():
-                outs[leaf] = (sums[leaf] + dot(blocks[EDGES + leaf], held[slot])).astype(BF)
-
-            @pl.when(code < 0)
-            def _():
-                outs[leaf] = sums[leaf].astype(BF)
-
-            return carry
-
-        lax.fori_loop(SIDE * r, SIDE * (r + 1), finish, 0)
-        backs[r].start()
+        total = total + sums[leaf]
+        sums[leaf] = total
+        outs[leaf] = total.astype(BF)
+        code, slot = extra_of(list_ref, slot_ref, leaf)
+
+        @pl.when(code >= 0)
+        def _(leaf=leaf, slot=slot):
+            outs[leaf] = (sums[leaf] + dot(blocks[EDGES + leaf], held[slot])).astype(BF)
+
+        if leaf % SIDE == SIDE - 1:
+            backs[leaf // SIDE].start()
     for back in backs:
         back.wait()
 
@@ -797,7 +778,7 @@
             pltpu.VMEM((EDGES + LEAVES, LEAF, LEAF), BF),
             pltpu.VMEM((LEAVES, LEAF, LEAF), F32),
             pltpu.VMEM((LEAVES, LEAF, LEAF), BF),
-            pltpu.SemaphoreType.DMA((26,)),
+            pltpu.SemaphoreType.DMA((28,)),
         ],
         compiler_params=pltpu.CompilerParams(vmem_limit_bytes=BIG),
         cost_estimate=pl.CostEstimate(flops=4_000_000_000, bytes_accessed=24_000_000, transcendentals=0),
@@ -831,7 +812,9 @@
     points = positions.reshape(LEAVES, 2, LEAF)
     basis = leaf_basis.reshape(LEAVES, RANK, LEAF)
     tree = transfer[0, 0]
-    listing = near_list.reshape(-1)
+    code_y, code_x = near_list // 5, near_list % 5
+    outer = (near_list >= 0) & ((code_y == 0) | (code_y == 4) | (code_x == 0) | (code_x == 4))
+    listing = jnp.max(jnp.where(outer, near_list, -1), axis=-1).reshape(-1)
     steps = gather_steps(wide, narrow)
     meta = window_slots(wide, narrow, steps)
 

time: 150 us -> 147 us (0.980)
  Pallas kernels: 89.3 us -> 86.5 us
where the time goes in v7:
time: 147 us; the launch traced here: 146 us
  Pallas kernels  86.5 us (59%)
  starting transfers between devices  36.4 us (25%)
  local copies, waits for them, and re-layouts  11.9 us (8%)
  waiting for transfers between devices  8.94 us (6%)
  other arithmetic  2.05 us (1%)
    pallas_call x3, Pallas kernels, near_own(): pl.pallas_call(body, out_shape=jax.ShapeDtypeStruct((leaves, LEAF, LEAF),...  30.4 us
    ppermute x10, starting transfers between devices, shift(): lax.ppermute(value, axis, [(i, i + steps) for i in range(count) if 0 <= i...  24.9 us
    pallas_call x2, Pallas kernels, edge_blocks(): pl.pallas_call(body, out_shape=jax.ShapeDtypeStruct((EDGES // 2 + 8, LEAF...  23.3 us
    pallas_call x1, Pallas kernels, finish(): pl.pallas_call(final_body, out_shape=jax.ShapeDtypeStruct((LEAVES, LEAF,...  12.1 us
    ppermute x5, starting transfers between devices, step(): lax.ppermute(value, axis, [(i, i ^ bit) for i in range(lax.axis_size(axis...  11.5 us
    pallas_call x1, Pallas kernels, local_far(): pl.pallas_call(local_body, out_shape=(jax.ShapeDtypeStruct((LEAVES, RANK,...  6.86 us
    pallas_call x1, Pallas kernels, top_far(): pl.pallas_call(top_body, out_shape=jax.ShapeDtypeStruct((LEAVES, RANK, LE...  6.24 us
    ppermute x10, waiting for transfers between devices, shift(): lax.ppermute(value, axis, [(i, i + steps) for i in range(count) if 0 <= i...  5.39 us
  transfers between devices with their start and end apart: 15, of which 2 were waited for; matrix products, arithmetic and copies ran while one was open for 6% of the time, Pallas kernels for 49%

profile of v7, /device:TPU:1, one launch (start us, length us, event | category | flops | bytes accessed | tf_op | source)
XLA Modules:
  0.0 146.4 jit_solution(13573195546553281418)
XLA Ops:
  0.0 3.1 %fusion.3 = (bf16[2,4,256,256]{3,2,1,0:T(8,128)(2,1)}, bf16[2,4,256,256]{3,2,1,0:T(8,128)(2,1)}) fusion(bf16[4,4,256,256]{3,2,1,0:T(8,128)(2,1)} %param.19), kind=kLoop, calls=%fused_computation.62 | loop fusion | bytes 4194304 | tf_op jit(solution)/shard_map/slice | solution.py:825
  3.1 2.0 %collective-permute-start.5 = (bf16[2,4,256,256]{3,2,1,0:T(8,128)(2,1)}, bf16[2,4,256,256]{3,2,1,0:T(8,128)(2,1)S(1)}, u32[]{:S(2)}, u32[]{:S(2)}) collective-permute-start(bf16[2,4,256,256]{3,2,1,0:T(8,128)(2,1)} %get-tuple-element.71), channel_id=1, source_target_pairs={{1,0},{2,1},{3,2},{5,4},{6,5},{7,6},{9,8},{10,9},{11,10},{13,12},{... | collective-permute-start | bytes 3145736 | tf_op jit(solution)/shard_map/ppermute | solution.py:119
  5.0 4.5 %collective-permute-start.4 = (bf16[2,4,256,256]{3,2,1,0:T(8,128)(2,1)}, bf16[2,4,256,256]{3,2,1,0:T(8,128)(2,1)}, u32[]{:S(2)}, u32[]{:S(2)}) collective-permute-start(bf16[2,4,256,256]{3,2,1,0:T(8,128)(2,1)} %get-tuple-element.72), channel_id=1, source_target_pairs={{0,1},{1,2},{2,3},{4,5},{5,6},{6,7},{8,9},{9,10},{10,11},{12,13},{... | collective-permute-start | bytes 3145736 | tf_op jit(solution)/shard_map/ppermute | solution.py:119
  9.5 4.6 %upward.1 = (bf16[816,256]{1,0:T(8,128)(2,1)}, bf16[816,256]{1,0:T(8,128)(2,1)}, bf16[816,256]{1,0:T(8,128)(2,1)}, bf16[816,256]{1,0:T(8,128)(2,1)}, bf16[1280,256]{1,0:T(8,128)(2,1)}, /*index=5*/bf16[80,256]{1,0:T(8,128)(2,1)}) custom-call(bf16[16,256,256]{2,1,0:T(8,128)(2,1)} %bitcast.21, bf16[16,64,256]{2,1,0:T(8,128)(2,1)} %bitcast.28, ...), custom_call_target="tpu_custom_call" | custom-call | flops 300000000 | bytes 5000000 | tf_op jit(solution)/shard_map/upward/pallas_call | solution.py:194
  14.1 1.3 collective-permute-start
  15.4 2.9 %collective-permute-start.2 = (bf16[816,256]{1,0:T(8,128)(2,1)}, bf16[816,256]{1,0:T(8,128)(2,1)}, u32[]{:S(2)}, u32[]{:S(2)}) collective-permute-start(bf16[816,256]{1,0:T(8,128)(2,1)} %get-tuple-element.40), channel_id=1, source_target_pairs={{0,4},{4,8},{8,12},{12,16},{16,20},{20,24},{24,28},{1,5},{5,9},{9,... | collective-permute-start | bytes 1253384 | tf_op jit(solution)/shard_map/ppermute | solution.py:119
  18.3 1.3 collective-permute-start.3
  20.3 9.1 %near_own.3.refs_4_.row0_any = f32[8,256,256]{2,1,0:T(8,128)} custom-call(bf16[80,256]{1,0:T(8,128)(2,1)} %get-tuple-element.38.after_ref, s32[52]{0:T(128)} %constant.222.clone.refs_0_, bf16[16,256,256]{2,1,0:T(8,128)(2,1)} %bitcast.22, f32[16,2,256]{2,1,0:T(2,128)} %bitcast.36, f32[16,1,256]{2,1,0:T(1,128)} %reshape.40.refs_3_), custom_call_target="tpu_custom_call" | custom-call | flops 6000000000 | bytes 4000000 | tf_op jit(solution)/shard_map/near_own/pallas_call | solution.py:570
  32.1 8.9 %near_own.4.refs_4_.row1_any = f32[8,256,256]{2,1,0:T(8,128)} custom-call(bf16[160,256]{1,0:T(8,128)(2,1)} %copy-done.7, s32[52]{0:T(128)} %constant.223.clone.refs_0_, bf16[16,256,256]{2,1,0:T(8,128)(2,1)} %bitcast.23, f32[16,2,256]{2,1,0:T(2,128)} %bitcast.37, f32[16,1,256]{2,1,0:T(1,128)} %reshape.40.refs_3_, f32[8,256,256]{2,1,0:T(8,128)} %near_own.3.refs_4_.row0_any), custom_call_target="tpu_custom_call" | custom-call | flops 6000000000 | bytes 4000000 | tf_op jit(solution)/shard_map/near_own/pallas_call | solution.py:570
  41.1 3.0 %join.1 = (bf16[1936,256]{1,0:T(8,128)(2,1)}, bf16[1936,256]{1,0:T(8,128)(2,1)}) custom-call(bf16[816,256]{1,0:T(8,128)(2,1)} %get-tuple-element.44.north_ref, bf16[816,256]{1,0:T(8,128)(2,1)} %get-tuple-element.45.south_ref, bf16[816,256]{1,0:T(8,128)(2,1)} %collective-permute-done.2.west_ref.west_any.refs_5_, ...), custom_call_target="tpu_custom_call" | custom-call | bytes 4000000 | tf_op jit(solution)/shard_map/join/pallas_call | solution.py:436
  44.1 3.0 %collective-permute-start.8 = (bf16[1936,256]{1,0:T(8,128)(2,1)}, bf16[1936,256]{1,0:T(8,128)(2,1)}, u32[]{:S(2)}, u32[]{:S(2)}) collective-permute-start(bf16[1936,256]{1,0:T(8,128)(2,1)} %get-tuple-element.49), channel_id=1, source_target_pairs={{0,1},{1,2},{2,3},{4,5},{5,6},{6,7},{8,9},{9,10},{10,11},{12,13},{... | collective-permute-start | bytes 2973704 | tf_op jit(solution)/shard_map/ppermute | solution.py:119
  47.1 2.2 %collective-permute-start.7 = (bf16[1936,256]{1,0:T(8,128)(2,1)}, bf16[1936,256]{1,0:T(8,128)(2,1)}, u32[]{:S(2)}, u32[]{:S(2)}) collective-permute-start(bf16[1936,256]{1,0:T(8,128)(2,1)} %get-tuple-element.48.after_ref), channel_id=1, source_target_pairs={{1,0},{2,1},{3,2},{5,4},{6,5},{7,6},{9,8},{10,9},{11,10},{13,12},{... | collective-permute-start | bytes 2973704 | tf_op jit(solution)/shard_map/ppermute | solution.py:119
  50.2 4.9 %collective-permute-start.6 = (bf16[320,256]{1,0:T(8,128)(2,1)S(1)}, bf16[320,256]{1,0:T(8,128)(2,1)S(1)}, u32[]{:S(2)}, u32[]{:S(2)}) collective-permute-start(bf16[320,256]{1,0:T(8,128)(2,1)S(1)} %pad_maximum_fusion.3), channel_id=1, source_target_pairs={{0,16},{4,20},{8,24},{12,28},{16,0},{20,4},{24,8},{28,12},{1,17},{... | collective-permute-start | bytes 491528 | tf_op jit(solution)/shard_map/ppermute | solution.py:831
  55.1 1.8 %collective-permute-start.11 = (bf16[4,2,256,256]{3,2,1,0:T(8,128)(2,1)S(1)}, bf16[4,2,256,256]{3,2,1,0:T(8,128)(2,1)S(1)}, u32[]{:S(2)}, u32[]{:S(2)}) collective-permute-start(bf16[4,2,256,256]{3,2,1,0:T(8,128)(2,1)S(1)} %get-tuple-element.58), channel_id=1, source_target_pairs={{0,4},{4,8},{8,12},{12,16},{16,20},{20,24},{24,28},{1,5},{5,9},{9,... | collective-permute-start | bytes 3145736 | tf_op jit(solution)/shard_map/ppermute | solution.py:119
  56.9 1.5 %collective-permute-start.12 = (bf16[4,2,256,256]{3,2,1,0:T(8,128)(2,1)S(1)}, bf16[4,2,256,256]{3,2,1,0:T(8,128)(2,1)S(1)}, u32[]{:S(2)}, u32[]{:S(2)}) collective-permute-start(bf16[4,2,256,256]{3,2,1,0:T(8,128)(2,1)S(1)} %get-tuple-element.59), channel_id=1, source_target_pairs={{4,0},{8,4},{12,8},{16,12},{20,16},{24,20},{28,24},{5,1},{9,5},{13... | collective-permute-start | bytes 3145736 | tf_op jit(solution)/shard_map/ppermute | solution.py:119
  58.4 12.4 %near_own.5.row2_any = f32[8,256,256]{2,1,0:T(8,128)} custom-call(bf16[1936,256]{1,0:T(8,128)(2,1)} %get-tuple-element.48.after_ref, s32[64]{0:T(128)} %constant.224.clone.refs_0_, bf16[16,256,256]{2,1,0:T(8,128)(2,1)} %bitcast.24, f32[16,2,256]{2,1,0:T(2,128)} %bitcast.38, f32[16,1,256]{2,1,0:T(1,128)} %reshape.40.refs_3_, ...), custom_call_target="tpu_custom_call" | custom-call | flops 6000000000 | bytes 4000000 | tf_op jit(solution)/shard_map/near_own/pallas_call | solution.py:570
  70.8 0.7 constant_dynamic-update-slice_fusion.10
  71.5 4.4 %collective-permute-start.9 = (bf16[640,256]{1,0:T(8,128)(2,1)S(1)}, bf16[640,256]{1,0:T(8,128)(2,1)S(1)}, u32[]{:S(2)}, u32[]{:S(2)}) collective-permute-start(bf16[640,256]{1,0:T(8,128)(2,1)S(1)} %pad_maximum_fusion.2), channel_id=1, source_target_pairs={{0,8},{4,12},{8,0},{12,4},{16,24},{20,28},{24,16},{28,20},{1,9},{5... | collective-permute-start | bytes 983048 | tf_op jit(solution)/shard_map/ppermute | solution.py:831
  76.0 6.9 %local_far.1 = (f32[16,64,256]{2,1,0:T(8,128)}, f32[256,256]{1,0:T(8,128)}) custom-call(s32[16]{0:T(128)} %reshape.36.list_ref.refs_0_, bf16[1280,256]{1,0:T(8,128)(2,1)} %get-tuple-element.52.coef_any, bf16[816,256]{1,0:T(8,128)(2,1)} %collective-permute-done.2.west_ref.west_any.refs_5_, bf16[816,256]{1,0:T(8,128)(2,1)} %collective-permute-done.3.east_ref.east_any.refs_6_, ...), custom_call_target="tpu_custom_call" | custom-call | flops 5000000000 | bytes 8000000 | tf_op jit(solution)/shard_map/local_far/pallas_call | solution.py:292
  82.8 11.7 %edge_blocks.2.refs_3_.upper_blocks_any = bf16[30,256,256]{2,1,0:T(8,128)(2,1)} custom-call(s32[16]{0:T(128)} %reshape.36.list_ref.refs_0_, s32[88]{0:T(128)} %constant.228.clone.refs_1_, s32[64]{0:T(128)} %constant.229.clone.refs_2_.slot_ref, f32[256,256]{1,0:T(8,128)} %get-tuple-element.55.refs_3_.sum1_any, f32[16,2,256]{2,1,0:T(2,128)} %bitcast.39, ...), custom_call_target="tpu_custom_call" | custom-call | flops 6000000000 | bytes 8000000 | tf_op jit(solution)/shard_map/edge_blocks/pallas_call | solution.py:684
  94.5 0.7 constant_dynamic-update-slice_fusion.9
  95.2 0.8 constant_dynamic-update-slice_fusion.8
  96.4 11.6 %edge_blocks.3.lower_blocks_any = bf16[30,256,256]{2,1,0:T(8,128)(2,1)} custom-call(s32[16]{0:T(128)} %reshape.36.list_ref.refs_0_, s32[88]{0:T(128)} %constant.230.clone.refs_1_, s32[64]{0:T(128)} %constant.229.clone.refs_2_.slot_ref, bf16[30,256,256]{2,1,0:T(8,128)(2,1)} %edge_blocks.2.refs_3_.upper_blocks_any, f32[16,2,256]{2,1,0:T(2,128)} %bitcast.40, ...), custom_call_target="tpu_custom_call" | custom-call | flops 6000000000 | bytes 8000000 | tf_op jit(solution)/shard_map/edge_blocks/pallas_call | solution.py:684
  108.1 3.5 %collective-permute-done.10 = bf16[1280,256]{1,0:T(8,128)(2,1)} collective-permute-done((bf16[1280,256]{1,0:T(8,128)(2,1)S(1)}, bf16[1280,256]{1,0:T(8,128)(2,1)}, u32[]{:S(2)}, u32[]{:S(2)}) %collective-permute-start.10) | collective-permute-done | bytes 655392 | tf_op jit(solution)/shard_map/ppermute | solution.py:831
  111.9 3.8 %collective-permute-start.13 = (bf16[2,2,2,256,256]{4,3,2,1,0:T(8,128)(2,1)S(1)}, bf16[2,2,2,256,256]{4,3,2,1,0:T(8,128)(2,1)S(1)}, u32[]{:S(2)}, u32[]{:S(2)}) collective-permute-start(bf16[2,2,2,256,256]{4,3,2,1,0:T(8,128)(2,1)S(1)} %pad_maximum_fusion), channel_id=1, source_target_pairs={{0,1},{1,2},{2,3},{4,5},{5,6},{6,7},{8,9},{9,10},{10,11},{12,13},{... | collective-permute-start | bytes 3145736 | tf_op jit(solution)/shard_map/ppermute | solution.py:119
  115.8 1.1 pad_maximum_fusion.1
  116.9 1.9 %collective-permute-start.14 = (bf16[2,2,2,256,256]{4,3,2,1,0:T(8,128)(2,1)}, bf16[2,2,2,256,256]{4,3,2,1,0:T(8,128)(2,1)S(1)}, u32[]{:S(2)}, u32[]{:S(2)}) collective-permute-start(bf16[2,2,2,256,256]{4,3,2,1,0:T(8,128)(2,1)} %pad_maximum_fusion.1), channel_id=1, source_target_pairs={{1,0},{2,1},{3,2},{5,4},{6,5},{7,6},{9,8},{10,9},{11,10},{13,12},{... | collective-permute-start | bytes 3145736 | tf_op jit(solution)/shard_map/ppermute | solution.py:119
  119.6 2.0 %constant_dynamic-update-slice_fusion.7.all_any = bf16[2560,256]{1,0:T(8,128)(2,1)} fusion(bf16[2560,256]{1,0:T(8,128)(2,1)} %get-tuple-element.79, bf16[1280,256]{1,0:T(8,128)(2,1)} %collective-permute-done.10), kind=kLoop, calls=%fused_computation.15 | loop fusion | bytes 1310720 | tf_op jit(solution)/shard_map/concatenate | solution.py:869
  121.5 6.2 %top_far.1.field_ref = bf16[16,64,256]{2,1,0:T(8,128)(2,1)} custom-call(s32[74]{0:T(128)} %pad_add_fusion.meta_ref, bf16[2560,256]{1,0:T(8,128)(2,1)} %constant_dynamic-update-slice_fusion.7.all_any, bf16[256,2304]{1,0:T(8,128)(2,1)} %constant.231.clone.c2_any, bf16[256,2304]{1,0:T(8,128)(2,1)} %constant.232.clone.c3_any, bf16[21,64,64]{2,1,0:T(8,128)(2,1)} %bitcast.34, ...), custom_call_target="tpu_custom_call" | custom-call | flops 3000000000 | bytes 5000000 | tf_op jit(solution)/shard_map/top_far/pallas_call | solution.py:388
  127.8 5.4 %collective-permute-done.14 = bf16[2,2,2,256,256]{4,3,2,1,0:T(8,128)(2,1)S(1)} collective-permute-done((bf16[2,2,2,256,256]{4,3,2,1,0:T(8,128)(2,1)}, bf16[2,2,2,256,256]{4,3,2,1,0:T(8,128)(2,1)S(1)}, u32[]{:S(2)}, u32[]{:S(2)}) %collective-permute-start.14) | collective-permute-done | bytes 1048608 | tf_op jit(solution)/shard_map/ppermute | solution.py:119
  133.2 1.0 copy-done.5
  134.2 12.1 %finish.1 = bf16[16,256,256]{2,1,0:T(8,128)(2,1)} custom-call(s32[16]{0:T(128)} %reshape.36.list_ref.refs_0_, s32[64]{0:T(128)} %constant.229.clone.refs_2_.slot_ref, bf16[16,256,256]{2,1,0:T(8,128)(2,1)} %bitcast.25, bf16[8,256,256]{2,1,0:T(8,128)(2,1)} %bitcast.26, bf16[8,256,256]{2,1,0:T(8,128)(2,1)} %bitcast.27, bf16[8,256,256]{2,1,0:T(8,128)(2,1)} %bitcast.6.north_any, ...), custom_call_target="tpu_custom_call" | custom-call | flops 4000000000 | bytes 24000000 | tf_op jit(solution)/shard_map/finish/pallas_call | solution.py:771
  (52 shorter events, 5.6 us)
Async XLA Ops:
  3.1 38.0 %collective-permute-start.5 = (bf16[2,4,256,256]{3,2,1,0:T(8,128)(2,1)}, bf16[2,4,256,256]{3,2,1,0:T(8,128)(2,1)S(1)}, u32[]{:S(2)}, u32[]{:S(2)}) collective-permute-start(bf16[2,4,256,256]{3,2,1,0:T(8,128)(2,1)} %get-tuple-element.71), channel_id=1, source_target_pairs={{1,0},{2,1},{3,2},{5,4},{6,5},{7,6},{9,8},{10,9},{11,10},{13,12},{... | collective-permute-start | bytes 3145736 | tf_op jit(solution)/shard_map/ppermute | solution.py:119
  5.0 36.1 %collective-permute-start.4 = (bf16[2,4,256,256]{3,2,1,0:T(8,128)(2,1)}, bf16[2,4,256,256]{3,2,1,0:T(8,128)(2,1)}, u32[]{:S(2)}, u32[]{:S(2)}) collective-permute-start(bf16[2,4,256,256]{3,2,1,0:T(8,128)(2,1)} %get-tuple-element.72), channel_id=1, source_target_pairs={{0,1},{1,2},{2,3},{4,5},{5,6},{6,7},{8,9},{9,10},{10,11},{12,13},{... | collective-permute-start | bytes 3145736 | tf_op jit(solution)/shard_map/ppermute | solution.py:119
  9.5 10.1 %copy-start.8 = (f32[4,4,256]{2,1,0:T(4,128)S(1)}, f32[4,4,256]{2,1,0:T(4,128)}, u32[]{:S(2)}) copy-start(f32[4,4,256]{2,1,0:T(4,128)} %param.21) | copy-start | bytes 49156
  14.1 16.6 %collective-permute-start = (bf16[80,256]{1,0:T(8,128)(2,1)}, bf16[80,256]{1,0:T(8,128)(2,1)S(1)}, u32[]{:S(2)}, u32[]{:S(2)}) collective-permute-start(bf16[80,256]{1,0:T(8,128)(2,1)} %get-tuple-element.38.after_ref), channel_id=1, source_target_pairs={{0,4},{4,0},{8,12},{12,8},{16,20},{20,16},{24,28},{28,24},{1,5},{5... | collective-permute-start | bytes 122888 | tf_op jit(solution)/shard_map/ppermute | solution.py:831
  15.4 25.6 %collective-permute-start.2 = (bf16[816,256]{1,0:T(8,128)(2,1)}, bf16[816,256]{1,0:T(8,128)(2,1)}, u32[]{:S(2)}, u32[]{:S(2)}) collective-permute-start(bf16[816,256]{1,0:T(8,128)(2,1)} %get-tuple-element.40), channel_id=1, source_target_pairs={{0,4},{4,8},{8,12},{12,16},{16,20},{20,24},{24,28},{1,5},{5,9},{9,... | collective-permute-start | bytes 1253384 | tf_op jit(solution)/shard_map/ppermute | solution.py:119
  18.3 22.7 %collective-permute-start.3 = (bf16[816,256]{1,0:T(8,128)(2,1)}, bf16[816,256]{1,0:T(8,128)(2,1)}, u32[]{:S(2)}, u32[]{:S(2)}) collective-permute-start(bf16[816,256]{1,0:T(8,128)(2,1)} %get-tuple-element.41), channel_id=1, source_target_pairs={{4,0},{8,4},{12,8},{16,12},{20,16},{24,20},{28,24},{5,1},{9,5},{13... | collective-permute-start | bytes 1253384 | tf_op jit(solution)/shard_map/ppermute | solution.py:119
  20.2 9.1 %copy-start = (bf16[4,4,256,256]{3,2,1,0:T(8,128)(2,1)S(1)}, bf16[4,4,256,256]{3,2,1,0:T(8,128)(2,1)}, u32[]{:S(2)}) copy-start(bf16[4,4,256,256]{3,2,1,0:T(8,128)(2,1)} %param.19) | copy-start | bytes 6291460
  29.4 0.8 copy-start.6
  31.4 0.6 copy-start.7
  31.4 9.6 %collective-permute-start.1 = (bf16[160,256]{1,0:T(8,128)(2,1)S(1)}, bf16[160,256]{1,0:T(8,128)(2,1)S(1)}, u32[]{:S(2)}, u32[]{:S(2)}) collective-permute-start(bf16[160,256]{1,0:T(8,128)(2,1)S(1)} %get-tuple-element.87.after_ref), channel_id=1, source_target_pairs={{0,1},{1,0},{2,3},{3,2},{4,5},{5,4},{6,7},{7,6},{8,9},{9,8},{10,11... | collective-permute-start | bytes 245768 | tf_op jit(solution)/shard_map/ppermute | solution.py:831
  41.0 8.4 %copy-start.9 = (s32[4,4,10]{2,1,0:T(4,128)S(1)}, s32[4,4,10]{2,1,0:T(4,128)}, u32[]{:S(2)}) copy-start(s32[4,4,10]{2,1,0:T(4,128)} %param.24) | copy-start | bytes 1924
  41.1 29.7 %copy-start.3 = (bf16[2,4,256,256]{3,2,1,0:T(8,128)(2,1)}, bf16[2,4,256,256]{3,2,1,0:T(8,128)(2,1)S(1)}, u32[]{:S(2)}) copy-start(bf16[2,4,256,256]{3,2,1,0:T(8,128)(2,1)S(1)} %collective-permute-done.5) | copy-start | bytes 3145732
  44.1 27.4 %collective-permute-start.8 = (bf16[1936,256]{1,0:T(8,128)(2,1)}, bf16[1936,256]{1,0:T(8,128)(2,1)}, u32[]{:S(2)}, u32[]{:S(2)}) collective-permute-start(bf16[1936,256]{1,0:T(8,128)(2,1)} %get-tuple-element.49), channel_id=1, source_target_pairs={{0,1},{1,2},{2,3},{4,5},{5,6},{6,7},{8,9},{9,10},{10,11},{12,13},{... | collective-permute-start | bytes 2973704 | tf_op jit(solution)/shard_map/ppermute | solution.py:119
  47.1 24.4 %collective-permute-start.7 = (bf16[1936,256]{1,0:T(8,128)(2,1)}, bf16[1936,256]{1,0:T(8,128)(2,1)}, u32[]{:S(2)}, u32[]{:S(2)}) collective-permute-start(bf16[1936,256]{1,0:T(8,128)(2,1)} %get-tuple-element.48.after_ref), channel_id=1, source_target_pairs={{1,0},{2,1},{3,2},{5,4},{6,5},{7,6},{9,8},{10,9},{11,10},{13,12},{... | collective-permute-start | bytes 2973704 | tf_op jit(solution)/shard_map/ppermute | solution.py:119
  50.2 21.3 %collective-permute-start.6 = (bf16[320,256]{1,0:T(8,128)(2,1)S(1)}, bf16[320,256]{1,0:T(8,128)(2,1)S(1)}, u32[]{:S(2)}, u32[]{:S(2)}) collective-permute-start(bf16[320,256]{1,0:T(8,128)(2,1)S(1)} %pad_maximum_fusion.3), channel_id=1, source_target_pairs={{0,16},{4,20},{8,24},{12,28},{16,0},{20,4},{24,8},{28,12},{1,17},{... | collective-permute-start | bytes 491528 | tf_op jit(solution)/shard_map/ppermute | solution.py:831
  55.1 52.9 %collective-permute-start.11 = (bf16[4,2,256,256]{3,2,1,0:T(8,128)(2,1)S(1)}, bf16[4,2,256,256]{3,2,1,0:T(8,128)(2,1)S(1)}, u32[]{:S(2)}, u32[]{:S(2)}) collective-permute-start(bf16[4,2,256,256]{3,2,1,0:T(8,128)(2,1)S(1)} %get-tuple-element.58), channel_id=1, source_target_pairs={{0,4},{4,8},{8,12},{12,16},{16,20},{20,24},{24,28},{1,5},{5,9},{9,... | collective-permute-start | bytes 3145736 | tf_op jit(solution)/shard_map/ppermute | solution.py:119
  56.9 51.1 %collective-permute-start.12 = (bf16[4,2,256,256]{3,2,1,0:T(8,128)(2,1)S(1)}, bf16[4,2,256,256]{3,2,1,0:T(8,128)(2,1)S(1)}, u32[]{:S(2)}, u32[]{:S(2)}) collective-permute-start(bf16[4,2,256,256]{3,2,1,0:T(8,128)(2,1)S(1)} %get-tuple-element.59), channel_id=1, source_target_pairs={{4,0},{8,4},{12,8},{16,12},{20,16},{24,20},{28,24},{5,1},{9,5},{13... | collective-permute-start | bytes 3145736 | tf_op jit(solution)/shard_map/ppermute | solution.py:119
  71.5 23.7 %collective-permute-start.9 = (bf16[640,256]{1,0:T(8,128)(2,1)S(1)}, bf16[640,256]{1,0:T(8,128)(2,1)S(1)}, u32[]{:S(2)}, u32[]{:S(2)}) collective-permute-start(bf16[640,256]{1,0:T(8,128)(2,1)S(1)} %pad_maximum_fusion.2), channel_id=1, source_target_pairs={{0,8},{4,12},{8,0},{12,4},{16,24},{20,28},{24,16},{28,20},{1,9},{5... | collective-permute-start | bytes 983048 | tf_op jit(solution)/shard_map/ppermute | solution.py:831
  82.8 11.7 %copy-start.10 = (bf16[1280,256]{1,0:T(8,128)(2,1)S(1)}, bf16[1280,256]{1,0:T(8,128)(2,1)}, u32[]{:S(2)}) copy-start(bf16[1280,256]{1,0:T(8,128)(2,1)} %get-tuple-element.84) | copy-start | bytes 1966084
  96.0 15.6 %collective-permute-start.10 = (bf16[1280,256]{1,0:T(8,128)(2,1)S(1)}, bf16[1280,256]{1,0:T(8,128)(2,1)}, u32[]{:S(2)}, u32[]{:S(2)}) collective-permute-start(bf16[1280,256]{1,0:T(8,128)(2,1)S(1)} %get-tuple-element.80), channel_id=1, source_target_pairs={{0,2},{1,3},{2,0},{3,1},{4,6},{5,7},{6,4},{7,5},{8,10},{9,11},{10,... | collective-permute-start | bytes 1966088 | tf_op jit(solution)/shard_map/ppermute | solution.py:831
  108.0 3.8 %copy-start.1 = (bf16[4,2,256,256]{3,2,1,0:T(8,128)(2,1)}, bf16[4,2,256,256]{3,2,1,0:T(8,128)(2,1)S(1)}, u32[]{:S(2)}) copy-start(bf16[4,2,256,256]{3,2,1,0:T(8,128)(2,1)S(1)} %collective-permute-done.11) | copy-start | bytes 3145732
  108.1 3.7 %copy-start.2 = (bf16[4,2,256,256]{3,2,1,0:T(8,128)(2,1)}, bf16[4,2,256,256]{3,2,1,0:T(8,128)(2,1)S(1)}, u32[]{:S(2)}) copy-start(bf16[4,2,256,256]{3,2,1,0:T(8,128)(2,1)S(1)} %collective-permute-done.12) | copy-start | bytes 3145732
  111.9 7.0 %copy-start.11 = (s32[36]{0:T(128)S(1)}, s32[36]{0:T(128)}, u32[]{:S(2)}) copy-start(s32[36]{0:T(128)} %constant.221.clone) | copy-start | bytes 436
  111.9 7.0 %copy-start.12 = (s32[36]{0:T(128)S(1)}, s32[36]{0:T(128)}, u32[]{:S(2)}) copy-start(s32[36]{0:T(128)} %constant.220.clone) | copy-start | bytes 436
  111.9 15.8 %collective-permute-start.13 = (bf16[2,2,2,256,256]{4,3,2,1,0:T(8,128)(2,1)S(1)}, bf16[2,2,2,256,256]{4,3,2,1,0:T(8,128)(2,1)S(1)}, u32[]{:S(2)}, u32[]{:S(2)}) collective-permute-start(bf16[2,2,2,256,256]{4,3,2,1,0:T(8,128)(2,1)S(1)} %pad_maximum_fusion), channel_id=1, source_target_pairs={{0,1},{1,2},{2,3},{4,5},{5,6},{6,7},{8,9},{9,10},{10,11},{12,13},{... | collective-permute-start | bytes 3145736 | tf_op jit(solution)/shard_map/ppermute | solution.py:119
  116.9 16.3 %collective-permute-start.14 = (bf16[2,2,2,256,256]{4,3,2,1,0:T(8,128)(2,1)}, bf16[2,2,2,256,256]{4,3,2,1,0:T(8,128)(2,1)S(1)}, u32[]{:S(2)}, u32[]{:S(2)}) collective-permute-start(bf16[2,2,2,256,256]{4,3,2,1,0:T(8,128)(2,1)} %pad_maximum_fusion.1), channel_id=1, source_target_pairs={{1,0},{2,1},{3,2},{5,4},{6,5},{7,6},{9,8},{10,9},{11,10},{13,12},{... | collective-permute-start | bytes 3145736 | tf_op jit(solution)/shard_map/ppermute | solution.py:119
  127.8 5.4 %copy-start.4 = (bf16[2,2,2,256,256]{4,3,2,1,0:T(8,128)(2,1)}, bf16[2,2,2,256,256]{4,3,2,1,0:T(8,128)(2,1)S(1)}, u32[]{:S(2)}) copy-start(bf16[2,2,2,256,256]{4,3,2,1,0:T(8,128)(2,1)S(1)} %collective-permute-done.13) | copy-start | bytes 3145732
  133.2 1.0 copy-start.5

commit v8 on v7

--- a/solution.py
+++ b/solution.py
@@ -128,7 +128,8 @@
 
 
 def up_body(
-    q_any, basis_any, tree_any, pos_ref, east_ref, west_ref, north_ref, south_ref, coef_ref, give_ref, q_ref, basis_ref, tree_ref, sems
+    q_any, basis_any, tree_any, pos_ref, east_ref, west_ref, north_ref, south_ref, coef_ref, give_ref, to_east, to_west, to_north, to_south,
+    q_ref, basis_ref, tree_ref, sems
 ):
     loads = []
     for k in range(4):
@@ -138,11 +139,19 @@
     loads.append(pltpu.make_async_copy(tree_any, tree_ref, sems.at[8]))
     for load in loads:
         load.start()
+    backs = []
     level0 = []
     for leaf in range(LEAVES):
         if leaf % 4 == 0:
             loads[leaf // 2].wait()
             loads[leaf // 2 + 1].wait()
+            half = pl.ds(leaf // 2, 2)
+            for to, low in ((to_west, leaf), (to_east, leaf + 2)):
+                backs.append(pltpu.make_async_copy(q_ref.at[pl.ds(low, 2)], to.at[half], sems.at[9 + len(backs)]))
+                backs[-1].start()
+            to, row = (to_north, leaf) if leaf < 8 else (to_south, leaf - 8)
+            backs.append(pltpu.make_async_copy(q_ref.at[pl.ds(leaf, 4)], to.at[pl.ds(row, 4)], sems.at[9 + len(backs)]))
+            backs[-1].start()
         coef = dot(basis_ref[leaf], q_ref[leaf]).astype(BF)
         level0.append(coef)
         r, c = leaf // SIDE, leaf % SIDE
@@ -186,6 +195,8 @@
             at = 12 * RANK + 16 * part
             ref[at : at + 16] = held
             rest = rest - held.astype(F32)
+    for back in backs:
+        back.wait()
 
 
 def go_up(q, basis, tree, points):
@@ -200,14 +211,15 @@
             side,
             jax.ShapeDtypeStruct(((LEAVES + 4) * RANK, LEAF), BF),
             jax.ShapeDtypeStruct((PACK, LEAF), BF),
-        ),
+        )
+        + (jax.ShapeDtypeStruct((8, LEAF, LEAF), BF),) * 4,
         in_specs=[pl.BlockSpec(memory_space=pl.ANY)] * 3 + [vmem],
-        out_specs=[vmem] * 6,
+        out_specs=[vmem] * 6 + [pl.BlockSpec(memory_space=pl.ANY)] * 4,
         scratch_shapes=[
             pltpu.VMEM((LEAVES, LEAF, LEAF), BF),
             pltpu.VMEM((LEAVES, RANK, LEAF), BF),
             pltpu.VMEM((TOP + 1, RANK, RANK), BF),
-            pltpu.SemaphoreType.DMA((9,)),
+            pltpu.SemaphoreType.DMA((21,)),
         ],
         compiler_params=pltpu.CompilerParams(vmem_limit_bytes=BIG),
         cost_estimate=pl.CostEstimate(flops=300_000_000, bytes_accessed=5_000_000, transcendentals=0),
@@ -322,10 +334,10 @@
 
 
 def top_body(
-    meta_ref, all_any, c2_any, c3_any, tree_any, sum0_any, sum1_any, field_ref, win, parents, c2_ref, c3_ref, all_ref, tree_ref, sum0, sum1, sems
+    meta_ref, mine_any, other_any, c2_any, c3_any, tree_any, sum0_any, sum1_any, field_ref, win, parents, c2_ref, c3_ref, all_ref, tree_ref, sum0, sum1, sems
 ):
     loads = []
-    for k, (source, to) in enumerate(((all_any, all_ref), (tree_any, tree_ref), (sum1_any, sum1), (sum0_any, sum0))):
+    for k, (source, to) in enumerate(((mine_any, all_ref.at[pl.ds(0, mine_any.shape[0])]), (other_any, all_ref.at[pl.ds(mine_any.shape[0], mine_any.shape[0])]), (tree_any, tree_ref), (sum1_any, sum1), (sum0_any, sum0))):
         loads.append(pltpu.make_async_copy(source, to, sems.at[2 + k]))
         loads[-1].start()
 
@@ -338,6 +350,7 @@
     slabs = [slab(c2_any, c2_ref, 0), slab(c3_any, c3_ref, 1)]
 
     loads[0].wait()
+    loads[1].wait()
 
     def lift(group, carry):
         total = jnp.zeros((RANK, LEAF), F32)
@@ -363,7 +376,7 @@
     field3 = dot(c3_ref[...], win[...]).astype(BF)
     fill(0, all_ref, PACK)
     slabs[0].wait()
-    for load in loads[1:]:
+    for load in loads[2:]:
         load.wait()
     field2 = (dot(c2_ref[...], win[...]) + dot_first(tree_ref[TOP], field3)).astype(BF)
     field1 = []
@@ -380,31 +393,32 @@
     return list_ref[leaf]
 
 
-def top_far(meta, gathered, tree, sum0, sum1):
+def top_far(meta, mine, other, tree, sum0, sum1):
     vmem = pl.BlockSpec(memory_space=pltpu.VMEM)
     smem = pl.BlockSpec(memory_space=pltpu.SMEM)
     anywhere = pl.BlockSpec(memory_space=pl.ANY)
-    devices = gathered.shape[0] // PACK
+    rows = 2 * mine.shape[0]
+    devices = rows // PACK
     return pl.pallas_call(
         top_body,
         out_shape=jax.ShapeDtypeStruct((LEAVES, RANK, LEAF), BF),
-        in_specs=[smem] + [anywhere] * 6,
+        in_specs=[smem] + [anywhere] * 7,
         out_specs=vmem,
         scratch_shapes=[
             pltpu.VMEM((WINDOW * RANK, LEAF), BF),
             pltpu.VMEM((devices // 4 * RANK, LEAF), BF),
             pltpu.VMEM((RANK, WINDOW * RANK), BF),
             pltpu.VMEM((RANK, WINDOW * RANK), BF),
-            pltpu.VMEM(gathered.shape, BF),
+            pltpu.VMEM((rows, LEAF), BF),
             pltpu.VMEM((TOP + 1, RANK, RANK), BF),
             pltpu.VMEM((LEAVES, RANK, LEAF), F32),
             pltpu.VMEM((4 * RANK, LEAF), F32),
-            pltpu.SemaphoreType.DMA((6,)),
+            pltpu.SemaphoreType.DMA((7,)),
         ],
         compiler_params=pltpu.CompilerParams(vmem_limit_bytes=BIG),
         cost_estimate=pl.CostEstimate(flops=3_000_000_000, bytes_accessed=5_000_000, transcendentals=0),
         name="top_far",
-    )(meta, gathered, jnp.asarray(window_coupling(2)), jnp.asarray(window_coupling(3)), tree, sum0, sum1)
+    )(meta, mine, other, jnp.asarray(window_coupling(2)), jnp.asarray(window_coupling(3)), tree, sum0, sum1)
 
 
 def join_body(north_ref, south_ref, west_ref, east_ref, north_any, south_any, to_north, to_south, sems):
@@ -482,6 +496,17 @@
     spread_columns(rows, columns.at[leaf])
 
 
+def repeat(count, at_once, step):
+    def several(i, carry):
+        for k in range(at_once):
+            step(i * at_once + k)
+        return carry
+
+    lax.fori_loop(0, count // at_once, several, 0)
+    for i in range(count // at_once * at_once, count):
+        step(i)
+
+
 def own_pairs(first, last):
     pairs = []
     for r in range(first, last):
@@ -510,29 +535,37 @@
     lax.fori_loop(start, start + count, turn, 0)
     zero = jnp.int32(0)
 
-    def selves(i, carry):
-        for half in range(2):
-            leaf = start + 2 * i + half
-            block_into(blocks.at[2 * i + half], columns.at[leaf], pos_ref[leaf], zero, zero)
-        return carry
-
-    lax.fori_loop(0, count // 2, selves, 0)
+    def single(i):
+        block_into(blocks.at[i], columns.at[start + i], pos_ref[start + i], zero, zero)
+
+    repeat(count, 4, single)
+
+    def turned(i):
+        blocks[count + 2 * i + 1] = blocks[count + 2 * i].T
 
     def pair(i):
         at = 4 * i
         place = count + 2 * i
         target, source = table_ref[at], table_ref[at + 1]
         block_into(blocks.at[place], columns.at[target], pos_ref[source], table_ref[at + 2], table_ref[at + 3])
-        blocks[place + 1] = blocks[place].T
-
-    def both(i, carry):
-        pair(2 * i)
-        pair(2 * i + 1)
+
+    for i in range(4):
+        pair(i)
+
+    def four(i, carry):
+        for k in range(4):
+            turned(4 * i + k - 4)
+        for k in range(4):
+            pair(4 * i + k)
         return carry
 
-    lax.fori_loop(0, len(pairs) // 2, both, 0)
-    if len(pairs) % 2:
-        pair(len(pairs) - 1)
+    steps = len(pairs) // 4
+    lax.fori_loop(1, steps, four, 0)
+    for i in range(4 * steps - 4, 4 * steps):
+        turned(i)
+    for i in range(4 * steps, len(pairs)):
+        pair(i)
+        turned(i)
     for load in loads:
         load.wait()
     parts = {leaf: [(leaf - start, leaf)] for leaf in range(start, start + count)}
@@ -639,33 +672,28 @@
         for i in range(count):
             points[slots[k] + i] = whole[2 * (first + i) : 2 * (first + i) + 2]
 
-    def fixed(i, carry):
-        for half in range(2):
-            at = 8 * i + 4 * half
-            block_into(
-                out_ref.at[2 * i + half],
-                columns.at[table_ref[at]],
-                points[table_ref[at + 1]],
-                table_ref[at + 2],
-                table_ref[at + 3],
-            )
-        return carry
-
-    lax.fori_loop(0, EDGES // 4, fixed, 0)
+    def fixed(i):
+        at = 4 * i
+        block_into(
+            out_ref.at[i],
+            columns.at[table_ref[at]],
+            points[table_ref[at + 1]],
+            table_ref[at + 2],
+            table_ref[at + 3],
+        )
+
+    repeat(EDGES // 2, 4, fixed)
     backs = []
     for k, part in enumerate((pl.ds(0, EDGES // 2), pl.ds(EDGES // 2, 8))):
         backs.append(pltpu.make_async_copy(out_ref.at[part], out_any.at[part], sems.at[8 + k]))
     backs[0].start()
 
-    def extra(i, carry):
-        for half in range(2):
-            leaf = start + 2 * i + half
-            code, slot = extra_of(list_ref, slot_ref, leaf)
-            code = jnp.maximum(code, 0)
-            block_into(out_ref.at[EDGES // 2 + 2 * i + half], columns.at[leaf], points[slot], code // 5 - 2, code % 5 - 2)
-        return carry
-
-    lax.fori_loop(0, 4, extra, 0)
+    def extra(i):
+        code, slot = extra_of(list_ref, slot_ref, start + i)
+        code = jnp.maximum(code, 0)
+        block_into(out_ref.at[EDGES // 2 + i], columns.at[start + i], points[slot], code // 5 - 2, code % 5 - 2)
+
+    repeat(8, 4, extra)
     backs[1].start()
     for back in backs:
         back.wait()
@@ -818,11 +846,11 @@
     steps = gather_steps(wide, narrow)
     meta = window_slots(wide, narrow, steps)
 
-    east, west, north, south, coefs, give = go_up(q, basis, tree, points)
+    east, west, north, south, coefs, give, to_east, to_west, q_up, q_down = go_up(q, basis, tree, points)
     from_west = shift(east, "wide", 1)
     from_east = shift(west, "wide", -1)
-    q_north = shift(charges[2:4], "narrow", 1)
-    q_south = shift(charges[0:2], "narrow", -1)
+    q_north = shift(q_down, "narrow", 1)
+    q_south = shift(q_up, "narrow", -1)
 
     noise_rows = noise.reshape(LEAVES, 1, LEAF)
 
@@ -840,7 +868,6 @@
     gathered = jnp.concatenate([gathered, other], axis=0)
     other = step(gathered, 1)
     row1 = near_own(1, 2, q, points, noise_rows, gathered, [row0])
-    to_east, to_west = charges[:, 2:4], charges[:, 0:2]
     other, from_west, from_east, row1, to_east, to_west, q_north, q_south = tie(
         other, from_west, from_east, row1, to_east, to_west, q_north, q_south
     )
@@ -864,10 +891,9 @@
         if at == 4:
             lower_blocks = edge_blocks(1, listing, upper_blocks, points, from_west, from_east, from_north, from_south)
             other, lower_blocks, q_west, q_east = tie(other, lower_blocks, q_west, q_east)
-            q_north_corner = shift(jnp.stack([q_west[2:4], q_east[2:4]]), "narrow", 1)
-            q_south_corner = shift(jnp.stack([q_west[0:2], q_east[0:2]]), "narrow", -1)
-    gathered = jnp.concatenate([gathered, other], axis=0)
-    field = top_far(meta, gathered, tree, *sums)
+            q_north_corner = shift(jnp.stack([q_west[4:8], q_east[4:8]]), "narrow", 1)
+            q_south_corner = shift(jnp.stack([q_west[0:4], q_east[0:4]]), "narrow", -1)
+    field = top_far(meta, gathered, other, tree, *sums)
     q_north_corner, q_south_corner, field = tie(q_north_corner, q_south_corner, field)
     halos = [
         value.reshape(8, LEAF, LEAF)

time: 147 us -> 140 us (0.952)
  local copies, waits for them, and re-layouts: 11.9 us -> 5.49 us
    slice x2 -> x0, local copies, waits for them, and re-layouts: 3.26 us -> none  [the longest x1 3.07 us: per_device(): q_south = shift(charges[0:2], 'narrow', -1)]
    pallas_call x3, Pallas kernels: 30.4 us -> 28.6 us  [near_own(): pl.pallas_call(body, out_shape=jax.ShapeDtypeStruct((leaves, LEAF, LEAF),...]
    unnamed x31 -> x35, local copies, waits for them, and re-layouts: 5.22 us -> 3.47 us
  transfers between devices with their start and end apart: 15 -> 15, of which waited for: 2 -> 4; matrix products, arithmetic and copies ran while one was open for 6% -> 3% of each run, Pallas kernels for 49% -> 47%
where the time goes in v8:
time: 140 us
  Pallas kernels  85.8 us (61%)
  starting transfers between devices  36.4 us (26%)
  waiting for transfers between devices  9.21 us (7%)
  local copies, waits for them, and re-layouts  5.49 us (4%)
  other arithmetic  2 us (1%)
    pallas_call x3, Pallas kernels, near_own(): pl.pallas_call(body, out_shape=jax.ShapeDtypeStruct((leaves, LEAF, LEAF),...  28.6 us
    ppermute x10, starting transfers between devices, shift(): lax.ppermute(value, axis, [(i, i + steps) for i in range(count) if 0 <= i...  24.3 us
    pallas_call x2, Pallas kernels, edge_blocks(): pl.pallas_call(body, out_shape=jax.ShapeDtypeStruct((EDGES // 2 + 8, LEAF...  22.9 us
    pallas_call x1, Pallas kernels, finish(): pl.pallas_call(final_body, out_shape=jax.ShapeDtypeStruct((LEAVES, LEAF,...  12.7 us
    ppermute x5, starting transfers between devices, step(): lax.ppermute(value, axis, [(i, i ^ bit) for i in range(lax.axis_size(axis...  12.1 us
    pallas_call x1, Pallas kernels, local_far(): pl.pallas_call(local_body, out_shape=(jax.ShapeDtypeStruct((LEAVES, RANK,...  7.22 us
    pallas_call x1, Pallas kernels, top_far(): pl.pallas_call(top_body, out_shape=jax.ShapeDtypeStruct((LEAVES, RANK, LE...  6.23 us
    pallas_call x1, Pallas kernels, go_up(): pl.pallas_call(up_body, out_shape=(side, side, side, side, jax.ShapeDtype...  5.59 us
  transfers between devices with their start and end apart: 15, of which 4 were waited for; matrix products, arithmetic and copies ran while one was open for 3% of the time, Pallas kernels for 47%

profile of v8, /device:TPU:1, one launch (start us, length us, event | category | flops | bytes accessed | tf_op | source)
XLA Modules:
  0.0 139.6 jit_solution(1104624832817511887)
XLA Ops:
  0.0 5.6 %upward.1 = (bf16[816,256]{1,0:T(8,128)(2,1)}, bf16[816,256]{1,0:T(8,128)(2,1)}, bf16[816,256]{1,0:T(8,128)(2,1)}, bf16[816,256]{1,0:T(8,128)(2,1)}, bf16[1280,2...) custom-call(bf16[16,256,256]{2,1,0:T(8,128)(2,1)} %bitcast.17, ...), custom_call_target="tpu_custom_call" | custom-call | flops 300000000 | bytes 5000000 | tf_op jit(solution)/shard_map/upward/pallas_call | solution.py:205
  5.6 2.1 %collective-permute-start = (bf16[80,256]{1,0:T(8,128)(2,1)}, bf16[80,256]{1,0:T(8,128)(2,1)S(1)}, u32[]{:S(2)}, u32[]{:S(2)}) collective-permute-start(bf16[80,256]{1,0:T(8,128)(2,1)} %get-tuple-element.42.after_ref), channel_id=1, source_target_pairs={{0,4},{4,0},{8,12},{12,8},{16,20},{20,16},{24,28},{28,24},{1,5},{5... | collective-permute-start | bytes 122888 | tf_op jit(solution)/shard_map/ppermute | solution.py:859
  7.7 4.0 %collective-permute-start.4 = (bf16[8,256,256]{2,1,0:T(8,128)(2,1)}, bf16[8,256,256]{2,1,0:T(8,128)(2,1)S(1)}, u32[]{:S(2)}, u32[]{:S(2)}) collective-permute-start(bf16[8,256,256]{2,1,0:T(8,128)(2,1)} %get-tuple-element.49), channel_id=1, source_target_pairs={{0,1},{1,2},{2,3},{4,5},{5,6},{6,7},{8,9},{9,10},{10,11},{12,13},{... | collective-permute-start | bytes 3145736 | tf_op jit(solution)/shard_map/ppermute | solution.py:119
  11.7 1.9 %collective-permute-start.5 = (bf16[8,256,256]{2,1,0:T(8,128)(2,1)}, bf16[8,256,256]{2,1,0:T(8,128)(2,1)S(1)}, u32[]{:S(2)}, u32[]{:S(2)}) collective-permute-start(bf16[8,256,256]{2,1,0:T(8,128)(2,1)} %get-tuple-element.50), channel_id=1, source_target_pairs={{1,0},{2,1},{3,2},{5,4},{6,5},{7,6},{9,8},{10,9},{11,10},{13,12},{... | collective-permute-start | bytes 3145736 | tf_op jit(solution)/shard_map/ppermute | solution.py:119
  13.6 2.2 %collective-permute-start.2 = (bf16[816,256]{1,0:T(8,128)(2,1)}, bf16[816,256]{1,0:T(8,128)(2,1)S(1)}, u32[]{:S(2)}, u32[]{:S(2)}) collective-permute-start(bf16[816,256]{1,0:T(8,128)(2,1)} %get-tuple-element.44), channel_id=1, source_target_pairs={{0,4},{4,8},{8,12},{12,16},{16,20},{20,24},{24,28},{1,5},{5,9},{9,... | collective-permute-start | bytes 1253384 | tf_op jit(solution)/shard_map/ppermute | solution.py:119
  15.8 1.3 collective-permute-start.3
  17.1 0.6 reshape.28.refs_3_
  17.7 8.5 %near_own.3.refs_4_.row0_any = f32[8,256,256]{2,1,0:T(8,128)} custom-call(bf16[80,256]{1,0:T(8,128)(2,1)} %get-tuple-element.42.after_ref, s32[52]{0:T(128)} %constant.222.clone.refs_0_, bf16[16,256,256]{2,1,0:T(8,128)(2,1)} %bitcast.18, f32[16,2,256]{2,1,0:T(2,128)} %bitcast.29, f32[16,1,256]{2,1,0:T(1,128)} %reshape.28.refs_3_), custom_call_target="tpu_custom_call" | custom-call | flops 6000000000 | bytes 4000000 | tf_op jit(solution)/shard_map/near_own/pallas_call | solution.py:603
  26.9 0.6 constant_dynamic-update-slice_fusion
  27.5 0.6 copy-done.9
  28.2 8.5 %near_own.4.refs_4_.row1_any = f32[8,256,256]{2,1,0:T(8,128)} custom-call(bf16[160,256]{1,0:T(8,128)(2,1)} %copy-done.9, s32[52]{0:T(128)} %constant.223.clone.refs_0_, bf16[16,256,256]{2,1,0:T(8,128)(2,1)} %bitcast.19, f32[16,2,256]{2,1,0:T(2,128)} %bitcast.30, f32[16,1,256]{2,1,0:T(1,128)} %reshape.28.refs_3_, f32[8,256,256]{2,1,0:T(8,128)} %near_own.3.refs_4_.row0_any), custom_call_target="tpu_custom_call" | custom-call | flops 6000000000 | bytes 4000000 | tf_op jit(solution)/shard_map/near_own/pallas_call | solution.py:603
  36.7 1.0 copy-done.6
  37.9 2.6 %join.1 = (bf16[1936,256]{1,0:T(8,128)(2,1)}, bf16[1936,256]{1,0:T(8,128)(2,1)}) custom-call(bf16[816,256]{1,0:T(8,128)(2,1)} %get-tuple-element.52.north_ref, bf16[816,256]{1,0:T(8,128)(2,1)} %get-tuple-element.53.south_ref, bf16[816,256]{1,0:T(8,128)(2,1)} %copy-done.6, bf16[816,256]{1,0:T(8,128)(2,1)} %copy-done.7), custom_call_target="tpu_custom_call" | custom-call | bytes 4000000 | tf_op jit(solution)/shard_map/join/pallas_call | solution.py:450
  40.5 1.9 %collective-permute-start.7 = (bf16[1936,256]{1,0:T(8,128)(2,1)}, bf16[1936,256]{1,0:T(8,128)(2,1)}, u32[]{:S(2)}, u32[]{:S(2)}) collective-permute-start(bf16[1936,256]{1,0:T(8,128)(2,1)} %get-tuple-element.56.after_ref), channel_id=1, source_target_pairs={{1,0},{2,1},{3,2},{5,4},{6,5},{7,6},{9,8},{10,9},{11,10},{13,12},{... | collective-permute-start | bytes 2973704 | tf_op jit(solution)/shard_map/ppermute | solution.py:119
  42.4 3.9 %collective-permute-start.8 = (bf16[1936,256]{1,0:T(8,128)(2,1)}, bf16[1936,256]{1,0:T(8,128)(2,1)}, u32[]{:S(2)}, u32[]{:S(2)}) collective-permute-start(bf16[1936,256]{1,0:T(8,128)(2,1)} %get-tuple-element.57), channel_id=1, source_target_pairs={{0,1},{1,2},{2,3},{4,5},{5,6},{6,7},{8,9},{9,10},{10,11},{12,13},{... | collective-permute-start | bytes 2973704 | tf_op jit(solution)/shard_map/ppermute | solution.py:119
  47.2 5.4 %collective-permute-start.6 = (bf16[320,256]{1,0:T(8,128)(2,1)S(1)}, bf16[320,256]{1,0:T(8,128)(2,1)S(1)}, u32[]{:S(2)}, u32[]{:S(2)}) collective-permute-start(bf16[320,256]{1,0:T(8,128)(2,1)S(1)} %pad_maximum_fusion.3), channel_id=1, source_target_pairs={{0,16},{4,20},{8,24},{12,28},{16,0},{20,4},{24,8},{28,12},{1,17},{... | collective-permute-start | bytes 491528 | tf_op jit(solution)/shard_map/ppermute | solution.py:859
  52.5 1.8 %collective-permute-start.11 = (bf16[8,256,256]{2,1,0:T(8,128)(2,1)}, bf16[8,256,256]{2,1,0:T(8,128)(2,1)S(1)}, u32[]{:S(2)}, u32[]{:S(2)}) collective-permute-start(bf16[8,256,256]{2,1,0:T(8,128)(2,1)} %get-tuple-element.66), channel_id=1, source_target_pairs={{0,4},{4,8},{8,12},{12,16},{16,20},{20,24},{24,28},{1,5},{5,9},{9,... | collective-permute-start | bytes 3145736 | tf_op jit(solution)/shard_map/ppermute | solution.py:119
  54.3 1.5 %collective-permute-start.12 = (bf16[8,256,256]{2,1,0:T(8,128)(2,1)}, bf16[8,256,256]{2,1,0:T(8,128)(2,1)S(1)}, u32[]{:S(2)}, u32[]{:S(2)}) collective-permute-start(bf16[8,256,256]{2,1,0:T(8,128)(2,1)} %get-tuple-element.67), channel_id=1, source_target_pairs={{4,0},{8,4},{12,8},{16,12},{20,16},{24,20},{28,24},{5,1},{9,5},{13... | collective-permute-start | bytes 3145736 | tf_op jit(solution)/shard_map/ppermute | solution.py:119
  55.8 11.6 %near_own.5.row2_any = f32[8,256,256]{2,1,0:T(8,128)} custom-call(bf16[1936,256]{1,0:T(8,128)(2,1)} %get-tuple-element.56.after_ref, s32[64]{0:T(128)} %constant.224.clone.refs_0_, bf16[16,256,256]{2,1,0:T(8,128)(2,1)} %bitcast.20, f32[16,2,256]{2,1,0:T(2,128)} %bitcast.31, f32[16,1,256]{2,1,0:T(1,128)} %reshape.28.refs_3_, ...), custom_call_target="tpu_custom_call" | custom-call | flops 6000000000 | bytes 4000000 | tf_op jit(solution)/shard_map/near_own/pallas_call | solution.py:603
  67.5 4.4 %collective-permute-start.9 = (bf16[640,256]{1,0:T(8,128)(2,1)S(1)}, bf16[640,256]{1,0:T(8,128)(2,1)S(1)}, u32[]{:S(2)}, u32[]{:S(2)}) collective-permute-start(bf16[640,256]{1,0:T(8,128)(2,1)S(1)} %pad_maximum_fusion.2), channel_id=1, source_target_pairs={{0,8},{4,12},{8,0},{12,4},{16,24},{20,28},{24,16},{28,20},{1,9},{5... | collective-permute-start | bytes 983048 | tf_op jit(solution)/shard_map/ppermute | solution.py:859
  72.0 7.2 %local_far.1 = (f32[16,64,256]{2,1,0:T(8,128)}, f32[256,256]{1,0:T(8,128)}) custom-call(s32[16]{0:T(128)} %reshape.24.list_ref.refs_0_, bf16[1280,256]{1,0:T(8,128)(2,1)} %get-tuple-element.60.coef_any, bf16[816,256]{1,0:T(8,128)(2,1)} %copy-done.6, bf16[816,256]{1,0:T(8,128)(2,1)} %copy-done.7, bf16[1936,256]{1,0:T(8,128)(2,1)} %collective-permute-done.8.north_any.refs_7_, ...), custom_call_target="tpu_custom_call" | custom-call | flops 5000000000 | bytes 8000000 | tf_op jit(solution)/shard_map/local_far/pallas_call | solution.py:304
  79.2 11.4 %edge_blocks.2.refs_3_.upper_blocks_any = bf16[30,256,256]{2,1,0:T(8,128)(2,1)} custom-call(s32[16]{0:T(128)} %reshape.24.list_ref.refs_0_, s32[88]{0:T(128)} %constant.228.clone.refs_1_, s32[64]{0:T(128)} %constant.229.clone.refs_2_.slot_ref, f32[256,256]{1,0:T(8,128)} %get-tuple-element.63.refs_3_.sum1_any, f32[16,2,256]{2,1,0:T(2,128)} %bitcast.32, ...), custom_call_target="tpu_custom_call" | custom-call | flops 6000000000 | bytes 8000000 | tf_op jit(solution)/shard_map/edge_blocks/pallas_call | solution.py:712
  91.0 11.5 %edge_blocks.3.lower_blocks_any = bf16[30,256,256]{2,1,0:T(8,128)(2,1)} custom-call(s32[16]{0:T(128)} %reshape.24.list_ref.refs_0_, s32[88]{0:T(128)} %constant.230.clone.refs_1_, s32[64]{0:T(128)} %constant.229.clone.refs_2_.slot_ref, bf16[30,256,256]{2,1,0:T(8,128)(2,1)} %edge_blocks.2.refs_3_.upper_blocks_any, f32[16,2,256]{2,1,0:T(2,128)} %bitcast.33, ...), custom_call_target="tpu_custom_call" | custom-call | flops 6000000000 | bytes 8000000 | tf_op jit(solution)/shard_map/edge_blocks/pallas_call | solution.py:712
  102.5 4.1 %collective-permute-done.10.other_any = bf16[1280,256]{1,0:T(8,128)(2,1)} collective-permute-done((bf16[1280,256]{1,0:T(8,128)(2,1)S(1)}, bf16[1280,256]{1,0:T(8,128)(2,1)}, u32[]{:S(2)}, u32[]{:S(2)}) %collective-permute-start.10) | collective-permute-done | bytes 655392 | tf_op jit(solution)/shard_map/ppermute | solution.py:859
  106.9 3.6 %collective-permute-start.14 = (bf16[2,4,256,256]{3,2,1,0:T(8,128)(2,1)S(1)}, bf16[2,4,256,256]{3,2,1,0:T(8,128)(2,1)S(1)}, u32[]{:S(2)}, u32[]{:S(2)}) collective-permute-start(bf16[2,4,256,256]{3,2,1,0:T(8,128)(2,1)S(1)} %pad_maximum_fusion.1), channel_id=1, source_target_pairs={{1,0},{2,1},{3,2},{5,4},{6,5},{7,6},{9,8},{10,9},{11,10},{13,12},{... | collective-permute-start | bytes 3145736 | tf_op jit(solution)/shard_map/ppermute | solution.py:119
  110.5 1.1 pad_maximum_fusion
  111.6 2.1 %collective-permute-start.13 = (bf16[2,4,256,256]{3,2,1,0:T(8,128)(2,1)}, bf16[2,4,256,256]{3,2,1,0:T(8,128)(2,1)S(1)}, u32[]{:S(2)}, u32[]{:S(2)}) collective-permute-start(bf16[2,4,256,256]{3,2,1,0:T(8,128)(2,1)} %pad_maximum_fusion), channel_id=1, source_target_pairs={{0,1},{1,2},{2,3},{4,5},{5,6},{6,7},{8,9},{9,10},{10,11},{12,13},{... | collective-permute-start | bytes 3145736 | tf_op jit(solution)/shard_map/ppermute | solution.py:119
  114.5 6.2 %top_far.1.field_ref = bf16[16,64,256]{2,1,0:T(8,128)(2,1)} custom-call(s32[74]{0:T(128)} %pad_add_fusion.meta_ref, bf16[1280,256]{1,0:T(8,128)(2,1)} %copy-done.13, bf16[1280,256]{1,0:T(8,128)(2,1)} %collective-permute-done.10.other_any, bf16[256,2304]{1,0:T(8,128)(2,1)} %constant.231.clone.c2_any, bf16[256,2304]{1,0:T(8,128)(2,1)} %constant.232.clone.c3_any, ...), custom_call_target="tpu_custom_call" | custom-call | flops 3000000000 | bytes 5000000 | tf_op jit(solution)/shard_map/top_far/pallas_call | solution.py:402
  120.7 2.3 %collective-permute-done.14 = bf16[2,4,256,256]{3,2,1,0:T(8,128)(2,1)S(1)} collective-permute-done((bf16[2,4,256,256]{3,2,1,0:T(8,128)(2,1)S(1)}, bf16[2,4,256,256]{3,2,1,0:T(8,128)(2,1)S(1)}, u32[]{:S(2)}, u32[]{:S(2)}) %collective-permute-start.14) | collective-permute-done | bytes 1048608 | tf_op jit(solution)/shard_map/ppermute | solution.py:119
  123.0 2.8 %collective-permute-done.13 = bf16[2,4,256,256]{3,2,1,0:T(8,128)(2,1)S(1)} collective-permute-done((bf16[2,4,256,256]{3,2,1,0:T(8,128)(2,1)}, bf16[2,4,256,256]{3,2,1,0:T(8,128)(2,1)S(1)}, u32[]{:S(2)}, u32[]{:S(2)}) %collective-permute-start.13) | collective-permute-done | bytes 1048608 | tf_op jit(solution)/shard_map/ppermute | solution.py:119
  125.8 1.0 copy-done.5
  126.8 12.7 %finish.1 = bf16[16,256,256]{2,1,0:T(8,128)(2,1)} custom-call(s32[16]{0:T(128)} %reshape.24.list_ref.refs_0_, s32[64]{0:T(128)} %constant.229.clone.refs_2_.slot_ref, bf16[16,256,256]{2,1,0:T(8,128)(2,1)} %bitcast.21, bf16[8,256,256]{2,1,0:T(8,128)(2,1)} %copy-done, bf16[8,256,256]{2,1,0:T(8,128)(2,1)} %copy-done.1, bf16[8,256,256]{2,1,0:T(8,128)(2,1)} %copy-done.2, ...), custom_call_target="tpu_custom_call" | custom-call | flops 4000000000 | bytes 24000000 | tf_op jit(solution)/shard_map/finish/pallas_call | solution.py:799
  (55 shorter events, 2.8 us)
Async XLA Ops:
  0.0 17.1 %copy-start.10 = (f32[4,4,256]{2,1,0:T(4,128)S(1)}, f32[4,4,256]{2,1,0:T(4,128)}, u32[]{:S(2)}) copy-start(f32[4,4,256]{2,1,0:T(4,128)} %param.21) | copy-start | bytes 49156
  5.6 21.3 %collective-permute-start = (bf16[80,256]{1,0:T(8,128)(2,1)}, bf16[80,256]{1,0:T(8,128)(2,1)S(1)}, u32[]{:S(2)}, u32[]{:S(2)}) collective-permute-start(bf16[80,256]{1,0:T(8,128)(2,1)} %get-tuple-element.42.after_ref), channel_id=1, source_target_pairs={{0,4},{4,0},{8,12},{12,8},{16,20},{20,16},{24,28},{28,24},{1,5},{5... | collective-permute-start | bytes 122888 | tf_op jit(solution)/shard_map/ppermute | solution.py:859
  7.7 29.0 %collective-permute-start.4 = (bf16[8,256,256]{2,1,0:T(8,128)(2,1)}, bf16[8,256,256]{2,1,0:T(8,128)(2,1)S(1)}, u32[]{:S(2)}, u32[]{:S(2)}) collective-permute-start(bf16[8,256,256]{2,1,0:T(8,128)(2,1)} %get-tuple-element.49), channel_id=1, source_target_pairs={{0,1},{1,2},{2,3},{4,5},{5,6},{6,7},{8,9},{9,10},{10,11},{12,13},{... | collective-permute-start | bytes 3145736 | tf_op jit(solution)/shard_map/ppermute | solution.py:119
  11.7 25.0 %collective-permute-start.5 = (bf16[8,256,256]{2,1,0:T(8,128)(2,1)}, bf16[8,256,256]{2,1,0:T(8,128)(2,1)S(1)}, u32[]{:S(2)}, u32[]{:S(2)}) collective-permute-start(bf16[8,256,256]{2,1,0:T(8,128)(2,1)} %get-tuple-element.50), channel_id=1, source_target_pairs={{1,0},{2,1},{3,2},{5,4},{6,5},{7,6},{9,8},{10,9},{11,10},{13,12},{... | collective-permute-start | bytes 3145736 | tf_op jit(solution)/shard_map/ppermute | solution.py:119
  13.6 23.0 %collective-permute-start.2 = (bf16[816,256]{1,0:T(8,128)(2,1)}, bf16[816,256]{1,0:T(8,128)(2,1)S(1)}, u32[]{:S(2)}, u32[]{:S(2)}) collective-permute-start(bf16[816,256]{1,0:T(8,128)(2,1)} %get-tuple-element.44), channel_id=1, source_target_pairs={{0,4},{4,8},{8,12},{12,16},{16,20},{20,24},{24,28},{1,5},{5,9},{9,... | collective-permute-start | bytes 1253384 | tf_op jit(solution)/shard_map/ppermute | solution.py:119
  15.8 20.9 %collective-permute-start.3 = (bf16[816,256]{1,0:T(8,128)(2,1)}, bf16[816,256]{1,0:T(8,128)(2,1)S(1)}, u32[]{:S(2)}, u32[]{:S(2)}) collective-permute-start(bf16[816,256]{1,0:T(8,128)(2,1)} %get-tuple-element.45), channel_id=1, source_target_pairs={{4,0},{8,4},{12,8},{16,12},{20,16},{24,20},{28,24},{5,1},{9,5},{13... | collective-permute-start | bytes 1253384 | tf_op jit(solution)/shard_map/ppermute | solution.py:119
  17.7 8.5 %copy-start.8 = (bf16[80,256]{1,0:T(8,128)(2,1)S(1)}, bf16[80,256]{1,0:T(8,128)(2,1)}, u32[]{:S(2)}) copy-start(bf16[80,256]{1,0:T(8,128)(2,1)} %get-tuple-element.42.after_ref) | copy-start | bytes 122884
  27.5 0.6 copy-start.9
  27.5 18.8 %copy-start.11 = (s32[4,4,10]{2,1,0:T(4,128)S(1)}, s32[4,4,10]{2,1,0:T(4,128)}, u32[]{:S(2)}) copy-start(s32[4,4,10]{2,1,0:T(4,128)} %param.24) | copy-start | bytes 1924
  27.5 9.1 %collective-permute-start.1 = (bf16[160,256]{1,0:T(8,128)(2,1)S(1)}, bf16[160,256]{1,0:T(8,128)(2,1)S(1)}, u32[]{:S(2)}, u32[]{:S(2)}) collective-permute-start(bf16[160,256]{1,0:T(8,128)(2,1)S(1)} %get-tuple-element.83.after_ref), channel_id=1, source_target_pairs={{0,1},{1,0},{2,3},{3,2},{4,5},{5,4},{6,7},{7,6},{8,9},{9,8},{10,11... | collective-permute-start | bytes 245768 | tf_op jit(solution)/shard_map/ppermute | solution.py:859
  36.7 1.1 copy-start.6
  36.7 1.2 copy-start.7
  36.7 30.7 %copy-start.2 = (bf16[8,256,256]{2,1,0:T(8,128)(2,1)}, bf16[8,256,256]{2,1,0:T(8,128)(2,1)S(1)}, u32[]{:S(2)}) copy-start(bf16[8,256,256]{2,1,0:T(8,128)(2,1)S(1)} %collective-permute-done.4.north_any) | copy-start | bytes 3145732
  36.7 10.4 %copy-start.3 = (bf16[8,256,256]{2,1,0:T(8,128)(2,1)}, bf16[8,256,256]{2,1,0:T(8,128)(2,1)S(1)}, u32[]{:S(2)}) copy-start(bf16[8,256,256]{2,1,0:T(8,128)(2,1)S(1)} %collective-permute-done.5.south_any) | copy-start | bytes 3145732
  40.5 27.0 %collective-permute-start.7 = (bf16[1936,256]{1,0:T(8,128)(2,1)}, bf16[1936,256]{1,0:T(8,128)(2,1)}, u32[]{:S(2)}, u32[]{:S(2)}) collective-permute-start(bf16[1936,256]{1,0:T(8,128)(2,1)} %get-tuple-element.56.after_ref), channel_id=1, source_target_pairs={{1,0},{2,1},{3,2},{5,4},{6,5},{7,6},{9,8},{10,9},{11,10},{13,12},{... | collective-permute-start | bytes 2973704 | tf_op jit(solution)/shard_map/ppermute | solution.py:119
  42.4 25.1 %collective-permute-start.8 = (bf16[1936,256]{1,0:T(8,128)(2,1)}, bf16[1936,256]{1,0:T(8,128)(2,1)}, u32[]{:S(2)}, u32[]{:S(2)}) collective-permute-start(bf16[1936,256]{1,0:T(8,128)(2,1)} %get-tuple-element.57), channel_id=1, source_target_pairs={{0,1},{1,2},{2,3},{4,5},{5,6},{6,7},{8,9},{9,10},{10,11},{12,13},{... | collective-permute-start | bytes 2973704 | tf_op jit(solution)/shard_map/ppermute | solution.py:119
  47.2 20.3 %copy-start.12 = (bf16[1280,256]{1,0:T(8,128)(2,1)S(1)}, bf16[1280,256]{1,0:T(8,128)(2,1)}, u32[]{:S(2)}) copy-start(bf16[1280,256]{1,0:T(8,128)(2,1)} %get-tuple-element.84) | copy-start | bytes 1966084
  47.2 20.3 %collective-permute-start.6 = (bf16[320,256]{1,0:T(8,128)(2,1)S(1)}, bf16[320,256]{1,0:T(8,128)(2,1)S(1)}, u32[]{:S(2)}, u32[]{:S(2)}) collective-permute-start(bf16[320,256]{1,0:T(8,128)(2,1)S(1)} %pad_maximum_fusion.3), channel_id=1, source_target_pairs={{0,16},{4,20},{8,24},{12,28},{16,0},{20,4},{24,8},{28,12},{1,17},{... | collective-permute-start | bytes 491528 | tf_op jit(solution)/shard_map/ppermute | solution.py:859
  52.5 49.9 %collective-permute-start.11 = (bf16[8,256,256]{2,1,0:T(8,128)(2,1)}, bf16[8,256,256]{2,1,0:T(8,128)(2,1)S(1)}, u32[]{:S(2)}, u32[]{:S(2)}) collective-permute-start(bf16[8,256,256]{2,1,0:T(8,128)(2,1)} %get-tuple-element.66), channel_id=1, source_target_pairs={{0,4},{4,8},{8,12},{12,16},{16,20},{20,24},{24,28},{1,5},{5,9},{9,... | collective-permute-start | bytes 3145736 | tf_op jit(solution)/shard_map/ppermute | solution.py:119
  54.3 48.1 %collective-permute-start.12 = (bf16[8,256,256]{2,1,0:T(8,128)(2,1)}, bf16[8,256,256]{2,1,0:T(8,128)(2,1)S(1)}, u32[]{:S(2)}, u32[]{:S(2)}) collective-permute-start(bf16[8,256,256]{2,1,0:T(8,128)(2,1)} %get-tuple-element.67), channel_id=1, source_target_pairs={{4,0},{8,4},{12,8},{16,12},{20,16},{24,20},{28,24},{5,1},{9,5},{13... | collective-permute-start | bytes 3145736 | tf_op jit(solution)/shard_map/ppermute | solution.py:119
  67.5 23.2 %collective-permute-start.9 = (bf16[640,256]{1,0:T(8,128)(2,1)S(1)}, bf16[640,256]{1,0:T(8,128)(2,1)S(1)}, u32[]{:S(2)}, u32[]{:S(2)}) collective-permute-start(bf16[640,256]{1,0:T(8,128)(2,1)S(1)} %pad_maximum_fusion.2), channel_id=1, source_target_pairs={{0,8},{4,12},{8,0},{12,4},{16,24},{20,28},{24,16},{28,20},{1,9},{5... | collective-permute-start | bytes 983048 | tf_op jit(solution)/shard_map/ppermute | solution.py:859
  90.8 11.7 %copy-start.13 = (bf16[1280,256]{1,0:T(8,128)(2,1)}, bf16[1280,256]{1,0:T(8,128)(2,1)S(1)}, u32[]{:S(2)}) copy-start(bf16[1280,256]{1,0:T(8,128)(2,1)S(1)} %constant_dynamic-update-slice_fusion.2.mine_any) | copy-start | bytes 1966084
  90.8 15.8 %collective-permute-start.10 = (bf16[1280,256]{1,0:T(8,128)(2,1)S(1)}, bf16[1280,256]{1,0:T(8,128)(2,1)}, u32[]{:S(2)}, u32[]{:S(2)}) collective-permute-start(bf16[1280,256]{1,0:T(8,128)(2,1)S(1)} %constant_dynamic-update-slice_fusion.2.mine_any), channel_id=1, source_target_pairs={{0,2},{1,3},{2,0},{3,1},{4,6},{5,7},{6,4},{7,5},{8,10},{9,11},{10,... | collective-permute-start | bytes 1966088 | tf_op jit(solution)/shard_map/ppermute | solution.py:859
  102.5 4.3 %copy-start = (bf16[8,256,256]{2,1,0:T(8,128)(2,1)}, bf16[8,256,256]{2,1,0:T(8,128)(2,1)S(1)}, u32[]{:S(2)}) copy-start(bf16[8,256,256]{2,1,0:T(8,128)(2,1)S(1)} %collective-permute-done.11.west_any) | copy-start | bytes 3145732
  102.5 4.2 %copy-start.1 = (bf16[8,256,256]{2,1,0:T(8,128)(2,1)}, bf16[8,256,256]{2,1,0:T(8,128)(2,1)S(1)}, u32[]{:S(2)}) copy-start(bf16[8,256,256]{2,1,0:T(8,128)(2,1)S(1)} %collective-permute-done.12.east_any) | copy-start | bytes 3145732
  106.7 7.1 %copy-start.14 = (s32[36]{0:T(128)S(1)}, s32[36]{0:T(128)}, u32[]{:S(2)}) copy-start(s32[36]{0:T(128)} %constant.220.clone) | copy-start | bytes 436
  106.8 7.1 %copy-start.15 = (s32[36]{0:T(128)S(1)}, s32[36]{0:T(128)}, u32[]{:S(2)}) copy-start(s32[36]{0:T(128)} %constant.221.clone) | copy-start | bytes 436
  106.9 16.1 %collective-permute-start.14 = (bf16[2,4,256,256]{3,2,1,0:T(8,128)(2,1)S(1)}, bf16[2,4,256,256]{3,2,1,0:T(8,128)(2,1)S(1)}, u32[]{:S(2)}, u32[]{:S(2)}) collective-permute-start(bf16[2,4,256,256]{3,2,1,0:T(8,128)(2,1)S(1)} %pad_maximum_fusion.1), channel_id=1, source_target_pairs={{1,0},{2,1},{3,2},{5,4},{6,5},{7,6},{9,8},{10,9},{11,10},{13,12},{... | collective-permute-start | bytes 3145736 | tf_op jit(solution)/shard_map/ppermute | solution.py:119
  111.6 14.2 %collective-permute-start.13 = (bf16[2,4,256,256]{3,2,1,0:T(8,128)(2,1)}, bf16[2,4,256,256]{3,2,1,0:T(8,128)(2,1)S(1)}, u32[]{:S(2)}, u32[]{:S(2)}) collective-permute-start(bf16[2,4,256,256]{3,2,1,0:T(8,128)(2,1)} %pad_maximum_fusion), channel_id=1, source_target_pairs={{0,1},{1,2},{2,3},{4,5},{5,6},{6,7},{8,9},{9,10},{10,11},{12,13},{... | collective-permute-start | bytes 3145736 | tf_op jit(solution)/shard_map/ppermute | solution.py:119
  123.0 2.8 %copy-start.4 = (bf16[2,4,256,256]{3,2,1,0:T(8,128)(2,1)}, bf16[2,4,256,256]{3,2,1,0:T(8,128)(2,1)S(1)}, u32[]{:S(2)}) copy-start(bf16[2,4,256,256]{3,2,1,0:T(8,128)(2,1)S(1)} %collective-permute-done.14) | copy-start | bytes 3145732
  125.8 1.0 copy-start.5

commit v9 on v8

--- a/solution.py
+++ b/solution.py
@@ -864,20 +864,18 @@
     gathered = give
     other = step(gathered, 0)
     row0 = near_own(0, 1, q, points, noise_rows, give, [])
-    other, row0 = tie(other, row0)
+    other, row0, to_east, to_west, q_north, q_south = tie(other, row0, to_east, to_west, q_north, q_south)
+    q_west = shift(to_east, "wide", 1)
+    q_east = shift(to_west, "wide", -1)
     gathered = jnp.concatenate([gathered, other], axis=0)
     other = step(gathered, 1)
     row1 = near_own(1, 2, q, points, noise_rows, gathered, [row0])
-    other, from_west, from_east, row1, to_east, to_west, q_north, q_south = tie(
-        other, from_west, from_east, row1, to_east, to_west, q_north, q_south
-    )
+    other, from_west, from_east, row1 = tie(other, from_west, from_east, row1)
     gathered = jnp.concatenate([gathered, other], axis=0)
     other = step(gathered, 2)
     to_north, to_south = join(north, south, from_west, from_east)
     from_south = shift(to_north, "narrow", -1)
     from_north = shift(to_south, "narrow", 1)
-    q_west = shift(to_east, "wide", 1)
-    q_east = shift(to_west, "wide", -1)
     row2 = near_own(2, 4, q, points, noise_rows, to_north, [row1])
     other, from_south, from_north, row2 = tie(other, from_south, from_north, row2)
     gathered = jnp.concatenate([gathered, other], axis=0)

time: 140 us -> 158 us (1.13)
  waiting for transfers between devices: 9.21 us -> 28.5 us
  starting transfers between devices: 36.4 us -> 34.6 us
    ppermute x5, waiting for transfers between devices: 4.14 us -> 23.3 us  [step(): lax.ppermute(value, axis, [(i, i ^ bit) for i in range(lax.axis_size(axis...]
    ppermute x5, starting transfers between devices: 12.1 us -> 6.87 us  [step(): lax.ppermute(value, axis, [(i, i ^ bit) for i in range(lax.axis_size(axis...]
    ppermute x10, starting transfers between devices: 24.3 us -> 27.7 us  [shift(): lax.ppermute(value, axis, [(i, i + steps) for i in range(count) if 0 <= i...]
    unnamed x35 -> x37, local copies, waits for them, and re-layouts: 3.47 us -> 3.87 us
  transfers between devices with their start and end apart: 15 -> 15, of which waited for: 4 -> 5; matrix products, arithmetic and copies ran while one was open for 3% -> 3% of each run, Pallas kernels for 47% -> 41%
where the time goes in v9:
time: 158 us
  Pallas kernels  86 us (54%)
  starting transfers between devices  34.6 us (22%)
  waiting for transfers between devices  28.5 us (18%)
  local copies, waits for them, and re-layouts  6.09 us (4%)
  other arithmetic  2.05 us (1%)
    pallas_call x3, Pallas kernels, near_own(): pl.pallas_call(body, out_shape=jax.ShapeDtypeStruct((leaves, LEAF, LEAF),...  28.8 us
    ppermute x10, starting transfers between devices, shift(): lax.ppermute(value, axis, [(i, i + steps) for i in range(count) if 0 <= i...  27.7 us
    ppermute x5, waiting for transfers between devices, step(): lax.ppermute(value, axis, [(i, i ^ bit) for i in range(lax.axis_size(axis...  23.3 us
    pallas_call x2, Pallas kernels, edge_blocks(): pl.pallas_call(body, out_shape=jax.ShapeDtypeStruct((EDGES // 2 + 8, LEAF...  22.9 us
    pallas_call x1, Pallas kernels, finish(): pl.pallas_call(final_body, out_shape=jax.ShapeDtypeStruct((LEAVES, LEAF,...  12.7 us
    pallas_call x1, Pallas kernels, local_far(): pl.pallas_call(local_body, out_shape=(jax.ShapeDtypeStruct((LEAVES, RANK,...  7.24 us
    ppermute x5, starting transfers between devices, step(): lax.ppermute(value, axis, [(i, i ^ bit) for i in range(lax.axis_size(axis...  6.87 us
    pallas_call x1, Pallas kernels, top_far(): pl.pallas_call(top_body, out_shape=jax.ShapeDtypeStruct((LEAVES, RANK, LE...  6.21 us
  transfers between devices with their start and end apart: 15, of which 5 were waited for; matrix products, arithmetic and copies ran while one was open for 3% of the time, Pallas kernels for 41%

profile of v9, /device:TPU:1, one launch (start us, length us, event | category | flops | bytes accessed | tf_op | source)
XLA Modules:
  0.0 157.8 jit_solution(10930731086716135436)
XLA Ops:
  0.0 5.6 %upward.1 = (bf16[816,256]{1,0:T(8,128)(2,1)}, bf16[816,256]{1,0:T(8,128)(2,1)}, bf16[816,256]{1,0:T(8,128)(2,1)}, bf16[816,256]{1,0:T(8,128)(2,1)}, bf16[1280,2...) custom-call(bf16[16,256,256]{2,1,0:T(8,128)(2,1)} %bitcast.17, ...), custom_call_target="tpu_custom_call" | custom-call | flops 300000000 | bytes 5000000 | tf_op jit(solution)/shard_map/upward/pallas_call | solution.py:205
  5.6 4.5 %collective-permute-start.1 = (bf16[8,256,256]{2,1,0:T(8,128)(2,1)}, bf16[8,256,256]{2,1,0:T(8,128)(2,1)S(1)}, u32[]{:S(2)}, u32[]{:S(2)}) collective-permute-start(bf16[8,256,256]{2,1,0:T(8,128)(2,1)} %get-tuple-element.45), channel_id=1, source_target_pairs={{0,1},{1,2},{2,3},{4,5},{5,6},{6,7},{8,9},{9,10},{10,11},{12,13},{... | collective-permute-start | bytes 3145736 | tf_op jit(solution)/shard_map/ppermute | solution.py:119
  10.1 1.9 %collective-permute-start.2 = (bf16[8,256,256]{2,1,0:T(8,128)(2,1)}, bf16[8,256,256]{2,1,0:T(8,128)(2,1)S(1)}, u32[]{:S(2)}, u32[]{:S(2)}) collective-permute-start(bf16[8,256,256]{2,1,0:T(8,128)(2,1)} %get-tuple-element.46), channel_id=1, source_target_pairs={{1,0},{2,1},{3,2},{5,4},{6,5},{7,6},{9,8},{10,9},{11,10},{13,12},{... | collective-permute-start | bytes 3145736 | tf_op jit(solution)/shard_map/ppermute | solution.py:119
  12.0 1.3 collective-permute-start
  13.3 2.2 %collective-permute-start.4 = (bf16[816,256]{1,0:T(8,128)(2,1)}, bf16[816,256]{1,0:T(8,128)(2,1)S(1)}, u32[]{:S(2)}, u32[]{:S(2)}) collective-permute-start(bf16[816,256]{1,0:T(8,128)(2,1)} %get-tuple-element.48), channel_id=1, source_target_pairs={{0,4},{4,8},{8,12},{12,16},{16,20},{20,24},{24,28},{1,5},{5,9},{9,... | collective-permute-start | bytes 1253384 | tf_op jit(solution)/shard_map/ppermute | solution.py:119
  15.5 1.3 collective-permute-start.5
  17.4 8.5 %near_own.3.refs_4_.row0_any = f32[8,256,256]{2,1,0:T(8,128)} custom-call(bf16[80,256]{1,0:T(8,128)(2,1)} %get-tuple-element.42.after_ref, s32[52]{0:T(128)} %constant.222.clone.refs_0_, bf16[16,256,256]{2,1,0:T(8,128)(2,1)} %bitcast.18, f32[16,2,256]{2,1,0:T(2,128)} %bitcast.29, f32[16,1,256]{2,1,0:T(1,128)} %reshape.28.refs_3_), custom_call_target="tpu_custom_call" | custom-call | flops 6000000000 | bytes 4000000 | tf_op jit(solution)/shard_map/near_own/pallas_call | solution.py:603
  26.7 0.8 constant_dynamic-update-slice_fusion
  28.2 8.5 %near_own.4.refs_4_.row1_any = f32[8,256,256]{2,1,0:T(8,128)} custom-call(bf16[160,256]{1,0:T(8,128)(2,1)} %copy-done.9, s32[52]{0:T(128)} %constant.223.clone.refs_0_, bf16[16,256,256]{2,1,0:T(8,128)(2,1)} %bitcast.19, f32[16,2,256]{2,1,0:T(2,128)} %bitcast.30, f32[16,1,256]{2,1,0:T(1,128)} %reshape.28.refs_3_, f32[8,256,256]{2,1,0:T(8,128)} %near_own.3.refs_4_.row0_any), custom_call_target="tpu_custom_call" | custom-call | flops 6000000000 | bytes 4000000 | tf_op jit(solution)/shard_map/near_own/pallas_call | solution.py:603
  36.7 0.7 copy-done.6
  37.6 2.6 %join.1 = (bf16[1936,256]{1,0:T(8,128)(2,1)}, bf16[1936,256]{1,0:T(8,128)(2,1)}) custom-call(bf16[816,256]{1,0:T(8,128)(2,1)} %get-tuple-element.52.north_ref, bf16[816,256]{1,0:T(8,128)(2,1)} %get-tuple-element.53.south_ref, bf16[816,256]{1,0:T(8,128)(2,1)} %copy-done.6, bf16[816,256]{1,0:T(8,128)(2,1)} %copy-done.7), custom_call_target="tpu_custom_call" | custom-call | bytes 4000000 | tf_op jit(solution)/shard_map/join/pallas_call | solution.py:450
  40.2 1.9 %collective-permute-start.7 = (bf16[1936,256]{1,0:T(8,128)(2,1)}, bf16[1936,256]{1,0:T(8,128)(2,1)}, u32[]{:S(2)}, u32[]{:S(2)}) collective-permute-start(bf16[1936,256]{1,0:T(8,128)(2,1)} %get-tuple-element.56.after_ref), channel_id=1, source_target_pairs={{1,0},{2,1},{3,2},{5,4},{6,5},{7,6},{9,8},{10,9},{11,10},{13,12},{... | collective-permute-start | bytes 2973704 | tf_op jit(solution)/shard_map/ppermute | solution.py:119
  42.2 4.0 %collective-permute-start.8 = (bf16[1936,256]{1,0:T(8,128)(2,1)}, bf16[1936,256]{1,0:T(8,128)(2,1)}, u32[]{:S(2)}, u32[]{:S(2)}) collective-permute-start(bf16[1936,256]{1,0:T(8,128)(2,1)} %get-tuple-element.57), channel_id=1, source_target_pairs={{0,1},{1,2},{2,3},{4,5},{5,6},{6,7},{8,9},{9,10},{10,11},{12,13},{... | collective-permute-start | bytes 2973704 | tf_op jit(solution)/shard_map/ppermute | solution.py:119
  47.0 4.8 %collective-permute-start.11 = (bf16[8,256,256]{2,1,0:T(8,128)(2,1)}, bf16[8,256,256]{2,1,0:T(8,128)(2,1)S(1)}, u32[]{:S(2)}, u32[]{:S(2)}) collective-permute-start(bf16[8,256,256]{2,1,0:T(8,128)(2,1)} %get-tuple-element.66), channel_id=1, source_target_pairs={{0,4},{4,8},{8,12},{12,16},{16,20},{20,24},{24,28},{1,5},{5,9},{9,... | collective-permute-start | bytes 3145736 | tf_op jit(solution)/shard_map/ppermute | solution.py:119
  51.8 1.3 collective-permute-start.12
  53.1 5.4 %collective-permute-start.6 = (bf16[320,256]{1,0:T(8,128)(2,1)S(1)}, bf16[320,256]{1,0:T(8,128)(2,1)S(1)}, u32[]{:S(2)}, u32[]{:S(2)}) collective-permute-start(bf16[320,256]{1,0:T(8,128)(2,1)S(1)} %pad_maximum_fusion.3), channel_id=1, source_target_pairs={{0,16},{4,20},{8,24},{12,28},{16,0},{20,4},{24,8},{28,12},{1,17},{... | collective-permute-start | bytes 491528 | tf_op jit(solution)/shard_map/ppermute | solution.py:859
  58.5 11.8 %near_own.5.row2_any = f32[8,256,256]{2,1,0:T(8,128)} custom-call(bf16[1936,256]{1,0:T(8,128)(2,1)} %get-tuple-element.56.after_ref, s32[64]{0:T(128)} %constant.224.clone.refs_0_, bf16[16,256,256]{2,1,0:T(8,128)(2,1)} %bitcast.20, f32[16,2,256]{2,1,0:T(2,128)} %bitcast.31, f32[16,1,256]{2,1,0:T(1,128)} %reshape.28.refs_3_, ...), custom_call_target="tpu_custom_call" | custom-call | flops 6000000000 | bytes 4000000 | tf_op jit(solution)/shard_map/near_own/pallas_call | solution.py:603
  70.4 18.4 %collective-permute-done.6 = bf16[320,256]{1,0:T(8,128)(2,1)S(1)} collective-permute-done((bf16[320,256]{1,0:T(8,128)(2,1)S(1)}, bf16[320,256]{1,0:T(8,128)(2,1)S(1)}, u32[]{:S(2)}, u32[]{:S(2)}) %collective-permute-start.6) | collective-permute-done | bytes 163872 | tf_op jit(solution)/shard_map/ppermute | solution.py:859
  88.9 7.2 %local_far.1 = (f32[16,64,256]{2,1,0:T(8,128)}, f32[256,256]{1,0:T(8,128)}) custom-call(s32[16]{0:T(128)} %reshape.24.list_ref.refs_0_, bf16[1280,256]{1,0:T(8,128)(2,1)} %get-tuple-element.60.coef_any, bf16[816,256]{1,0:T(8,128)(2,1)} %copy-done.6, bf16[816,256]{1,0:T(8,128)(2,1)} %copy-done.7, bf16[1936,256]{1,0:T(8,128)(2,1)} %collective-permute-done.8.north_any.refs_7_, ...), custom_call_target="tpu_custom_call" | custom-call | flops 5000000000 | bytes 8000000 | tf_op jit(solution)/shard_map/local_far/pallas_call | solution.py:304
  96.2 11.4 %edge_blocks.2.refs_3_.upper_blocks_any = bf16[30,256,256]{2,1,0:T(8,128)(2,1)} custom-call(s32[16]{0:T(128)} %reshape.24.list_ref.refs_0_, s32[88]{0:T(128)} %constant.228.clone.refs_1_, s32[64]{0:T(128)} %constant.229.clone.refs_2_.slot_ref, f32[256,256]{1,0:T(8,128)} %get-tuple-element.63.refs_3_.sum1_any, f32[16,2,256]{2,1,0:T(2,128)} %bitcast.32, ...), custom_call_target="tpu_custom_call" | custom-call | flops 6000000000 | bytes 8000000 | tf_op jit(solution)/shard_map/edge_blocks/pallas_call | solution.py:712
  107.7 11.5 %edge_blocks.3.lower_blocks_any = bf16[30,256,256]{2,1,0:T(8,128)(2,1)} custom-call(s32[16]{0:T(128)} %reshape.24.list_ref.refs_0_, s32[88]{0:T(128)} %constant.230.clone.refs_1_, s32[64]{0:T(128)} %constant.229.clone.refs_2_.slot_ref, bf16[30,256,256]{2,1,0:T(8,128)(2,1)} %edge_blocks.2.refs_3_.upper_blocks_any, f32[16,2,256]{2,1,0:T(2,128)} %bitcast.33, ...), custom_call_target="tpu_custom_call" | custom-call | flops 6000000000 | bytes 8000000 | tf_op jit(solution)/shard_map/edge_blocks/pallas_call | solution.py:712
  119.3 4.9 %collective-permute-done.10.other_any = bf16[1280,256]{1,0:T(8,128)(2,1)S(1)} collective-permute-done((bf16[1280,256]{1,0:T(8,128)(2,1)S(1)}, bf16[1280,256]{1,0:T(8,128)(2,1)S(1)}, u32[]{:S(2)}, u32[]{:S(2)}) %collective-permute-start.10) | collective-permute-done | bytes 655392 | tf_op jit(solution)/shard_map/ppermute | solution.py:859
  124.3 0.7 copy-done.16
  125.1 2.9 %collective-permute-start.14 = (bf16[2,4,256,256]{3,2,1,0:T(8,128)(2,1)S(1)}, bf16[2,4,256,256]{3,2,1,0:T(8,128)(2,1)S(1)}, u32[]{:S(2)}, u32[]{:S(2)}) collective-permute-start(bf16[2,4,256,256]{3,2,1,0:T(8,128)(2,1)S(1)} %pad_maximum_fusion.1), channel_id=1, source_target_pairs={{1,0},{2,1},{3,2},{5,4},{6,5},{7,6},{9,8},{10,9},{11,10},{13,12},{... | collective-permute-start | bytes 3145736 | tf_op jit(solution)/shard_map/ppermute | solution.py:119
  128.0 1.1 pad_maximum_fusion
  129.0 2.9 %collective-permute-start.13 = (bf16[2,4,256,256]{3,2,1,0:T(8,128)(2,1)}, bf16[2,4,256,256]{3,2,1,0:T(8,128)(2,1)S(1)}, u32[]{:S(2)}, u32[]{:S(2)}) collective-permute-start(bf16[2,4,256,256]{3,2,1,0:T(8,128)(2,1)} %pad_maximum_fusion), channel_id=1, source_target_pairs={{0,1},{1,2},{2,3},{4,5},{5,6},{6,7},{8,9},{9,10},{10,11},{12,13},{... | collective-permute-start | bytes 3145736 | tf_op jit(solution)/shard_map/ppermute | solution.py:119
  132.1 0.7 pad_add_fusion.meta_ref
  132.8 6.2 %top_far.1.field_ref = bf16[16,64,256]{2,1,0:T(8,128)(2,1)} custom-call(s32[74]{0:T(128)} %pad_add_fusion.meta_ref, bf16[1280,256]{1,0:T(8,128)(2,1)} %copy-done.13, bf16[1280,256]{1,0:T(8,128)(2,1)} %copy-done.16, bf16[256,2304]{1,0:T(8,128)(2,1)} %constant.231.clone.c2_any, bf16[256,2304]{1,0:T(8,128)(2,1)} %constant.232.clone.c3_any, ...), custom_call_target="tpu_custom_call" | custom-call | flops 3000000000 | bytes 5000000 | tf_op jit(solution)/shard_map/top_far/pallas_call | solution.py:402
  139.0 2.2 %collective-permute-done.14 = bf16[2,4,256,256]{3,2,1,0:T(8,128)(2,1)S(1)} collective-permute-done((bf16[2,4,256,256]{3,2,1,0:T(8,128)(2,1)S(1)}, bf16[2,4,256,256]{3,2,1,0:T(8,128)(2,1)S(1)}, u32[]{:S(2)}, u32[]{:S(2)}) %collective-permute-start.14) | collective-permute-done | bytes 1048608 | tf_op jit(solution)/shard_map/ppermute | solution.py:119
  141.2 2.8 %collective-permute-done.13 = bf16[2,4,256,256]{3,2,1,0:T(8,128)(2,1)S(1)} collective-permute-done((bf16[2,4,256,256]{3,2,1,0:T(8,128)(2,1)}, bf16[2,4,256,256]{3,2,1,0:T(8,128)(2,1)S(1)}, u32[]{:S(2)}, u32[]{:S(2)}) %collective-permute-start.13) | collective-permute-done | bytes 1048608 | tf_op jit(solution)/shard_map/ppermute | solution.py:119
  144.0 1.0 copy-done.5
  145.0 12.7 %finish.1 = bf16[16,256,256]{2,1,0:T(8,128)(2,1)} custom-call(s32[16]{0:T(128)} %reshape.24.list_ref.refs_0_, s32[64]{0:T(128)} %constant.229.clone.refs_2_.slot_ref, bf16[16,256,256]{2,1,0:T(8,128)(2,1)} %bitcast.21, bf16[8,256,256]{2,1,0:T(8,128)(2,1)} %copy-done, bf16[8,256,256]{2,1,0:T(8,128)(2,1)} %copy-done.1, bf16[8,256,256]{2,1,0:T(8,128)(2,1)} %copy-done.2, ...), custom_call_target="tpu_custom_call" | custom-call | flops 4000000000 | bytes 24000000 | tf_op jit(solution)/shard_map/finish/pallas_call | solution.py:799
  (57 shorter events, 3.6 us)
Async XLA Ops:
  0.0 16.8 %copy-start.10 = (f32[4,4,256]{2,1,0:T(4,128)S(1)}, f32[4,4,256]{2,1,0:T(4,128)}, u32[]{:S(2)}) copy-start(f32[4,4,256]{2,1,0:T(4,128)} %param.21) | copy-start | bytes 49156
  5.6 21.0 %collective-permute-start.1 = (bf16[8,256,256]{2,1,0:T(8,128)(2,1)}, bf16[8,256,256]{2,1,0:T(8,128)(2,1)S(1)}, u32[]{:S(2)}, u32[]{:S(2)}) collective-permute-start(bf16[8,256,256]{2,1,0:T(8,128)(2,1)} %get-tuple-element.45), channel_id=1, source_target_pairs={{0,1},{1,2},{2,3},{4,5},{5,6},{6,7},{8,9},{9,10},{10,11},{12,13},{... | collective-permute-start | bytes 3145736 | tf_op jit(solution)/shard_map/ppermute | solution.py:119
  10.1 16.6 %collective-permute-start.2 = (bf16[8,256,256]{2,1,0:T(8,128)(2,1)}, bf16[8,256,256]{2,1,0:T(8,128)(2,1)S(1)}, u32[]{:S(2)}, u32[]{:S(2)}) collective-permute-start(bf16[8,256,256]{2,1,0:T(8,128)(2,1)} %get-tuple-element.46), channel_id=1, source_target_pairs={{1,0},{2,1},{3,2},{5,4},{6,5},{7,6},{9,8},{10,9},{11,10},{13,12},{... | collective-permute-start | bytes 3145736 | tf_op jit(solution)/shard_map/ppermute | solution.py:119
  12.0 14.5 %collective-permute-start = (bf16[80,256]{1,0:T(8,128)(2,1)}, bf16[80,256]{1,0:T(8,128)(2,1)S(1)}, u32[]{:S(2)}, u32[]{:S(2)}) collective-permute-start(bf16[80,256]{1,0:T(8,128)(2,1)} %get-tuple-element.42.after_ref), channel_id=1, source_target_pairs={{0,4},{4,0},{8,12},{12,8},{16,20},{20,16},{24,28},{28,24},{1,5},{5... | collective-permute-start | bytes 122888 | tf_op jit(solution)/shard_map/ppermute | solution.py:859
  13.3 23.3 %collective-permute-start.4 = (bf16[816,256]{1,0:T(8,128)(2,1)}, bf16[816,256]{1,0:T(8,128)(2,1)S(1)}, u32[]{:S(2)}, u32[]{:S(2)}) collective-permute-start(bf16[816,256]{1,0:T(8,128)(2,1)} %get-tuple-element.48), channel_id=1, source_target_pairs={{0,4},{4,8},{8,12},{12,16},{16,20},{20,24},{24,28},{1,5},{5,9},{9,... | collective-permute-start | bytes 1253384 | tf_op jit(solution)/shard_map/ppermute | solution.py:119
  15.5 21.2 %collective-permute-start.5 = (bf16[816,256]{1,0:T(8,128)(2,1)}, bf16[816,256]{1,0:T(8,128)(2,1)S(1)}, u32[]{:S(2)}, u32[]{:S(2)}) collective-permute-start(bf16[816,256]{1,0:T(8,128)(2,1)} %get-tuple-element.49), channel_id=1, source_target_pairs={{4,0},{8,4},{12,8},{16,12},{20,16},{24,20},{28,24},{5,1},{9,5},{13... | collective-permute-start | bytes 1253384 | tf_op jit(solution)/shard_map/ppermute | solution.py:119
  17.4 8.5 %copy-start.8 = (bf16[80,256]{1,0:T(8,128)(2,1)S(1)}, bf16[80,256]{1,0:T(8,128)(2,1)}, u32[]{:S(2)}) copy-start(bf16[80,256]{1,0:T(8,128)(2,1)} %get-tuple-element.42.after_ref) | copy-start | bytes 122884
  26.6 10.1 %copy-start.2 = (bf16[8,256,256]{2,1,0:T(8,128)(2,1)}, bf16[8,256,256]{2,1,0:T(8,128)(2,1)S(1)}, u32[]{:S(2)}) copy-start(bf16[8,256,256]{2,1,0:T(8,128)(2,1)S(1)} %collective-permute-done.1.north_any) | copy-start | bytes 3145732
  26.7 9.9 %copy-start.3 = (bf16[8,256,256]{2,1,0:T(8,128)(2,1)}, bf16[8,256,256]{2,1,0:T(8,128)(2,1)S(1)}, u32[]{:S(2)}) copy-start(bf16[8,256,256]{2,1,0:T(8,128)(2,1)S(1)} %collective-permute-done.2.south_any) | copy-start | bytes 3145732
  27.5 0.6 copy-start.9
  27.5 18.6 %copy-start.11 = (s32[4,4,10]{2,1,0:T(4,128)S(1)}, s32[4,4,10]{2,1,0:T(4,128)}, u32[]{:S(2)}) copy-start(s32[4,4,10]{2,1,0:T(4,128)} %param.24) | copy-start | bytes 1924
  27.5 9.2 %collective-permute-start.3 = (bf16[160,256]{1,0:T(8,128)(2,1)S(1)}, bf16[160,256]{1,0:T(8,128)(2,1)S(1)}, u32[]{:S(2)}, u32[]{:S(2)}) collective-permute-start(bf16[160,256]{1,0:T(8,128)(2,1)S(1)} %get-tuple-element.83.after_ref), channel_id=1, source_target_pairs={{0,1},{1,0},{2,3},{3,2},{4,5},{5,4},{6,7},{7,6},{8,9},{9,8},{10,11... | collective-permute-start | bytes 245768 | tf_op jit(solution)/shard_map/ppermute | solution.py:859
  36.7 0.8 copy-start.6
  36.7 0.9 copy-start.7
  40.2 48.6 %collective-permute-start.7 = (bf16[1936,256]{1,0:T(8,128)(2,1)}, bf16[1936,256]{1,0:T(8,128)(2,1)}, u32[]{:S(2)}, u32[]{:S(2)}) collective-permute-start(bf16[1936,256]{1,0:T(8,128)(2,1)} %get-tuple-element.56.after_ref), channel_id=1, source_target_pairs={{1,0},{2,1},{3,2},{5,4},{6,5},{7,6},{9,8},{10,9},{11,10},{13,12},{... | collective-permute-start | bytes 2973704 | tf_op jit(solution)/shard_map/ppermute | solution.py:119
  42.2 46.6 %collective-permute-start.8 = (bf16[1936,256]{1,0:T(8,128)(2,1)}, bf16[1936,256]{1,0:T(8,128)(2,1)}, u32[]{:S(2)}, u32[]{:S(2)}) collective-permute-start(bf16[1936,256]{1,0:T(8,128)(2,1)} %get-tuple-element.57), channel_id=1, source_target_pairs={{0,1},{1,2},{2,3},{4,5},{5,6},{6,7},{8,9},{9,10},{10,11},{12,13},{... | collective-permute-start | bytes 2973704 | tf_op jit(solution)/shard_map/ppermute | solution.py:119
  47.0 72.3 %collective-permute-start.11 = (bf16[8,256,256]{2,1,0:T(8,128)(2,1)}, bf16[8,256,256]{2,1,0:T(8,128)(2,1)S(1)}, u32[]{:S(2)}, u32[]{:S(2)}) collective-permute-start(bf16[8,256,256]{2,1,0:T(8,128)(2,1)} %get-tuple-element.66), channel_id=1, source_target_pairs={{0,4},{4,8},{8,12},{12,16},{16,20},{20,24},{24,28},{1,5},{5,9},{9,... | collective-permute-start | bytes 3145736 | tf_op jit(solution)/shard_map/ppermute | solution.py:119
  51.8 67.5 %collective-permute-start.12 = (bf16[8,256,256]{2,1,0:T(8,128)(2,1)}, bf16[8,256,256]{2,1,0:T(8,128)(2,1)S(1)}, u32[]{:S(2)}, u32[]{:S(2)}) collective-permute-start(bf16[8,256,256]{2,1,0:T(8,128)(2,1)} %get-tuple-element.67), channel_id=1, source_target_pairs={{4,0},{8,4},{12,8},{16,12},{20,16},{24,20},{28,24},{5,1},{9,5},{13... | collective-permute-start | bytes 3145736 | tf_op jit(solution)/shard_map/ppermute | solution.py:119
  53.1 17.3 %copy-start.12 = (bf16[1280,256]{1,0:T(8,128)(2,1)S(1)}, bf16[1280,256]{1,0:T(8,128)(2,1)}, u32[]{:S(2)}) copy-start(bf16[1280,256]{1,0:T(8,128)(2,1)} %get-tuple-element.84) | copy-start | bytes 1966084
  53.1 35.7 %collective-permute-start.6 = (bf16[320,256]{1,0:T(8,128)(2,1)S(1)}, bf16[320,256]{1,0:T(8,128)(2,1)S(1)}, u32[]{:S(2)}, u32[]{:S(2)}) collective-permute-start(bf16[320,256]{1,0:T(8,128)(2,1)S(1)} %pad_maximum_fusion.3), channel_id=1, source_target_pairs={{0,16},{4,20},{8,24},{12,28},{16,0},{20,4},{24,8},{28,12},{1,17},{... | collective-permute-start | bytes 491528 | tf_op jit(solution)/shard_map/ppermute | solution.py:859
  88.8 18.8 %collective-permute-start.9 = (bf16[640,256]{1,0:T(8,128)(2,1)S(1)}, bf16[640,256]{1,0:T(8,128)(2,1)S(1)}, u32[]{:S(2)}, u32[]{:S(2)}) collective-permute-start(bf16[640,256]{1,0:T(8,128)(2,1)S(1)} %pad_maximum_fusion.2), channel_id=1, source_target_pairs={{0,8},{4,12},{8,0},{12,4},{16,24},{20,28},{24,16},{28,20},{1,9},{5... | collective-permute-start | bytes 983048 | tf_op jit(solution)/shard_map/ppermute | solution.py:859
  107.7 11.6 %copy-start.13 = (bf16[1280,256]{1,0:T(8,128)(2,1)}, bf16[1280,256]{1,0:T(8,128)(2,1)S(1)}, u32[]{:S(2)}) copy-start(bf16[1280,256]{1,0:T(8,128)(2,1)S(1)} %constant_dynamic-update-slice_fusion.2.mine_any) | copy-start | bytes 1966084
  107.7 16.5 %collective-permute-start.10 = (bf16[1280,256]{1,0:T(8,128)(2,1)S(1)}, bf16[1280,256]{1,0:T(8,128)(2,1)S(1)}, u32[]{:S(2)}, u32[]{:S(2)}) collective-permute-start(bf16[1280,256]{1,0:T(8,128)(2,1)S(1)} %constant_dynamic-update-slice_fusion.2.mine_any), channel_id=1, source_target_pairs={{0,2},{1,3},{2,0},{3,1},{4,6},{5,7},{6,4},{7,5},{8,10},{9,11},{10,... | collective-permute-start | bytes 1966088 | tf_op jit(solution)/shard_map/ppermute | solution.py:859
  119.3 5.1 %copy-start = (bf16[8,256,256]{2,1,0:T(8,128)(2,1)}, bf16[8,256,256]{2,1,0:T(8,128)(2,1)S(1)}, u32[]{:S(2)}) copy-start(bf16[8,256,256]{2,1,0:T(8,128)(2,1)S(1)} %collective-permute-done.11.west_any) | copy-start | bytes 3145732
  119.3 5.1 %copy-start.1 = (bf16[8,256,256]{2,1,0:T(8,128)(2,1)}, bf16[8,256,256]{2,1,0:T(8,128)(2,1)S(1)}, u32[]{:S(2)}) copy-start(bf16[8,256,256]{2,1,0:T(8,128)(2,1)S(1)} %collective-permute-done.12.east_any) | copy-start | bytes 3145732
  124.1 0.9 copy-start.16
  125.0 7.0 %copy-start.14 = (s32[36]{0:T(128)S(1)}, s32[36]{0:T(128)}, u32[]{:S(2)}) copy-start(s32[36]{0:T(128)} %constant.220.clone) | copy-start | bytes 436
  125.0 7.1 %copy-start.15 = (s32[36]{0:T(128)S(1)}, s32[36]{0:T(128)}, u32[]{:S(2)}) copy-start(s32[36]{0:T(128)} %constant.221.clone) | copy-start | bytes 436
  125.1 16.1 %collective-permute-start.14 = (bf16[2,4,256,256]{3,2,1,0:T(8,128)(2,1)S(1)}, bf16[2,4,256,256]{3,2,1,0:T(8,128)(2,1)S(1)}, u32[]{:S(2)}, u32[]{:S(2)}) collective-permute-start(bf16[2,4,256,256]{3,2,1,0:T(8,128)(2,1)S(1)} %pad_maximum_fusion.1), channel_id=1, source_target_pairs={{1,0},{2,1},{3,2},{5,4},{6,5},{7,6},{9,8},{10,9},{11,10},{13,12},{... | collective-permute-start | bytes 3145736 | tf_op jit(solution)/shard_map/ppermute | solution.py:119
  129.0 14.9 %collective-permute-start.13 = (bf16[2,4,256,256]{3,2,1,0:T(8,128)(2,1)}, bf16[2,4,256,256]{3,2,1,0:T(8,128)(2,1)S(1)}, u32[]{:S(2)}, u32[]{:S(2)}) collective-permute-start(bf16[2,4,256,256]{3,2,1,0:T(8,128)(2,1)} %pad_maximum_fusion), channel_id=1, source_target_pairs={{0,1},{1,2},{2,3},{4,5},{5,6},{6,7},{8,9},{9,10},{10,11},{12,13},{... | collective-permute-start | bytes 3145736 | tf_op jit(solution)/shard_map/ppermute | solution.py:119
  141.2 2.8 %copy-start.4 = (bf16[2,4,256,256]{3,2,1,0:T(8,128)(2,1)}, bf16[2,4,256,256]{3,2,1,0:T(8,128)(2,1)S(1)}, u32[]{:S(2)}) copy-start(bf16[2,4,256,256]{3,2,1,0:T(8,128)(2,1)S(1)} %collective-permute-done.14) | copy-start | bytes 3145732
  144.0 1.0 copy-start.5

commit v10 on v8

--- a/solution.py
+++ b/solution.py
@@ -480,15 +480,18 @@
 def block_into(to, columns, points, shift_y, shift_x):
     source_x = (points[0:1] + shift_x.astype(F32)) * waves
     source_y = (points[1:2] + shift_y.astype(F32)) * waves
-    rows = 32
+    rows = 16
+    source_x = jnp.broadcast_to(source_x, (rows, LEAF))
+    source_y = jnp.broadcast_to(source_y, (rows, LEAF))
     for i in range(0, LEAF, rows):
-        for j in (0, 128):
-            to[i : i + rows, j : j + 128] = kernel_of(
-                columns[i : i + rows, 0:128],
-                columns[i : i + rows, 128:256],
-                jnp.broadcast_to(source_x[:, j : j + 128], (rows, 128)),
-                jnp.broadcast_to(source_y[:, j : j + 128], (rows, 128)),
-            )
+        target_x = columns[i : i + rows, 0:128]
+        target_y = columns[i : i + rows, 128:256]
+        to[i : i + rows] = kernel_of(
+            jnp.concatenate([target_x, target_x], axis=1),
+            jnp.concatenate([target_y, target_y], axis=1),
+            source_x,
+            source_y,
+        )
 
 
 def turn_points(columns, leaf, position, noise):

time: 140 us -> 140 us (level)
  Pallas kernels: 85.8 us -> 84.2 us
  transfers between devices with their start and end apart: 15 -> 15, of which waited for: 4 -> 4; matrix products, arithmetic and copies ran while one was open for 3% -> 3% of each run, Pallas kernels for 47% -> 46%
where the time goes in v10:
time: 140 us; the launch traced here: 139 us
  Pallas kernels  84.2 us (60%)
  starting transfers between devices  36.2 us (26%)
  waiting for transfers between devices  10.2 us (7%)
  local copies, waits for them, and re-layouts  5.49 us (4%)
  other arithmetic  2 us (1%)
    pallas_call x3, Pallas kernels, near_own(): pl.pallas_call(body, out_shape=jax.ShapeDtypeStruct((leaves, LEAF, LEAF),...  28.3 us
    ppermute x10, starting transfers between devices, shift(): lax.ppermute(value, axis, [(i, i + steps) for i in range(count) if 0 <= i...  24.3 us
    pallas_call x2, Pallas kernels, edge_blocks(): pl.pallas_call(body, out_shape=jax.ShapeDtypeStruct((EDGES // 2 + 8, LEAF...  22.6 us
    pallas_call x1, Pallas kernels, finish(): pl.pallas_call(final_body, out_shape=jax.ShapeDtypeStruct((LEAVES, LEAF,...  12.1 us
    ppermute x5, starting transfers between devices, step(): lax.ppermute(value, axis, [(i, i ^ bit) for i in range(lax.axis_size(axis...  12 us
    pallas_call x1, Pallas kernels, local_far(): pl.pallas_call(local_body, out_shape=(jax.ShapeDtypeStruct((LEAVES, RANK,...  6.7 us
    pallas_call x1, Pallas kernels, top_far(): pl.pallas_call(top_body, out_shape=jax.ShapeDtypeStruct((LEAVES, RANK, LE...  6.23 us
    pallas_call x1, Pallas kernels, go_up(): pl.pallas_call(up_body, out_shape=(side, side, side, side, jax.ShapeDtype...  5.59 us
  transfers between devices with their start and end apart: 15, of which 4 were waited for; matrix products, arithmetic and copies ran while one was open for 3% of the time, Pallas kernels for 46%

profile of v10, /device:TPU:1, one launch (start us, length us, event | category | flops | bytes accessed | tf_op | source)
XLA Modules:
  0.0 138.8 jit_solution(11088614180616211905)
XLA Ops:
  0.0 5.6 %upward.1 = (bf16[816,256]{1,0:T(8,128)(2,1)}, bf16[816,256]{1,0:T(8,128)(2,1)}, bf16[816,256]{1,0:T(8,128)(2,1)}, bf16[816,256]{1,0:T(8,128)(2,1)}, bf16[1280,2...) custom-call(bf16[16,256,256]{2,1,0:T(8,128)(2,1)} %bitcast.17, ...), custom_call_target="tpu_custom_call" | custom-call | flops 300000000 | bytes 5000000 | tf_op jit(solution)/shard_map/upward/pallas_call | solution.py:205
  5.6 2.1 %collective-permute-start = (bf16[80,256]{1,0:T(8,128)(2,1)}, bf16[80,256]{1,0:T(8,128)(2,1)S(1)}, u32[]{:S(2)}, u32[]{:S(2)}) collective-permute-start(bf16[80,256]{1,0:T(8,128)(2,1)} %get-tuple-element.42.after_ref), channel_id=1, source_target_pairs={{0,4},{4,0},{8,12},{12,8},{16,20},{20,16},{24,28},{28,24},{1,5},{5... | collective-permute-start | bytes 122888 | tf_op jit(solution)/shard_map/ppermute | solution.py:862
  7.7 4.0 %collective-permute-start.4 = (bf16[8,256,256]{2,1,0:T(8,128)(2,1)}, bf16[8,256,256]{2,1,0:T(8,128)(2,1)S(1)}, u32[]{:S(2)}, u32[]{:S(2)}) collective-permute-start(bf16[8,256,256]{2,1,0:T(8,128)(2,1)} %get-tuple-element.49), channel_id=1, source_target_pairs={{0,1},{1,2},{2,3},{4,5},{5,6},{6,7},{8,9},{9,10},{10,11},{12,13},{... | collective-permute-start | bytes 3145736 | tf_op jit(solution)/shard_map/ppermute | solution.py:119
  11.7 1.9 %collective-permute-start.5 = (bf16[8,256,256]{2,1,0:T(8,128)(2,1)}, bf16[8,256,256]{2,1,0:T(8,128)(2,1)S(1)}, u32[]{:S(2)}, u32[]{:S(2)}) collective-permute-start(bf16[8,256,256]{2,1,0:T(8,128)(2,1)} %get-tuple-element.50), channel_id=1, source_target_pairs={{1,0},{2,1},{3,2},{5,4},{6,5},{7,6},{9,8},{10,9},{11,10},{13,12},{... | collective-permute-start | bytes 3145736 | tf_op jit(solution)/shard_map/ppermute | solution.py:119
  13.6 2.2 %collective-permute-start.2 = (bf16[816,256]{1,0:T(8,128)(2,1)}, bf16[816,256]{1,0:T(8,128)(2,1)S(1)}, u32[]{:S(2)}, u32[]{:S(2)}) collective-permute-start(bf16[816,256]{1,0:T(8,128)(2,1)} %get-tuple-element.44), channel_id=1, source_target_pairs={{0,4},{4,8},{8,12},{12,16},{16,20},{20,24},{24,28},{1,5},{5,9},{9,... | collective-permute-start | bytes 1253384 | tf_op jit(solution)/shard_map/ppermute | solution.py:119
  15.8 1.3 collective-permute-start.3
  17.7 8.4 %near_own.3.refs_4_.row0_any = f32[8,256,256]{2,1,0:T(8,128)} custom-call(bf16[80,256]{1,0:T(8,128)(2,1)} %get-tuple-element.42.after_ref, s32[52]{0:T(128)} %constant.222.clone.refs_0_, bf16[16,256,256]{2,1,0:T(8,128)(2,1)} %bitcast.18, f32[16,2,256]{2,1,0:T(2,128)} %bitcast.29, f32[16,1,256]{2,1,0:T(1,128)} %reshape.28.refs_3_), custom_call_target="tpu_custom_call" | custom-call | flops 6000000000 | bytes 4000000 | tf_op jit(solution)/shard_map/near_own/pallas_call | solution.py:606
  26.8 0.6 constant_dynamic-update-slice_fusion
  27.4 0.6 copy-done.9
  28.1 8.4 %near_own.4.refs_4_.row1_any = f32[8,256,256]{2,1,0:T(8,128)} custom-call(bf16[160,256]{1,0:T(8,128)(2,1)} %copy-done.9, s32[52]{0:T(128)} %constant.223.clone.refs_0_, bf16[16,256,256]{2,1,0:T(8,128)(2,1)} %bitcast.19, f32[16,2,256]{2,1,0:T(2,128)} %bitcast.30, f32[16,1,256]{2,1,0:T(1,128)} %reshape.28.refs_3_, f32[8,256,256]{2,1,0:T(8,128)} %near_own.3.refs_4_.row0_any), custom_call_target="tpu_custom_call" | custom-call | flops 6000000000 | bytes 4000000 | tf_op jit(solution)/shard_map/near_own/pallas_call | solution.py:606
  36.5 1.0 copy-done.6
  37.7 2.6 %join.1 = (bf16[1936,256]{1,0:T(8,128)(2,1)}, bf16[1936,256]{1,0:T(8,128)(2,1)}) custom-call(bf16[816,256]{1,0:T(8,128)(2,1)} %get-tuple-element.52.north_ref, bf16[816,256]{1,0:T(8,128)(2,1)} %get-tuple-element.53.south_ref, bf16[816,256]{1,0:T(8,128)(2,1)} %copy-done.6, bf16[816,256]{1,0:T(8,128)(2,1)} %copy-done.7), custom_call_target="tpu_custom_call" | custom-call | bytes 4000000 | tf_op jit(solution)/shard_map/join/pallas_call | solution.py:450
  40.3 1.9 %collective-permute-start.7 = (bf16[1936,256]{1,0:T(8,128)(2,1)}, bf16[1936,256]{1,0:T(8,128)(2,1)}, u32[]{:S(2)}, u32[]{:S(2)}) collective-permute-start(bf16[1936,256]{1,0:T(8,128)(2,1)} %get-tuple-element.56.after_ref), channel_id=1, source_target_pairs={{1,0},{2,1},{3,2},{5,4},{6,5},{7,6},{9,8},{10,9},{11,10},{13,12},{... | collective-permute-start | bytes 2973704 | tf_op jit(solution)/shard_map/ppermute | solution.py:119
  42.2 3.9 %collective-permute-start.8 = (bf16[1936,256]{1,0:T(8,128)(2,1)}, bf16[1936,256]{1,0:T(8,128)(2,1)}, u32[]{:S(2)}, u32[]{:S(2)}) collective-permute-start(bf16[1936,256]{1,0:T(8,128)(2,1)} %get-tuple-element.57), channel_id=1, source_target_pairs={{0,1},{1,2},{2,3},{4,5},{5,6},{6,7},{8,9},{9,10},{10,11},{12,13},{... | collective-permute-start | bytes 2973704 | tf_op jit(solution)/shard_map/ppermute | solution.py:119
  47.0 5.4 %collective-permute-start.6 = (bf16[320,256]{1,0:T(8,128)(2,1)S(1)}, bf16[320,256]{1,0:T(8,128)(2,1)S(1)}, u32[]{:S(2)}, u32[]{:S(2)}) collective-permute-start(bf16[320,256]{1,0:T(8,128)(2,1)S(1)} %pad_maximum_fusion.3), channel_id=1, source_target_pairs={{0,16},{4,20},{8,24},{12,28},{16,0},{20,4},{24,8},{28,12},{1,17},{... | collective-permute-start | bytes 491528 | tf_op jit(solution)/shard_map/ppermute | solution.py:862
  52.3 1.8 %collective-permute-start.11 = (bf16[8,256,256]{2,1,0:T(8,128)(2,1)}, bf16[8,256,256]{2,1,0:T(8,128)(2,1)S(1)}, u32[]{:S(2)}, u32[]{:S(2)}) collective-permute-start(bf16[8,256,256]{2,1,0:T(8,128)(2,1)} %get-tuple-element.66), channel_id=1, source_target_pairs={{0,4},{4,8},{8,12},{12,16},{16,20},{20,24},{24,28},{1,5},{5,9},{9,... | collective-permute-start | bytes 3145736 | tf_op jit(solution)/shard_map/ppermute | solution.py:119
  54.1 1.5 %collective-permute-start.12 = (bf16[8,256,256]{2,1,0:T(8,128)(2,1)}, bf16[8,256,256]{2,1,0:T(8,128)(2,1)S(1)}, u32[]{:S(2)}, u32[]{:S(2)}) collective-permute-start(bf16[8,256,256]{2,1,0:T(8,128)(2,1)} %get-tuple-element.67), channel_id=1, source_target_pairs={{4,0},{8,4},{12,8},{16,12},{20,16},{24,20},{28,24},{5,1},{9,5},{13... | collective-permute-start | bytes 3145736 | tf_op jit(solution)/shard_map/ppermute | solution.py:119
  55.6 11.5 %near_own.5.row2_any = f32[8,256,256]{2,1,0:T(8,128)} custom-call(bf16[1936,256]{1,0:T(8,128)(2,1)} %get-tuple-element.56.after_ref, s32[64]{0:T(128)} %constant.224.clone.refs_0_, bf16[16,256,256]{2,1,0:T(8,128)(2,1)} %bitcast.20, f32[16,2,256]{2,1,0:T(2,128)} %bitcast.31, f32[16,1,256]{2,1,0:T(1,128)} %reshape.28.refs_3_, ...), custom_call_target="tpu_custom_call" | custom-call | flops 6000000000 | bytes 4000000 | tf_op jit(solution)/shard_map/near_own/pallas_call | solution.py:606
  67.2 4.4 %collective-permute-start.9 = (bf16[640,256]{1,0:T(8,128)(2,1)S(1)}, bf16[640,256]{1,0:T(8,128)(2,1)S(1)}, u32[]{:S(2)}, u32[]{:S(2)}) collective-permute-start(bf16[640,256]{1,0:T(8,128)(2,1)S(1)} %pad_maximum_fusion.2), channel_id=1, source_target_pairs={{0,8},{4,12},{8,0},{12,4},{16,24},{20,28},{24,16},{28,20},{1,9},{5... | collective-permute-start | bytes 983048 | tf_op jit(solution)/shard_map/ppermute | solution.py:862
  71.7 6.7 %local_far.1 = (f32[16,64,256]{2,1,0:T(8,128)}, f32[256,256]{1,0:T(8,128)}) custom-call(s32[16]{0:T(128)} %reshape.24.list_ref.refs_0_, bf16[1280,256]{1,0:T(8,128)(2,1)} %get-tuple-element.60.coef_any, bf16[816,256]{1,0:T(8,128)(2,1)} %copy-done.6, bf16[816,256]{1,0:T(8,128)(2,1)} %copy-done.7, bf16[1936,256]{1,0:T(8,128)(2,1)} %collective-permute-done.8.north_any.refs_7_, ...), custom_call_target="tpu_custom_call" | custom-call | flops 5000000000 | bytes 8000000 | tf_op jit(solution)/shard_map/local_far/pallas_call | solution.py:304
  78.4 11.3 %edge_blocks.2.refs_3_.upper_blocks_any = bf16[30,256,256]{2,1,0:T(8,128)(2,1)} custom-call(s32[16]{0:T(128)} %reshape.24.list_ref.refs_0_, s32[88]{0:T(128)} %constant.228.clone.refs_1_, s32[64]{0:T(128)} %constant.229.clone.refs_2_.slot_ref, f32[256,256]{1,0:T(8,128)} %get-tuple-element.63.refs_3_.sum1_any, f32[16,2,256]{2,1,0:T(2,128)} %bitcast.32, ...), custom_call_target="tpu_custom_call" | custom-call | flops 6000000000 | bytes 8000000 | tf_op jit(solution)/shard_map/edge_blocks/pallas_call | solution.py:715
  89.7 0.8 collective-permute-done.9
  90.6 11.3 %edge_blocks.3.lower_blocks_any = bf16[30,256,256]{2,1,0:T(8,128)(2,1)} custom-call(s32[16]{0:T(128)} %reshape.24.list_ref.refs_0_, s32[88]{0:T(128)} %constant.230.clone.refs_1_, s32[64]{0:T(128)} %constant.229.clone.refs_2_.slot_ref, bf16[30,256,256]{2,1,0:T(8,128)(2,1)} %edge_blocks.2.refs_3_.upper_blocks_any, f32[16,2,256]{2,1,0:T(2,128)} %bitcast.33, ...), custom_call_target="tpu_custom_call" | custom-call | flops 6000000000 | bytes 8000000 | tf_op jit(solution)/shard_map/edge_blocks/pallas_call | solution.py:715
  102.0 4.3 %collective-permute-done.10.other_any = bf16[1280,256]{1,0:T(8,128)(2,1)} collective-permute-done((bf16[1280,256]{1,0:T(8,128)(2,1)S(1)}, bf16[1280,256]{1,0:T(8,128)(2,1)}, u32[]{:S(2)}, u32[]{:S(2)}) %collective-permute-start.10) | collective-permute-done | bytes 655392 | tf_op jit(solution)/shard_map/ppermute | solution.py:862
  106.7 3.6 %collective-permute-start.14 = (bf16[2,4,256,256]{3,2,1,0:T(8,128)(2,1)S(1)}, bf16[2,4,256,256]{3,2,1,0:T(8,128)(2,1)S(1)}, u32[]{:S(2)}, u32[]{:S(2)}) collective-permute-start(bf16[2,4,256,256]{3,2,1,0:T(8,128)(2,1)S(1)} %pad_maximum_fusion.1), channel_id=1, source_target_pairs={{1,0},{2,1},{3,2},{5,4},{6,5},{7,6},{9,8},{10,9},{11,10},{13,12},{... | collective-permute-start | bytes 3145736 | tf_op jit(solution)/shard_map/ppermute | solution.py:119
  110.3 1.1 pad_maximum_fusion
  111.4 2.1 %collective-permute-start.13 = (bf16[2,4,256,256]{3,2,1,0:T(8,128)(2,1)}, bf16[2,4,256,256]{3,2,1,0:T(8,128)(2,1)S(1)}, u32[]{:S(2)}, u32[]{:S(2)}) collective-permute-start(bf16[2,4,256,256]{3,2,1,0:T(8,128)(2,1)} %pad_maximum_fusion), channel_id=1, source_target_pairs={{0,1},{1,2},{2,3},{4,5},{5,6},{6,7},{8,9},{9,10},{10,11},{12,13},{... | collective-permute-start | bytes 3145736 | tf_op jit(solution)/shard_map/ppermute | solution.py:119
  114.3 6.2 %top_far.1.field_ref = bf16[16,64,256]{2,1,0:T(8,128)(2,1)} custom-call(s32[74]{0:T(128)} %pad_add_fusion.meta_ref, bf16[1280,256]{1,0:T(8,128)(2,1)} %copy-done.13, bf16[1280,256]{1,0:T(8,128)(2,1)} %collective-permute-done.10.other_any, bf16[256,2304]{1,0:T(8,128)(2,1)} %constant.231.clone.c2_any, bf16[256,2304]{1,0:T(8,128)(2,1)} %constant.232.clone.c3_any, ...), custom_call_target="tpu_custom_call" | custom-call | flops 3000000000 | bytes 5000000 | tf_op jit(solution)/shard_map/top_far/pallas_call | solution.py:402
  120.5 2.3 %collective-permute-done.14 = bf16[2,4,256,256]{3,2,1,0:T(8,128)(2,1)S(1)} collective-permute-done((bf16[2,4,256,256]{3,2,1,0:T(8,128)(2,1)S(1)}, bf16[2,4,256,256]{3,2,1,0:T(8,128)(2,1)S(1)}, u32[]{:S(2)}, u32[]{:S(2)}) %collective-permute-start.14) | collective-permute-done | bytes 1048608 | tf_op jit(solution)/shard_map/ppermute | solution.py:119
  122.8 2.8 %collective-permute-done.13 = bf16[2,4,256,256]{3,2,1,0:T(8,128)(2,1)S(1)} collective-permute-done((bf16[2,4,256,256]{3,2,1,0:T(8,128)(2,1)}, bf16[2,4,256,256]{3,2,1,0:T(8,128)(2,1)S(1)}, u32[]{:S(2)}, u32[]{:S(2)}) %collective-permute-start.13) | collective-permute-done | bytes 1048608 | tf_op jit(solution)/shard_map/ppermute | solution.py:119
  125.6 1.0 copy-done.5
  126.6 12.1 %finish.1 = bf16[16,256,256]{2,1,0:T(8,128)(2,1)} custom-call(s32[16]{0:T(128)} %reshape.24.list_ref.refs_0_, s32[64]{0:T(128)} %constant.229.clone.refs_2_.slot_ref, bf16[16,256,256]{2,1,0:T(8,128)(2,1)} %bitcast.21, bf16[8,256,256]{2,1,0:T(8,128)(2,1)} %copy-done, bf16[8,256,256]{2,1,0:T(8,128)(2,1)} %copy-done.1, bf16[8,256,256]{2,1,0:T(8,128)(2,1)} %copy-done.2, ...), custom_call_target="tpu_custom_call" | custom-call | flops 4000000000 | bytes 24000000 | tf_op jit(solution)/shard_map/finish/pallas_call | solution.py:802
  (55 shorter events, 3.3 us)
Async XLA Ops:
  0.0 17.1 %copy-start.10 = (f32[4,4,256]{2,1,0:T(4,128)S(1)}, f32[4,4,256]{2,1,0:T(4,128)}, u32[]{:S(2)}) copy-start(f32[4,4,256]{2,1,0:T(4,128)} %param.21) | copy-start | bytes 49156
  5.6 21.2 %collective-permute-start = (bf16[80,256]{1,0:T(8,128)(2,1)}, bf16[80,256]{1,0:T(8,128)(2,1)S(1)}, u32[]{:S(2)}, u32[]{:S(2)}) collective-permute-start(bf16[80,256]{1,0:T(8,128)(2,1)} %get-tuple-element.42.after_ref), channel_id=1, source_target_pairs={{0,4},{4,0},{8,12},{12,8},{16,20},{20,16},{24,28},{28,24},{1,5},{5... | collective-permute-start | bytes 122888 | tf_op jit(solution)/shard_map/ppermute | solution.py:862
  7.7 28.8 %collective-permute-start.4 = (bf16[8,256,256]{2,1,0:T(8,128)(2,1)}, bf16[8,256,256]{2,1,0:T(8,128)(2,1)S(1)}, u32[]{:S(2)}, u32[]{:S(2)}) collective-permute-start(bf16[8,256,256]{2,1,0:T(8,128)(2,1)} %get-tuple-element.49), channel_id=1, source_target_pairs={{0,1},{1,2},{2,3},{4,5},{5,6},{6,7},{8,9},{9,10},{10,11},{12,13},{... | collective-permute-start | bytes 3145736 | tf_op jit(solution)/shard_map/ppermute | solution.py:119
  11.7 24.8 %collective-permute-start.5 = (bf16[8,256,256]{2,1,0:T(8,128)(2,1)}, bf16[8,256,256]{2,1,0:T(8,128)(2,1)S(1)}, u32[]{:S(2)}, u32[]{:S(2)}) collective-permute-start(bf16[8,256,256]{2,1,0:T(8,128)(2,1)} %get-tuple-element.50), channel_id=1, source_target_pairs={{1,0},{2,1},{3,2},{5,4},{6,5},{7,6},{9,8},{10,9},{11,10},{13,12},{... | collective-permute-start | bytes 3145736 | tf_op jit(solution)/shard_map/ppermute | solution.py:119
  13.6 22.8 %collective-permute-start.2 = (bf16[816,256]{1,0:T(8,128)(2,1)}, bf16[816,256]{1,0:T(8,128)(2,1)S(1)}, u32[]{:S(2)}, u32[]{:S(2)}) collective-permute-start(bf16[816,256]{1,0:T(8,128)(2,1)} %get-tuple-element.44), channel_id=1, source_target_pairs={{0,4},{4,8},{8,12},{12,16},{16,20},{20,24},{24,28},{1,5},{5,9},{9,... | collective-permute-start | bytes 1253384 | tf_op jit(solution)/shard_map/ppermute | solution.py:119
  15.8 20.7 %collective-permute-start.3 = (bf16[816,256]{1,0:T(8,128)(2,1)}, bf16[816,256]{1,0:T(8,128)(2,1)S(1)}, u32[]{:S(2)}, u32[]{:S(2)}) collective-permute-start(bf16[816,256]{1,0:T(8,128)(2,1)} %get-tuple-element.45), channel_id=1, source_target_pairs={{4,0},{8,4},{12,8},{16,12},{20,16},{24,20},{28,24},{5,1},{9,5},{13... | collective-permute-start | bytes 1253384 | tf_op jit(solution)/shard_map/ppermute | solution.py:119
  17.7 8.4 %copy-start.8 = (bf16[80,256]{1,0:T(8,128)(2,1)S(1)}, bf16[80,256]{1,0:T(8,128)(2,1)}, u32[]{:S(2)}) copy-start(bf16[80,256]{1,0:T(8,128)(2,1)} %get-tuple-element.42.after_ref) | copy-start | bytes 122884
  27.4 0.6 copy-start.9
  27.4 18.7 %copy-start.11 = (s32[4,4,10]{2,1,0:T(4,128)S(1)}, s32[4,4,10]{2,1,0:T(4,128)}, u32[]{:S(2)}) copy-start(s32[4,4,10]{2,1,0:T(4,128)} %param.24) | copy-start | bytes 1924
  27.4 9.0 %collective-permute-start.1 = (bf16[160,256]{1,0:T(8,128)(2,1)S(1)}, bf16[160,256]{1,0:T(8,128)(2,1)S(1)}, u32[]{:S(2)}, u32[]{:S(2)}) collective-permute-start(bf16[160,256]{1,0:T(8,128)(2,1)S(1)} %get-tuple-element.83.after_ref), channel_id=1, source_target_pairs={{0,1},{1,0},{2,3},{3,2},{4,5},{5,4},{6,7},{7,6},{8,9},{9,8},{10,11... | collective-permute-start | bytes 245768 | tf_op jit(solution)/shard_map/ppermute | solution.py:862
  36.5 1.1 copy-start.6
  36.5 1.2 copy-start.7
  36.5 30.7 %copy-start.2 = (bf16[8,256,256]{2,1,0:T(8,128)(2,1)}, bf16[8,256,256]{2,1,0:T(8,128)(2,1)S(1)}, u32[]{:S(2)}) copy-start(bf16[8,256,256]{2,1,0:T(8,128)(2,1)S(1)} %collective-permute-done.4.north_any) | copy-start | bytes 3145732
  36.5 10.4 %copy-start.3 = (bf16[8,256,256]{2,1,0:T(8,128)(2,1)}, bf16[8,256,256]{2,1,0:T(8,128)(2,1)S(1)}, u32[]{:S(2)}) copy-start(bf16[8,256,256]{2,1,0:T(8,128)(2,1)S(1)} %collective-permute-done.5.south_any) | copy-start | bytes 3145732
  40.3 26.9 %collective-permute-start.7 = (bf16[1936,256]{1,0:T(8,128)(2,1)}, bf16[1936,256]{1,0:T(8,128)(2,1)}, u32[]{:S(2)}, u32[]{:S(2)}) collective-permute-start(bf16[1936,256]{1,0:T(8,128)(2,1)} %get-tuple-element.56.after_ref), channel_id=1, source_target_pairs={{1,0},{2,1},{3,2},{5,4},{6,5},{7,6},{9,8},{10,9},{11,10},{13,12},{... | collective-permute-start | bytes 2973704 | tf_op jit(solution)/shard_map/ppermute | solution.py:119
  42.2 25.0 %collective-permute-start.8 = (bf16[1936,256]{1,0:T(8,128)(2,1)}, bf16[1936,256]{1,0:T(8,128)(2,1)}, u32[]{:S(2)}, u32[]{:S(2)}) collective-permute-start(bf16[1936,256]{1,0:T(8,128)(2,1)} %get-tuple-element.57), channel_id=1, source_target_pairs={{0,1},{1,2},{2,3},{4,5},{5,6},{6,7},{8,9},{9,10},{10,11},{12,13},{... | collective-permute-start | bytes 2973704 | tf_op jit(solution)/shard_map/ppermute | solution.py:119
  46.9 20.2 %copy-start.12 = (bf16[1280,256]{1,0:T(8,128)(2,1)S(1)}, bf16[1280,256]{1,0:T(8,128)(2,1)}, u32[]{:S(2)}) copy-start(bf16[1280,256]{1,0:T(8,128)(2,1)} %get-tuple-element.84) | copy-start | bytes 1966084
  47.0 20.2 %collective-permute-start.6 = (bf16[320,256]{1,0:T(8,128)(2,1)S(1)}, bf16[320,256]{1,0:T(8,128)(2,1)S(1)}, u32[]{:S(2)}, u32[]{:S(2)}) collective-permute-start(bf16[320,256]{1,0:T(8,128)(2,1)S(1)} %pad_maximum_fusion.3), channel_id=1, source_target_pairs={{0,16},{4,20},{8,24},{12,28},{16,0},{20,4},{24,8},{28,12},{1,17},{... | collective-permute-start | bytes 491528 | tf_op jit(solution)/shard_map/ppermute | solution.py:862
  52.3 49.7 %collective-permute-start.11 = (bf16[8,256,256]{2,1,0:T(8,128)(2,1)}, bf16[8,256,256]{2,1,0:T(8,128)(2,1)S(1)}, u32[]{:S(2)}, u32[]{:S(2)}) collective-permute-start(bf16[8,256,256]{2,1,0:T(8,128)(2,1)} %get-tuple-element.66), channel_id=1, source_target_pairs={{0,4},{4,8},{8,12},{12,16},{16,20},{20,24},{24,28},{1,5},{5,9},{9,... | collective-permute-start | bytes 3145736 | tf_op jit(solution)/shard_map/ppermute | solution.py:119
  54.1 47.9 %collective-permute-start.12 = (bf16[8,256,256]{2,1,0:T(8,128)(2,1)}, bf16[8,256,256]{2,1,0:T(8,128)(2,1)S(1)}, u32[]{:S(2)}, u32[]{:S(2)}) collective-permute-start(bf16[8,256,256]{2,1,0:T(8,128)(2,1)} %get-tuple-element.67), channel_id=1, source_target_pairs={{4,0},{8,4},{12,8},{16,12},{20,16},{24,20},{28,24},{5,1},{9,5},{13... | collective-permute-start | bytes 3145736 | tf_op jit(solution)/shard_map/ppermute | solution.py:119
  67.2 23.3 %collective-permute-start.9 = (bf16[640,256]{1,0:T(8,128)(2,1)S(1)}, bf16[640,256]{1,0:T(8,128)(2,1)S(1)}, u32[]{:S(2)}, u32[]{:S(2)}) collective-permute-start(bf16[640,256]{1,0:T(8,128)(2,1)S(1)} %pad_maximum_fusion.2), channel_id=1, source_target_pairs={{0,8},{4,12},{8,0},{12,4},{16,24},{20,28},{24,16},{28,20},{1,9},{5... | collective-permute-start | bytes 983048 | tf_op jit(solution)/shard_map/ppermute | solution.py:862
  90.5 11.4 %copy-start.13 = (bf16[1280,256]{1,0:T(8,128)(2,1)}, bf16[1280,256]{1,0:T(8,128)(2,1)S(1)}, u32[]{:S(2)}) copy-start(bf16[1280,256]{1,0:T(8,128)(2,1)S(1)} %constant_dynamic-update-slice_fusion.2.mine_any) | copy-start | bytes 1966084
  90.6 15.8 %collective-permute-start.10 = (bf16[1280,256]{1,0:T(8,128)(2,1)S(1)}, bf16[1280,256]{1,0:T(8,128)(2,1)}, u32[]{:S(2)}, u32[]{:S(2)}) collective-permute-start(bf16[1280,256]{1,0:T(8,128)(2,1)S(1)} %constant_dynamic-update-slice_fusion.2.mine_any), channel_id=1, source_target_pairs={{0,2},{1,3},{2,0},{3,1},{4,6},{5,7},{6,4},{7,5},{8,10},{9,11},{10,... | collective-permute-start | bytes 1966088 | tf_op jit(solution)/shard_map/ppermute | solution.py:862
  102.0 4.5 %copy-start = (bf16[8,256,256]{2,1,0:T(8,128)(2,1)}, bf16[8,256,256]{2,1,0:T(8,128)(2,1)S(1)}, u32[]{:S(2)}) copy-start(bf16[8,256,256]{2,1,0:T(8,128)(2,1)S(1)} %collective-permute-done.11.west_any) | copy-start | bytes 3145732
  102.0 4.5 %copy-start.1 = (bf16[8,256,256]{2,1,0:T(8,128)(2,1)}, bf16[8,256,256]{2,1,0:T(8,128)(2,1)S(1)}, u32[]{:S(2)}) copy-start(bf16[8,256,256]{2,1,0:T(8,128)(2,1)S(1)} %collective-permute-done.12.east_any) | copy-start | bytes 3145732
  106.5 7.1 %copy-start.14 = (s32[36]{0:T(128)S(1)}, s32[36]{0:T(128)}, u32[]{:S(2)}) copy-start(s32[36]{0:T(128)} %constant.220.clone) | copy-start | bytes 436
  106.6 7.1 %copy-start.15 = (s32[36]{0:T(128)S(1)}, s32[36]{0:T(128)}, u32[]{:S(2)}) copy-start(s32[36]{0:T(128)} %constant.221.clone) | copy-start | bytes 436
  106.7 16.1 %collective-permute-start.14 = (bf16[2,4,256,256]{3,2,1,0:T(8,128)(2,1)S(1)}, bf16[2,4,256,256]{3,2,1,0:T(8,128)(2,1)S(1)}, u32[]{:S(2)}, u32[]{:S(2)}) collective-permute-start(bf16[2,4,256,256]{3,2,1,0:T(8,128)(2,1)S(1)} %pad_maximum_fusion.1), channel_id=1, source_target_pairs={{1,0},{2,1},{3,2},{5,4},{6,5},{7,6},{9,8},{10,9},{11,10},{13,12},{... | collective-permute-start | bytes 3145736 | tf_op jit(solution)/shard_map/ppermute | solution.py:119
  111.4 14.2 %collective-permute-start.13 = (bf16[2,4,256,256]{3,2,1,0:T(8,128)(2,1)}, bf16[2,4,256,256]{3,2,1,0:T(8,128)(2,1)S(1)}, u32[]{:S(2)}, u32[]{:S(2)}) collective-permute-start(bf16[2,4,256,256]{3,2,1,0:T(8,128)(2,1)} %pad_maximum_fusion), channel_id=1, source_target_pairs={{0,1},{1,2},{2,3},{4,5},{5,6},{6,7},{8,9},{9,10},{10,11},{12,13},{... | collective-permute-start | bytes 3145736 | tf_op jit(solution)/shard_map/ppermute | solution.py:119
  122.8 2.8 %copy-start.4 = (bf16[2,4,256,256]{3,2,1,0:T(8,128)(2,1)}, bf16[2,4,256,256]{3,2,1,0:T(8,128)(2,1)S(1)}, u32[]{:S(2)}) copy-start(bf16[2,4,256,256]{3,2,1,0:T(8,128)(2,1)S(1)} %collective-permute-done.14) | copy-start | bytes 3145732
  125.6 1.0 copy-start.5
